TPU v7x, 32 devices: a whole 2x2x4 slice. The times are simulated.
32 devices in a mesh: ctx: 4 (over y, core), uly: 8 (over z, x).
Axes of the slice: x: 2, y: 2, z: 4, core: 2. Of those that a mesh axis runs over, the one named last changes fastest.
Arguments:
- queries: bfloat16 [3072, 4096], P(('ctx', 'uly')), may hold values from -6 to 6
- keys: bfloat16 [3072, 4096], P(('ctx', 'uly')), may hold values from -6 to 6
- values: bfloat16 [3072, 4096], P(('ctx', 'uly')), may hold values from -6 to 6
- doc_ids: int32 [3072], P(('ctx', 'uly')), may hold values from 0 to 7, never falling along the last dimension, each value on 1 to 1536 neighbouring positions
- decay_rate: float32 [64], P('uly'), may hold values from 6.510417e-05 to 0.05
- norm_gain: float32 [4096], replicated, may hold values from 0.1 to 1.9
Outputs:
- attended: bfloat16 [3072, 4096], P(('ctx', 'uly'))
Inputs may be any that keep to these rules, and one draw needn't show every extreme that they name: doc_ids never fall along the sequence; every document has 1 to 1536 tokens and one has exactly that many.
All inputs are finite; a program needn't handle non-finite values.
Results may differ from a plain program's by a relative error of at most 0.0034.
Values may be sent and summed in bfloat16 or wider, within the bound.
No kernel may reach another device: no remote copies, remote signals or barrier semaphores. Data moves between devices by JAX's collectives and lax.ppermute only.
A program may use at most 64 MiB of HBM per device.

v0:
```python
import jax
import jax.numpy as jnp
from jax import lax
from jax.sharding import PartitionSpec as P

HD = 64
BLK = 256


def from_behind(value, axis, steps):
    count = lax.axis_size(axis)
    first, last = (max(0, -steps), min(count, count - steps))
    return lax.ppermute(value, axis, [(source, source + steps) for source in range(first, last)])


def state_pass(keys3, values3, ids, rate, blk, start_state, start_last):
    length, heads, width = keys3.shape
    count = length // blk
    kblocks = keys3.reshape(count, blk, heads, width)
    vblocks = values3.reshape(count, blk, heads, width)
    iblocks = ids.reshape(count, blk)
    position = jnp.arange(blk).astype(jnp.float32)

    def advance(carry, pieces):
        state, last = carry
        kblock, vblock, iblock = pieces
        endid = iblock[blk - 1]
        keep = jnp.where(endid == last, jnp.exp(-rate * blk), jnp.float32(0.0))
        weights = jnp.where(
            (iblock == endid)[None, :],
            jnp.exp(-rate[:, None] * (blk - 1 - position)[None, :]),
            jnp.float32(0.0),
        )
        scaled = kblock.astype(jnp.float32) * jnp.transpose(weights)[:, :, None]
        fresh = jnp.einsum(
            "shd,she->hde", scaled, vblock.astype(jnp.float32), precision=lax.Precision.HIGHEST
        )
        return ((keep[:, None, None] * state + fresh, endid), (state, last))

    final, entries = lax.scan(advance, (start_state, start_last), (kblocks, vblocks, iblocks))
    return (final, entries)


def block_output(qblock, kblock, vblock, iblock, state, last, rate):
    blk = qblock.shape[0]
    position = jnp.arange(blk).astype(jnp.float32)
    q32 = qblock.astype(jnp.float32)
    scores = jnp.einsum("thd,shd->hts", qblock, kblock, preferred_element_type=jnp.float32)
    diff = position[:, None] - position[None, :]
    mask = (diff >= 0) & (iblock[:, None] == iblock[None, :])
    weight = jnp.where(
        mask[None], jnp.exp(-rate[:, None, None] * jnp.maximum(diff, 0.0)[None]), jnp.float32(0.0)
    )
    probs = (scores * weight).astype(jnp.bfloat16)
    intra = jnp.einsum("hts,shd->thd", probs, vblock, preferred_element_type=jnp.float32)
    factor = (
        jnp.exp(-rate[None, :] * (position + 1.0)[:, None])
        * (iblock == last).astype(jnp.float32)[:, None]
    )
    inter = (
        jnp.einsum("thd,hde->the", q32, state, precision=lax.Precision.HIGHEST) * factor[:, :, None]
    )
    return intra + inter


def combine_with(rate):

    def combine(earlier, later):
        state_one, count_one, last_one = earlier
        state_two, count_two, last_two = later
        linked = (count_two == 0.0) | (last_one == last_two)
        factor = jnp.where(linked, jnp.exp(-rate * count_two), jnp.float32(0.0))
        merged = state_two + factor[:, None, None] * state_one
        return (merged, count_one + count_two, jnp.where(count_two > 0.0, last_two, last_one))

    return combine


def fetch_queries(queries):
    return lax.all_to_all(queries, "uly", split_axis=1, concat_axis=0, tiled=True)


def local(queries, keys, values, doc_ids, decay_rate, norm_gain):
    heads_here = decay_rate.shape[0]
    slice_ids = lax.all_gather(doc_ids, "uly", axis=0, tiled=True)
    length = slice_ids.shape[0]
    k_here, v_here = (
        lax.all_to_all(keys, "uly", split_axis=1, concat_axis=0, tiled=True),
        lax.all_to_all(values, "uly", split_axis=1, concat_axis=0, tiled=True),
    )
    q_here = fetch_queries(queries)
    k3 = k_here.reshape(length, heads_here, HD)
    v3 = v_here.reshape(length, heads_here, HD)
    zero_state = jnp.zeros((heads_here, HD, HD), jnp.float32)
    final, entries = state_pass(k3, v3, slice_ids, decay_rate, BLK, zero_state, jnp.int32(-1))
    element = (final[0], jnp.float32(length), final[1].astype(jnp.float32))
    combine = combine_with(decay_rate)

    def relay(step, incoming):
        return from_behind(combine(incoming, element), "ctx", 1)

    start = (zero_state, jnp.float32(0.0), jnp.float32(0.0))
    carried = lax.fori_loop(0, lax.axis_size("ctx") - 1, relay, start)
    q3 = q_here.reshape(length, heads_here, HD)
    count = length // BLK
    states, lasts = entries

    def one(pieces):
        qblock, kblock, vblock, iblock, state, last = pieces
        return block_output(qblock, kblock, vblock, iblock, state, last, decay_rate)

    raw = lax.map(
        one,
        (
            q3.reshape(count, BLK, heads_here, HD),
            k3.reshape(count, BLK, heads_here, HD),
            v3.reshape(count, BLK, heads_here, HD),
            slice_ids.reshape(count, BLK),
            states,
            lasts,
        ),
    )
    raw = raw.reshape(length, heads_here, HD)
    carry_state, carry_count, carry_last = carried
    position = jnp.arange(length).astype(jnp.float32)
    factor = (
        jnp.exp(-decay_rate[None, :] * (position + 1.0)[:, None])
        * (slice_ids.astype(jnp.float32) == carry_last).astype(jnp.float32)[:, None]
    )
    raw = (
        raw
        + jnp.einsum(
            "thd,hde->the", q3.astype(jnp.float32), carry_state, precision=lax.Precision.HIGHEST
        )
        * factor[:, :, None]
    )
    total_width = norm_gain.shape[0]
    partial_sq = jnp.sum(raw * raw, axis=(1, 2))
    total_sq = lax.psum(partial_sq, "uly")
    scale = lax.rsqrt(total_sq / total_width + 1e-06)
    gain_here = lax.dynamic_slice_in_dim(
        norm_gain, lax.axis_index("uly") * (heads_here * HD), heads_here * HD
    )
    normed = (raw * scale[:, None, None] * gain_here.reshape(1, heads_here, HD)).astype(
        jnp.bfloat16
    )
    return lax.all_to_all(
        normed.reshape(length, heads_here * HD), "uly", split_axis=0, concat_axis=1, tiled=True
    )


def solution(mesh):
    in_specs = (
        P(("ctx", "uly"), None),
        P(("ctx", "uly"), None),
        P(("ctx", "uly"), None),
        P(("ctx", "uly")),
        P("uly"),
        P(),
    )
    out_specs = P(("ctx", "uly"), None)
    return jax.shard_map(local, mesh=mesh, in_specs=in_specs, out_specs=out_specs, check_vma=False)
```

profile of v0, /device:TPU:0, one launch (start us, length us, event | category | flops | bytes accessed | tf_op | source)
XLA Modules:
  0.0 234.1 jit_solution(6035201677817020089)
XLA Ops:
  0.0 2.2 copy.88
  2.2 7.3 %all-to-all-start = ((bf16[96,8,512]{2,0,1:T(8,128)(2,1)}), bf16[96,8,512]{2,0,1:T(8,128)(2,1)S(1)}, u32[]{:S(2)}, u32[]{:S(2)}) async-start(bf16[96,8,512]{2,0,1:T(8,128)(2,1)} %bitcast.87), calls=%async_computation | async-start | bytes 1572864 | tf_op jit(solution)/shard_map/all_to_all | solution.py:89
  10.4 19.2 %all-to-all-done = bf16[96,8,512]{2,0,1:T(8,128)(2,1)S(1)} async-done(((bf16[96,8,512]{2,0,1:T(8,128)(2,1)}), bf16[96,8,512]{2,0,1:T(8,128)(2,1)S(1)}, u32[]{:S(2)}, u32[]{:S(2)}) %all-to-all-start) | async-done | bytes 786464 | tf_op jit(solution)/shard_map/all_to_all | solution.py:89
  29.6 3.6 %all-to-all-start.1 = ((bf16[96,8,512]{2,0,1:T(8,128)(2,1)}), bf16[96,8,512]{2,0,1:T(8,128)(2,1)S(1)}, u32[]{:S(2)}, u32[]{:S(2)}) async-start(bf16[96,8,512]{2,0,1:T(8,128)(2,1)} %bitcast.86), calls=%async_computation.1 | async-start | bytes 1572864 | tf_op jit(solution)/shard_map/all_to_all | solution.py:80
  34.2 19.3 %all-to-all-done.1 = bf16[96,8,512]{2,0,1:T(8,128)(2,1)S(1)} async-done(((bf16[96,8,512]{2,0,1:T(8,128)(2,1)}), bf16[96,8,512]{2,0,1:T(8,128)(2,1)S(1)}, u32[]{:S(2)}, u32[]{:S(2)}) %all-to-all-start.1) | async-done | bytes 786464 | tf_op jit(solution)/shard_map/all_to_all | solution.py:80
  53.5 4.2 %all-to-all-start.2 = ((bf16[96,8,512]{2,0,1:T(8,128)(2,1)}), bf16[96,8,512]{2,0,1:T(8,128)(2,1)}, u32[]{:S(2)}, u32[]{:S(2)}) async-start(bf16[96,8,512]{2,0,1:T(8,128)(2,1)} %bitcast.85), calls=%async_computation.2 | async-start | bytes 1572864 | tf_op jit(solution)/shard_map/all_to_all | solution.py:88
  59.3 18.4 %all-reduce = s32[768]{0:T(1024)S(1)} all-reduce(s32[768]{0:T(1024)S(1)} %dynamic-update-slice), channel_id=1, replica_groups=mesh['ctx'=4,'uly'=8] {'uly'}, use_global_device_ids=true, to_apply=%add | all-reduce | flops 768 | bytes 6144
  82.6 2.7 %copy.58 = bf16[3,256,8,64]{1,3,2,0:T(8,128)(2,1)} copy(bf16[3,256,8,64]{3,2,1,0:T(8,128)(2,1)} %reshape.357) | data formatting | bytes 1572864 | tf_op jit(solution)/shard_map/while | solution.py:112
  86.2 2.5 %reshape.358 = bf16[3,256,8,64]{3,2,1,0:T(8,128)(2,1)S(1)} reshape(bf16[8,96,512]{2,1,0:T(8,128)(2,1)} %bitcast.14) | data formatting | bytes 1572864 | tf_op jit(solution)/shard_map/reshape;reshape | solution.py:116
  90.3 14.6 %while.47 = (s32[]{:T(128)}, f32[8,64,64]{2,1,0:T(8,128)S(1)}, s32[]{:T(128)}, f32[3,8,64,64]{3,2,1,0:T(8,128)}, s32[3]{0:T(128)S(1)}, /*index=5*/s32[3,256]{1,0...) while((s32[]{:T(128)}, f32[8,64,64]{2,1,0:T(8,128)S(1)}, ...), condition=%wide.region_1.2_spmd.clone, body=%wide.region_0.1_spmd.clone.sunk | while | flops 101061392 | bytes 1333041 | solution.py:40
  105.0 53.4 %while.45 = (s32[]{:T(128)}, f32[3,256,8,64]{1,0,3,2:T(4,128)}, bf16[3,256,8,64]{1,3,2,0:T(8,128)(2,1)S(1)}, bf16[3,256,8,64]{1,3,2,0:T(8,128)(2,1)S(1)}, bf16[3...) while((s32[]{:T(128)}, f32[3,256,8,64]{1,0,3,2:T(4,128)}, ...), condition=%wide.region_3.4_spmd, body=%wide.region_2.3_spmd.sunk | while | flops 237638912 | bytes 5666997 | solution.py:112
  108.1 1.8 fusion.61
  110.5 12.3 %dynamic_update_slice.24 = f32[3,256,8,64]{1,0,3,2:T(4,128)} dynamic-update-slice(f32[3,256,8,64]{1,0,3,2:T(4,128)} %get-tuple-element.727, f32[1,256,8,64]{1,0,3,2:T(1,128)S(1)} %copy.90, s32[]{:T(128)S(6)} %copy.112, s32[]{:T(128)} %constant.94.clone.1..sunk, s32[]{:T(128)} %constant.94.clone.1..sunk, s32[]{:T(128)} %constant.94.clone.1..sunk) | dynamic-update-slice | bytes 1048580 | tf_op jit(solution)/shard_map/while/body/jit(dynamic_update_index_in_dim)/dynamic_update_slice | solution.py:112
  128.3 12.3 %dynamic_update_slice.24 = f32[3,256,8,64]{1,0,3,2:T(4,128)} dynamic-update-slice(f32[3,256,8,64]{1,0,3,2:T(4,128)} %get-tuple-element.727, f32[1,256,8,64]{1,0,3,2:T(1,128)S(1)} %copy.90, s32[]{:T(128)S(6)} %copy.112, s32[]{:T(128)} %constant.94.clone.1..sunk, s32[]{:T(128)} %constant.94.clone.1..sunk, s32[]{:T(128)} %constant.94.clone.1..sunk) | dynamic-update-slice | bytes 1048580 | tf_op jit(solution)/shard_map/while/body/jit(dynamic_update_index_in_dim)/dynamic_update_slice | solution.py:112
  146.1 12.3 %dynamic_update_slice.24 = f32[3,256,8,64]{1,0,3,2:T(4,128)} dynamic-update-slice(f32[3,256,8,64]{1,0,3,2:T(4,128)} %get-tuple-element.727, f32[1,256,8,64]{1,0,3,2:T(1,128)S(1)} %copy.90, s32[]{:T(128)S(6)} %copy.112, s32[]{:T(128)} %constant.94.clone.1..sunk, s32[]{:T(128)} %constant.94.clone.1..sunk, s32[]{:T(128)} %constant.94.clone.1..sunk) | dynamic-update-slice | bytes 1048580 | tf_op jit(solution)/shard_map/while/body/jit(dynamic_update_index_in_dim)/dynamic_update_slice | solution.py:112
  158.4 3.0 %reshape.347 = f32[768,8,64]{0,2,1:T(8,128)S(1)} reshape(f32[3,256,8,64]{1,0,3,2:T(4,128)} %get-tuple-element.320) | data formatting | bytes 3145728 | tf_op jit(solution)/shard_map/reshape | solution.py:123
  161.4 2.1 collective-permute-start.1
  165.3 19.0 %while.46 = (s32[]{:T(128)}, f32[8,64,64]{2,1,0:T(8,128)S(1)}, f32[]{:T(128)}, f32[]{:T(128)}, f32[8,1,1]{0,2,1:T(1,128)S(1)}, /*index=5*/f32[8,64,64]{2,1,0:T(8,128)S(1)}, f32[]{:T(128)}, s32[]{:T(128)}) while((s32[]{:T(128)}, f32[8,64,64]{2,1,0:T(8,128)S(1)}, f32[]{:T(128)}, f32[]{:T(128)}, f32[8,1,1]{0,2,1:T(1,128)S(1)}, ...), condition=%wide.region_5.6_spmd, body=%wide.region_4.5_spmd.sunk | while | flops 65555 | bytes 917743 | solution.py:103
  165.4 4.2 %collective-permute-start = (f32[8,64,64]{2,1,0:T(8,128)S(1)}, f32[8,64,64]{2,1,0:T(8,128)S(1)}, u32[]{:S(2)}, u32[]{:S(2)}) collective-permute-start(f32[8,64,64]{2,1,0:T(8,128)S(1)} %multiply_add_fusion.2), channel_id=1, source_target_pairs={{0,8},{8,16},{16,24},{1,9},{9,17},{17,25},{2,10},{10,18},{18,26},{... | collective-permute-start | bytes 393224 | tf_op jit(solution)/shard_map/while/body/eval_jaxpr/ppermute | solution.py:13
  170.9 4.5 %collective-permute-start = (f32[8,64,64]{2,1,0:T(8,128)S(1)}, f32[8,64,64]{2,1,0:T(8,128)S(1)}, u32[]{:S(2)}, u32[]{:S(2)}) collective-permute-start(f32[8,64,64]{2,1,0:T(8,128)S(1)} %multiply_add_fusion.2), channel_id=1, source_target_pairs={{0,8},{8,16},{16,24},{1,9},{9,17},{17,25},{2,10},{10,18},{18,26},{... | collective-permute-start | bytes 393224 | tf_op jit(solution)/shard_map/while/body/eval_jaxpr/ppermute | solution.py:13
  176.6 6.6 %collective-permute-start = (f32[8,64,64]{2,1,0:T(8,128)S(1)}, f32[8,64,64]{2,1,0:T(8,128)S(1)}, u32[]{:S(2)}, u32[]{:S(2)}) collective-permute-start(f32[8,64,64]{2,1,0:T(8,128)S(1)} %multiply_add_fusion.2), channel_id=1, source_target_pairs={{0,8},{8,16},{16,24},{1,9},{9,17},{17,25},{2,10},{10,18},{18,26},{... | collective-permute-start | bytes 393224 | tf_op jit(solution)/shard_map/while/body/eval_jaxpr/ppermute | solution.py:13
  184.4 2.1 multiply_reduce_fusion
  186.5 19.3 %psum.7 = f32[768]{0:T(1024)S(1)} all-reduce(f32[768]{0:T(1024)S(1)} %get-tuple-element.508), channel_id=1, replica_groups=mesh['ctx'=4,'uly'=8] {'uly'}, use_global_device_ids=true, to_apply=%region_7.8 | all-reduce | flops 768 | bytes 6144 | tf_op jit(solution)/shard_map/psum | solution.py:139
  209.2 23.9 %all_to_all.67 = bf16[8,96,512]{2,1,0:T(8,128)(2,1)S(1)} all-to-all(bf16[8,96,512]{2,1,0:T(8,128)(2,1)S(1)} %copy.65), channel_id=1, replica_groups=mesh['ctx'=4,'uly'=8] {'uly'}, dimensions={0} | all-to-all | bytes 1572864 | tf_op jit(solution)/shard_map/all_to_all | solution.py:147
  (111 shorter events, 43.4 us)
Async XLA Ops:
  0.0 9.4 %copy-start.3 = (bf16[96,4096]{1,0:T(8,128)(2,1)S(1)}, bf16[96,4096]{1,0:T(8,128)(2,1)}, u32[]{:S(2)}) copy-start(bf16[96,4096]{1,0:T(8,128)(2,1)} %param.12) | copy-start | bytes 2359300
  2.2 27.4 %all-to-all-start = ((bf16[96,8,512]{2,0,1:T(8,128)(2,1)}), bf16[96,8,512]{2,0,1:T(8,128)(2,1)S(1)}, u32[]{:S(2)}, u32[]{:S(2)}) async-start(bf16[96,8,512]{2,0,1:T(8,128)(2,1)} %bitcast.87), calls=%async_computation | async-start | bytes 1572864 | tf_op jit(solution)/shard_map/all_to_all | solution.py:89
  9.4 23.7 %copy-start.4 = (bf16[96,4096]{1,0:T(8,128)(2,1)S(1)}, bf16[96,4096]{1,0:T(8,128)(2,1)}, u32[]{:S(2)}) copy-start(bf16[96,4096]{1,0:T(8,128)(2,1)} %param.13) | copy-start | bytes 2359300
  29.6 23.9 %all-to-all-start.1 = ((bf16[96,8,512]{2,0,1:T(8,128)(2,1)}), bf16[96,8,512]{2,0,1:T(8,128)(2,1)S(1)}, u32[]{:S(2)}, u32[]{:S(2)}) async-start(bf16[96,8,512]{2,0,1:T(8,128)(2,1)} %bitcast.86), calls=%async_computation.1 | async-start | bytes 1572864 | tf_op jit(solution)/shard_map/all_to_all | solution.py:80
  33.2 24.7 %copy-start.7 = (u32[32]{0:T(128)S(1)}, u32[32]{0:T(128)}, u32[]{:S(2)}) copy-start(u32[32]{0:T(128)} %constant.105) | copy-start | bytes 388
  33.2 25.9 %copy-start.6 = (s32[96]{0:T(128)S(1)}, s32[96]{0:T(128)}, u32[]{:S(2)}) copy-start(s32[96]{0:T(128)} %param.15) | copy-start | bytes 1156
  33.2 45.4 %copy-start.5 = (f32[8]{0:T(128)S(1)}, f32[8]{0:T(128)}, u32[]{:S(2)}) copy-start(f32[8]{0:T(128)} %param.16) | copy-start | bytes 100
  53.5 32.7 %all-to-all-start.2 = ((bf16[96,8,512]{2,0,1:T(8,128)(2,1)}), bf16[96,8,512]{2,0,1:T(8,128)(2,1)}, u32[]{:S(2)}, u32[]{:S(2)}) async-start(bf16[96,8,512]{2,0,1:T(8,128)(2,1)} %bitcast.85), calls=%async_computation.2 | async-start | bytes 1572864 | tf_op jit(solution)/shard_map/all_to_all | solution.py:88
  88.7 1.7 copy-start
  158.4 5.1 %copy-start.1 = (bf16[8,96,512]{1,0,2:T(8,128)(2,1)S(1)}, bf16[8,96,512]{1,0,2:T(8,128)(2,1)}, u32[]{:S(2)}) copy-start(bf16[8,96,512]{1,0,2:T(8,128)(2,1)} %copy.63) | copy-start | bytes 2359300
  161.4 3.9 %collective-permute-start.1 = (f32[]{:T(128)}, f32[]{:T(128)}, u32[]{:S(2)}, u32[]{:S(2)}) collective-permute-start(f32[]{:T(128)} %convert_element_type.72), channel_id=1, source_target_pairs={{0,8},{8,16},{16,24},{1,9},{9,17},{17,25},{2,10},{10,18},{18,26},{... | collective-permute-start | bytes 20 | tf_op jit(solution)/shard_map/while/body/eval_jaxpr/ppermute | solution.py:13
  165.3 19.1 %copy-start.2 = (bf16[768,8,64]{0,2,1:T(8,128)(2,1)S(1)}, bf16[768,8,64]{0,2,1:T(8,128)(2,1)}, u32[]{:S(2)}) copy-start(bf16[768,8,64]{0,2,1:T(8,128)(2,1)} %reshape.348) | copy-start | bytes 2359300
  165.4 5.3 %collective-permute-start = (f32[8,64,64]{2,1,0:T(8,128)S(1)}, f32[8,64,64]{2,1,0:T(8,128)S(1)}, u32[]{:S(2)}, u32[]{:S(2)}) collective-permute-start(f32[8,64,64]{2,1,0:T(8,128)S(1)} %multiply_add_fusion.2), channel_id=1, source_target_pairs={{0,8},{8,16},{16,24},{1,9},{9,17},{17,25},{2,10},{10,18},{18,26},{... | collective-permute-start | bytes 393224 | tf_op jit(solution)/shard_map/while/body/eval_jaxpr/ppermute | solution.py:13
  170.9 5.6 %collective-permute-start = (f32[8,64,64]{2,1,0:T(8,128)S(1)}, f32[8,64,64]{2,1,0:T(8,128)S(1)}, u32[]{:S(2)}, u32[]{:S(2)}) collective-permute-start(f32[8,64,64]{2,1,0:T(8,128)S(1)} %multiply_add_fusion.2), channel_id=1, source_target_pairs={{0,8},{8,16},{16,24},{1,9},{9,17},{17,25},{2,10},{10,18},{18,26},{... | collective-permute-start | bytes 393224 | tf_op jit(solution)/shard_map/while/body/eval_jaxpr/ppermute | solution.py:13
  176.6 7.7 %collective-permute-start = (f32[8,64,64]{2,1,0:T(8,128)S(1)}, f32[8,64,64]{2,1,0:T(8,128)S(1)}, u32[]{:S(2)}, u32[]{:S(2)}) collective-permute-start(f32[8,64,64]{2,1,0:T(8,128)S(1)} %multiply_add_fusion.2), channel_id=1, source_target_pairs={{0,8},{8,16},{16,24},{1,9},{9,17},{17,25},{2,10},{10,18},{18,26},{... | collective-permute-start | bytes 393224 | tf_op jit(solution)/shard_map/while/body/eval_jaxpr/ppermute | solution.py:13
where the time goes:
time: 236 us; the launch traced here: 234 us
  local copies, waits for them, and re-layouts  67.7 us (29%)
  blocking collectives  61.6 us (26%)
  waiting for transfers between devices  39.9 us (17%)
  starting transfers between devices  32.4 us (14%)
  matrix products  16.1 us (7%)
  other arithmetic  9.35 us (4%)
  loops' own time  6.11 us (3%)
    dynamic_update_slice x6, local copies, waits for them, and re-layouts, local(): lax.map(one, (q3.reshape(count, BLK, heads_here, HD), k3.reshape(count, B...  38.6 us
    all_to_all x1, blocking collectives, local(): lax.all_to_all(normed.reshape(length, heads_here * HD), 'uly', split_axis...  23.9 us
    all_to_all x1, waiting for transfers between devices, fetch_queries(): lax.all_to_all(queries, 'uly', split_axis=1, concat_axis=0, tiled=True)  19.3 us
    psum x1, blocking collectives, local(): total_sq = lax.psum(partial_sq, 'uly')  19.3 us
    all_to_all x1, waiting for transfers between devices, local(): lax.all_to_all(values, 'uly', split_axis=1, concat_axis=0, tiled=True)  19.2 us
    unnamed x1, blocking collectives  18.4 us
    ppermute x4, starting transfers between devices, from_behind(): lax.ppermute(value, axis, [(source, source + steps) for source in range(f...  17.4 us
    all_to_all x1, starting transfers between devices, local(): lax.all_to_all(values, 'uly', split_axis=1, concat_axis=0, tiled=True)  7.25 us
  transfers between devices with their start and end apart: 7, of which 5 were waited for; matrix products, arithmetic and copies ran while one was open for 6% of the time, Pallas kernels for 0%

commit v1 on v0

v1 whole, which is shorter than its diff:
```python
import functools

import jax
import jax.numpy as jnp
from jax import lax
from jax.experimental import pallas as pl
from jax.experimental.pallas import tpu as pltpu
from jax.sharding import PartitionSpec as P

HD = 64
LANES = 2 * HD
NEVER = 1e9
BOTH_LAST = (((1,), (1,)), ((), ()))
BOTH_FIRST = (((0,), (0,)), ((), ()))


def rate_of(facts, head, here):
    return facts[head // here, head % here]


def pair_rate(facts, pair, here):
    lane = lax.broadcasted_iota(jnp.int32, (1, LANES), 1)
    return jnp.where(lane < HD, rate_of(facts, 2 * pair, here), rate_of(facts, 2 * pair + 1, here))


def ends_kernel(here, pairs, facts, idcol, k_ref, v_ref, out_ref):
    tokens = k_ref.shape[0]
    first = pl.program_id(0) * pairs
    lane = lax.broadcasted_iota(jnp.int32, (HD, LANES), 1)
    place = lax.broadcasted_iota(jnp.int32, (tokens, LANES), 0)
    ids = idcol[...]
    age = jnp.where(ids == ids[tokens - 1 :, :], (tokens - 1 - place).astype(jnp.float32), NEVER)
    for j in range(pairs):
        rate = pair_rate(facts, first + j, here)
        columns = slice(j * LANES, (j + 1) * LANES)
        weighted = k_ref[:, columns].astype(jnp.float32) * jnp.exp(-rate * age)
        high = weighted.astype(jnp.bfloat16)
        low = (weighted - high.astype(jnp.float32)).astype(jnp.bfloat16)
        v = v_ref[:, columns]
        both = lax.dot_general(high, v, BOTH_FIRST, preferred_element_type=jnp.float32)
        both += lax.dot_general(low, v, BOTH_FIRST, preferred_element_type=jnp.float32)
        out_ref[j * HD : (j + 1) * HD, :] = jnp.where(lane < HD, both[:HD], both[HD:]).astype(
            jnp.bfloat16
        )


def inner_kernel(here, pairs, facts, idcol, idrow, q_ref, k_ref, v_ref, out_ref):
    tokens = k_ref.shape[0]
    first = pl.program_id(0) * pairs
    lane = lax.broadcasted_iota(jnp.int32, (tokens, LANES), 1)
    t = lax.broadcasted_iota(jnp.int32, (tokens, tokens), 0)
    s = lax.broadcasted_iota(jnp.int32, (tokens, tokens), 1)
    seen = (t >= s) & (idcol[:, :tokens] == idrow[...])
    age = jnp.where(seen, (t - s).astype(jnp.float32), NEVER)
    for j in range(pairs):
        columns = slice(j * LANES, (j + 1) * LANES)
        q = q_ref[:, columns]
        zero = jnp.zeros_like(q)
        stacked = jnp.concatenate([jnp.where(lane < HD, q, zero), jnp.where(lane < HD, zero, q)], 0)
        scores = lax.dot_general(
            stacked, k_ref[:, columns], BOTH_LAST, preferred_element_type=jnp.float32
        )
        head = 2 * (first + j)
        weight = jnp.concatenate(
            [
                jnp.exp(-rate_of(facts, head, here) * age),
                jnp.exp(-rate_of(facts, head + 1, here) * age),
            ],
            0,
        )
        probs = (scores * weight).astype(jnp.bfloat16)
        got = jnp.dot(probs, v_ref[:, columns], preferred_element_type=jnp.float32)
        out_ref[:, columns] = jnp.where(lane < HD, got[:tokens], got[tokens:])


def scan_kernel(here, tokens, rows, facts, in_ref, out_ref):
    count = in_ref.shape[0]
    me = lax.axis_index("ctx") * lax.axis_size("uly") + lax.axis_index("uly")
    rate = pair_rate(facts, (me * rows) // HD, here)
    decay = jnp.exp(-rate * float(tokens))
    out_ref[0] = jnp.zeros(out_ref.shape[1:], out_ref.dtype)

    def step(i, state):
        linked = facts[i, here] == facts[jnp.maximum(i - 1, 0), here]
        state = in_ref[i].astype(jnp.float32) + jnp.where(linked, decay, 0.0) * state
        out_ref[i + 1] = state.astype(out_ref.dtype)
        return state

    lax.fori_loop(0, count - 1, step, jnp.zeros(in_ref.shape[1:], jnp.float32), unroll=min(count - 1, 31))


def norm_kernel(here, pairs, facts, idcol, q_ref, s_ref, inner_ref, gain, out_ref, raw):
    tokens = q_ref.shape[0]
    step = pl.program_id(0)
    first = step * pairs
    me = lax.axis_index("ctx") * lax.axis_size("uly") + lax.axis_index("uly")
    before = jnp.where(me > 0, facts[jnp.maximum(me - 1, 0), here], -1.0)
    lane = lax.broadcasted_iota(jnp.int32, (HD, LANES), 1)
    place = lax.broadcasted_iota(jnp.int32, (tokens, LANES), 0)
    age = jnp.where(idcol[...].astype(jnp.float32) == before, (place + 1).astype(jnp.float32), NEVER)
    for j in range(pairs):
        columns = slice(j * LANES, (j + 1) * LANES)
        state = s_ref[j * HD : (j + 1) * HD, :]
        zero = jnp.zeros_like(state)
        square = jnp.concatenate(
            [jnp.where(lane < HD, state, zero), jnp.where(lane < HD, zero, state)], 0
        )
        outer = jnp.dot(q_ref[:, columns], square, preferred_element_type=jnp.float32)
        rate = pair_rate(facts, first + j, here)
        raw[step, :, columns] = inner_ref[:, columns] + outer * jnp.exp(-rate * age)

    @pl.when(step == pl.num_programs(0) - 1)
    def _():
        parts, _, width = raw.shape
        total = jnp.zeros((tokens, LANES), jnp.float32)
        for part in range(parts):
            for j in range(width // LANES):
                value = raw[part, :, j * LANES : (j + 1) * LANES]
                total += value * value
        mean = jnp.sum(total, axis=1, keepdims=True) / float(parts * width)
        scale = jnp.broadcast_to(lax.rsqrt(mean + 1e-06), (tokens, LANES))
        for part in range(parts):
            for j in range(width // LANES):
                at = part * width + j * LANES
                value = raw[part, :, j * LANES : (j + 1) * LANES]
                out_ref[:, at : at + LANES] = (value * scale * gain[:, at : at + LANES]).astype(
                    jnp.bfloat16
                )


def local(queries, keys, values, doc_ids, decay_rate, norm_gain):
    tokens, width = queries.shape
    here = decay_rate.shape[0]
    axes = ("ctx", "uly")
    count = lax.axis_size("ctx") * lax.axis_size("uly")
    all_pairs = width // LANES
    steps = 4
    pairs = all_pairs // steps
    rows = all_pairs * HD // count

    own = jnp.concatenate([decay_rate, doc_ids[tokens - 1 :].astype(jnp.float32)])
    facts = lax.all_to_all(
        jnp.broadcast_to(own[None, :], (count, here + 1)), axes, split_axis=0, concat_axis=0, tiled=True
    )
    idcol = jnp.broadcast_to(doc_ids[:, None], (tokens, LANES))
    idrow = doc_ids[None, :]

    smem = pl.BlockSpec(memory_space=pltpu.SMEM)
    whole = lambda shape: pl.BlockSpec(shape, lambda i: (0,) * len(shape))
    part = pl.BlockSpec((tokens, pairs * LANES), lambda i: (0, i))
    state_part = pl.BlockSpec((pairs * HD, LANES), lambda i: (i, 0))
    params = pltpu.CompilerParams(vmem_limit_bytes=32 * 1024 * 1024)

    ends = pl.pallas_call(
        functools.partial(ends_kernel, here, pairs),
        grid=(steps,),
        in_specs=[smem, whole((tokens, LANES)), part, part],
        out_specs=state_part,
        out_shape=jax.ShapeDtypeStruct((all_pairs * HD, LANES), jnp.bfloat16),
        compiler_params=params,
        cost_estimate=pl.CostEstimate(flops=200_000_000, bytes_accessed=2_200_000, transcendentals=0),
        name="ends",
    )(facts, idcol, keys, values)
    pieces = lax.all_to_all(
        ends.reshape(count, rows, LANES), axes, split_axis=0, concat_axis=0, tiled=True
    )
    inner = pl.pallas_call(
        functools.partial(inner_kernel, here, pairs),
        grid=(steps,),
        in_specs=[smem, whole((tokens, LANES)), whole((1, tokens)), part, part, part],
        out_specs=part,
        out_shape=jax.ShapeDtypeStruct((tokens, width), jnp.float32),
        compiler_params=params,
        cost_estimate=pl.CostEstimate(
            flops=8_000_000_000, bytes_accessed=4_000_000, transcendentals=600_000
        ),
        name="inner",
    )(facts, idcol, idrow, queries, keys, values)
    before = pl.pallas_call(
        functools.partial(scan_kernel, here, tokens, rows),
        in_specs=[smem, pl.BlockSpec(memory_space=pltpu.VMEM)],
        out_specs=pl.BlockSpec(memory_space=pltpu.VMEM),
        out_shape=jax.ShapeDtypeStruct((count, rows, LANES), jnp.bfloat16),
        compiler_params=params,
        name="scan",
    )(facts, pieces)
    states = lax.all_to_all(before, axes, split_axis=0, concat_axis=0, tiled=True)
    return pl.pallas_call(
        functools.partial(norm_kernel, here, pairs),
        grid=(steps,),
        in_specs=[smem, whole((tokens, LANES)), part, state_part, part, whole((1, width))],
        out_specs=whole((tokens, width)),
        out_shape=jax.ShapeDtypeStruct((tokens, width), jnp.bfloat16),
        scratch_shapes=[pltpu.VMEM((steps, tokens, pairs * LANES), jnp.float32)],
        compiler_params=params,
        name="norm",
    )(facts, idcol, queries, states.reshape(all_pairs * HD, LANES), inner, norm_gain[None, :])


def solution(mesh):
    in_specs = (
        P(("ctx", "uly"), None),
        P(("ctx", "uly"), None),
        P(("ctx", "uly"), None),
        P(("ctx", "uly")),
        P("uly"),
        P(),
    )
    out_specs = P(("ctx", "uly"), None)
    return jax.shard_map(local, mesh=mesh, in_specs=in_specs, out_specs=out_specs, check_vma=False)
```

time: 236 us -> 64.8 us (0.27)
  local copies, waits for them, and re-layouts: 67.7 us -> 6.52 us
  starting transfers between devices: 32.4 us -> 2.61 us
  waiting for transfers between devices: 39.9 us -> 10.6 us
  blocking collectives: 61.6 us -> 32.4 us
  matrix products: 16.1 us -> 0 us
  Pallas kernels: 0 us -> 10.8 us
  other arithmetic: 9.35 us -> 0.73 us
  loops' own time: 6.11 us -> 0 us
    dynamic_update_slice x9 -> x0, local copies, waits for them, and re-layouts: 38.9 us -> none  [the longest x6 38.6 us: local(): lax.map(one, (q3.reshape(count, BLK, heads_here, HD), k3.reshape(count, B...]
    all_to_all x3 -> x1, waiting for transfers between devices: 38.6 us -> 10.6 us  [local(): lax.all_to_all(before, axes, split_axis=0, concat_axis=0, tiled=True)]
    psum x1 -> x0, blocking collectives: 19.3 us -> none  [local(): total_sq = lax.psum(partial_sq, 'uly')]
    unnamed x1 -> x0, blocking collectives: 18.4 us -> none
    ppermute x4 -> x0, starting transfers between devices: 17.4 us -> none  [from_behind(): lax.ppermute(value, axis, [(source, source + steps) for source in range(f...]
    dot_general x10 -> x0, matrix products: 16.1 us -> none  [the longest x3 5.52 us: block_output(): jnp.einsum('hts,shd->thd', probs, vblock, preferred_element_type=jnp.floa...]
    all_to_all x3 -> x1, starting transfers between devices: 15 us -> 2.61 us  [local(): lax.all_to_all(before, axes, split_axis=0, concat_axis=0, tiled=True)]
    pallas_call x0 -> x4, Pallas kernels: none -> 10.8 us  [the longest x1 3.42 us: local(): pl.pallas_call(functools.partial(inner_kernel, here, pairs), grid=(steps,...]
  transfers between devices with their start and end apart: 7 -> 1, of which waited for: 5 -> 1; matrix products, arithmetic and copies ran while one was open for 6% -> 0% of each run, Pallas kernels for 0% -> 5%
where the time goes in v1:
time: 64.8 us; the launch traced here: 64.4 us
  blocking collectives  32.4 us (50%)
  Pallas kernels  10.8 us (17%)
  waiting for transfers between devices  10.6 us (16%)
  local copies, waits for them, and re-layouts  6.52 us (10%)
  starting transfers between devices  2.61 us (4%)
  other arithmetic  0.73 us (1%)
  between operations  0.72 us (1%)
    all_to_all x1, blocking collectives, local(): lax.all_to_all(ends.reshape(count, rows, LANES), axes, split_axis=0, conc...  18.2 us
    all_to_all x1, blocking collectives, local(): lax.all_to_all(jnp.broadcast_to(own[None, :], (count, here + 1)), axes, s...  14.2 us
    all_to_all x1, waiting for transfers between devices, local(): lax.all_to_all(before, axes, split_axis=0, concat_axis=0, tiled=True)  10.6 us
    unnamed x14, local copies, waits for them, and re-layouts  4.55 us
    pallas_call x1, Pallas kernels, local(): pl.pallas_call(functools.partial(inner_kernel, here, pairs), grid=(steps,...  3.42 us
    pallas_call x1, Pallas kernels, local(): pl.pallas_call(functools.partial(norm_kernel, here, pairs), grid=(steps,)...  3.13 us
    all_to_all x1, starting transfers between devices, local(): lax.all_to_all(before, axes, split_axis=0, concat_axis=0, tiled=True)  2.61 us
    pallas_call x1, Pallas kernels, local(): pl.pallas_call(functools.partial(ends_kernel, here, pairs), grid=(steps,)...  2.45 us
  transfers between devices with their start and end apart: 1, of which 1 were waited for; matrix products, arithmetic and copies ran while one was open for 0% of the time, Pallas kernels for 5%

profile of v1, /device:TPU:0, one launch (start us, length us, event | category | flops | bytes accessed | tf_op | source)
XLA Modules:
  0.0 64.4 jit_solution(5455069676181031939)
XLA Ops:
  0.0 1.2 %slice.3 = s32[1]{0:T(128)} slice(s32[96]{0:T(128)} %param.9), slice={[95:96]} | slice | bytes 8 | tf_op jit(solution)/shard_map/slice | solution.py:141
  1.9 0.7 %pad_maximum_fusion = f32[9]{0:T(128)S(1)} fusion(f32[1]{0:T(128)S(6)} %convert_element_type.3, f32[8]{0:T(128)} %param.10), kind=kLoop, calls=%fused_computation | loop fusion | flops 9 | bytes 72 | tf_op jit(solution)/shard_map/concatenate | solution.py:141
  2.6 14.2 %all_to_all.18 = f32[32,1,9]{2,1,0:T(1,128)S(1)} all-to-all(f32[32,1,9]{2,1,0:T(1,128)S(1)} %broadcast_in_dim.8), channel_id=1, replica_groups=mesh['ctx'=4,'uly'=8] {'ctx','uly'}, dimensions={0} | all-to-all | bytes 2304 | tf_op jit(solution)/shard_map/all_to_all | solution.py:142
  16.9 0.7 %broadcast_in_dim.9.idcol = s32[96,128]{1,0:T(8,128)S(1)} broadcast(s32[96]{0:T(128)} %param.9), dimensions={0} | broadcast | bytes 49536 | tf_op jit(solution)/shard_map/broadcast_in_dim | solution.py:145
  17.6 0.0 copy-start.1
  17.6 1.1 %copy-done.1 = bf16[96,4096]{1,0:T(8,128)(2,1)S(1)} copy-done((bf16[96,4096]{1,0:T(8,128)(2,1)S(1)}, bf16[96,4096]{1,0:T(8,128)(2,1)}, u32[]{:S(2)}) %copy-start.1) | copy-done | bytes 786456
  18.7 0.0 copy-start.3
  18.7 1.1 %copy-done.3 = bf16[96,4096]{1,0:T(8,128)(2,1)S(1)} copy-done((bf16[96,4096]{1,0:T(8,128)(2,1)S(1)}, bf16[96,4096]{1,0:T(8,128)(2,1)}, u32[]{:S(2)}) %copy-start.3) | copy-done | bytes 786456
  19.9 2.5 %ends.1 = bf16[2048,128]{1,0:T(8,128)(2,1)S(1)} custom-call(f32[32,9]{1,0:T(8,128)S(1)} %bitcast.7, s32[96,128]{1,0:T(8,128)S(1)} %broadcast_in_dim.9.idcol, bf16[96,4096]{1,0:T(8,128)(2,1)S(1)} %copy-done.1, bf16[96,4096]{1,0:T(8,128)(2,1)S(1)} %copy-done.3), custom_call_target="tpu_custom_call" | custom-call | flops 200000000 | bytes 2200000 | tf_op jit(solution)/shard_map/ends/pallas_call | solution.py:154
  22.3 0.0 copy-start
  22.3 0.0 copy-start.6
  22.3 18.2 %all_to_all.19.in_ref = bf16[32,64,128]{2,1,0:T(8,128)(2,1)S(1)} all-to-all(bf16[32,64,128]{2,1,0:T(8,128)(2,1)S(1)} %bitcast.6), channel_id=1, replica_groups=mesh['ctx'=4,'uly'=8] {'ctx','uly'}, dimensions={0} | all-to-all | bytes 1048576 | tf_op jit(solution)/shard_map/all_to_all | solution.py:164
  40.5 1.8 %scan.1 = bf16[32,64,128]{2,1,0:T(8,128)(2,1)} custom-call(f32[32,9]{1,0:T(8,128)S(1)} %bitcast.8, bf16[32,64,128]{2,1,0:T(8,128)(2,1)S(1)} %all_to_all.19.in_ref), custom_call_target="tpu_custom_call" | custom-call | tf_op jit(solution)/shard_map/scan/pallas_call | solution.py:179
  42.3 2.6 %all-to-all-start.2 = ((bf16[32,64,128]{2,1,0:T(8,128)(2,1)}), bf16[32,64,128]{2,1,0:T(8,128)(2,1)S(1)}, u32[]{:S(2)}, u32[]{:S(2)}) async-start(bf16[32,64,128]{2,1,0:T(8,128)(2,1)} %scan.1), calls=%async_computation.2 | async-start | bytes 1048576 | tf_op jit(solution)/shard_map/all_to_all | solution.py:187
  44.9 0.0 copy-done
  44.9 0.0 copy-done.6
  44.9 0.0 copy-start.2
  45.0 1.1 %copy-done.2 = bf16[96,4096]{1,0:T(8,128)(2,1)S(1)} copy-done((bf16[96,4096]{1,0:T(8,128)(2,1)S(1)}, bf16[96,4096]{1,0:T(8,128)(2,1)}, u32[]{:S(2)}) %copy-start.2) | copy-done | bytes 786456
  46.1 0.0 copy-start.4
  46.1 1.1 %copy-done.4 = bf16[96,4096]{1,0:T(8,128)(2,1)S(1)} copy-done((bf16[96,4096]{1,0:T(8,128)(2,1)S(1)}, bf16[96,4096]{1,0:T(8,128)(2,1)}, u32[]{:S(2)}) %copy-start.4) | copy-done | bytes 786456
  47.2 3.4 %inner.1.inner_ref = f32[96,4096]{1,0:T(8,128)S(1)} custom-call(f32[32,9]{1,0:T(8,128)S(1)} %bitcast.9, s32[96,128]{1,0:T(8,128)S(1)} %broadcast_in_dim.9.idcol, s32[1,96]{1,0:T(1,128)S(1)} %bitcast.12, bf16[96,4096]{1,0:T(8,128)(2,1)S(1)} %copy-done, bf16[96,4096]{1,0:T(8,128)(2,1)S(1)} %copy-done.2, bf16[96,4096]{1,0:T(8,128)(2,1)S(1)} %copy-done.4), custom_call_target="tpu_custom_call" | custom-call | flops 8000000000 | bytes 4000000 | tf_op jit(solution)/shard_map/inner/pallas_call | solution.py:167
  50.6 10.6 %all-to-all-done.2 = bf16[32,64,128]{2,1,0:T(8,128)(2,1)S(1)} async-done(((bf16[32,64,128]{2,1,0:T(8,128)(2,1)}), bf16[32,64,128]{2,1,0:T(8,128)(2,1)S(1)}, u32[]{:S(2)}, u32[]{:S(2)}) %all-to-all-start.2) | async-done | bytes 524320 | tf_op jit(solution)/shard_map/all_to_all | solution.py:187
  61.3 0.0 copy-done.5
  61.3 3.1 %norm.1 = bf16[96,4096]{1,0:T(8,128)(2,1)} custom-call(f32[32,9]{1,0:T(8,128)S(1)} %bitcast.10, s32[96,128]{1,0:T(8,128)S(1)} %broadcast_in_dim.9.idcol, bf16[96,4096]{1,0:T(8,128)(2,1)S(1)} %copy-done, bf16[2048,128]{1,0:T(8,128)(2,1)S(1)} %bitcast.5, f32[96,4096]{1,0:T(8,128)S(1)} %inner.1.inner_ref, f32[1,4096]{1,0:T(1,128)S(1)} %bitcast.11), custom_call_target="tpu_custom_call" | custom-call | tf_op jit(solution)/shard_map/norm/pallas_call | solution.py:188
  (2 shorter events, 0.0 us)
Async XLA Ops:
  17.6 1.1 %copy-start.1 = (bf16[96,4096]{1,0:T(8,128)(2,1)S(1)}, bf16[96,4096]{1,0:T(8,128)(2,1)}, u32[]{:S(2)}) copy-start(bf16[96,4096]{1,0:T(8,128)(2,1)} %k_ref.3) | copy-start | bytes 2359300
  18.7 1.1 %copy-start.3 = (bf16[96,4096]{1,0:T(8,128)(2,1)S(1)}, bf16[96,4096]{1,0:T(8,128)(2,1)}, u32[]{:S(2)}) copy-start(bf16[96,4096]{1,0:T(8,128)(2,1)} %v_ref.3) | copy-start | bytes 2359300
  22.3 22.6 %copy-start = (bf16[96,4096]{1,0:T(8,128)(2,1)S(1)}, bf16[96,4096]{1,0:T(8,128)(2,1)}, u32[]{:S(2)}) copy-start(bf16[96,4096]{1,0:T(8,128)(2,1)} %q_ref.3) | copy-start | bytes 2359300
  22.3 22.6 %copy-start.6 = (s32[96]{0:T(128)S(1)}, s32[96]{0:T(128)}, u32[]{:S(2)}) copy-start(s32[96]{0:T(128)} %param.9) | copy-start | bytes 1156
  42.3 19.0 %all-to-all-start.2 = ((bf16[32,64,128]{2,1,0:T(8,128)(2,1)}), bf16[32,64,128]{2,1,0:T(8,128)(2,1)S(1)}, u32[]{:S(2)}, u32[]{:S(2)}) async-start(bf16[32,64,128]{2,1,0:T(8,128)(2,1)} %scan.1), calls=%async_computation.2 | async-start | bytes 1048576 | tf_op jit(solution)/shard_map/all_to_all | solution.py:187
  44.9 1.1 %copy-start.2 = (bf16[96,4096]{1,0:T(8,128)(2,1)S(1)}, bf16[96,4096]{1,0:T(8,128)(2,1)}, u32[]{:S(2)}) copy-start(bf16[96,4096]{1,0:T(8,128)(2,1)} %k_ref.3) | copy-start | bytes 2359300
  46.1 1.1 %copy-start.4 = (bf16[96,4096]{1,0:T(8,128)(2,1)S(1)}, bf16[96,4096]{1,0:T(8,128)(2,1)}, u32[]{:S(2)}) copy-start(bf16[96,4096]{1,0:T(8,128)(2,1)} %v_ref.3) | copy-start | bytes 2359300
  47.2 14.1 %copy-start.5 = (f32[4096]{0:T(1024)S(1)}, f32[4096]{0:T(1024)}, u32[]{:S(2)}) copy-start(f32[4096]{0:T(1024)} %param.11) | copy-start | bytes 49156

commit v2 on v1

v2 whole, which is shorter than its diff:
```python
import functools

import jax
import jax.numpy as jnp
from jax import lax
from jax.experimental import pallas as pl
from jax.experimental.pallas import tpu as pltpu
from jax.sharding import PartitionSpec as P

HD = 64
LANES = 2 * HD
NEVER = 1e9
BOTH_LAST = (((1,), (1,)), ((), ()))
BOTH_FIRST = (((0,), (0,)), ((), ()))


def rate_of(facts, head, here):
    return facts[head // here, head % here]


def pair_rate(facts, pair, here):
    lane = lax.broadcasted_iota(jnp.int32, (1, LANES), 1)
    return jnp.where(lane < HD, rate_of(facts, 2 * pair, here), rate_of(facts, 2 * pair + 1, here))


def facts_kernel(rates, ids, out_ref):
    lane = lax.broadcasted_iota(jnp.int32, out_ref.shape, 1)
    here = rates.shape[0]
    row = jnp.where(lane == here, ids[ids.shape[0] - 1].astype(jnp.float32), 0.0)
    for j in range(here):
        row = jnp.where(lane == j, rates[j], row)
    out_ref[...] = row


def turn_kernel(ids, k_ref, turned, idrow, idcol):
    tokens, width = k_ref.shape
    fill = jnp.full((1, LANES - tokens), -1.0, jnp.float32)
    row = jnp.concatenate([ids[...].astype(jnp.float32), fill], 1)
    idrow[...] = jnp.broadcast_to(row, idrow.shape)
    idcol[...] = jnp.transpose(jnp.broadcast_to(row, (LANES, LANES)))[:tokens]
    blank = jnp.zeros((LANES - tokens, LANES), jnp.float32)
    for j in range(width // LANES):
        columns = slice(j * LANES, (j + 1) * LANES)
        block = jnp.concatenate([k_ref[:, columns].astype(jnp.float32), blank], 0)
        turned[columns, :] = jnp.transpose(block)


def ends_kernel(here, facts, idrow, turned, v_ref, out_ref):
    tokens, width = v_ref.shape
    lane = lax.broadcasted_iota(jnp.int32, (HD, LANES), 1)
    place = lax.broadcasted_iota(jnp.int32, idrow.shape, 1)
    ids = idrow[...]
    last = ids[:, tokens - 1 : tokens]
    age = jnp.where(ids == last, (tokens - 1 - place).astype(jnp.float32), NEVER)
    blank = jnp.zeros((LANES - tokens, LANES), jnp.bfloat16)
    for j in range(width // LANES):
        weighted = []
        for head in (2 * j, 2 * j + 1):
            weight = jnp.exp(-rate_of(facts, head, here) * age)
            keys = turned[head * HD : (head + 1) * HD, :].reshape(HD // 8, 8, LANES)
            weighted.append((keys * weight[None]).reshape(HD, LANES))
        weighted = jnp.concatenate(weighted, 0)
        high = weighted.astype(jnp.bfloat16)
        low = (weighted - high.astype(jnp.float32)).astype(jnp.bfloat16)
        v = v_ref[:, j * LANES : (j + 1) * LANES]
        both = jnp.dot(
            jnp.concatenate([high, low], 1),
            jnp.concatenate([v, blank, v, blank], 0),
            preferred_element_type=jnp.float32,
        )
        out_ref[j * HD : (j + 1) * HD, :] = jnp.where(lane < HD, both[:HD], both[HD:]).astype(
            jnp.bfloat16
        )


def inner_kernel(here, pairs, facts, idcol, idrow, q_ref, k_ref, v_ref, out_ref):
    tokens = k_ref.shape[0]
    first = pl.program_id(0) * pairs
    lane = lax.broadcasted_iota(jnp.int32, (tokens, LANES), 1)
    t = lax.broadcasted_iota(jnp.int32, (tokens, tokens), 0)
    s = lax.broadcasted_iota(jnp.int32, (tokens, tokens), 1)
    seen = (t >= s) & (idcol[:, :tokens] == idrow[:1, :tokens])
    age = jnp.where(seen, (t - s).astype(jnp.float32), NEVER)
    for j in range(pairs):
        columns = slice(j * LANES, (j + 1) * LANES)
        q = q_ref[:, columns]
        zero = jnp.zeros_like(q)
        stacked = jnp.concatenate([jnp.where(lane < HD, q, zero), jnp.where(lane < HD, zero, q)], 0)
        scores = lax.dot_general(
            stacked, k_ref[:, columns], BOTH_LAST, preferred_element_type=jnp.float32
        )
        head = 2 * (first + j)
        weight = jnp.concatenate(
            [
                jnp.exp(-rate_of(facts, head, here) * age),
                jnp.exp(-rate_of(facts, head + 1, here) * age),
            ],
            0,
        )
        probs = (scores * weight).astype(jnp.bfloat16)
        got = jnp.dot(probs, v_ref[:, columns], preferred_element_type=jnp.float32)
        out_ref[:, columns] = jnp.where(lane < HD, got[:tokens], got[tokens:])


def scan_kernel(here, tokens, rows, facts, in_ref, out_ref):
    count = in_ref.shape[0]
    me = lax.axis_index("ctx") * lax.axis_size("uly") + lax.axis_index("uly")
    rate = pair_rate(facts, (me * rows) // HD, here)
    decay = jnp.exp(-rate * float(tokens))
    out_ref[0] = jnp.zeros(out_ref.shape[1:], out_ref.dtype)

    def step(i, state):
        linked = facts[i, here] == facts[jnp.maximum(i - 1, 0), here]
        state = in_ref[i].astype(jnp.float32) + jnp.where(linked, decay, 0.0) * state
        out_ref[i + 1] = state.astype(out_ref.dtype)
        return state

    lax.fori_loop(0, count - 1, step, jnp.zeros(in_ref.shape[1:], jnp.float32), unroll=min(count - 1, 31))


def norm_kernel(here, facts, idcol, q_ref, s_ref, inner_ref, gain, out_ref, raw):
    tokens, width = q_ref.shape
    me = lax.axis_index("ctx") * lax.axis_size("uly") + lax.axis_index("uly")
    before = jnp.where(me > 0, facts[jnp.maximum(me - 1, 0), here], -1.0)
    lane = lax.broadcasted_iota(jnp.int32, (HD, LANES), 1)
    place = lax.broadcasted_iota(jnp.int32, (tokens, LANES), 0)
    age = jnp.where(idcol[...] == before, (place + 1).astype(jnp.float32), NEVER)
    total = jnp.zeros((tokens, LANES), jnp.float32)
    for j in range(width // LANES):
        columns = slice(j * LANES, (j + 1) * LANES)
        state = s_ref[j * HD : (j + 1) * HD, :]
        zero = jnp.zeros_like(state)
        square = jnp.concatenate(
            [jnp.where(lane < HD, state, zero), jnp.where(lane < HD, zero, state)], 0
        )
        outer = jnp.dot(q_ref[:, columns], square, preferred_element_type=jnp.float32)
        rate = pair_rate(facts, j, here)
        value = inner_ref[:, columns] + outer * jnp.exp(-rate * age)
        total += value * value
        raw[:, columns] = value
    mean = jnp.sum(total, axis=1, keepdims=True) / float(width)
    scale = jnp.broadcast_to(lax.rsqrt(mean + 1e-06), (tokens, LANES))
    for j in range(width // LANES):
        columns = slice(j * LANES, (j + 1) * LANES)
        out_ref[:, columns] = (raw[:, columns] * scale * gain[:, columns]).astype(jnp.bfloat16)


def local(queries, keys, values, doc_ids, decay_rate, norm_gain):
    tokens, width = queries.shape
    here = decay_rate.shape[0]
    axes = ("ctx", "uly")
    count = lax.axis_size("ctx") * lax.axis_size("uly")
    all_pairs = width // LANES
    steps = 4
    pairs = all_pairs // steps
    rows = all_pairs * HD // count

    smem = pl.BlockSpec(memory_space=pltpu.SMEM)
    vmem = pl.BlockSpec(memory_space=pltpu.VMEM)
    whole = lambda shape: pl.BlockSpec(shape, lambda i: (0,) * len(shape))
    part = pl.BlockSpec((tokens, pairs * LANES), lambda i: (0, i))
    params = pltpu.CompilerParams(vmem_limit_bytes=32 * 1024 * 1024)

    own = pl.pallas_call(
        facts_kernel,
        in_specs=[smem, smem],
        out_specs=vmem,
        out_shape=jax.ShapeDtypeStruct((count, LANES), jnp.float32),
        compiler_params=params,
        name="facts",
    )(decay_rate, doc_ids)
    facts = lax.all_to_all(own, axes, split_axis=0, concat_axis=0, tiled=True)
    turned, idrow, idcol = pl.pallas_call(
        turn_kernel,
        in_specs=[vmem, vmem],
        out_specs=[vmem, vmem, vmem],
        out_shape=[
            jax.ShapeDtypeStruct((width, LANES), jnp.float32),
            jax.ShapeDtypeStruct((8, LANES), jnp.float32),
            jax.ShapeDtypeStruct((tokens, LANES), jnp.float32),
        ],
        compiler_params=params,
        cost_estimate=pl.CostEstimate(flops=0, bytes_accessed=12_000_000, transcendentals=0),
        name="turn",
    )(doc_ids[None, :], keys)
    ends = pl.pallas_call(
        functools.partial(ends_kernel, here),
        in_specs=[smem, vmem, vmem, vmem],
        out_specs=vmem,
        out_shape=jax.ShapeDtypeStruct((all_pairs * HD, LANES), jnp.bfloat16),
        compiler_params=params,
        name="ends",
    )(facts, idrow, turned, values)
    pieces = lax.all_to_all(
        ends.reshape(count, rows, LANES), axes, split_axis=0, concat_axis=0, tiled=True
    )
    inner = pl.pallas_call(
        functools.partial(inner_kernel, here, pairs),
        grid=(steps,),
        in_specs=[smem, whole((tokens, LANES)), whole((8, LANES)), part, part, part],
        out_specs=part,
        out_shape=jax.ShapeDtypeStruct((tokens, width), jnp.float32),
        compiler_params=params,
        cost_estimate=pl.CostEstimate(
            flops=8_000_000_000, bytes_accessed=4_000_000, transcendentals=600_000
        ),
        name="inner",
    )(facts, idcol, idrow, queries, keys, values)
    before = pl.pallas_call(
        functools.partial(scan_kernel, here, tokens, rows),
        in_specs=[smem, vmem],
        out_specs=vmem,
        out_shape=jax.ShapeDtypeStruct((count, rows, LANES), jnp.bfloat16),
        compiler_params=params,
        name="scan",
    )(facts, pieces)
    states = lax.all_to_all(before, axes, split_axis=0, concat_axis=0, tiled=True)
    return pl.pallas_call(
        functools.partial(norm_kernel, here),
        in_specs=[smem, vmem, vmem, vmem, vmem, vmem],
        out_specs=vmem,
        out_shape=jax.ShapeDtypeStruct((tokens, width), jnp.bfloat16),
        scratch_shapes=[pltpu.VMEM((tokens, width), jnp.float32)],
        compiler_params=params,
        name="norm",
    )(facts, idcol, queries, states.reshape(all_pairs * HD, LANES), inner, norm_gain[None, :])


def solution(mesh):
    in_specs = (
        P(("ctx", "uly"), None),
        P(("ctx", "uly"), None),
        P(("ctx", "uly"), None),
        P(("ctx", "uly")),
        P("uly"),
        P(),
    )
    out_specs = P(("ctx", "uly"), None)
    return jax.shard_map(local, mesh=mesh, in_specs=in_specs, out_specs=out_specs, check_vma=False)
```

time: 64.8 us -> 61.5 us (0.949)
  blocking collectives: 32.4 us -> 18.2 us
  starting transfers between devices: 2.61 us -> 9.9 us
  waiting for transfers between devices: 10.6 us -> 15.5 us
  other arithmetic: 0.73 us -> 0 us
    all_to_all x1 -> x0, blocking collectives: 14.2 us -> none  [local(): lax.all_to_all(jnp.broadcast_to(own[None, :], (count, here + 1)), axes, s...]
    all_to_all x0 -> x1, starting transfers between devices: none -> 7.3 us  [local(): facts = lax.all_to_all(own, axes, split_axis=0, concat_axis=0, tiled=True)]
    all_to_all x0 -> x1, waiting for transfers between devices: none -> 4.87 us  [local(): facts = lax.all_to_all(own, axes, split_axis=0, concat_axis=0, tiled=True)]
    unnamed x14 -> x18, local copies, waits for them, and re-layouts: 4.55 us -> 6.5 us
    slice x1 -> x0, local copies, waits for them, and re-layouts: 1.24 us -> none  [local(): doc_ids[tokens - 1:].astype(jnp.float32)]
    broadcast_in_dim x2 -> x0, local copies, waits for them, and re-layouts: 0.74 us -> none  [the longest x1 0.73 us: local(): idcol = jnp.broadcast_to(doc_ids[:, None], (tokens, LANES))]
    concatenate x1 -> x0, other arithmetic: 0.73 us -> none  [local(): jnp.concatenate([decay_rate, doc_ids[tokens - 1:].astype(jnp.float32)])]
    pallas_call x2 -> x4, Pallas kernels: 5.58 us -> 5.69 us  [the longest x1 2.6 us: local(): pl.pallas_call(functools.partial(norm_kernel, here), in_specs=[smem, vmem...]
  transfers between devices with their start and end apart: 1 -> 2, of which waited for: 1 -> 2; matrix products, arithmetic and copies ran while one was open for 0% -> 0% of each run, Pallas kernels for 5% -> 6%
where the time goes in v2:
time: 61.5 us; the launch traced here: 61.1 us
  blocking collectives  18.2 us (30%)
  waiting for transfers between devices  15.5 us (25%)
  Pallas kernels  10.9 us (18%)
  starting transfers between devices  9.9 us (16%)
  local copies, waits for them, and re-layouts  6.5 us (11%)
    all_to_all x1, blocking collectives, local(): lax.all_to_all(ends.reshape(count, rows, LANES), axes, split_axis=0, conc...  18.2 us
    all_to_all x1, waiting for transfers between devices, local(): lax.all_to_all(before, axes, split_axis=0, concat_axis=0, tiled=True)  10.6 us
    all_to_all x1, starting transfers between devices, local(): facts = lax.all_to_all(own, axes, split_axis=0, concat_axis=0, tiled=True)  7.3 us
    unnamed x18, local copies, waits for them, and re-layouts  6.5 us
    all_to_all x1, waiting for transfers between devices, local(): facts = lax.all_to_all(own, axes, split_axis=0, concat_axis=0, tiled=True)  4.87 us
    pallas_call x1, Pallas kernels, local(): pl.pallas_call(functools.partial(inner_kernel, here, pairs), grid=(steps,...  3.42 us
    all_to_all x1, starting transfers between devices, local(): lax.all_to_all(before, axes, split_axis=0, concat_axis=0, tiled=True)  2.61 us
    pallas_call x1, Pallas kernels, local(): pl.pallas_call(functools.partial(norm_kernel, here), in_specs=[smem, vmem...  2.6 us
  transfers between devices with their start and end apart: 2, of which 2 were waited for; matrix products, arithmetic and copies ran while one was open for 0% of the time, Pallas kernels for 6%

profile of v2, /device:TPU:0, one launch (start us, length us, event | category | flops | bytes accessed | tf_op | source)
XLA Modules:
  0.0 61.1 jit_solution(4860694933915476132)
XLA Ops:
  0.0 0.7 %copy-done.6 = s32[96]{0:T(128)S(1)} copy-done((s32[96]{0:T(128)S(1)}, s32[96]{0:T(128)}, u32[]{:S(2)}) %copy-start.6) | copy-done | bytes 408
  0.7 0.0 copy-start.8
  0.7 0.7 %copy-done.8 = f32[8]{0:T(128)S(1)} copy-done((f32[8]{0:T(128)S(1)}, f32[8]{0:T(128)}, u32[]{:S(2)}) %copy-start.8) | copy-done | bytes 56
  1.3 1.2 %facts.1 = f32[32,128]{1,0:T(8,128)} custom-call(f32[8]{0:T(128)S(1)} %copy-done.8, s32[96]{0:T(128)S(1)} %copy-done.6), custom_call_target="tpu_custom_call" | custom-call | tf_op jit(solution)/shard_map/facts/pallas_call | solution.py:164
  2.5 7.3 %all-to-all-start = ((f32[32,1,128]{2,1,0:T(1,128)}), f32[32,1,128]{2,1,0:T(1,128)S(1)}, u32[]{:S(2)}, u32[]{:S(2)}) async-start(f32[32,1,128]{2,1,0:T(1,128)} %bitcast.1), calls=%async_computation | async-start | bytes 32768 | tf_op jit(solution)/shard_map/all_to_all | solution.py:172
  9.8 0.0 copy-start.1
  9.8 1.1 %copy-done.1 = bf16[96,4096]{1,0:T(8,128)(2,1)S(1)} copy-done((bf16[96,4096]{1,0:T(8,128)(2,1)S(1)}, bf16[96,4096]{1,0:T(8,128)(2,1)}, u32[]{:S(2)}) %copy-start.1) | copy-done | bytes 786456
  10.9 0.7 %copy-done.7 = s32[96]{0:T(128)S(1)} copy-done((s32[96]{0:T(128)S(1)}, s32[96]{0:T(128)}, u32[]{:S(2)}) %copy-start.7) | copy-done | bytes 408
  11.6 0.4 turn.1
  11.9 4.9 %all-to-all-done = f32[32,1,128]{2,1,0:T(1,128)S(1)} async-done(((f32[32,1,128]{2,1,0:T(1,128)}), f32[32,1,128]{2,1,0:T(1,128)S(1)}, u32[]{:S(2)}, u32[]{:S(2)}) %all-to-all-start) | async-done | bytes 16416 | tf_op jit(solution)/shard_map/all_to_all | solution.py:172
  16.8 1.1 %copy-done.3 = bf16[96,4096]{1,0:T(8,128)(2,1)S(1)} copy-done((bf16[96,4096]{1,0:T(8,128)(2,1)S(1)}, bf16[96,4096]{1,0:T(8,128)(2,1)}, u32[]{:S(2)}) %copy-start.3) | copy-done | bytes 786456
  17.9 1.6 %ends.1 = bf16[2048,128]{1,0:T(8,128)(2,1)S(1)} custom-call(f32[32,128]{1,0:T(8,128)S(1)} %bitcast.10, f32[8,128]{1,0:T(8,128)S(1)} %get-tuple-element.9.idrow, f32[4096,128]{1,0:T(8,128)S(1)} %get-tuple-element.10.turned, bf16[96,4096]{1,0:T(8,128)(2,1)S(1)} %copy-done.3), custom_call_target="tpu_custom_call" | custom-call | tf_op jit(solution)/shard_map/ends/pallas_call | solution.py:186
  19.5 0.0 copy-start
  19.5 18.2 %all_to_all.21.in_ref = bf16[32,64,128]{2,1,0:T(8,128)(2,1)S(1)} all-to-all(bf16[32,64,128]{2,1,0:T(8,128)(2,1)S(1)} %bitcast.9), channel_id=1, replica_groups=mesh['ctx'=4,'uly'=8] {'ctx','uly'}, dimensions={0} | all-to-all | bytes 1048576 | tf_op jit(solution)/shard_map/all_to_all | solution.py:194
  37.7 1.8 %scan.1 = bf16[32,64,128]{2,1,0:T(8,128)(2,1)} custom-call(f32[32,128]{1,0:T(8,128)S(1)} %bitcast.11, bf16[32,64,128]{2,1,0:T(8,128)(2,1)S(1)} %all_to_all.21.in_ref), custom_call_target="tpu_custom_call" | custom-call | tf_op jit(solution)/shard_map/scan/pallas_call | solution.py:209
  39.5 2.6 %all-to-all-start.2 = ((bf16[32,64,128]{2,1,0:T(8,128)(2,1)}), bf16[32,64,128]{2,1,0:T(8,128)(2,1)S(1)}, u32[]{:S(2)}, u32[]{:S(2)}) async-start(bf16[32,64,128]{2,1,0:T(8,128)(2,1)} %scan.1), calls=%async_computation.2 | async-start | bytes 1048576 | tf_op jit(solution)/shard_map/all_to_all | solution.py:217
  42.1 0.0 copy-done
  42.1 0.0 copy-start.2
  42.1 1.1 %copy-done.2 = bf16[96,4096]{1,0:T(8,128)(2,1)S(1)} copy-done((bf16[96,4096]{1,0:T(8,128)(2,1)S(1)}, bf16[96,4096]{1,0:T(8,128)(2,1)}, u32[]{:S(2)}) %copy-start.2) | copy-done | bytes 786456
  43.3 1.1 %copy-done.4 = bf16[96,4096]{1,0:T(8,128)(2,1)S(1)} copy-done((bf16[96,4096]{1,0:T(8,128)(2,1)S(1)}, bf16[96,4096]{1,0:T(8,128)(2,1)}, u32[]{:S(2)}) %copy-start.4) | copy-done | bytes 786456
  44.4 3.4 %inner.1.inner_ref = f32[96,4096]{1,0:T(8,128)S(1)} custom-call(f32[32,128]{1,0:T(8,128)S(1)} %bitcast.12, f32[96,128]{1,0:T(8,128)S(1)} %get-tuple-element.8.idcol, f32[8,128]{1,0:T(8,128)S(1)} %get-tuple-element.9.idrow, bf16[96,4096]{1,0:T(8,128)(2,1)S(1)} %copy-done, bf16[96,4096]{1,0:T(8,128)(2,1)S(1)} %copy-done.2, bf16[96,4096]{1,0:T(8,128)(2,1)S(1)} %copy-done.4), custom_call_target="tpu_custom_call" | custom-call | flops 8000000000 | bytes 4000000 | tf_op jit(solution)/shard_map/inner/pallas_call | solution.py:197
  47.8 10.6 %all-to-all-done.2 = bf16[32,64,128]{2,1,0:T(8,128)(2,1)S(1)} async-done(((bf16[32,64,128]{2,1,0:T(8,128)(2,1)}), bf16[32,64,128]{2,1,0:T(8,128)(2,1)S(1)}, u32[]{:S(2)}, u32[]{:S(2)}) %all-to-all-start.2) | async-done | bytes 524320 | tf_op jit(solution)/shard_map/all_to_all | solution.py:217
  58.5 0.0 copy-done.5
  58.5 2.6 %norm.1 = bf16[96,4096]{1,0:T(8,128)(2,1)} custom-call(f32[32,128]{1,0:T(8,128)S(1)} %bitcast.13, f32[96,128]{1,0:T(8,128)S(1)} %get-tuple-element.8.idcol, bf16[96,4096]{1,0:T(8,128)(2,1)S(1)} %copy-done, bf16[2048,128]{1,0:T(8,128)(2,1)S(1)} %bitcast.8, f32[96,4096]{1,0:T(8,128)S(1)} %inner.1.inner_ref, f32[1,4096]{1,0:T(1,128)S(1)} %bitcast.14), custom_call_target="tpu_custom_call" | custom-call | tf_op jit(solution)/shard_map/norm/pallas_call | solution.py:218
  (5 shorter events, 0.0 us)
Async XLA Ops:
  0.0 0.7 %copy-start.6 = (s32[96]{0:T(128)S(1)}, s32[96]{0:T(128)}, u32[]{:S(2)}) copy-start(s32[96]{0:T(128)} %ids.1) | copy-start | bytes 1156
  0.7 0.7 %copy-start.8 = (f32[8]{0:T(128)S(1)}, f32[8]{0:T(128)}, u32[]{:S(2)}) copy-start(f32[8]{0:T(128)} %rates.1) | copy-start | bytes 100
  2.5 14.3 %all-to-all-start = ((f32[32,1,128]{2,1,0:T(1,128)}), f32[32,1,128]{2,1,0:T(1,128)S(1)}, u32[]{:S(2)}, u32[]{:S(2)}) async-start(f32[32,1,128]{2,1,0:T(1,128)} %bitcast.1), calls=%async_computation | async-start | bytes 32768 | tf_op jit(solution)/shard_map/all_to_all | solution.py:172
  9.8 1.1 %copy-start.1 = (bf16[96,4096]{1,0:T(8,128)(2,1)S(1)}, bf16[96,4096]{1,0:T(8,128)(2,1)}, u32[]{:S(2)}) copy-start(bf16[96,4096]{1,0:T(8,128)(2,1)} %k_ref.3) | copy-start | bytes 2359300
  10.9 0.7 %copy-start.7 = (s32[96]{0:T(128)S(1)}, s32[96]{0:T(128)}, u32[]{:S(2)}) copy-start(s32[96]{0:T(128)} %ids.1) | copy-start | bytes 1156
  16.8 1.1 %copy-start.3 = (bf16[96,4096]{1,0:T(8,128)(2,1)S(1)}, bf16[96,4096]{1,0:T(8,128)(2,1)}, u32[]{:S(2)}) copy-start(bf16[96,4096]{1,0:T(8,128)(2,1)} %v_ref.3) | copy-start | bytes 2359300
  19.5 22.6 %copy-start = (bf16[96,4096]{1,0:T(8,128)(2,1)S(1)}, bf16[96,4096]{1,0:T(8,128)(2,1)}, u32[]{:S(2)}) copy-start(bf16[96,4096]{1,0:T(8,128)(2,1)} %q_ref.3) | copy-start | bytes 2359300
  39.5 19.0 %all-to-all-start.2 = ((bf16[32,64,128]{2,1,0:T(8,128)(2,1)}), bf16[32,64,128]{2,1,0:T(8,128)(2,1)S(1)}, u32[]{:S(2)}, u32[]{:S(2)}) async-start(bf16[32,64,128]{2,1,0:T(8,128)(2,1)} %scan.1), calls=%async_computation.2 | async-start | bytes 1048576 | tf_op jit(solution)/shard_map/all_to_all | solution.py:217
  42.1 1.1 %copy-start.2 = (bf16[96,4096]{1,0:T(8,128)(2,1)S(1)}, bf16[96,4096]{1,0:T(8,128)(2,1)}, u32[]{:S(2)}) copy-start(bf16[96,4096]{1,0:T(8,128)(2,1)} %k_ref.3) | copy-start | bytes 2359300
  43.3 1.1 %copy-start.4 = (bf16[96,4096]{1,0:T(8,128)(2,1)S(1)}, bf16[96,4096]{1,0:T(8,128)(2,1)}, u32[]{:S(2)}) copy-start(bf16[96,4096]{1,0:T(8,128)(2,1)} %v_ref.3) | copy-start | bytes 2359300
  44.4 14.1 %copy-start.5 = (f32[4096]{0:T(1024)S(1)}, f32[4096]{0:T(1024)}, u32[]{:S(2)}) copy-start(f32[4096]{0:T(1024)} %param.11) | copy-start | bytes 49156

commit v3 on v2

v3 whole, which is shorter than its diff:
```python
import functools

import jax
import jax.numpy as jnp
from jax import lax
from jax.experimental import pallas as pl
from jax.experimental.pallas import tpu as pltpu
from jax.sharding import PartitionSpec as P

HD = 64
LANES = 2 * HD
NEVER = 1e9
BOTH_LAST = (((1,), (1,)), ((), ()))


def rate_of(facts, head, here):
    return facts[pl.ds(head // here, 1), head % here : head % here + 1]


def pair_rate(facts, pair, here):
    lane = lax.broadcasted_iota(jnp.int32, (1, LANES), 1)
    rates = []
    for head in (2 * pair, 2 * pair + 1):
        row = facts[pl.ds(lax.div(head, here), 1), :]
        rates.append(
            jnp.sum(jnp.where(lane == lax.rem(head, here), row, 0.0), axis=1, keepdims=True)
        )
    return jnp.where(lane < HD, rates[0], rates[1])


def turn_kernel(ids, k_ref, v_ref, turned, filled, idrow, idcol):
    tokens, width = k_ref.shape
    fill = jnp.full((1, LANES - tokens), -1.0, jnp.float32)
    row = jnp.concatenate([ids[...].astype(jnp.float32), fill], 1)
    idrow[...] = jnp.broadcast_to(row, idrow.shape)
    idcol[...] = jnp.transpose(jnp.broadcast_to(row, (LANES, LANES)))[:tokens]
    filled[:tokens, :] = v_ref[...]
    filled[tokens:, :] = jnp.zeros((LANES - tokens, width), filled.dtype)
    blank = jnp.zeros((LANES - tokens, LANES), jnp.float32)
    for j in range(width // LANES):
        columns = slice(j * LANES, (j + 1) * LANES)
        block = jnp.concatenate([k_ref[:, columns].astype(jnp.float32), blank], 0)
        turned[columns, :] = jnp.transpose(block)


def ends_kernel(here, tokens, facts, idrow, turned, v_ref, out_ref):
    width = v_ref.shape[1]
    lane = lax.broadcasted_iota(jnp.int32, (HD, LANES), 1)
    place = lax.broadcasted_iota(jnp.int32, idrow.shape, 1)
    ids = idrow[...]
    last = ids[:, tokens - 1 : tokens]
    age = jnp.where(ids == last, (tokens - 1 - place).astype(jnp.float32), NEVER)
    for j in range(width // LANES):
        weighted = []
        for head in (2 * j, 2 * j + 1):
            weight = jnp.exp(-rate_of(facts, head, here) * age)
            keys = turned[head * HD : (head + 1) * HD, :].reshape(HD // 8, 8, LANES)
            weighted.append((keys * weight[None]).reshape(HD, LANES))
        weighted = jnp.concatenate(weighted, 0)
        high = weighted.astype(jnp.bfloat16)
        low = (weighted - high.astype(jnp.float32)).astype(jnp.bfloat16)
        v = v_ref[:, j * LANES : (j + 1) * LANES]
        both = jnp.dot(
            jnp.concatenate([high, low], 1),
            jnp.concatenate([v, v], 0),
            preferred_element_type=jnp.float32,
        )
        out_ref[j * HD : (j + 1) * HD, :] = jnp.where(lane < HD, both[:HD], both[HD:]).astype(
            jnp.bfloat16
        )


def inner_kernel(
    here, pairs, rows, facts, idcol, idrow, q_ref, k_ref, v_ref, out_ref, fade_ref, link_ref
):
    tokens = k_ref.shape[0]
    step = pl.program_id(0)
    first = step * pairs
    me = lax.axis_index("ctx") * lax.axis_size("uly") + lax.axis_index("uly")

    @pl.when(step == 0)
    def _():
        last = facts[:, LANES - 1 :]
        earlier = jnp.concatenate([last[:1], last[:-1]], 0)
        decay = jnp.exp(-pair_rate(facts, lax.div(me * rows, HD), here) * float(tokens))
        link_ref[...] = jnp.where(last == earlier, decay, 0.0)

    lane = lax.broadcasted_iota(jnp.int32, (tokens, LANES), 1)
    place = lax.broadcasted_iota(jnp.int32, (tokens, LANES), 0)
    t = lax.broadcasted_iota(jnp.int32, (tokens, tokens), 0)
    s = lax.broadcasted_iota(jnp.int32, (tokens, tokens), 1)
    seen = (t >= s) & (idcol[:, :tokens] == idrow[:1, :tokens])
    age = jnp.where(seen, (t - s).astype(jnp.float32), NEVER)
    before = jnp.where(me > 0, facts[pl.ds(jnp.maximum(me - 1, 0), 1), LANES - 1 :], -1.0)
    since = jnp.where(idcol[...] == before, (place + 1).astype(jnp.float32), NEVER)
    for j in range(pairs):
        columns = slice(j * LANES, (j + 1) * LANES)
        q = q_ref[:, columns]
        zero = jnp.zeros_like(q)
        stacked = jnp.concatenate([jnp.where(lane < HD, q, zero), jnp.where(lane < HD, zero, q)], 0)
        scores = lax.dot_general(
            stacked, k_ref[:, columns], BOTH_LAST, preferred_element_type=jnp.float32
        )
        rates = [
            facts[
                pl.ds(lax.div(2 * (first + j) + one, here), 1),
                (2 * j + one) % here : (2 * j + one) % here + 1,
            ]
            for one in (0, 1)
        ]
        weight = jnp.concatenate([jnp.exp(-rate * age) for rate in rates], 0)
        probs = (scores * weight).astype(jnp.bfloat16)
        got = jnp.dot(probs, v_ref[:, columns], preferred_element_type=jnp.float32)
        out_ref[:, columns] = jnp.where(lane < HD, got[:tokens], got[tokens:])
        fade_ref[:, columns] = jnp.exp(-jnp.where(lane < HD, rates[0], rates[1]) * since)


def scan_kernel(link, in_ref, out_ref):
    count = in_ref.shape[0]
    out_ref[0] = jnp.zeros(out_ref.shape[1:], out_ref.dtype)

    def step(i, state):
        state = in_ref[i].astype(jnp.float32) + link[pl.ds(i, 1), :] * state
        out_ref[i + 1] = state.astype(out_ref.dtype)
        return state

    zero = jnp.zeros(in_ref.shape[1:], jnp.float32)
    lax.fori_loop(0, count - 1, step, zero, unroll=min(count - 1, 31))


def norm_kernel(q_ref, s_ref, inner_ref, fade_ref, gain, out_ref, raw, done, sems):
    tokens, width = q_ref.shape
    lane = lax.broadcasted_iota(jnp.int32, (HD, LANES), 1)
    zero = jnp.zeros((HD, LANES), s_ref.dtype)
    total = jnp.zeros((tokens, LANES), jnp.float32)
    for j in range(0, width // LANES, 2):
        square = []
        for one in (0, 1):
            state = s_ref[(j + one) * HD : (j + one + 1) * HD, :]
            for half in (jnp.where(lane < HD, state, zero), jnp.where(lane < HD, zero, state)):
                square.append(jnp.concatenate([zero, half] if one else [half, zero], 1))
        columns = slice(j * LANES, (j + 2) * LANES)
        outer = jnp.dot(
            q_ref[:, columns], jnp.concatenate(square, 0), preferred_element_type=jnp.float32
        )
        value = inner_ref[:, columns] + outer * fade_ref[:, columns]
        total += value[:, :LANES] * value[:, :LANES] + value[:, LANES:] * value[:, LANES:]
        raw[:, columns] = value
    mean = jnp.sum(total, axis=1, keepdims=True) / float(width)
    scale = jnp.broadcast_to(lax.rsqrt(mean + 1e-06), (tokens, LANES))
    parts = sems.shape[0]
    share = width // parts
    copies = []
    for part in range(parts):
        for at in range(part * share, (part + 1) * share, LANES):
            columns = slice(at, at + LANES)
            done[:, columns] = (raw[:, columns] * scale * gain[:, columns]).astype(jnp.bfloat16)
        columns = slice(part * share, (part + 1) * share)
        copies.append(
            pltpu.make_async_copy(done.at[:, columns], out_ref.at[:, columns], sems.at[part])
        )
        copies[-1].start()
    for copy in copies:
        copy.wait()


def local(queries, keys, values, doc_ids, decay_rate, norm_gain):
    tokens, width = queries.shape
    here = decay_rate.shape[0]
    axes = ("ctx", "uly")
    count = lax.axis_size("ctx") * lax.axis_size("uly")
    all_pairs = width // LANES
    steps = 4
    pairs = all_pairs // steps
    rows = all_pairs * HD // count

    vmem = pl.BlockSpec(memory_space=pltpu.VMEM)
    whole = lambda shape: pl.BlockSpec(shape, lambda i: (0,) * len(shape))
    part = pl.BlockSpec((tokens, pairs * LANES), lambda i: (0, i))
    params = pltpu.CompilerParams(vmem_limit_bytes=32 * 1024 * 1024)
    shape = jax.ShapeDtypeStruct

    own = jnp.pad(decay_rate, (0, LANES - here)) + jnp.pad(
        doc_ids.astype(jnp.float32), (LANES - tokens, 0)
    )
    facts = lax.all_to_all(
        jnp.broadcast_to(own[None, :], (count, LANES)), axes, split_axis=0, concat_axis=0, tiled=True
    )
    turned, filled, idrow, idcol = pl.pallas_call(
        turn_kernel,
        in_specs=[vmem] * 3,
        out_specs=[vmem] * 4,
        out_shape=[
            shape((width, LANES), jnp.float32),
            shape((LANES, width), jnp.bfloat16),
            shape((8, LANES), jnp.float32),
            shape((tokens, LANES), jnp.float32),
        ],
        compiler_params=params,
        cost_estimate=pl.CostEstimate(flops=0, bytes_accessed=12_000_000, transcendentals=0),
        name="turn",
    )(doc_ids[None, :], keys, values)
    ends = pl.pallas_call(
        functools.partial(ends_kernel, here, tokens),
        in_specs=[vmem] * 4,
        out_specs=vmem,
        out_shape=shape((all_pairs * HD, LANES), jnp.bfloat16),
        compiler_params=params,
        name="ends",
    )(facts, idrow, turned, filled)
    pieces = lax.all_to_all(
        ends.reshape(count, rows, LANES), axes, split_axis=0, concat_axis=0, tiled=True
    )
    inner, fade, link = pl.pallas_call(
        functools.partial(inner_kernel, here, pairs, rows),
        grid=(steps,),
        in_specs=[whole((count, LANES)), whole((tokens, LANES)), whole((8, LANES)), part, part, part],
        out_specs=[part, part, whole((count, LANES))],
        out_shape=[
            shape((tokens, width), jnp.float32),
            shape((tokens, width), jnp.float32),
            shape((count, LANES), jnp.float32),
        ],
        compiler_params=params,
        cost_estimate=pl.CostEstimate(
            flops=8_000_000_000, bytes_accessed=4_000_000, transcendentals=600_000
        ),
        name="inner",
    )(facts, idcol, idrow, queries, keys, values)
    before = pl.pallas_call(
        scan_kernel,
        in_specs=[vmem] * 2,
        out_specs=vmem,
        out_shape=shape((count, rows, LANES), jnp.bfloat16),
        compiler_params=params,
        name="scan",
    )(link, pieces)
    states = lax.all_to_all(before, axes, split_axis=0, concat_axis=0, tiled=True)
    return pl.pallas_call(
        norm_kernel,
        in_specs=[vmem] * 5,
        out_specs=pl.BlockSpec(memory_space=pl.ANY),
        out_shape=shape((tokens, width), jnp.bfloat16),
        scratch_shapes=[
            pltpu.VMEM((tokens, width), jnp.float32),
            pltpu.VMEM((tokens, width), jnp.bfloat16),
            pltpu.SemaphoreType.DMA((4,)),
        ],
        compiler_params=params,
        name="norm",
    )(queries, states.reshape(all_pairs * HD, LANES), inner, fade, norm_gain[None, :])


def solution(mesh):
    in_specs = (
        P(("ctx", "uly"), None),
        P(("ctx", "uly"), None),
        P(("ctx", "uly"), None),
        P(("ctx", "uly")),
        P("uly"),
        P(),
    )
    out_specs = P(("ctx", "uly"), None)
    return jax.shard_map(local, mesh=mesh, in_specs=in_specs, out_specs=out_specs, check_vma=False)
```

time: 61.5 us -> 57.6 us (0.937)
  Pallas kernels: 10.9 us -> 6.86 us
  waiting for transfers between devices: 15.5 us -> 12.4 us
  local copies, waits for them, and re-layouts: 6.5 us -> 8.09 us
  other arithmetic: 0 us -> 1.39 us
    pallas_call x6 -> x5, Pallas kernels: 10.9 us -> 6.86 us  [the longest x1 3.04 us: local(): pl.pallas_call(functools.partial(inner_kernel, here, pairs, rows), grid=(...]
    all_to_all x2, waiting for transfers between devices: 15.5 us -> 12.4 us  [the longest x1 8.73 us: local(): lax.all_to_all(ends.reshape(count, rows, LANES), axes, split_axis=0, conc...]
    unnamed x18 -> x20, local copies, waits for them, and re-layouts: 6.5 us -> 7.48 us
    add x0 -> x1, other arithmetic: none -> 0.73 us  [local(): jnp.pad(decay_rate, (0, LANES - here))]
    convert_element_type x0 -> x1, other arithmetic: none -> 0.66 us  [local(): doc_ids.astype(jnp.float32)]
    broadcast_in_dim x0 -> x1, local copies, waits for them, and re-layouts: none -> 0.62 us  [local(): jnp.broadcast_to(own[None, :], (count, LANES))]
where the time goes in v3:
time: 57.6 us; the launch traced here: 57.1 us
  blocking collectives  18.3 us (32%)
  waiting for transfers between devices  12.4 us (22%)
  starting transfers between devices  9.9 us (17%)
  local copies, waits for them, and re-layouts  8.09 us (14%)
  Pallas kernels  6.86 us (12%)
  other arithmetic  1.39 us (2%)
    all_to_all x1, blocking collectives, local(): lax.all_to_all(before, axes, split_axis=0, concat_axis=0, tiled=True)  18.3 us
    all_to_all x1, waiting for transfers between devices, local(): lax.all_to_all(ends.reshape(count, rows, LANES), axes, split_axis=0, conc...  8.73 us
    unnamed x20, local copies, waits for them, and re-layouts  7.48 us
    all_to_all x1, starting transfers between devices, local(): lax.all_to_all(jnp.broadcast_to(own[None, :], (count, LANES)), axes, spli...  7.3 us
    all_to_all x1, waiting for transfers between devices, local(): lax.all_to_all(jnp.broadcast_to(own[None, :], (count, LANES)), axes, spli...  3.71 us
    pallas_call x1, Pallas kernels, local(): pl.pallas_call(functools.partial(inner_kernel, here, pairs, rows), grid=(...  3.04 us
    all_to_all x1, starting transfers between devices, local(): lax.all_to_all(ends.reshape(count, rows, LANES), axes, split_axis=0, conc...  2.61 us
    pallas_call x1, Pallas kernels, local(): pl.pallas_call(norm_kernel, in_specs=[vmem] * 5, out_specs=pl.BlockSpec(m...  1.7 us
  transfers between devices with their start and end apart: 2, of which 2 were waited for; matrix products, arithmetic and copies ran while one was open for 0% of the time, Pallas kernels for 6%

profile of v3, /device:TPU:0, one launch (start us, length us, event | category | flops | bytes accessed | tf_op | source)
XLA Modules:
  0.0 57.1 jit_solution(13153737735231796763)
XLA Ops:
  0.0 0.7 %convert_element_type.7 = f32[96]{0:T(128)S(1)} convert(s32[96]{0:T(128)} %param.9) | non-fusion elementwise | flops 96 | bytes 768 | tf_op jit(solution)/shard_map/convert_element_type | solution.py:184
  0.7 0.7 %pad_add_fusion = f32[128]{0:T(128)S(1)} fusion(f32[96]{0:T(128)S(1)} %convert_element_type.7, f32[8]{0:T(128)} %param.10), kind=kLoop, calls=%fused_computation | loop fusion | flops 128 | bytes 928 | tf_op jit(solution)/shard_map/add | solution.py:183
  1.4 0.6 %broadcast_in_dim.12 = f32[32,1,128]{2,1,0:T(1,128)} broadcast(f32[128]{0:T(128)S(1)} %pad_add_fusion), dimensions={2} | broadcast | bytes 16896 | tf_op jit(solution)/shard_map/broadcast_in_dim | solution.py:187
  2.0 7.3 %all-to-all-start = ((f32[32,1,128]{2,1,0:T(1,128)}), f32[32,1,128]{2,1,0:T(1,128)S(1)}, u32[]{:S(2)}, u32[]{:S(2)}) async-start(f32[32,1,128]{2,1,0:T(1,128)} %broadcast_in_dim.12), calls=%async_computation | async-start | bytes 32768 | tf_op jit(solution)/shard_map/all_to_all | solution.py:186
  9.3 0.0 copy-start.4
  9.3 1.1 %copy-done.4 = bf16[96,4096]{1,0:T(8,128)(2,1)S(1)} copy-done((bf16[96,4096]{1,0:T(8,128)(2,1)S(1)}, bf16[96,4096]{1,0:T(8,128)(2,1)}, u32[]{:S(2)}) %copy-start.4) | copy-done | bytes 786456
  10.4 1.1 %copy-done.6 = bf16[96,4096]{1,0:T(8,128)(2,1)S(1)} copy-done((bf16[96,4096]{1,0:T(8,128)(2,1)S(1)}, bf16[96,4096]{1,0:T(8,128)(2,1)}, u32[]{:S(2)}) %copy-start.6) | copy-done | bytes 786456
  11.6 0.7 %copy-done.9 = s32[96]{0:T(128)S(1)} copy-done((s32[96]{0:T(128)S(1)}, s32[96]{0:T(128)}, u32[]{:S(2)}) %copy-start.9) | copy-done | bytes 408
  12.2 0.4 turn.1
  12.6 3.7 %all-to-all-done = f32[32,1,128]{2,1,0:T(1,128)S(1)} async-done(((f32[32,1,128]{2,1,0:T(1,128)}), f32[32,1,128]{2,1,0:T(1,128)S(1)}, u32[]{:S(2)}, u32[]{:S(2)}) %all-to-all-start) | async-done | bytes 16416 | tf_op jit(solution)/shard_map/all_to_all | solution.py:186
  16.4 1.6 %ends.1 = bf16[2048,128]{1,0:T(8,128)(2,1)} custom-call(f32[32,128]{1,0:T(8,128)S(1)} %bitcast.6, f32[8,128]{1,0:T(8,128)S(1)} %get-tuple-element.13.idrow, f32[4096,128]{1,0:T(8,128)S(1)} %get-tuple-element.15.turned, bf16[128,4096]{1,0:T(8,128)(2,1)S(1)} %get-tuple-element.16.v_ref), custom_call_target="tpu_custom_call" | custom-call | tf_op jit(solution)/shard_map/ends/pallas_call | solution.py:203
  17.9 2.6 %all-to-all-start.1 = ((bf16[32,64,128]{2,1,0:T(8,128)(2,1)}), bf16[32,64,128]{2,1,0:T(8,128)(2,1)S(1)}, u32[]{:S(2)}, u32[]{:S(2)}) async-start(bf16[32,64,128]{2,1,0:T(8,128)(2,1)} %bitcast.2), calls=%async_computation.1 | async-start | bytes 1048576 | tf_op jit(solution)/shard_map/all_to_all | solution.py:211
  20.6 0.0 copy-start.2
  20.6 1.1 %copy-done.2 = bf16[96,4096]{1,0:T(8,128)(2,1)S(1)} copy-done((bf16[96,4096]{1,0:T(8,128)(2,1)S(1)}, bf16[96,4096]{1,0:T(8,128)(2,1)}, u32[]{:S(2)}) %copy-start.2) | copy-done | bytes 786456
  21.7 1.1 %copy-done.5 = bf16[96,4096]{1,0:T(8,128)(2,1)S(1)} copy-done((bf16[96,4096]{1,0:T(8,128)(2,1)S(1)}, bf16[96,4096]{1,0:T(8,128)(2,1)}, u32[]{:S(2)}) %copy-start.5) | copy-done | bytes 786456
  22.8 1.1 %copy-done.7 = bf16[96,4096]{1,0:T(8,128)(2,1)S(1)} copy-done((bf16[96,4096]{1,0:T(8,128)(2,1)S(1)}, bf16[96,4096]{1,0:T(8,128)(2,1)}, u32[]{:S(2)}) %copy-start.7) | copy-done | bytes 786456
  24.0 3.0 %inner.1 = (f32[96,4096]{1,0:T(8,128)S(1)}, f32[96,4096]{1,0:T(8,128)S(1)}, f32[32,128]{1,0:T(8,128)S(1)}) custom-call(f32[32,128]{1,0:T(8,128)S(1)} %bitcast.7, f32[96,128]{1,0:T(8,128)S(1)} %get-tuple-element.12.idcol, f32[8,128]{1,0:T(8,128)S(1)} %get-tuple-element.13.idrow, bf16[96,4096]{1,0:T(8,128)(2,1)S(1)} %copy-done.2, ...), custom_call_target="tpu_custom_call" | custom-call | flops 8000000000 | bytes 4000000 | tf_op jit(solution)/shard_map/inner/pallas_call | solution.py:214
  27.0 1.2 %copy-done = f32[96,4096]{1,0:T(8,128)} copy-done((f32[96,4096]{1,0:T(8,128)}, f32[96,4096]{1,0:T(8,128)S(1)}, u32[]{:S(2)}) %copy-start) | copy-done | bytes 1572888
  28.2 8.7 %all-to-all-done.1.in_ref = bf16[32,64,128]{2,1,0:T(8,128)(2,1)S(1)} async-done(((bf16[32,64,128]{2,1,0:T(8,128)(2,1)}), bf16[32,64,128]{2,1,0:T(8,128)(2,1)S(1)}, u32[]{:S(2)}, u32[]{:S(2)}) %all-to-all-start.1) | async-done | bytes 524320 | tf_op jit(solution)/shard_map/all_to_all | solution.py:211
  36.9 0.1 scan.1
  37.0 18.3 %all_to_all.18 = bf16[32,64,128]{2,1,0:T(8,128)(2,1)S(1)} all-to-all(bf16[32,64,128]{2,1,0:T(8,128)(2,1)S(1)} %scan.1), channel_id=1, replica_groups=mesh['ctx'=4,'uly'=8] {'ctx','uly'}, dimensions={0} | all-to-all | bytes 1048576 | tf_op jit(solution)/shard_map/all_to_all | solution.py:238
  55.4 0.0 copy-done.3
  55.4 0.0 copy-done.1
  55.4 1.7 %norm.1 = bf16[96,4096]{1,0:T(8,128)(2,1)} custom-call(bf16[96,4096]{1,0:T(8,128)(2,1)S(1)} %copy-done.3, bf16[2048,128]{1,0:T(8,128)(2,1)S(1)} %bitcast.5, f32[96,4096]{1,0:T(8,128)S(1)} %get-tuple-element.17.inner_ref, f32[96,4096]{1,0:T(8,128)S(1)} %copy-done.1, f32[1,4096]{1,0:T(1,128)S(1)} %bitcast.8), custom_call_target="tpu_custom_call" | custom-call | tf_op jit(solution)/shard_map/norm/pallas_call | solution.py:239
  (9 shorter events, 0.0 us)
Async XLA Ops:
  2.0 14.3 %all-to-all-start = ((f32[32,1,128]{2,1,0:T(1,128)}), f32[32,1,128]{2,1,0:T(1,128)S(1)}, u32[]{:S(2)}, u32[]{:S(2)}) async-start(f32[32,1,128]{2,1,0:T(1,128)} %broadcast_in_dim.12), calls=%async_computation | async-start | bytes 32768 | tf_op jit(solution)/shard_map/all_to_all | solution.py:186
  9.3 1.1 %copy-start.4 = (bf16[96,4096]{1,0:T(8,128)(2,1)S(1)}, bf16[96,4096]{1,0:T(8,128)(2,1)}, u32[]{:S(2)}) copy-start(bf16[96,4096]{1,0:T(8,128)(2,1)} %k_ref.3) | copy-start | bytes 2359300
  10.4 1.1 %copy-start.6 = (bf16[96,4096]{1,0:T(8,128)(2,1)S(1)}, bf16[96,4096]{1,0:T(8,128)(2,1)}, u32[]{:S(2)}) copy-start(bf16[96,4096]{1,0:T(8,128)(2,1)} %v_ref.3) | copy-start | bytes 2359300
  11.6 0.7 %copy-start.9 = (s32[96]{0:T(128)S(1)}, s32[96]{0:T(128)}, u32[]{:S(2)}) copy-start(s32[96]{0:T(128)} %param.9) | copy-start | bytes 1156
  17.9 19.0 %all-to-all-start.1 = ((bf16[32,64,128]{2,1,0:T(8,128)(2,1)}), bf16[32,64,128]{2,1,0:T(8,128)(2,1)S(1)}, u32[]{:S(2)}, u32[]{:S(2)}) async-start(bf16[32,64,128]{2,1,0:T(8,128)(2,1)} %bitcast.2), calls=%async_computation.1 | async-start | bytes 1048576 | tf_op jit(solution)/shard_map/all_to_all | solution.py:211
  20.6 1.1 %copy-start.2 = (bf16[96,4096]{1,0:T(8,128)(2,1)S(1)}, bf16[96,4096]{1,0:T(8,128)(2,1)}, u32[]{:S(2)}) copy-start(bf16[96,4096]{1,0:T(8,128)(2,1)} %q_ref.3) | copy-start | bytes 2359300
  21.7 1.1 %copy-start.5 = (bf16[96,4096]{1,0:T(8,128)(2,1)S(1)}, bf16[96,4096]{1,0:T(8,128)(2,1)}, u32[]{:S(2)}) copy-start(bf16[96,4096]{1,0:T(8,128)(2,1)} %k_ref.3) | copy-start | bytes 2359300
  22.8 1.1 %copy-start.7 = (bf16[96,4096]{1,0:T(8,128)(2,1)S(1)}, bf16[96,4096]{1,0:T(8,128)(2,1)}, u32[]{:S(2)}) copy-start(bf16[96,4096]{1,0:T(8,128)(2,1)} %v_ref.3) | copy-start | bytes 2359300
  24.0 31.4 %copy-start.3 = (bf16[96,4096]{1,0:T(8,128)(2,1)S(1)}, bf16[96,4096]{1,0:T(8,128)(2,1)}, u32[]{:S(2)}) copy-start(bf16[96,4096]{1,0:T(8,128)(2,1)} %q_ref.3) | copy-start | bytes 2359300
  27.0 1.2 %copy-start = (f32[96,4096]{1,0:T(8,128)}, f32[96,4096]{1,0:T(8,128)S(1)}, u32[]{:S(2)}) copy-start(f32[96,4096]{1,0:T(8,128)S(1)} %get-tuple-element.18.fade_ref) | copy-start | bytes 4718596
  28.2 27.2 %copy-start.8 = (f32[4096]{0:T(1024)S(1)}, f32[4096]{0:T(1024)}, u32[]{:S(2)}) copy-start(f32[4096]{0:T(1024)} %param.11) | copy-start | bytes 49156
  36.9 18.5 %copy-start.1 = (f32[96,4096]{1,0:T(8,128)S(1)}, f32[96,4096]{1,0:T(8,128)}, u32[]{:S(2)}) copy-start(f32[96,4096]{1,0:T(8,128)} %copy-done) | copy-start | bytes 4718596

commit v4 on v3

--- a/solution.py
+++ b/solution.py
@@ -18,12 +18,13 @@
 
 
 def pair_rate(facts, pair, here):
+    place = lax.broadcasted_iota(jnp.int32, (1, here), 1)
     lane = lax.broadcasted_iota(jnp.int32, (1, LANES), 1)
     rates = []
     for head in (2 * pair, 2 * pair + 1):
         row = facts[pl.ds(lax.div(head, here), 1), :]
         rates.append(
-            jnp.sum(jnp.where(lane == lax.rem(head, here), row, 0.0), axis=1, keepdims=True)
+            jnp.sum(jnp.where(place == lax.rem(head, here), row, 0.0), axis=1, keepdims=True)
         )
     return jnp.where(lane < HD, rates[0], rates[1])
 
@@ -43,7 +44,7 @@
         turned[columns, :] = jnp.transpose(block)
 
 
-def ends_kernel(here, tokens, facts, idrow, turned, v_ref, out_ref):
+def ends_kernel(here, tokens, rows, facts, idrow, turned, v_ref, out_ref):
     width = v_ref.shape[1]
     lane = lax.broadcasted_iota(jnp.int32, (HD, LANES), 1)
     place = lax.broadcasted_iota(jnp.int32, idrow.shape, 1)
@@ -65,25 +66,35 @@
             jnp.concatenate([v, v], 0),
             preferred_element_type=jnp.float32,
         )
-        out_ref[j * HD : (j + 1) * HD, :] = jnp.where(lane < HD, both[:HD], both[HD:]).astype(
-            jnp.bfloat16
-        )
+        state = jnp.where(lane < HD, both[:HD], both[HD:])
+        share = min(rows, HD)
+        for at in range(0, HD, share):
+            owner, start = divmod(j * HD + at, rows)
+            out_ref[owner, start : start + share, :] = state[at : at + share].astype(jnp.bfloat16)
+    mark = jnp.broadcast_to(last, (out_ref.shape[1] - rows, LANES)).astype(jnp.bfloat16)
+    for owner in range(out_ref.shape[0]):
+        out_ref[owner, rows:, :] = mark
 
 
 def inner_kernel(
-    here, pairs, rows, facts, idcol, idrow, q_ref, k_ref, v_ref, out_ref, fade_ref, link_ref
+    here, pairs, rows, chunks, facts, idcol, idrow, earlier, q_ref, k_ref, v_ref,
+    out_ref, fade_ref, one_ref, half_ref
 ):
     tokens = k_ref.shape[0]
     step = pl.program_id(0)
     first = step * pairs
-    me = lax.axis_index("ctx") * lax.axis_size("uly") + lax.axis_index("uly")
+    ctx, uly = lax.axis_index("ctx"), lax.axis_index("uly")
 
     @pl.when(step == 0)
     def _():
-        last = facts[:, LANES - 1 :]
-        earlier = jnp.concatenate([last[:1], last[:-1]], 0)
-        decay = jnp.exp(-pair_rate(facts, lax.div(me * rows, HD), here) * float(tokens))
-        link_ref[...] = jnp.where(last == earlier, decay, 0.0)
+        owner = ctx * chunks + lax.rem(uly, chunks)
+        share = min(rows, HD)
+        for at in range(0, rows, share):
+            rate = pair_rate(facts, lax.div(owner * rows + at, HD), here)
+            for ref, length in ((one_ref, tokens), (half_ref, tokens * chunks)):
+                ref[at : at + share, :] = jnp.broadcast_to(
+                    jnp.exp(-rate * float(length)), (share, LANES)
+                )
 
     lane = lax.broadcasted_iota(jnp.int32, (tokens, LANES), 1)
     place = lax.broadcasted_iota(jnp.int32, (tokens, LANES), 0)
@@ -91,7 +102,7 @@
     s = lax.broadcasted_iota(jnp.int32, (tokens, tokens), 1)
     seen = (t >= s) & (idcol[:, :tokens] == idrow[:1, :tokens])
     age = jnp.where(seen, (t - s).astype(jnp.float32), NEVER)
-    before = jnp.where(me > 0, facts[pl.ds(jnp.maximum(me - 1, 0), 1), LANES - 1 :], -1.0)
+    before = jnp.where(ctx + uly > 0, earlier[:1, tokens - 1 : tokens], -1.0)
     since = jnp.where(idcol[...] == before, (place + 1).astype(jnp.float32), NEVER)
     for j in range(pairs):
         columns = slice(j * LANES, (j + 1) * LANES)
@@ -115,17 +126,61 @@
         fade_ref[:, columns] = jnp.exp(-jnp.where(lane < HD, rates[0], rates[1]) * since)
 
 
-def scan_kernel(link, in_ref, out_ref):
-    count = in_ref.shape[0]
-    out_ref[0] = jnp.zeros(out_ref.shape[1:], out_ref.dtype)
-
-    def step(i, state):
-        state = in_ref[i].astype(jnp.float32) + link[pl.ds(i, 1), :] * state
-        out_ref[i + 1] = state.astype(out_ref.dtype)
-        return state
-
-    zero = jnp.zeros(in_ref.shape[1:], jnp.float32)
-    lax.fori_loop(0, count - 1, step, zero, unroll=min(count - 1, 31))
+def few(count):
+    return count if count <= 8 else 1
+
+
+def half_kernel(chunks, one, in_ref, out_ref):
+    count, rows = in_ref.shape[0], one.shape[0]
+
+    def slice_end(c, _):
+        start = c * chunks
+
+        def step(j, carry):
+            state, last = carry
+            piece = in_ref[start + j]
+            own = piece[rows : rows + 1].astype(jnp.float32)
+            linked = jnp.where(own == last, one[...], 0.0)
+            return (piece[:rows].astype(jnp.float32) + linked * state, own)
+
+        piece = in_ref[start]
+        begin = (piece[:rows].astype(jnp.float32), piece[rows : rows + 1].astype(jnp.float32))
+        state, _ = lax.fori_loop(1, chunks, step, begin, unroll=few(chunks - 1))
+        out_ref[c, :rows, :] = state.astype(out_ref.dtype)
+        out_ref[c, rows:, :] = in_ref[start + chunks - 1][rows:]
+        return 0
+
+    lax.fori_loop(0, count // chunks, slice_end, 0, unroll=few(count // chunks))
+
+
+def scan_kernel(chunks, one, half, in_ref, other, out_ref):
+    count, rows = in_ref.shape[0], one.shape[0]
+    later = lax.axis_index("uly") >= chunks
+
+    def over_other(state, last, c, wanted):
+        piece = other[c]
+        own = piece[rows : rows + 1].astype(jnp.float32)
+        linked = jnp.where(own == last, half[...], 0.0)
+        moved = piece[:rows].astype(jnp.float32) + linked * state
+        return jnp.where(wanted, moved, state), jnp.where(wanted, own, last)
+
+    def over_slice(c, carry):
+        carry = over_other(*carry, c, later)
+
+        def step(j, carry):
+            state, last = carry
+            at = c * chunks + j
+            out_ref[at] = state.astype(out_ref.dtype)
+            piece = in_ref[at]
+            own = piece[rows : rows + 1].astype(jnp.float32)
+            linked = jnp.where(own == last, one[...], 0.0)
+            return (piece[:rows].astype(jnp.float32) + linked * state, own)
+
+        carry = lax.fori_loop(0, chunks, step, carry, unroll=few(chunks))
+        return over_other(*carry, c, jnp.logical_not(later))
+
+    begin = (jnp.zeros((rows, LANES), jnp.float32), jnp.full((1, LANES), -1.0, jnp.float32))
+    lax.fori_loop(0, count // chunks, over_slice, begin, unroll=few(count // chunks))
 
 
 def norm_kernel(q_ref, s_ref, inner_ref, fade_ref, gain, out_ref, raw, done, sems):
@@ -168,11 +223,24 @@
     tokens, width = queries.shape
     here = decay_rate.shape[0]
     axes = ("ctx", "uly")
-    count = lax.axis_size("ctx") * lax.axis_size("uly")
+    slices, members = lax.axis_size("ctx"), lax.axis_size("uly")
+    chunks = members // 2
+    group = slices * chunks
     all_pairs = width // LANES
     steps = 4
     pairs = all_pairs // steps
-    rows = all_pairs * HD // count
+    rows = all_pairs * HD // group
+    groups = [
+        [c * members + half * chunks + u for c in range(slices) for u in range(chunks)]
+        for half in (0, 1)
+    ]
+    device = lambda c, u: c * members + u
+    swap = [
+        (device(c, u), device(c, (u + chunks) % members))
+        for c in range(slices)
+        for u in range(members)
+    ]
+    forward = [(i, i + 1) for i in range(slices * members - 1)]
 
     vmem = pl.BlockSpec(memory_space=pltpu.VMEM)
     whole = lambda shape: pl.BlockSpec(shape, lambda i: (0,) * len(shape))
@@ -180,11 +248,9 @@
     params = pltpu.CompilerParams(vmem_limit_bytes=32 * 1024 * 1024)
     shape = jax.ShapeDtypeStruct
 
-    own = jnp.pad(decay_rate, (0, LANES - here)) + jnp.pad(
-        doc_ids.astype(jnp.float32), (LANES - tokens, 0)
-    )
     facts = lax.all_to_all(
-        jnp.broadcast_to(own[None, :], (count, LANES)), axes, split_axis=0, concat_axis=0, tiled=True
+        jnp.broadcast_to(decay_rate[None, :], (members, here)),
+        "uly", split_axis=0, concat_axis=0, tiled=True,
     )
     turned, filled, idrow, idcol = pl.pallas_call(
         turn_kernel,
@@ -200,42 +266,58 @@
         cost_estimate=pl.CostEstimate(flops=0, bytes_accessed=12_000_000, transcendentals=0),
         name="turn",
     )(doc_ids[None, :], keys, values)
+    earlier = lax.ppermute(idrow, axes, forward)
     ends = pl.pallas_call(
-        functools.partial(ends_kernel, here, tokens),
+        functools.partial(ends_kernel, here, tokens, rows),
         in_specs=[vmem] * 4,
         out_specs=vmem,
-        out_shape=shape((all_pairs * HD, LANES), jnp.bfloat16),
+        out_shape=shape((group, rows + 8, LANES), jnp.bfloat16),
         compiler_params=params,
         name="ends",
     )(facts, idrow, turned, filled)
     pieces = lax.all_to_all(
-        ends.reshape(count, rows, LANES), axes, split_axis=0, concat_axis=0, tiled=True
+        ends, axes, split_axis=0, concat_axis=0, axis_index_groups=groups, tiled=True
     )
-    inner, fade, link = pl.pallas_call(
-        functools.partial(inner_kernel, here, pairs, rows),
+    inner, fade, one, half = pl.pallas_call(
+        functools.partial(inner_kernel, here, pairs, rows, chunks),
         grid=(steps,),
-        in_specs=[whole((count, LANES)), whole((tokens, LANES)), whole((8, LANES)), part, part, part],
-        out_specs=[part, part, whole((count, LANES))],
+        in_specs=[
+            whole((members, here)), whole((tokens, LANES)), whole((8, LANES)), whole((8, LANES)),
+            part, part, part,
+        ],
+        out_specs=[part, part, whole((rows, LANES)), whole((rows, LANES))],
         out_shape=[
             shape((tokens, width), jnp.float32),
             shape((tokens, width), jnp.float32),
-            shape((count, LANES), jnp.float32),
+            shape((rows, LANES), jnp.float32),
+            shape((rows, LANES), jnp.float32),
         ],
         compiler_params=params,
         cost_estimate=pl.CostEstimate(
             flops=8_000_000_000, bytes_accessed=4_000_000, transcendentals=600_000
         ),
         name="inner",
-    )(facts, idcol, idrow, queries, keys, values)
-    before = pl.pallas_call(
-        scan_kernel,
+    )(facts, idcol, idrow, earlier, queries, keys, values)
+    halves = pl.pallas_call(
+        functools.partial(half_kernel, chunks),
         in_specs=[vmem] * 2,
         out_specs=vmem,
-        out_shape=shape((count, rows, LANES), jnp.bfloat16),
+        out_shape=shape((slices, rows + 8, LANES), jnp.bfloat16),
+        compiler_params=params,
+        name="half",
+    )(one, pieces)
+    other = lax.ppermute(halves, axes, swap)
+    before = pl.pallas_call(
+        functools.partial(scan_kernel, chunks),
+        in_specs=[vmem] * 4,
+        out_specs=vmem,
+        out_shape=shape((group, rows, LANES), jnp.bfloat16),
         compiler_params=params,
         name="scan",
-    )(link, pieces)
-    states = lax.all_to_all(before, axes, split_axis=0, concat_axis=0, tiled=True)
+    )(one, half, pieces, other)
+    states = lax.all_to_all(
+        before, axes, split_axis=0, concat_axis=0, axis_index_groups=groups, tiled=True
+    )
     return pl.pallas_call(
         norm_kernel,
         in_specs=[vmem] * 5,

time: 57.6 us -> 61.4 us (1.066)
  starting transfers between devices: 9.9 us -> 17.3 us
  waiting for transfers between devices: 12.4 us -> 7.67 us
  blocking collectives: 18.3 us -> 19.8 us
  other arithmetic: 1.39 us -> 0 us
  local copies, waits for them, and re-layouts: 8.09 us -> 8.74 us
    all_to_all x2, waiting for transfers between devices: 12.4 us -> 3.07 us  [the longest x1 3.06 us: local(): lax.all_to_all(jnp.broadcast_to(decay_rate[None, :], (members, here)), 'u...]
    ppermute x0 -> x2, starting transfers between devices: none -> 6.43 us  [the longest x1 3.7 us: local(): earlier = lax.ppermute(idrow, axes, forward)]
    ppermute x0 -> x2, waiting for transfers between devices: none -> 4.6 us  [the longest x1 3.29 us: local(): other = lax.ppermute(halves, axes, swap)]
    all_to_all x1, blocking collectives: 18.3 us -> 19.8 us  [local(): lax.all_to_all(before, axes, split_axis=0, concat_axis=0, axis_index_grou...]
    all_to_all x2, starting transfers between devices: 9.9 us -> 10.8 us  [the longest x1 7.25 us: local(): lax.all_to_all(jnp.broadcast_to(decay_rate[None, :], (members, here)), 'u...]
    add x1 -> x0, other arithmetic: 0.73 us -> none  [local(): jnp.pad(decay_rate, (0, LANES - here))]
    convert_element_type x1 -> x0, other arithmetic: 0.66 us -> none  [local(): doc_ids.astype(jnp.float32)]
    broadcast_in_dim x1, local copies, waits for them, and re-layouts: 0.62 us -> 1.25 us  [local(): jnp.broadcast_to(decay_rate[None, :], (members, here))]
  transfers between devices with their start and end apart: 2 -> 4, of which waited for: 2 -> 3; matrix products, arithmetic and copies ran while one was open for 0% -> 0% of each run, Pallas kernels for 6% -> 6%
where the time goes in v4:
time: 61.4 us; the launch traced here: 60.8 us
  blocking collectives  19.8 us (32%)
  starting transfers between devices  17.3 us (28%)
  local copies, waits for them, and re-layouts  8.74 us (14%)
  waiting for transfers between devices  7.67 us (12%)
  Pallas kernels  7.22 us (12%)
    all_to_all x1, blocking collectives, local(): lax.all_to_all(before, axes, split_axis=0, concat_axis=0, axis_index_grou...  19.8 us
    unnamed x20, local copies, waits for them, and re-layouts  7.49 us
    all_to_all x1, starting transfers between devices, local(): lax.all_to_all(jnp.broadcast_to(decay_rate[None, :], (members, here)), 'u...  7.25 us
    ppermute x1, starting transfers between devices, local(): earlier = lax.ppermute(idrow, axes, forward)  3.7 us
    all_to_all x1, starting transfers between devices, local(): lax.all_to_all(ends, axes, split_axis=0, concat_axis=0, axis_index_groups...  3.58 us
    ppermute x1, waiting for transfers between devices, local(): other = lax.ppermute(halves, axes, swap)  3.29 us
    pallas_call x1, Pallas kernels, local(): pl.pallas_call(functools.partial(inner_kernel, here, pairs, rows, chunks)...  3.08 us
    all_to_all x1, waiting for transfers between devices, local(): lax.all_to_all(jnp.broadcast_to(decay_rate[None, :], (members, here)), 'u...  3.06 us
  transfers between devices with their start and end apart: 4, of which 3 were waited for; matrix products, arithmetic and copies ran while one was open for 0% of the time, Pallas kernels for 6%

profile of v4, /device:TPU:0, one launch (start us, length us, event | category | flops | bytes accessed | tf_op | source)
XLA Modules:
  0.0 60.8 jit_solution(15420992001508624733)
XLA Ops:
  0.0 1.2 %broadcast_in_dim.12 = f32[8,1,8]{2,1,0:T(1,128)} broadcast(f32[8]{0:T(128)} %param.10), dimensions={2} | broadcast | bytes 288 | tf_op jit(solution)/shard_map/broadcast_in_dim | solution.py:252
  1.2 7.3 %all-to-all-start = ((f32[8,1,8]{2,1,0:T(1,128)}), f32[8,1,8]{2,1,0:T(1,128)S(1)}, u32[]{:S(2)}, u32[]{:S(2)}) async-start(f32[8,1,8]{2,1,0:T(1,128)} %broadcast_in_dim.12), calls=%async_computation | async-start | bytes 8192 | tf_op jit(solution)/shard_map/all_to_all | solution.py:251
  8.5 1.1 %copy-done.4 = bf16[96,4096]{1,0:T(8,128)(2,1)S(1)} copy-done((bf16[96,4096]{1,0:T(8,128)(2,1)S(1)}, bf16[96,4096]{1,0:T(8,128)(2,1)}, u32[]{:S(2)}) %copy-start.4) | copy-done | bytes 786456
  9.6 1.1 %copy-done.6 = bf16[96,4096]{1,0:T(8,128)(2,1)S(1)} copy-done((bf16[96,4096]{1,0:T(8,128)(2,1)S(1)}, bf16[96,4096]{1,0:T(8,128)(2,1)}, u32[]{:S(2)}) %copy-start.6) | copy-done | bytes 786456
  10.8 0.7 %copy-done.9 = s32[96]{0:T(128)S(1)} copy-done((s32[96]{0:T(128)S(1)}, s32[96]{0:T(128)}, u32[]{:S(2)}) %copy-start.9) | copy-done | bytes 408
  11.4 0.4 turn.1
  11.8 3.1 %all-to-all-done = f32[8,1,8]{2,1,0:T(1,128)S(1)} async-done(((f32[8,1,8]{2,1,0:T(1,128)}), f32[8,1,8]{2,1,0:T(1,128)S(1)}, u32[]{:S(2)}, u32[]{:S(2)}) %all-to-all-start) | async-done | bytes 288 | tf_op jit(solution)/shard_map/all_to_all | solution.py:251
  14.9 1.6 %ends.1 = bf16[16,136,128]{2,1,0:T(8,128)(2,1)} custom-call(f32[8,8]{1,0:T(8,128)S(1)} %bitcast.6, f32[8,128]{1,0:T(8,128)S(1)} %get-tuple-element.14.idrow, f32[4096,128]{1,0:T(8,128)S(1)} %get-tuple-element.17.turned, bf16[128,4096]{1,0:T(8,128)(2,1)S(1)} %get-tuple-element.18.v_ref), custom_call_target="tpu_custom_call" | custom-call | tf_op jit(solution)/shard_map/ends/pallas_call | solution.py:270
  16.5 3.6 %all-to-all-start.1 = ((bf16[16,136,128]{2,1,0:T(8,128)(2,1)}), bf16[16,136,128]{2,1,0:T(8,128)(2,1)S(1)}, u32[]{:S(2)}, u32[]{:S(2)}) async-start(bf16[16,136,128]{2,1,0:T(8,128)(2,1)} %ends.1), calls=%async_computation.1 | async-start | bytes 1114112 | tf_op jit(solution)/shard_map/all_to_all | solution.py:278
  20.1 3.7 %collective-permute-start = (f32[8,128]{1,0:T(8,128)S(1)}, f32[8,128]{1,0:T(8,128)S(1)}, u32[]{:S(2)}, u32[]{:S(2)}) collective-permute-start(f32[8,128]{1,0:T(8,128)S(1)} %get-tuple-element.14.idrow), channel_id=1, source_target_pairs={{0,1},{1,2},{2,3},{3,4},{4,5},{5,6},{6,7},{7,8},{8,9},{9,10},{10,1... | collective-permute-start | bytes 12296 | tf_op jit(solution)/shard_map/ppermute | solution.py:269
  23.8 1.3 %collective-permute-done.earlier = f32[8,128]{1,0:T(8,128)S(1)} collective-permute-done((f32[8,128]{1,0:T(8,128)S(1)}, f32[8,128]{1,0:T(8,128)S(1)}, u32[]{:S(2)}, u32[]{:S(2)}) %collective-permute-start) | collective-permute-done | bytes 4128 | tf_op jit(solution)/shard_map/ppermute | solution.py:269
  25.1 1.1 %copy-done.2 = bf16[96,4096]{1,0:T(8,128)(2,1)S(1)} copy-done((bf16[96,4096]{1,0:T(8,128)(2,1)S(1)}, bf16[96,4096]{1,0:T(8,128)(2,1)}, u32[]{:S(2)}) %copy-start.2) | copy-done | bytes 786456
  26.2 1.1 %copy-done.5 = bf16[96,4096]{1,0:T(8,128)(2,1)S(1)} copy-done((bf16[96,4096]{1,0:T(8,128)(2,1)S(1)}, bf16[96,4096]{1,0:T(8,128)(2,1)}, u32[]{:S(2)}) %copy-start.5) | copy-done | bytes 786456
  27.4 1.1 %copy-done.7 = bf16[96,4096]{1,0:T(8,128)(2,1)S(1)} copy-done((bf16[96,4096]{1,0:T(8,128)(2,1)S(1)}, bf16[96,4096]{1,0:T(8,128)(2,1)}, u32[]{:S(2)}) %copy-start.7) | copy-done | bytes 786456
  28.5 3.1 %inner.1 = (f32[96,4096]{1,0:T(8,128)S(1)}, f32[96,4096]{1,0:T(8,128)S(1)}, f32[128,128]{1,0:T(8,128)S(1)}, f32[128,128]{1,0:T(8,128)S(1)}) custom-call(f32[8,8]{1,0:T(8,128)S(1)} %bitcast.7, f32[96,128]{1,0:T(8,128)S(1)} %get-tuple-element.13.idcol, f32[8,128]{1,0:T(8,128)S(1)} %get-tuple-element.14.idrow, f32[8,128]{1,0:T(8,128)S(1)} %collective-permute-done.earlier, ...), custom_call_target="tpu_custom_call" | custom-call | flops 8000000000 | bytes 4000000 | tf_op jit(solution)/shard_map/inner/pallas_call | solution.py:281
  31.6 0.0 copy-start
  31.6 1.2 %copy-done = f32[96,4096]{1,0:T(8,128)} copy-done((f32[96,4096]{1,0:T(8,128)}, f32[96,4096]{1,0:T(8,128)S(1)}, u32[]{:S(2)}) %copy-start) | copy-done | bytes 1572888
  32.8 0.0 all-to-all-done.1.in_ref
  32.8 0.1 half.1
  32.9 2.7 %collective-permute-start.1 = (bf16[4,136,128]{2,1,0:T(8,128)(2,1)S(1)}, bf16[4,136,128]{2,1,0:T(8,128)(2,1)S(1)}, u32[]{:S(2)}, u32[]{:S(2)}) collective-permute-start(bf16[4,136,128]{2,1,0:T(8,128)(2,1)S(1)} %half.1), channel_id=1, source_target_pairs={{0,4},{1,5},{2,6},{3,7},{4,0},{5,1},{6,2},{7,3},{8,12},{9,13},{10,... | collective-permute-start | bytes 417800 | tf_op jit(solution)/shard_map/ppermute | solution.py:309
  35.6 3.3 %collective-permute-done.1.other = bf16[4,136,128]{2,1,0:T(8,128)(2,1)S(1)} collective-permute-done((bf16[4,136,128]{2,1,0:T(8,128)(2,1)S(1)}, bf16[4,136,128]{2,1,0:T(8,128)(2,1)S(1)}, u32[]{:S(2)}, u32[]{:S(2)}) %collective-permute-start.1) | collective-permute-done | bytes 139296 | tf_op jit(solution)/shard_map/ppermute | solution.py:309
  38.9 0.3 scan.1
  39.2 19.8 %all_to_all.18 = bf16[16,128,128]{2,1,0:T(8,128)(2,1)S(1)} all-to-all(bf16[16,128,128]{2,1,0:T(8,128)(2,1)S(1)} %scan.1), channel_id=1, replica_groups={{0,1,2,3,8,9,10,11,16,17,18,19,24,25,26,27},{4,5,6,7,12,13,14,15,20,21,..., dimensions={0} | all-to-all | bytes 1048576 | tf_op jit(solution)/shard_map/all_to_all | solution.py:318
  59.1 1.8 %norm.1 = bf16[96,4096]{1,0:T(8,128)(2,1)} custom-call(bf16[96,4096]{1,0:T(8,128)(2,1)S(1)} %copy-done.3, bf16[2048,128]{1,0:T(8,128)(2,1)S(1)} %bitcast.4, f32[96,4096]{1,0:T(8,128)S(1)} %get-tuple-element.19.inner_ref, f32[96,4096]{1,0:T(8,128)S(1)} %copy-done.1, f32[1,4096]{1,0:T(1,128)S(1)} %bitcast.5), custom_call_target="tpu_custom_call" | custom-call | tf_op jit(solution)/shard_map/norm/pallas_call | solution.py:321
  (12 shorter events, 0.0 us)
Async XLA Ops:
  1.2 13.6 %all-to-all-start = ((f32[8,1,8]{2,1,0:T(1,128)}), f32[8,1,8]{2,1,0:T(1,128)S(1)}, u32[]{:S(2)}, u32[]{:S(2)}) async-start(f32[8,1,8]{2,1,0:T(1,128)} %broadcast_in_dim.12), calls=%async_computation | async-start | bytes 8192 | tf_op jit(solution)/shard_map/all_to_all | solution.py:251
  8.5 1.1 %copy-start.4 = (bf16[96,4096]{1,0:T(8,128)(2,1)S(1)}, bf16[96,4096]{1,0:T(8,128)(2,1)}, u32[]{:S(2)}) copy-start(bf16[96,4096]{1,0:T(8,128)(2,1)} %k_ref.3) | copy-start | bytes 2359300
  9.6 1.1 %copy-start.6 = (bf16[96,4096]{1,0:T(8,128)(2,1)S(1)}, bf16[96,4096]{1,0:T(8,128)(2,1)}, u32[]{:S(2)}) copy-start(bf16[96,4096]{1,0:T(8,128)(2,1)} %v_ref.3) | copy-start | bytes 2359300
  10.8 0.7 %copy-start.9 = (s32[96]{0:T(128)S(1)}, s32[96]{0:T(128)}, u32[]{:S(2)}) copy-start(s32[96]{0:T(128)} %param.9) | copy-start | bytes 1156
  16.5 16.3 %all-to-all-start.1 = ((bf16[16,136,128]{2,1,0:T(8,128)(2,1)}), bf16[16,136,128]{2,1,0:T(8,128)(2,1)S(1)}, u32[]{:S(2)}, u32[]{:S(2)}) async-start(bf16[16,136,128]{2,1,0:T(8,128)(2,1)} %ends.1), calls=%async_computation.1 | async-start | bytes 1114112 | tf_op jit(solution)/shard_map/all_to_all | solution.py:278
  20.1 5.0 %collective-permute-start = (f32[8,128]{1,0:T(8,128)S(1)}, f32[8,128]{1,0:T(8,128)S(1)}, u32[]{:S(2)}, u32[]{:S(2)}) collective-permute-start(f32[8,128]{1,0:T(8,128)S(1)} %get-tuple-element.14.idrow), channel_id=1, source_target_pairs={{0,1},{1,2},{2,3},{3,4},{4,5},{5,6},{6,7},{7,8},{8,9},{9,10},{10,1... | collective-permute-start | bytes 12296 | tf_op jit(solution)/shard_map/ppermute | solution.py:269
  25.1 1.1 %copy-start.2 = (bf16[96,4096]{1,0:T(8,128)(2,1)S(1)}, bf16[96,4096]{1,0:T(8,128)(2,1)}, u32[]{:S(2)}) copy-start(bf16[96,4096]{1,0:T(8,128)(2,1)} %q_ref.3) | copy-start | bytes 2359300
  26.2 1.1 %copy-start.5 = (bf16[96,4096]{1,0:T(8,128)(2,1)S(1)}, bf16[96,4096]{1,0:T(8,128)(2,1)}, u32[]{:S(2)}) copy-start(bf16[96,4096]{1,0:T(8,128)(2,1)} %k_ref.3) | copy-start | bytes 2359300
  27.4 1.1 %copy-start.7 = (bf16[96,4096]{1,0:T(8,128)(2,1)S(1)}, bf16[96,4096]{1,0:T(8,128)(2,1)}, u32[]{:S(2)}) copy-start(bf16[96,4096]{1,0:T(8,128)(2,1)} %v_ref.3) | copy-start | bytes 2359300
  31.6 1.2 %copy-start = (f32[96,4096]{1,0:T(8,128)}, f32[96,4096]{1,0:T(8,128)S(1)}, u32[]{:S(2)}) copy-start(f32[96,4096]{1,0:T(8,128)S(1)} %get-tuple-element.20.fade_ref) | copy-start | bytes 4718596
  32.8 26.3 %copy-start.1 = (f32[96,4096]{1,0:T(8,128)S(1)}, f32[96,4096]{1,0:T(8,128)}, u32[]{:S(2)}) copy-start(f32[96,4096]{1,0:T(8,128)} %copy-done) | copy-start | bytes 4718596
  32.8 26.3 %copy-start.3 = (bf16[96,4096]{1,0:T(8,128)(2,1)S(1)}, bf16[96,4096]{1,0:T(8,128)(2,1)}, u32[]{:S(2)}) copy-start(bf16[96,4096]{1,0:T(8,128)(2,1)} %q_ref.3) | copy-start | bytes 2359300
  32.8 26.3 %copy-start.8 = (f32[4096]{0:T(1024)S(1)}, f32[4096]{0:T(1024)}, u32[]{:S(2)}) copy-start(f32[4096]{0:T(1024)} %param.11) | copy-start | bytes 49156
  32.9 6.0 %collective-permute-start.1 = (bf16[4,136,128]{2,1,0:T(8,128)(2,1)S(1)}, bf16[4,136,128]{2,1,0:T(8,128)(2,1)S(1)}, u32[]{:S(2)}, u32[]{:S(2)}) collective-permute-start(bf16[4,136,128]{2,1,0:T(8,128)(2,1)S(1)} %half.1), channel_id=1, source_target_pairs={{0,4},{1,5},{2,6},{3,7},{4,0},{5,1},{6,2},{7,3},{8,12},{9,13},{10,... | collective-permute-start | bytes 417800 | tf_op jit(solution)/shard_map/ppermute | solution.py:309

commit v5 on v4

--- a/solution.py
+++ b/solution.py
@@ -10,7 +10,6 @@
 HD = 64
 LANES = 2 * HD
 NEVER = 1e9
-BOTH_LAST = (((1,), (1,)), ((), ()))
 
 
 def rate_of(facts, head, here):
@@ -29,19 +28,33 @@
     return jnp.where(lane < HD, rates[0], rates[1])
 
 
-def turn_kernel(ids, k_ref, v_ref, turned, filled, idrow, idcol):
+def turn_kernel(ids, k_ref, v_ref, turned, filled, idrow, idcol, ids_here, keys, sems):
     tokens, width = k_ref.shape
+    parts = sems.shape[0] - 2
+    share = width // parts
+    copies = [pltpu.make_async_copy(ids, ids_here, sems.at[parts])]
+    for part in range(parts):
+        columns = slice(part * share, (part + 1) * share)
+        copies.append(
+            pltpu.make_async_copy(k_ref.at[:, columns], keys.at[:, columns], sems.at[part])
+        )
+    copies.append(pltpu.make_async_copy(v_ref, filled.at[:tokens, :], sems.at[parts + 1]))
+    for copy in copies:
+        copy.start()
+    filled[tokens:, :] = jnp.zeros((LANES - tokens, width), filled.dtype)
+    copies[0].wait()
     fill = jnp.full((1, LANES - tokens), -1.0, jnp.float32)
-    row = jnp.concatenate([ids[...].astype(jnp.float32), fill], 1)
+    row = jnp.concatenate([ids_here[...].astype(jnp.float32), fill], 1)
     idrow[...] = jnp.broadcast_to(row, idrow.shape)
     idcol[...] = jnp.transpose(jnp.broadcast_to(row, (LANES, LANES)))[:tokens]
-    filled[:tokens, :] = v_ref[...]
-    filled[tokens:, :] = jnp.zeros((LANES - tokens, width), filled.dtype)
     blank = jnp.zeros((LANES - tokens, LANES), jnp.float32)
-    for j in range(width // LANES):
-        columns = slice(j * LANES, (j + 1) * LANES)
-        block = jnp.concatenate([k_ref[:, columns].astype(jnp.float32), blank], 0)
-        turned[columns, :] = jnp.transpose(block)
+    for part in range(parts):
+        copies[part + 1].wait()
+        for at in range(part * share, (part + 1) * share, LANES):
+            columns = slice(at, at + LANES)
+            block = jnp.concatenate([keys[:, columns].astype(jnp.float32), blank], 0)
+            turned[columns, :] = jnp.transpose(block)
+    copies[-1].wait()
 
 
 def ends_kernel(here, tokens, rows, facts, idrow, turned, v_ref, out_ref):
@@ -77,53 +90,35 @@
 
 
 def inner_kernel(
-    here, pairs, rows, chunks, facts, idcol, idrow, earlier, q_ref, k_ref, v_ref,
-    out_ref, fade_ref, one_ref, half_ref
+    here, rows, chunks, facts, idcol, idrow, q_ref, turned, v_ref, out_ref, one_ref, half_ref, rates_ref
 ):
-    tokens = k_ref.shape[0]
-    step = pl.program_id(0)
-    first = step * pairs
-    ctx, uly = lax.axis_index("ctx"), lax.axis_index("uly")
-
-    @pl.when(step == 0)
-    def _():
-        owner = ctx * chunks + lax.rem(uly, chunks)
-        share = min(rows, HD)
-        for at in range(0, rows, share):
-            rate = pair_rate(facts, lax.div(owner * rows + at, HD), here)
-            for ref, length in ((one_ref, tokens), (half_ref, tokens * chunks)):
-                ref[at : at + share, :] = jnp.broadcast_to(
-                    jnp.exp(-rate * float(length)), (share, LANES)
-                )
-
+    tokens, width = q_ref.shape
+    owner = lax.axis_index("ctx") * chunks + lax.rem(lax.axis_index("uly"), chunks)
+    share = min(rows, HD)
+    for at in range(0, rows, share):
+        rate = pair_rate(facts, lax.div(owner * rows + at, HD), here)
+        for ref, length in ((one_ref, tokens), (half_ref, tokens * chunks)):
+            ref[at : at + share, :] = jnp.broadcast_to(
+                jnp.exp(-rate * float(length)), (share, LANES)
+            )
     lane = lax.broadcasted_iota(jnp.int32, (tokens, LANES), 1)
-    place = lax.broadcasted_iota(jnp.int32, (tokens, LANES), 0)
-    t = lax.broadcasted_iota(jnp.int32, (tokens, tokens), 0)
-    s = lax.broadcasted_iota(jnp.int32, (tokens, tokens), 1)
-    seen = (t >= s) & (idcol[:, :tokens] == idrow[:1, :tokens])
-    age = jnp.where(seen, (t - s).astype(jnp.float32), NEVER)
-    before = jnp.where(ctx + uly > 0, earlier[:1, tokens - 1 : tokens], -1.0)
-    since = jnp.where(idcol[...] == before, (place + 1).astype(jnp.float32), NEVER)
-    for j in range(pairs):
+    t = lax.broadcasted_iota(jnp.int32, (tokens, LANES), 0)
+    seen = (t >= lane) & (idcol[...] == idrow[:1, :])
+    age = jnp.where(seen, (t - lane).astype(jnp.float32), NEVER)
+    for j in range(width // LANES):
         columns = slice(j * LANES, (j + 1) * LANES)
         q = q_ref[:, columns]
         zero = jnp.zeros_like(q)
         stacked = jnp.concatenate([jnp.where(lane < HD, q, zero), jnp.where(lane < HD, zero, q)], 0)
-        scores = lax.dot_general(
-            stacked, k_ref[:, columns], BOTH_LAST, preferred_element_type=jnp.float32
-        )
-        rates = [
-            facts[
-                pl.ds(lax.div(2 * (first + j) + one, here), 1),
-                (2 * j + one) % here : (2 * j + one) % here + 1,
-            ]
-            for one in (0, 1)
-        ]
+        scores = jnp.dot(
+            stacked, turned[columns, :].astype(jnp.bfloat16), preferred_element_type=jnp.float32
+        )
+        rates = [rate_of(facts, 2 * j + one, here) for one in (0, 1)]
         weight = jnp.concatenate([jnp.exp(-rate * age) for rate in rates], 0)
         probs = (scores * weight).astype(jnp.bfloat16)
         got = jnp.dot(probs, v_ref[:, columns], preferred_element_type=jnp.float32)
         out_ref[:, columns] = jnp.where(lane < HD, got[:tokens], got[tokens:])
-        fade_ref[:, columns] = jnp.exp(-jnp.where(lane < HD, rates[0], rates[1]) * since)
+        rates_ref[:, columns] = jnp.where(lane[:1] < HD, rates[0], rates[1])
 
 
 def few(count):
@@ -155,6 +150,7 @@
 
 def scan_kernel(chunks, one, half, in_ref, other, out_ref):
     count, rows = in_ref.shape[0], one.shape[0]
+    marks = (out_ref.shape[1] - rows, LANES)
     later = lax.axis_index("uly") >= chunks
 
     def over_other(state, last, c, wanted):
@@ -170,7 +166,8 @@
         def step(j, carry):
             state, last = carry
             at = c * chunks + j
-            out_ref[at] = state.astype(out_ref.dtype)
+            out_ref[at, :rows, :] = state.astype(out_ref.dtype)
+            out_ref[at, rows:, :] = jnp.broadcast_to(last, marks).astype(out_ref.dtype)
             piece = in_ref[at]
             own = piece[rows : rows + 1].astype(jnp.float32)
             linked = jnp.where(own == last, one[...], 0.0)
@@ -183,24 +180,37 @@
     lax.fori_loop(0, count // chunks, over_slice, begin, unroll=few(count // chunks))
 
 
-def norm_kernel(q_ref, s_ref, inner_ref, fade_ref, gain, out_ref, raw, done, sems):
+def norm_kernel(rows, idcol, rates, q_ref, s_ref, inner_ref, gain, out_ref, raw, done, sems):
     tokens, width = q_ref.shape
     lane = lax.broadcasted_iota(jnp.int32, (HD, LANES), 1)
+    place = lax.broadcasted_iota(jnp.int32, (tokens, LANES), 0)
+    before = s_ref[0, rows : rows + 8, :].astype(jnp.float32)[:1]
+    age = jnp.where(idcol[...] == before, (place + 1).astype(jnp.float32), NEVER)
     zero = jnp.zeros((HD, LANES), s_ref.dtype)
     total = jnp.zeros((tokens, LANES), jnp.float32)
+    share = min(rows, HD)
     for j in range(0, width // LANES, 2):
         square = []
         for one in (0, 1):
-            state = s_ref[(j + one) * HD : (j + one + 1) * HD, :]
+            state = [
+                s_ref[at // rows, at % rows : at % rows + share, :]
+                for at in range((j + one) * HD, (j + one + 1) * HD, share)
+            ]
+            if len(state) > 1:
+                state = [jnp.concatenate([s.astype(jnp.float32) for s in state], 0).astype(zero.dtype)]
+            state = state[0]
             for half in (jnp.where(lane < HD, state, zero), jnp.where(lane < HD, zero, state)):
                 square.append(jnp.concatenate([zero, half] if one else [half, zero], 1))
         columns = slice(j * LANES, (j + 2) * LANES)
         outer = jnp.dot(
             q_ref[:, columns], jnp.concatenate(square, 0), preferred_element_type=jnp.float32
         )
-        value = inner_ref[:, columns] + outer * fade_ref[:, columns]
-        total += value[:, :LANES] * value[:, :LANES] + value[:, LANES:] * value[:, LANES:]
-        raw[:, columns] = value
+        for one in (0, 1):
+            columns = slice((j + one) * LANES, (j + one + 1) * LANES)
+            fade = jnp.exp(-rates[:, columns] * age)
+            value = inner_ref[:, columns] + outer[:, one * LANES : (one + 1) * LANES] * fade
+            total += value * value
+            raw[:, columns] = value
     mean = jnp.sum(total, axis=1, keepdims=True) / float(width)
     scale = jnp.broadcast_to(lax.rsqrt(mean + 1e-06), (tokens, LANES))
     parts = sems.shape[0]
@@ -227,8 +237,6 @@
     chunks = members // 2
     group = slices * chunks
     all_pairs = width // LANES
-    steps = 4
-    pairs = all_pairs // steps
     rows = all_pairs * HD // group
     groups = [
         [c * members + half * chunks + u for c in range(slices) for u in range(chunks)]
@@ -240,11 +248,8 @@
         for c in range(slices)
         for u in range(members)
     ]
-    forward = [(i, i + 1) for i in range(slices * members - 1)]
 
     vmem = pl.BlockSpec(memory_space=pltpu.VMEM)
-    whole = lambda shape: pl.BlockSpec(shape, lambda i: (0,) * len(shape))
-    part = pl.BlockSpec((tokens, pairs * LANES), lambda i: (0, i))
     params = pltpu.CompilerParams(vmem_limit_bytes=32 * 1024 * 1024)
     shape = jax.ShapeDtypeStruct
 
@@ -254,7 +259,7 @@
     )
     turned, filled, idrow, idcol = pl.pallas_call(
         turn_kernel,
-        in_specs=[vmem] * 3,
+        in_specs=[pl.BlockSpec(memory_space=pltpu.HBM)] * 3,
         out_specs=[vmem] * 4,
         out_shape=[
             shape((width, LANES), jnp.float32),
@@ -262,11 +267,15 @@
             shape((8, LANES), jnp.float32),
             shape((tokens, LANES), jnp.float32),
         ],
+        scratch_shapes=[
+            pltpu.VMEM((1, tokens), jnp.int32),
+            pltpu.VMEM((tokens, width), jnp.bfloat16),
+            pltpu.SemaphoreType.DMA((6,)),
+        ],
         compiler_params=params,
         cost_estimate=pl.CostEstimate(flops=0, bytes_accessed=12_000_000, transcendentals=0),
         name="turn",
     )(doc_ids[None, :], keys, values)
-    earlier = lax.ppermute(idrow, axes, forward)
     ends = pl.pallas_call(
         functools.partial(ends_kernel, here, tokens, rows),
         in_specs=[vmem] * 4,
@@ -278,26 +287,22 @@
     pieces = lax.all_to_all(
         ends, axes, split_axis=0, concat_axis=0, axis_index_groups=groups, tiled=True
     )
-    inner, fade, one, half = pl.pallas_call(
-        functools.partial(inner_kernel, here, pairs, rows, chunks),
-        grid=(steps,),
-        in_specs=[
-            whole((members, here)), whole((tokens, LANES)), whole((8, LANES)), whole((8, LANES)),
-            part, part, part,
-        ],
-        out_specs=[part, part, whole((rows, LANES)), whole((rows, LANES))],
+    inner, one, half, rates = pl.pallas_call(
+        functools.partial(inner_kernel, here, rows, chunks),
+        in_specs=[vmem] * 6,
+        out_specs=[vmem] * 4,
         out_shape=[
-            shape((tokens, width), jnp.float32),
             shape((tokens, width), jnp.float32),
             shape((rows, LANES), jnp.float32),
             shape((rows, LANES), jnp.float32),
+            shape((1, width), jnp.float32),
         ],
         compiler_params=params,
         cost_estimate=pl.CostEstimate(
             flops=8_000_000_000, bytes_accessed=4_000_000, transcendentals=600_000
         ),
         name="inner",
-    )(facts, idcol, idrow, earlier, queries, keys, values)
+    )(facts, idcol, idrow, queries, turned, filled)
     halves = pl.pallas_call(
         functools.partial(half_kernel, chunks),
         in_specs=[vmem] * 2,
@@ -311,7 +316,7 @@
         functools.partial(scan_kernel, chunks),
         in_specs=[vmem] * 4,
         out_specs=vmem,
-        out_shape=shape((group, rows, LANES), jnp.bfloat16),
+        out_shape=shape((group, rows + 8, LANES), jnp.bfloat16),
         compiler_params=params,
         name="scan",
     )(one, half, pieces, other)
@@ -319,8 +324,8 @@
         before, axes, split_axis=0, concat_axis=0, axis_index_groups=groups, tiled=True
     )
     return pl.pallas_call(
-        norm_kernel,
-        in_specs=[vmem] * 5,
+        functools.partial(norm_kernel, rows),
+        in_specs=[vmem] * 6,
         out_specs=pl.BlockSpec(memory_space=pl.ANY),
         out_shape=shape((tokens, width), jnp.bfloat16),
         scratch_shapes=[
@@ -330,7 +335,7 @@
         ],
         compiler_params=params,
         name="norm",
-    )(queries, states.reshape(all_pairs * HD, LANES), inner, fade, norm_gain[None, :])
+    )(idcol, rates, queries, states, inner, norm_gain[None, :])
 
 
 def solution(mesh):

time: 61.4 us -> 58.6 us (0.954)
  blocking collectives: 19.8 us -> 13.6 us
  waiting for transfers between devices: 7.67 us -> 12.2 us
  local copies, waits for them, and re-layouts: 8.74 us -> 12.9 us
  starting transfers between devices: 17.3 us -> 13.4 us
  Pallas kernels: 7.22 us -> 5.8 us
    all_to_all x1, blocking collectives: 19.8 us -> 13.6 us  [local(): lax.all_to_all(before, axes, split_axis=0, concat_axis=0, axis_index_grou...]
    unnamed x20 -> x36, local copies, waits for them, and re-layouts: 7.49 us -> 11.7 us
    ppermute x1, waiting for transfers between devices: 3.29 us -> 7.17 us  [local(): other = lax.ppermute(halves, axes, swap)]
    ppermute x1 -> x0, starting transfers between devices: 3.7 us -> none  [local(): earlier = lax.ppermute(idrow, axes, forward)]
    all_to_all x1, waiting for transfers between devices: 0.01 us -> 3.44 us  [local(): lax.all_to_all(ends, axes, split_axis=0, concat_axis=0, axis_index_groups...]
    all_to_all x1, waiting for transfers between devices: 3.06 us -> 1.58 us  [local(): lax.all_to_all(jnp.broadcast_to(decay_rate[None, :], (members, here)), 'u...]
    pallas_call x3, Pallas kernels: 5.24 us -> 3.83 us  [the longest x1 1.76 us: local(): pl.pallas_call(functools.partial(norm_kernel, rows), in_specs=[vmem] * 6,...]
    ppermute x1 -> x0, waiting for transfers between devices: 1.31 us -> none  [local(): earlier = lax.ppermute(idrow, axes, forward)]
  transfers between devices with their start and end apart: 4 -> 3, of which waited for: 3 -> 3; matrix products, arithmetic and copies ran while one was open for 0% -> 0% of each run, Pallas kernels for 6% -> 4%
where the time goes in v5:
time: 58.6 us; the launch traced here: 58 us
  blocking collectives  13.6 us (23%)
  starting transfers between devices  13.4 us (23%)
  local copies, waits for them, and re-layouts  12.9 us (22%)
  waiting for transfers between devices  12.2 us (21%)
  Pallas kernels  5.8 us (10%)
    all_to_all x1, blocking collectives, local(): lax.all_to_all(before, axes, split_axis=0, concat_axis=0, axis_index_grou...  13.6 us
    unnamed x36, local copies, waits for them, and re-layouts  11.7 us
    all_to_all x1, starting transfers between devices, local(): lax.all_to_all(jnp.broadcast_to(decay_rate[None, :], (members, here)), 'u...  7.25 us
    ppermute x1, waiting for transfers between devices, local(): other = lax.ppermute(halves, axes, swap)  7.17 us
    all_to_all x1, starting transfers between devices, local(): lax.all_to_all(ends, axes, split_axis=0, concat_axis=0, axis_index_groups...  3.68 us
    all_to_all x1, waiting for transfers between devices, local(): lax.all_to_all(ends, axes, split_axis=0, concat_axis=0, axis_index_groups...  3.44 us
    ppermute x1, starting transfers between devices, local(): other = lax.ppermute(halves, axes, swap)  2.43 us
    pallas_call x1, Pallas kernels, local(): pl.pallas_call(functools.partial(norm_kernel, rows), in_specs=[vmem] * 6,...  1.76 us
  transfers between devices with their start and end apart: 3, of which 3 were waited for; matrix products, arithmetic and copies ran while one was open for 0% of the time, Pallas kernels for 4%

profile of v5, /device:TPU:0, one launch (start us, length us, event | category | flops | bytes accessed | tf_op | source)
XLA Modules:
  0.0 58.0 jit_solution(6343254554626270406)
XLA Ops:
  0.0 1.2 %broadcast_in_dim.13 = f32[8,1,8]{2,1,0:T(1,128)} broadcast(f32[8]{0:T(128)} %param.10), dimensions={2} | broadcast | bytes 288 | tf_op jit(solution)/shard_map/broadcast_in_dim | solution.py:257
  1.2 7.3 %all-to-all-start = ((f32[8,1,8]{2,1,0:T(1,128)}), f32[8,1,8]{2,1,0:T(1,128)S(1)}, u32[]{:S(2)}, u32[]{:S(2)}) async-start(f32[8,1,8]{2,1,0:T(1,128)} %broadcast_in_dim.13), calls=%async_computation | async-start | bytes 8192 | tf_op jit(solution)/shard_map/all_to_all | solution.py:256
  8.5 1.1 %copy-done.5 = bf16[96,4096]{1,0:T(8,128)(2,1)S(1)} copy-done((bf16[96,4096]{1,0:T(8,128)(2,1)S(1)}, bf16[96,4096]{1,0:T(8,128)(2,1)}, u32[]{:S(2)}) %copy-start.5) | copy-done | bytes 786456
  9.6 1.1 %copy-done.6 = bf16[96,4096]{1,0:T(8,128)(2,1)S(1)} copy-done((bf16[96,4096]{1,0:T(8,128)(2,1)S(1)}, bf16[96,4096]{1,0:T(8,128)(2,1)}, u32[]{:S(2)}) %copy-start.6) | copy-done | bytes 786456
  10.8 0.7 %copy-done.17 = s32[96]{0:T(128)S(1)} copy-done((s32[96]{0:T(128)S(1)}, s32[96]{0:T(128)}, u32[]{:S(2)}) %copy-start.17) | copy-done | bytes 408
  11.4 0.9 %turn.1 = (f32[4096,128]{1,0:T(8,128)S(1)}, bf16[128,4096]{1,0:T(8,128)(2,1)S(1)}, f32[8,128]{1,0:T(8,128)S(1)}, f32[96,128]{1,0:T(8,128)S(1)}) custom-call(s32[1,96]{1,0:T(1,128)S(1)} %bitcast.6, bf16[96,4096]{1,0:T(8,128)(2,1)S(1)} %copy-done.5, bf16[96,4096]{1,0:T(8,128)(2,1)S(1)} %copy-done.6), custom_call_target="tpu_custom_call" | custom-call | bytes 12000000 | tf_op jit(solution)/shard_map/turn/pallas_call | solution.py:260
  12.3 1.0 %copy-done.2 = bf16[128,4096]{1,0:T(8,128)(2,1)} copy-done((bf16[128,4096]{1,0:T(8,128)(2,1)}, bf16[128,4096]{1,0:T(8,128)(2,1)S(1)}, u32[]{:S(2)}) %copy-start.2) | copy-done | bytes 1048600
  13.3 1.6 %all-to-all-done = f32[8,1,8]{2,1,0:T(1,128)S(1)} async-done(((f32[8,1,8]{2,1,0:T(1,128)}), f32[8,1,8]{2,1,0:T(1,128)S(1)}, u32[]{:S(2)}, u32[]{:S(2)}) %all-to-all-start) | async-done | bytes 288 | tf_op jit(solution)/shard_map/all_to_all | solution.py:256
  14.9 1.2 %copy-done.3 = bf16[128,4096]{1,0:T(8,128)(2,1)S(1)} copy-done((bf16[128,4096]{1,0:T(8,128)(2,1)S(1)}, bf16[128,4096]{1,0:T(8,128)(2,1)}, u32[]{:S(2)}) %copy-start.3) | copy-done | bytes 1048600
  16.1 1.6 %ends.1 = bf16[16,136,128]{2,1,0:T(8,128)(2,1)} custom-call(f32[8,8]{1,0:T(8,128)S(1)} %bitcast.3, f32[8,128]{1,0:T(8,128)S(1)} %get-tuple-element.14.idrow, f32[4096,128]{1,0:T(8,128)S(1)} %get-tuple-element.15.turned, bf16[128,4096]{1,0:T(8,128)(2,1)S(1)} %copy-done.3), custom_call_target="tpu_custom_call" | custom-call | tf_op jit(solution)/shard_map/ends/pallas_call | solution.py:279
  17.7 3.7 %all-to-all-start.1 = ((bf16[16,136,128]{2,1,0:T(8,128)(2,1)}), bf16[16,136,128]{2,1,0:T(8,128)(2,1)S(1)}, u32[]{:S(2)}, u32[]{:S(2)}) async-start(bf16[16,136,128]{2,1,0:T(8,128)(2,1)} %ends.1), calls=%async_computation.1 | async-start | bytes 1114112 | tf_op jit(solution)/shard_map/all_to_all | solution.py:287
  21.4 1.2 %copy-done.4 = bf16[128,4096]{1,0:T(8,128)(2,1)S(1)} copy-done((bf16[128,4096]{1,0:T(8,128)(2,1)S(1)}, bf16[128,4096]{1,0:T(8,128)(2,1)}, u32[]{:S(2)}) %copy-start.4) | copy-done | bytes 1048600
  22.7 0.7 %copy-done.11 = f32[8,1,8]{2,1,0:T(1,128)S(1)} copy-done((f32[8,1,8]{2,1,0:T(1,128)S(1)}, f32[8,1,8]{2,1,0:T(1,128)}, u32[]{:S(2)}) %copy-start.11) | copy-done | bytes 280
  23.3 0.7 %copy-done.16 = f32[8,128]{1,0:T(8,128)S(1)} copy-done((f32[8,128]{1,0:T(8,128)S(1)}, f32[8,128]{1,0:T(8,128)}, u32[]{:S(2)}) %copy-start.16) | copy-done | bytes 4120
  24.0 1.2 %inner.1 = (f32[96,4096]{1,0:T(8,128)S(1)}, f32[128,128]{1,0:T(8,128)S(1)}, f32[128,128]{1,0:T(8,128)S(1)}, f32[1,4096]{1,0:T(1,128)S(1)}) custom-call(f32[8,8]{1,0:T(8,128)S(1)} %bitcast.4, f32[96,128]{1,0:T(8,128)S(1)} %get-tuple-element.13.idcol, f32[8,128]{1,0:T(8,128)S(1)} %copy-done.16, bf16[96,4096]{1,0:T(8,128)(2,1)S(1)} %copy-done.7, ...), custom_call_target="tpu_custom_call" | custom-call | flops 8000000000 | bytes 4000000 | tf_op jit(solution)/shard_map/inner/pallas_call | solution.py:290
  25.2 1.1 %copy-done = f32[96,4096]{1,0:T(8,128)} copy-done((f32[96,4096]{1,0:T(8,128)}, f32[96,4096]{1,0:T(8,128)S(1)}, u32[]{:S(2)}) %copy-start) | copy-done | bytes 1572888
  26.4 0.6 %copy-done.8 = f32[128,128]{1,0:T(8,128)} copy-done((f32[128,128]{1,0:T(8,128)}, f32[128,128]{1,0:T(8,128)S(1)}, u32[]{:S(2)}) %copy-start.8) | copy-done | bytes 65560
  27.6 3.4 %all-to-all-done.1.in_ref = bf16[16,136,128]{2,1,0:T(8,128)(2,1)S(1)} async-done(((bf16[16,136,128]{2,1,0:T(8,128)(2,1)}), bf16[16,136,128]{2,1,0:T(8,128)(2,1)S(1)}, u32[]{:S(2)}, u32[]{:S(2)}) %all-to-all-start.1) | async-done | bytes 557088 | tf_op jit(solution)/shard_map/all_to_all | solution.py:287
  31.2 2.4 %collective-permute-start = (bf16[4,136,128]{2,1,0:T(8,128)(2,1)S(1)}, bf16[4,136,128]{2,1,0:T(8,128)(2,1)S(1)}, u32[]{:S(2)}, u32[]{:S(2)}) collective-permute-start(bf16[4,136,128]{2,1,0:T(8,128)(2,1)S(1)} %half.1), channel_id=1, source_target_pairs={{0,4},{1,5},{2,6},{3,7},{4,0},{5,1},{6,2},{7,3},{8,12},{9,13},{10,... | collective-permute-start | bytes 417800 | tf_op jit(solution)/shard_map/ppermute | solution.py:314
  33.6 7.2 %collective-permute-done.other = bf16[4,136,128]{2,1,0:T(8,128)(2,1)S(1)} collective-permute-done((bf16[4,136,128]{2,1,0:T(8,128)(2,1)S(1)}, bf16[4,136,128]{2,1,0:T(8,128)(2,1)S(1)}, u32[]{:S(2)}, u32[]{:S(2)}) %collective-permute-start) | collective-permute-done | bytes 139296 | tf_op jit(solution)/shard_map/ppermute | solution.py:314
  40.8 0.8 %copy-done.9 = f32[128,128]{1,0:T(8,128)S(1)} copy-done((f32[128,128]{1,0:T(8,128)S(1)}, f32[128,128]{1,0:T(8,128)}, u32[]{:S(2)}) %copy-start.9) | copy-done | bytes 65560
  41.9 13.6 %all_to_all.18.s_ref = bf16[16,136,128]{2,1,0:T(8,128)(2,1)S(1)} all-to-all(bf16[16,136,128]{2,1,0:T(8,128)(2,1)S(1)} %scan.1), channel_id=1, replica_groups={{0,1,2,3,8,9,10,11,16,17,18,19,24,25,26,27},{4,5,6,7,12,13,14,15,20,21,..., dimensions={0} | all-to-all | bytes 1114112 | tf_op jit(solution)/shard_map/all_to_all | solution.py:323
  55.5 0.7 %copy-done.12 = f32[4096]{0:T(1024)S(1)} copy-done((f32[4096]{0:T(1024)S(1)}, f32[4096]{0:T(1024)}, u32[]{:S(2)}) %copy-start.12) | copy-done | bytes 16408
  56.2 1.8 %norm.1 = bf16[96,4096]{1,0:T(8,128)(2,1)} custom-call(f32[96,128]{1,0:T(8,128)S(1)} %get-tuple-element.13.idcol, f32[1,4096]{1,0:T(1,128)S(1)} %copy-done.14, bf16[96,4096]{1,0:T(8,128)(2,1)S(1)} %copy-done.7, bf16[16,136,128]{2,1,0:T(8,128)(2,1)S(1)} %all_to_all.18.s_ref, f32[96,4096]{1,0:T(8,128)S(1)} %copy-done.1, f32[1,4096]{1,0:T(1,128)S(1)} %bitcast.5), custom_call_target="tpu_custom_call" | custom-call | tf_op jit(solution)/shard_map/norm/pallas_call | solution.py:326
  (26 shorter events, 1.0 us)
Async XLA Ops:
  1.2 13.6 %all-to-all-start = ((f32[8,1,8]{2,1,0:T(1,128)}), f32[8,1,8]{2,1,0:T(1,128)S(1)}, u32[]{:S(2)}, u32[]{:S(2)}) async-start(f32[8,1,8]{2,1,0:T(1,128)} %broadcast_in_dim.13), calls=%async_computation | async-start | bytes 8192 | tf_op jit(solution)/shard_map/all_to_all | solution.py:256
  8.5 1.1 %copy-start.5 = (bf16[96,4096]{1,0:T(8,128)(2,1)S(1)}, bf16[96,4096]{1,0:T(8,128)(2,1)}, u32[]{:S(2)}) copy-start(bf16[96,4096]{1,0:T(8,128)(2,1)} %k_ref.1) | copy-start | bytes 2359300
  9.6 1.1 %copy-start.6 = (bf16[96,4096]{1,0:T(8,128)(2,1)S(1)}, bf16[96,4096]{1,0:T(8,128)(2,1)}, u32[]{:S(2)}) copy-start(bf16[96,4096]{1,0:T(8,128)(2,1)} %v_ref.1) | copy-start | bytes 2359300
  10.8 0.7 %copy-start.17 = (s32[96]{0:T(128)S(1)}, s32[96]{0:T(128)}, u32[]{:S(2)}) copy-start(s32[96]{0:T(128)} %param.9) | copy-start | bytes 1156
  12.3 1.0 %copy-start.2 = (bf16[128,4096]{1,0:T(8,128)(2,1)}, bf16[128,4096]{1,0:T(8,128)(2,1)S(1)}, u32[]{:S(2)}) copy-start(bf16[128,4096]{1,0:T(8,128)(2,1)S(1)} %get-tuple-element.16.v_ref) | copy-start | bytes 3145732
  13.3 4.4 %copy-start.15 = (f32[8,128]{1,0:T(8,128)}, f32[8,128]{1,0:T(8,128)S(1)}, u32[]{:S(2)}) copy-start(f32[8,128]{1,0:T(8,128)S(1)} %get-tuple-element.14.idrow) | copy-start | bytes 12292
  14.9 2.8 %copy-start.10 = (f32[8,1,8]{2,1,0:T(1,128)}, f32[8,1,8]{2,1,0:T(1,128)S(1)}, u32[]{:S(2)}) copy-start(f32[8,1,8]{2,1,0:T(1,128)S(1)} %all-to-all-done) | copy-start | bytes 772
  14.9 1.2 %copy-start.3 = (bf16[128,4096]{1,0:T(8,128)(2,1)S(1)}, bf16[128,4096]{1,0:T(8,128)(2,1)}, u32[]{:S(2)}) copy-start(bf16[128,4096]{1,0:T(8,128)(2,1)} %copy-done.2) | copy-start | bytes 3145732
  16.1 5.3 %copy-start.7 = (bf16[96,4096]{1,0:T(8,128)(2,1)S(1)}, bf16[96,4096]{1,0:T(8,128)(2,1)}, u32[]{:S(2)}) copy-start(bf16[96,4096]{1,0:T(8,128)(2,1)} %q_ref.3) | copy-start | bytes 2359300
  17.7 13.3 %all-to-all-start.1 = ((bf16[16,136,128]{2,1,0:T(8,128)(2,1)}), bf16[16,136,128]{2,1,0:T(8,128)(2,1)S(1)}, u32[]{:S(2)}, u32[]{:S(2)}) async-start(bf16[16,136,128]{2,1,0:T(8,128)(2,1)} %ends.1), calls=%async_computation.1 | async-start | bytes 1114112 | tf_op jit(solution)/shard_map/all_to_all | solution.py:287
  21.4 1.2 %copy-start.4 = (bf16[128,4096]{1,0:T(8,128)(2,1)S(1)}, bf16[128,4096]{1,0:T(8,128)(2,1)}, u32[]{:S(2)}) copy-start(bf16[128,4096]{1,0:T(8,128)(2,1)} %copy-done.2) | copy-start | bytes 3145732
  22.7 0.7 %copy-start.11 = (f32[8,1,8]{2,1,0:T(1,128)S(1)}, f32[8,1,8]{2,1,0:T(1,128)}, u32[]{:S(2)}) copy-start(f32[8,1,8]{2,1,0:T(1,128)} %copy-done.10) | copy-start | bytes 772
  23.3 0.7 %copy-start.16 = (f32[8,128]{1,0:T(8,128)S(1)}, f32[8,128]{1,0:T(8,128)}, u32[]{:S(2)}) copy-start(f32[8,128]{1,0:T(8,128)} %copy-done.15) | copy-start | bytes 12292
  25.2 1.2 %copy-start = (f32[96,4096]{1,0:T(8,128)}, f32[96,4096]{1,0:T(8,128)S(1)}, u32[]{:S(2)}) copy-start(f32[96,4096]{1,0:T(8,128)S(1)} %get-tuple-element.20.inner_ref) | copy-start | bytes 4718596
  26.4 0.6 %copy-start.8 = (f32[128,128]{1,0:T(8,128)}, f32[128,128]{1,0:T(8,128)S(1)}, u32[]{:S(2)}) copy-start(f32[128,128]{1,0:T(8,128)S(1)} %get-tuple-element.19.half) | copy-start | bytes 196612
  27.0 0.6 %copy-start.13 = (f32[1,4096]{1,0:T(1,128)}, f32[1,4096]{1,0:T(1,128)S(1)}, u32[]{:S(2)}) copy-start(f32[1,4096]{1,0:T(1,128)S(1)} %get-tuple-element.17.rates) | copy-start | bytes 49156
  31.0 24.4 %copy-start.1 = (f32[96,4096]{1,0:T(8,128)S(1)}, f32[96,4096]{1,0:T(8,128)}, u32[]{:S(2)}) copy-start(f32[96,4096]{1,0:T(8,128)} %copy-done) | copy-start | bytes 4718596
  31.2 9.6 %collective-permute-start = (bf16[4,136,128]{2,1,0:T(8,128)(2,1)S(1)}, bf16[4,136,128]{2,1,0:T(8,128)(2,1)S(1)}, u32[]{:S(2)}, u32[]{:S(2)}) collective-permute-start(bf16[4,136,128]{2,1,0:T(8,128)(2,1)S(1)} %half.1), channel_id=1, source_target_pairs={{0,4},{1,5},{2,6},{3,7},{4,0},{5,1},{6,2},{7,3},{8,12},{9,13},{10,... | collective-permute-start | bytes 417800 | tf_op jit(solution)/shard_map/ppermute | solution.py:314
  40.8 0.8 %copy-start.9 = (f32[128,128]{1,0:T(8,128)S(1)}, f32[128,128]{1,0:T(8,128)}, u32[]{:S(2)}) copy-start(f32[128,128]{1,0:T(8,128)} %copy-done.8) | copy-start | bytes 196612
  41.6 13.8 %copy-start.14 = (f32[1,4096]{1,0:T(1,128)S(1)}, f32[1,4096]{1,0:T(1,128)}, u32[]{:S(2)}) copy-start(f32[1,4096]{1,0:T(1,128)} %copy-done.13) | copy-start | bytes 49156
  55.5 0.7 %copy-start.12 = (f32[4096]{0:T(1024)S(1)}, f32[4096]{0:T(1024)}, u32[]{:S(2)}) copy-start(f32[4096]{0:T(1024)} %param.11) | copy-start | bytes 49156

commit v6 on v3

v6 whole, which is shorter than its diff:
```python
import functools

import jax
import jax.numpy as jnp
from jax import lax
from jax.experimental import pallas as pl
from jax.experimental.pallas import tpu as pltpu
from jax.sharding import PartitionSpec as P

HD = 64
LANES = 2 * HD
NEVER = 1e9


def rate_of(facts, head, here):
    return facts[head // here : head // here + 1, head % here : head % here + 1]


def pair_rate(facts, pair, here):
    lane = lax.broadcasted_iota(jnp.int32, (1, LANES), 1)
    rates = []
    for head in (2 * pair, 2 * pair + 1):
        row = facts[pl.ds(lax.div(head, here), 1), :]
        rates.append(
            jnp.sum(jnp.where(lane == lax.rem(head, here), row, 0.0), axis=1, keepdims=True)
        )
    return jnp.where(lane < HD, rates[0], rates[1])


def pair_kernel(rates, ids, next_rates, next_ids, out_ref):
    here, tokens = rates.shape[1], ids.shape[1]
    me = lax.axis_index("uly")
    place = lax.broadcasted_iota(jnp.int32, out_ref.shape, 0)
    out = jnp.zeros(out_ref.shape, jnp.float32)
    for member, rate, document in ((me, rates, ids), (me ^ 1, next_rates, next_ids)):
        last = document[:, tokens - 1 :].astype(jnp.float32)
        row = jnp.concatenate([rate[...], jnp.broadcast_to(last, (1, LANES - here))], 1)
        out = jnp.where(place == member, row, out)
    out_ref[...] = out


def turn_kernel(ids, k_ref, v_ref, turned, filled, idrow, idcol, ids_here, keys, sems):
    tokens, width = k_ref.shape
    parts = sems.shape[0] - 2
    share = width // parts
    copies = [pltpu.make_async_copy(ids, ids_here, sems.at[parts])]
    for part in range(parts):
        columns = slice(part * share, (part + 1) * share)
        copies.append(
            pltpu.make_async_copy(k_ref.at[:, columns], keys.at[:, columns], sems.at[part])
        )
    copies.append(pltpu.make_async_copy(v_ref, filled.at[:tokens, :], sems.at[parts + 1]))
    for copy in copies:
        copy.start()
    filled[tokens:, :] = jnp.zeros((LANES - tokens, width), filled.dtype)
    copies[0].wait()
    fill = jnp.full((1, LANES - tokens), -1.0, jnp.float32)
    row = jnp.concatenate([ids_here[...].astype(jnp.float32), fill], 1)
    idrow[...] = jnp.broadcast_to(row, idrow.shape)
    idcol[...] = jnp.transpose(jnp.broadcast_to(row, (LANES, LANES)))[:tokens]
    blank = jnp.zeros((LANES - tokens, LANES), jnp.float32)
    for part in range(parts):
        copies[part + 1].wait()
        for at in range(part * share, (part + 1) * share, LANES):
            columns = slice(at, at + LANES)
            block = jnp.concatenate([keys[:, columns].astype(jnp.float32), blank], 0)
            turned[columns, :] = jnp.transpose(block)
    copies[-1].wait()


def ends_kernel(here, tokens, known, found, idrow, turned, v_ref, out_ref):
    width = v_ref.shape[1]
    facts = known[...] + found[...]
    lane = lax.broadcasted_iota(jnp.int32, (HD, LANES), 1)
    place = lax.broadcasted_iota(jnp.int32, idrow.shape, 1)
    ids = idrow[...]
    last = ids[:, tokens - 1 : tokens]
    age = jnp.where(ids == last, (tokens - 1 - place).astype(jnp.float32), NEVER)
    for j in range(width // LANES):
        weighted = []
        for head in (2 * j, 2 * j + 1):
            weight = jnp.exp(-rate_of(facts, head, here) * age)
            keys = turned[head * HD : (head + 1) * HD, :].reshape(HD // 8, 8, LANES)
            weighted.append((keys * weight[None]).reshape(HD, LANES))
        weighted = jnp.concatenate(weighted, 0)
        high = weighted.astype(jnp.bfloat16)
        low = (weighted - high.astype(jnp.float32)).astype(jnp.bfloat16)
        v = v_ref[:, j * LANES : (j + 1) * LANES]
        both = jnp.dot(
            jnp.concatenate([high, low], 1),
            jnp.concatenate([v, v], 0),
            preferred_element_type=jnp.float32,
        )
        out_ref[j * HD : (j + 1) * HD, :] = jnp.where(lane < HD, both[:HD], both[HD:]).astype(
            jnp.bfloat16
        )


def inner_kernel(
    here, known, found, idcol, idrow, q_ref, turned, v_ref, ends, out_ref, facts, rates_ref
):
    tokens, width = q_ref.shape
    facts[...] = known[...] + found[...]
    lane = lax.broadcasted_iota(jnp.int32, (tokens, LANES), 1)
    t = lax.broadcasted_iota(jnp.int32, (tokens, LANES), 0)
    seen = (t >= lane) & (idcol[...] == idrow[:1, :])
    age = jnp.where(seen, (t - lane).astype(jnp.float32), NEVER)
    for j in range(width // LANES):
        columns = slice(j * LANES, (j + 1) * LANES)
        q = q_ref[:, columns]
        zero = jnp.zeros_like(q)
        stacked = jnp.concatenate([jnp.where(lane < HD, q, zero), jnp.where(lane < HD, zero, q)], 0)
        scores = jnp.dot(
            stacked, turned[columns, :].astype(jnp.bfloat16), preferred_element_type=jnp.float32
        )
        rates = [rate_of(facts, 2 * j + one, here) for one in (0, 1)]
        weight = jnp.concatenate([jnp.exp(-rate * age) for rate in rates], 0)
        probs = (scores * weight).astype(jnp.bfloat16)
        got = jnp.dot(probs, v_ref[:, columns], preferred_element_type=jnp.float32)
        out_ref[:, columns] = jnp.where(lane < HD, got[:tokens], got[tokens:])
        rates_ref[:, columns] = jnp.where(lane[:1] < HD, rates[0], rates[1])


def link_kernel(here, tokens, rows, facts, *refs):
    others, (link, before, last) = refs[:-3], refs[-3:]
    members, slices = facts.shape[0], len(others) + 1
    ctx, uly = lax.axis_index("ctx"), lax.axis_index("uly")
    for back, tile in enumerate((facts, *others)):
        at = lax.rem(ctx + slices - back, slices) * members
        last[pl.ds(pl.multiple_of(at, members), members), :] = jnp.broadcast_to(
            tile[:, LANES - 1 :], (members, LANES)
        )
    me = ctx * members + uly
    decay = jnp.exp(-pair_rate(facts, lax.div(me * rows, HD), here) * float(tokens))
    now = last[...]
    then = jnp.concatenate([now[:1], now[:-1]], 0)
    link[...] = jnp.where(now == then, decay, 0.0)
    before[...] = jnp.where(me > 0, last[pl.ds(jnp.maximum(me - 1, 0), 1), :], -1.0)


def scan_kernel(link, in_ref, out_ref):
    count = in_ref.shape[0]
    out_ref[0] = jnp.zeros(out_ref.shape[1:], out_ref.dtype)

    def step(i, state):
        state = in_ref[i].astype(jnp.float32) + link[pl.ds(i, 1), :] * state
        out_ref[i + 1] = state.astype(out_ref.dtype)
        return state

    zero = jnp.zeros(in_ref.shape[1:], jnp.float32)
    lax.fori_loop(0, count - 1, step, zero, unroll=min(count - 1, 31))


def norm_kernel(idcol, before, rates, q_ref, s_ref, inner_ref, gain, out_ref, raw, done, sems):
    tokens, width = q_ref.shape
    lane = lax.broadcasted_iota(jnp.int32, (HD, LANES), 1)
    place = lax.broadcasted_iota(jnp.int32, (tokens, LANES), 0)
    age = jnp.where(idcol[...] == before[...], (place + 1).astype(jnp.float32), NEVER)
    zero = jnp.zeros((HD, LANES), s_ref.dtype)
    total = jnp.zeros((tokens, LANES), jnp.float32)
    for j in range(0, width // LANES, 2):
        square = []
        for one in (0, 1):
            state = s_ref[(j + one) * HD : (j + one + 1) * HD, :]
            for half in (jnp.where(lane < HD, state, zero), jnp.where(lane < HD, zero, state)):
                square.append(jnp.concatenate([zero, half] if one else [half, zero], 1))
        columns = slice(j * LANES, (j + 2) * LANES)
        outer = jnp.dot(
            q_ref[:, columns], jnp.concatenate(square, 0), preferred_element_type=jnp.float32
        )
        for one in (0, 1):
            columns = slice((j + one) * LANES, (j + one + 1) * LANES)
            fade = jnp.exp(-rates[:, columns] * age)
            value = inner_ref[:, columns] + outer[:, one * LANES : (one + 1) * LANES] * fade
            total += value * value
            raw[:, columns] = value
    mean = jnp.sum(total, axis=1, keepdims=True) / float(width)
    scale = jnp.broadcast_to(lax.rsqrt(mean + 1e-06), (tokens, LANES))
    parts = sems.shape[0]
    share = width // parts
    copies = []
    for part in range(parts):
        for at in range(part * share, (part + 1) * share, LANES):
            columns = slice(at, at + LANES)
            done[:, columns] = (raw[:, columns] * scale * gain[:, columns]).astype(jnp.bfloat16)
        columns = slice(part * share, (part + 1) * share)
        copies.append(
            pltpu.make_async_copy(done.at[:, columns], out_ref.at[:, columns], sems.at[part])
        )
        copies[-1].start()
    for copy in copies:
        copy.wait()


def local(queries, keys, values, doc_ids, decay_rate, norm_gain):
    tokens, width = queries.shape
    here = decay_rate.shape[0]
    axes = ("ctx", "uly")
    slices, members = lax.axis_size("ctx"), lax.axis_size("uly")
    count = slices * members
    all_pairs = width // LANES
    rows = all_pairs * HD // count

    vmem = pl.BlockSpec(memory_space=pltpu.VMEM)
    params = pltpu.CompilerParams(vmem_limit_bytes=32 * 1024 * 1024)
    shape = jax.ShapeDtypeStruct
    tile = shape((members, LANES), jnp.float32)

    def swapped(value, reach):
        return lax.ppermute(value, "uly", [(u, u ^ reach) for u in range(members)])

    next_rates, next_ids = swapped(decay_rate, 1), swapped(doc_ids, 1)
    known = pl.pallas_call(
        pair_kernel,
        in_specs=[vmem] * 4,
        out_specs=vmem,
        out_shape=tile,
        compiler_params=params,
        name="pair",
    )(decay_rate[None, :], doc_ids[None, :], next_rates[None, :], next_ids[None, :])
    reach, found = 2, jnp.zeros(tile.shape, tile.dtype)
    while reach < members:
        known = known + found if reach > 2 else known
        found = swapped(known, reach)
        reach *= 2

    turned, filled, idrow, idcol = pl.pallas_call(
        turn_kernel,
        in_specs=[pl.BlockSpec(memory_space=pl.ANY)] * 3,
        out_specs=[vmem] * 4,
        out_shape=[
            shape((width, LANES), jnp.float32),
            shape((LANES, width), jnp.bfloat16),
            shape((8, LANES), jnp.float32),
            shape((tokens, LANES), jnp.float32),
        ],
        scratch_shapes=[
            pltpu.VMEM((1, tokens), jnp.int32),
            pltpu.VMEM((tokens, width), jnp.bfloat16),
            pltpu.SemaphoreType.DMA((6,)),
        ],
        compiler_params=params,
        cost_estimate=pl.CostEstimate(flops=0, bytes_accessed=12_000_000, transcendentals=0),
        name="turn",
    )(doc_ids[None, :], keys, values)
    ends = pl.pallas_call(
        functools.partial(ends_kernel, here, tokens),
        in_specs=[vmem] * 5,
        out_specs=vmem,
        out_shape=shape((all_pairs * HD, LANES), jnp.bfloat16),
        compiler_params=params,
        name="ends",
    )(known, found, idrow, turned, filled)
    pieces = lax.all_to_all(
        ends.reshape(count, rows, LANES), axes, split_axis=0, concat_axis=0, tiled=True
    )
    inner, facts, rates = pl.pallas_call(
        functools.partial(inner_kernel, here),
        in_specs=[vmem] * 7 + [pl.BlockSpec(memory_space=pl.ANY)],
        out_specs=[vmem] * 3,
        out_shape=[shape((tokens, width), jnp.float32), tile, shape((1, width), jnp.float32)],
        compiler_params=params,
        cost_estimate=pl.CostEstimate(
            flops=8_000_000_000, bytes_accessed=4_000_000, transcendentals=600_000
        ),
        name="inner",
    )(known, found, idcol, idrow, queries, turned, filled, ends)
    others = [
        lax.ppermute(facts, "ctx", [(c, (c + ahead) % slices) for c in range(slices)])
        for ahead in range(1, slices)
    ]
    link, before = pl.pallas_call(
        functools.partial(link_kernel, here, tokens, rows),
        in_specs=[vmem] * slices,
        out_specs=[vmem] * 2,
        out_shape=[shape((count, LANES), jnp.float32), shape((1, LANES), jnp.float32)],
        scratch_shapes=[pltpu.VMEM((count, LANES), jnp.float32)],
        compiler_params=params,
        name="link",
    )(facts, *others)
    moved = pl.pallas_call(
        scan_kernel,
        in_specs=[vmem] * 2,
        out_specs=vmem,
        out_shape=shape((count, rows, LANES), jnp.bfloat16),
        compiler_params=params,
        name="scan",
    )(link, pieces)
    states = lax.all_to_all(moved, axes, split_axis=0, concat_axis=0, tiled=True)
    return pl.pallas_call(
        norm_kernel,
        in_specs=[vmem] * 7,
        out_specs=pl.BlockSpec(memory_space=pl.ANY),
        out_shape=shape((tokens, width), jnp.bfloat16),
        scratch_shapes=[
            pltpu.VMEM((tokens, width), jnp.float32),
            pltpu.VMEM((tokens, width), jnp.bfloat16),
            pltpu.SemaphoreType.DMA((4,)),
        ],
        compiler_params=params,
        name="norm",
    )(idcol, before, rates, queries, states.reshape(all_pairs * HD, LANES), inner, norm_gain[None, :])


def solution(mesh):
    in_specs = (
        P(("ctx", "uly"), None),
        P(("ctx", "uly"), None),
        P(("ctx", "uly"), None),
        P(("ctx", "uly")),
        P("uly"),
        P(),
    )
    out_specs = P(("ctx", "uly"), None)
    return jax.shard_map(local, mesh=mesh, in_specs=in_specs, out_specs=out_specs, check_vma=False)
```

time: 57.6 us -> 60.7 us (1.054)
  waiting for transfers between devices: 12.4 us -> 16.3 us
  starting transfers between devices: 9.9 us -> 12.8 us
  other arithmetic: 1.39 us -> 0.01 us
  Pallas kernels: 6.86 us -> 5.73 us
  local copies, waits for them, and re-layouts: 8.09 us -> 6.96 us
    ppermute x0 -> x7, starting transfers between devices: none -> 9.17 us  [the longest x4 7.14 us: swapped(): return lax.ppermute(value, 'uly', [(u, u ^ reach) for u in range(members)])]
    ppermute x0 -> x7, waiting for transfers between devices: none -> 8.82 us  [the longest x4 5.68 us: swapped(): return lax.ppermute(value, 'uly', [(u, u ^ reach) for u in range(members)])]
    all_to_all x1 -> x0, starting transfers between devices: 7.3 us -> none  [local(): lax.all_to_all(jnp.broadcast_to(own[None, :], (count, LANES)), axes, spli...]
    all_to_all x1 -> x0, waiting for transfers between devices: 3.71 us -> none  [local(): lax.all_to_all(jnp.broadcast_to(own[None, :], (count, LANES)), axes, spli...]
    all_to_all x1, waiting for transfers between devices: 8.73 us -> 7.49 us  [local(): lax.all_to_all(ends.reshape(count, rows, LANES), axes, split_axis=0, conc...]
    pallas_call x3 -> x5, Pallas kernels: 5.14 us -> 4 us  [the longest x1 1.77 us: local(): pl.pallas_call(norm_kernel, in_specs=[vmem] * 7, out_specs=pl.BlockSpec(m...]
    all_to_all x1, starting transfers between devices: 2.61 us -> 3.66 us  [local(): lax.all_to_all(ends.reshape(count, rows, LANES), axes, split_axis=0, conc...]
    add x1, other arithmetic: 0.73 us -> 0.01 us  [local(): known = known + found if reach > 2 else known]
  transfers between devices with their start and end apart: 2 -> 8, of which waited for: 2 -> 5; matrix products, arithmetic and copies ran while one was open for 0% -> 0% of each run, Pallas kernels for 6% -> 4%
where the time goes in v6:
time: 60.7 us; the launch traced here: 60.3 us
  blocking collectives  18.4 us (30%)
  waiting for transfers between devices  16.3 us (27%)
  starting transfers between devices  12.8 us (21%)
  local copies, waits for them, and re-layouts  6.96 us (11%)
  Pallas kernels  5.73 us (9%)
    all_to_all x1, blocking collectives, local(): lax.all_to_all(moved, axes, split_axis=0, concat_axis=0, tiled=True)  18.4 us
    all_to_all x1, waiting for transfers between devices, local(): lax.all_to_all(ends.reshape(count, rows, LANES), axes, split_axis=0, conc...  7.49 us
    ppermute x4, starting transfers between devices, swapped(): return lax.ppermute(value, 'uly', [(u, u ^ reach) for u in range(members)])  7.14 us
    unnamed x20, local copies, waits for them, and re-layouts  6.96 us
    ppermute x4, waiting for transfers between devices, swapped(): return lax.ppermute(value, 'uly', [(u, u ^ reach) for u in range(members)])  5.68 us
    all_to_all x1, starting transfers between devices, local(): lax.all_to_all(ends.reshape(count, rows, LANES), axes, split_axis=0, conc...  3.66 us
    ppermute x3, waiting for transfers between devices, local(): lax.ppermute(facts, 'ctx', [(c, (c + ahead) % slices) for c in range(slic...  3.14 us
    ppermute x3, starting transfers between devices, local(): lax.ppermute(facts, 'ctx', [(c, (c + ahead) % slices) for c in range(slic...  2.03 us
  transfers between devices with their start and end apart: 8, of which 5 were waited for; matrix products, arithmetic and copies ran while one was open for 0% of the time, Pallas kernels for 4%

profile of v6, /device:TPU:0, one launch (start us, length us, event | category | flops | bytes accessed | tf_op | source)
XLA Modules:
  0.0 60.3 jit_solution(11744079191517915172)
XLA Ops:
  0.0 2.9 %collective-permute-start.1 = (s32[96]{0:T(128)}, s32[96]{0:T(128)S(1)}, u32[]{:S(2)}, u32[]{:S(2)}) collective-permute-start(s32[96]{0:T(128)} %param.9), channel_id=1, source_target_pairs={{0,1},{1,0},{2,3},{3,2},{4,5},{5,4},{6,7},{7,6},{8,9},{9,8},{10,11... | collective-permute-start | bytes 1160 | tf_op jit(solution)/shard_map/ppermute | solution.py:210
  3.0 3.6 %collective-permute-done = f32[8]{0:T(128)S(1)} collective-permute-done((f32[8]{0:T(128)}, f32[8]{0:T(128)S(1)}, u32[]{:S(2)}, u32[]{:S(2)}) %collective-permute-start) | collective-permute-done | bytes 64 | tf_op jit(solution)/shard_map/ppermute | solution.py:210
  6.6 0.7 %copy-done.8 = s32[96]{0:T(128)S(1)} copy-done((s32[96]{0:T(128)S(1)}, s32[96]{0:T(128)}, u32[]{:S(2)}) %copy-start.8) | copy-done | bytes 408
  7.3 0.7 %copy-done.9 = f32[8]{0:T(128)S(1)} copy-done((f32[8]{0:T(128)S(1)}, f32[8]{0:T(128)}, u32[]{:S(2)}) %copy-start.9) | copy-done | bytes 56
  8.0 1.6 %collective-permute-start.2 = (f32[8,128]{1,0:T(8,128)S(1)}, f32[8,128]{1,0:T(8,128)S(1)}, u32[]{:S(2)}, u32[]{:S(2)}) collective-permute-start(f32[8,128]{1,0:T(8,128)S(1)} %pair.1), channel_id=1, source_target_pairs={{0,2},{1,3},{2,0},{3,1},{4,6},{5,7},{6,4},{7,5},{8,10},{9,11},{10,... | collective-permute-start | bytes 12296 | tf_op jit(solution)/shard_map/ppermute | solution.py:210
  9.6 2.0 %collective-permute-done.2 = f32[8,128]{1,0:T(8,128)S(1)} collective-permute-done((f32[8,128]{1,0:T(8,128)S(1)}, f32[8,128]{1,0:T(8,128)S(1)}, u32[]{:S(2)}, u32[]{:S(2)}) %collective-permute-start.2) | collective-permute-done | bytes 4128 | tf_op jit(solution)/shard_map/ppermute | solution.py:210
  11.6 2.6 %collective-permute-start.3 = (f32[8,128]{1,0:T(8,128)S(1)}, f32[8,128]{1,0:T(8,128)S(1)}, u32[]{:S(2)}, u32[]{:S(2)}) collective-permute-start(f32[8,128]{1,0:T(8,128)S(1)} %add.3.known), channel_id=1, source_target_pairs={{0,4},{1,5},{2,6},{3,7},{4,0},{5,1},{6,2},{7,3},{8,12},{9,13},{10,... | collective-permute-start | bytes 12296 | tf_op jit(solution)/shard_map/ppermute | solution.py:210
  14.2 1.1 %copy-done.4 = bf16[96,4096]{1,0:T(8,128)(2,1)S(1)} copy-done((bf16[96,4096]{1,0:T(8,128)(2,1)S(1)}, bf16[96,4096]{1,0:T(8,128)(2,1)}, u32[]{:S(2)}) %copy-start.4) | copy-done | bytes 786456
  15.3 1.1 %copy-done.5 = bf16[96,4096]{1,0:T(8,128)(2,1)S(1)} copy-done((bf16[96,4096]{1,0:T(8,128)(2,1)S(1)}, bf16[96,4096]{1,0:T(8,128)(2,1)}, u32[]{:S(2)}) %copy-start.5) | copy-done | bytes 786456
  16.5 0.9 %turn.1 = (f32[4096,128]{1,0:T(8,128)S(1)}, bf16[128,4096]{1,0:T(8,128)(2,1)S(1)}, f32[8,128]{1,0:T(8,128)S(1)}, f32[96,128]{1,0:T(8,128)S(1)}) custom-call(s32[1,96]{1,0:T(1,128)S(1)} %bitcast.10, bf16[96,4096]{1,0:T(8,128)(2,1)S(1)} %copy-done.4, bf16[96,4096]{1,0:T(8,128)(2,1)S(1)} %copy-done.5), custom_call_target="tpu_custom_call" | custom-call | bytes 12000000 | tf_op jit(solution)/shard_map/turn/pallas_call | solution.py:227
  17.4 1.6 %ends.1 = bf16[2048,128]{1,0:T(8,128)(2,1)} custom-call(f32[8,128]{1,0:T(8,128)S(1)} %add.3.known, f32[8,128]{1,0:T(8,128)S(1)} %collective-permute-done.3.found, f32[8,128]{1,0:T(8,128)S(1)} %get-tuple-element.15.idrow, f32[4096,128]{1,0:T(8,128)S(1)} %get-tuple-element.16.turned, bf16[128,4096]{1,0:T(8,128)(2,1)S(1)} %get-tuple-element.17.v_ref), custom_call_target="tpu_custom_call" | custom-call | tf_op jit(solution)/shard_map/ends/pallas_call | solution.py:246
  19.0 1.0 %copy-done.2 = bf16[128,4096]{1,0:T(8,128)(2,1)} copy-done((bf16[128,4096]{1,0:T(8,128)(2,1)}, bf16[128,4096]{1,0:T(8,128)(2,1)S(1)}, u32[]{:S(2)}) %copy-start.2) | copy-done | bytes 1048600
  20.0 3.7 %all-to-all-start = ((bf16[32,64,128]{2,1,0:T(8,128)(2,1)}), bf16[32,64,128]{2,1,0:T(8,128)(2,1)S(1)}, u32[]{:S(2)}, u32[]{:S(2)}) async-start(bf16[32,64,128]{2,1,0:T(8,128)(2,1)} %bitcast.4), calls=%async_computation | async-start | bytes 1048576 | tf_op jit(solution)/shard_map/all_to_all | solution.py:254
  23.7 1.2 %copy-done.3 = bf16[128,4096]{1,0:T(8,128)(2,1)S(1)} copy-done((bf16[128,4096]{1,0:T(8,128)(2,1)S(1)}, bf16[128,4096]{1,0:T(8,128)(2,1)}, u32[]{:S(2)}) %copy-start.3) | copy-done | bytes 1048600
  24.9 1.2 %inner.1 = (f32[96,4096]{1,0:T(8,128)S(1)}, f32[8,128]{1,0:T(8,128)S(1)}, f32[1,4096]{1,0:T(1,128)S(1)}) custom-call(f32[8,128]{1,0:T(8,128)S(1)} %add.3.known, f32[8,128]{1,0:T(8,128)S(1)} %collective-permute-done.3.found, f32[96,128]{1,0:T(8,128)S(1)} %get-tuple-element.14.idcol, f32[8,128]{1,0:T(8,128)S(1)} %get-tuple-element.15.idrow, ...), custom_call_target="tpu_custom_call" | custom-call | flops 8000000000 | bytes 4000000 | tf_op jit(solution)/shard_map/inner/pallas_call | solution.py:257
  26.1 1.2 %copy-done = f32[96,4096]{1,0:T(8,128)} copy-done((f32[96,4096]{1,0:T(8,128)}, f32[96,4096]{1,0:T(8,128)S(1)}, u32[]{:S(2)}) %copy-start) | copy-done | bytes 1572888
  27.3 1.5 %collective-permute-start.6 = (f32[8,128]{1,0:T(8,128)S(1)}, f32[8,128]{1,0:T(8,128)S(1)}, u32[]{:S(2)}, u32[]{:S(2)}) collective-permute-start(f32[8,128]{1,0:T(8,128)S(1)} %get-tuple-element.18.facts), channel_id=1, source_target_pairs={{0,24},{8,0},{16,8},{24,16},{1,25},{9,1},{17,9},{25,17},{2,26},{10... | collective-permute-start | bytes 12296 | tf_op jit(solution)/shard_map/ppermute | solution.py:269
  28.8 0.4 collective-permute-start.5
  29.1 0.1 collective-permute-start.4
  29.3 0.8 %collective-permute-done.6.refs_2_ = f32[8,128]{1,0:T(8,128)S(1)} collective-permute-done((f32[8,128]{1,0:T(8,128)S(1)}, f32[8,128]{1,0:T(8,128)S(1)}, u32[]{:S(2)}, u32[]{:S(2)}) %collective-permute-start.6) | collective-permute-done | bytes 4128 | tf_op jit(solution)/shard_map/ppermute | solution.py:269
  30.1 2.3 %collective-permute-done.5.refs_1_ = f32[8,128]{1,0:T(8,128)S(1)} collective-permute-done((f32[8,128]{1,0:T(8,128)S(1)}, f32[8,128]{1,0:T(8,128)S(1)}, u32[]{:S(2)}, u32[]{:S(2)}) %collective-permute-start.5) | collective-permute-done | bytes 4128 | tf_op jit(solution)/shard_map/ppermute | solution.py:269
  32.5 7.5 %all-to-all-done.in_ref = bf16[32,64,128]{2,1,0:T(8,128)(2,1)S(1)} async-done(((bf16[32,64,128]{2,1,0:T(8,128)(2,1)}), bf16[32,64,128]{2,1,0:T(8,128)(2,1)S(1)}, u32[]{:S(2)}, u32[]{:S(2)}) %all-to-all-start) | async-done | bytes 524320 | tf_op jit(solution)/shard_map/all_to_all | solution.py:254
  40.1 18.4 %all_to_all.10 = bf16[32,64,128]{2,1,0:T(8,128)(2,1)S(1)} all-to-all(bf16[32,64,128]{2,1,0:T(8,128)(2,1)S(1)} %scan.1), channel_id=1, replica_groups=mesh['ctx'=4,'uly'=8] {'ctx','uly'}, dimensions={0} | all-to-all | bytes 1048576 | tf_op jit(solution)/shard_map/all_to_all | solution.py:289
  58.6 1.8 %norm.1 = bf16[96,4096]{1,0:T(8,128)(2,1)} custom-call(f32[96,128]{1,0:T(8,128)S(1)} %get-tuple-element.14.idcol, f32[1,128]{1,0:T(1,128)S(1)} %get-tuple-element.19.before, f32[1,4096]{1,0:T(1,128)S(1)} %get-tuple-element.20.rates, bf16[96,4096]{1,0:T(8,128)(2,1)S(1)} %copy-done.6, bf16[2048,128]{1,0:T(8,128)(2,1)S(1)} %bitcast.7, ...), custom_call_target="tpu_custom_call" | custom-call | tf_op jit(solution)/shard_map/norm/pallas_call | solution.py:290
  (21 shorter events, 0.3 us)
Async XLA Ops:
  0.0 6.6 %collective-permute-start.1 = (s32[96]{0:T(128)}, s32[96]{0:T(128)S(1)}, u32[]{:S(2)}, u32[]{:S(2)}) collective-permute-start(s32[96]{0:T(128)} %param.9), channel_id=1, source_target_pairs={{0,1},{1,0},{2,3},{3,2},{4,5},{5,4},{6,7},{7,6},{8,9},{9,8},{10,11... | collective-permute-start | bytes 1160 | tf_op jit(solution)/shard_map/ppermute | solution.py:210
  2.9 3.7 %collective-permute-start = (f32[8]{0:T(128)}, f32[8]{0:T(128)S(1)}, u32[]{:S(2)}, u32[]{:S(2)}) collective-permute-start(f32[8]{0:T(128)} %param.10), channel_id=1, source_target_pairs={{0,1},{1,0},{2,3},{3,2},{4,5},{5,4},{6,7},{7,6},{8,9},{9,8},{10,11... | collective-permute-start | bytes 104 | tf_op jit(solution)/shard_map/ppermute | solution.py:210
  6.6 0.7 %copy-start.8 = (s32[96]{0:T(128)S(1)}, s32[96]{0:T(128)}, u32[]{:S(2)}) copy-start(s32[96]{0:T(128)} %param.9) | copy-start | bytes 1156
  7.3 0.7 %copy-start.9 = (f32[8]{0:T(128)S(1)}, f32[8]{0:T(128)}, u32[]{:S(2)}) copy-start(f32[8]{0:T(128)} %param.10) | copy-start | bytes 100
  8.0 3.6 %collective-permute-start.2 = (f32[8,128]{1,0:T(8,128)S(1)}, f32[8,128]{1,0:T(8,128)S(1)}, u32[]{:S(2)}, u32[]{:S(2)}) collective-permute-start(f32[8,128]{1,0:T(8,128)S(1)} %pair.1), channel_id=1, source_target_pairs={{0,2},{1,3},{2,0},{3,1},{4,6},{5,7},{6,4},{7,5},{8,10},{9,11},{10,... | collective-permute-start | bytes 12296 | tf_op jit(solution)/shard_map/ppermute | solution.py:210
  11.6 5.8 %collective-permute-start.3 = (f32[8,128]{1,0:T(8,128)S(1)}, f32[8,128]{1,0:T(8,128)S(1)}, u32[]{:S(2)}, u32[]{:S(2)}) collective-permute-start(f32[8,128]{1,0:T(8,128)S(1)} %add.3.known), channel_id=1, source_target_pairs={{0,4},{1,5},{2,6},{3,7},{4,0},{5,1},{6,2},{7,3},{8,12},{9,13},{10,... | collective-permute-start | bytes 12296 | tf_op jit(solution)/shard_map/ppermute | solution.py:210
  14.2 1.1 %copy-start.4 = (bf16[96,4096]{1,0:T(8,128)(2,1)S(1)}, bf16[96,4096]{1,0:T(8,128)(2,1)}, u32[]{:S(2)}) copy-start(bf16[96,4096]{1,0:T(8,128)(2,1)} %k_ref.1) | copy-start | bytes 2359300
  15.3 1.1 %copy-start.5 = (bf16[96,4096]{1,0:T(8,128)(2,1)S(1)}, bf16[96,4096]{1,0:T(8,128)(2,1)}, u32[]{:S(2)}) copy-start(bf16[96,4096]{1,0:T(8,128)(2,1)} %v_ref.1) | copy-start | bytes 2359300
  17.4 6.3 %copy-start.6 = (bf16[96,4096]{1,0:T(8,128)(2,1)S(1)}, bf16[96,4096]{1,0:T(8,128)(2,1)}, u32[]{:S(2)}) copy-start(bf16[96,4096]{1,0:T(8,128)(2,1)} %q_ref.3) | copy-start | bytes 2359300
  19.0 1.0 %copy-start.2 = (bf16[128,4096]{1,0:T(8,128)(2,1)}, bf16[128,4096]{1,0:T(8,128)(2,1)S(1)}, u32[]{:S(2)}) copy-start(bf16[128,4096]{1,0:T(8,128)(2,1)S(1)} %get-tuple-element.17.v_ref) | copy-start | bytes 3145732
  20.0 20.0 %all-to-all-start = ((bf16[32,64,128]{2,1,0:T(8,128)(2,1)}), bf16[32,64,128]{2,1,0:T(8,128)(2,1)S(1)}, u32[]{:S(2)}, u32[]{:S(2)}) async-start(bf16[32,64,128]{2,1,0:T(8,128)(2,1)} %bitcast.4), calls=%async_computation | async-start | bytes 1048576 | tf_op jit(solution)/shard_map/all_to_all | solution.py:254
  23.7 1.2 %copy-start.3 = (bf16[128,4096]{1,0:T(8,128)(2,1)S(1)}, bf16[128,4096]{1,0:T(8,128)(2,1)}, u32[]{:S(2)}) copy-start(bf16[128,4096]{1,0:T(8,128)(2,1)} %copy-done.2) | copy-start | bytes 3145732
  26.1 1.2 %copy-start = (f32[96,4096]{1,0:T(8,128)}, f32[96,4096]{1,0:T(8,128)S(1)}, u32[]{:S(2)}) copy-start(f32[96,4096]{1,0:T(8,128)S(1)} %get-tuple-element.22.inner_ref) | copy-start | bytes 4718596
  27.3 31.3 %copy-start.7 = (f32[4096]{0:T(1024)S(1)}, f32[4096]{0:T(1024)}, u32[]{:S(2)}) copy-start(f32[4096]{0:T(1024)} %param.11) | copy-start | bytes 49156
  27.3 31.3 %copy-start.1 = (f32[96,4096]{1,0:T(8,128)S(1)}, f32[96,4096]{1,0:T(8,128)}, u32[]{:S(2)}) copy-start(f32[96,4096]{1,0:T(8,128)} %copy-done) | copy-start | bytes 4718596
  27.3 2.9 %collective-permute-start.6 = (f32[8,128]{1,0:T(8,128)S(1)}, f32[8,128]{1,0:T(8,128)S(1)}, u32[]{:S(2)}, u32[]{:S(2)}) collective-permute-start(f32[8,128]{1,0:T(8,128)S(1)} %get-tuple-element.18.facts), channel_id=1, source_target_pairs={{0,24},{8,0},{16,8},{24,16},{1,25},{9,1},{17,9},{25,17},{2,26},{10... | collective-permute-start | bytes 12296 | tf_op jit(solution)/shard_map/ppermute | solution.py:269
  28.8 3.6 %collective-permute-start.5 = (f32[8,128]{1,0:T(8,128)S(1)}, f32[8,128]{1,0:T(8,128)S(1)}, u32[]{:S(2)}, u32[]{:S(2)}) collective-permute-start(f32[8,128]{1,0:T(8,128)S(1)} %get-tuple-element.18.facts), channel_id=1, source_target_pairs={{0,16},{8,24},{16,0},{24,8},{1,17},{9,25},{17,1},{25,9},{2,18},{10... | collective-permute-start | bytes 12296 | tf_op jit(solution)/shard_map/ppermute | solution.py:269
  29.1 3.3 %collective-permute-start.4 = (f32[8,128]{1,0:T(8,128)S(1)}, f32[8,128]{1,0:T(8,128)S(1)}, u32[]{:S(2)}, u32[]{:S(2)}) collective-permute-start(f32[8,128]{1,0:T(8,128)S(1)} %get-tuple-element.18.facts), channel_id=1, source_target_pairs={{0,8},{8,16},{16,24},{24,0},{1,9},{9,17},{17,25},{25,1},{2,10},{10... | collective-permute-start | bytes 12296 | tf_op jit(solution)/shard_map/ppermute | solution.py:269

commit v7 on v6

--- a/solution.py
+++ b/solution.py
@@ -27,50 +27,29 @@
     return jnp.where(lane < HD, rates[0], rates[1])
 
 
-def pair_kernel(rates, ids, next_rates, next_ids, out_ref):
-    here, tokens = rates.shape[1], ids.shape[1]
-    me = lax.axis_index("uly")
-    place = lax.broadcasted_iota(jnp.int32, out_ref.shape, 0)
-    out = jnp.zeros(out_ref.shape, jnp.float32)
-    for member, rate, document in ((me, rates, ids), (me ^ 1, next_rates, next_ids)):
-        last = document[:, tokens - 1 :].astype(jnp.float32)
-        row = jnp.concatenate([rate[...], jnp.broadcast_to(last, (1, LANES - here))], 1)
-        out = jnp.where(place == member, row, out)
-    out_ref[...] = out
-
-
-def turn_kernel(ids, k_ref, v_ref, turned, filled, idrow, idcol, ids_here, keys, sems):
+def turn_kernel(row_ref, k_ref, v_ref, turned, filled, idrow, idcol):
     tokens, width = k_ref.shape
-    parts = sems.shape[0] - 2
-    share = width // parts
-    copies = [pltpu.make_async_copy(ids, ids_here, sems.at[parts])]
-    for part in range(parts):
-        columns = slice(part * share, (part + 1) * share)
-        copies.append(
-            pltpu.make_async_copy(k_ref.at[:, columns], keys.at[:, columns], sems.at[part])
-        )
-    copies.append(pltpu.make_async_copy(v_ref, filled.at[:tokens, :], sems.at[parts + 1]))
-    for copy in copies:
-        copy.start()
-    filled[tokens:, :] = jnp.zeros((LANES - tokens, width), filled.dtype)
-    copies[0].wait()
     fill = jnp.full((1, LANES - tokens), -1.0, jnp.float32)
-    row = jnp.concatenate([ids_here[...].astype(jnp.float32), fill], 1)
+    row = jnp.concatenate([row_ref[:, LANES - tokens :], fill], 1)
     idrow[...] = jnp.broadcast_to(row, idrow.shape)
     idcol[...] = jnp.transpose(jnp.broadcast_to(row, (LANES, LANES)))[:tokens]
+    filled[:tokens, :] = v_ref[...]
+    filled[tokens:, :] = jnp.zeros((LANES - tokens, width), filled.dtype)
     blank = jnp.zeros((LANES - tokens, LANES), jnp.float32)
-    for part in range(parts):
-        copies[part + 1].wait()
-        for at in range(part * share, (part + 1) * share, LANES):
-            columns = slice(at, at + LANES)
-            block = jnp.concatenate([keys[:, columns].astype(jnp.float32), blank], 0)
-            turned[columns, :] = jnp.transpose(block)
-    copies[-1].wait()
-
-
-def ends_kernel(here, tokens, known, found, idrow, turned, v_ref, out_ref):
+    for j in range(width // LANES):
+        columns = slice(j * LANES, (j + 1) * LANES)
+        block = jnp.concatenate([k_ref[:, columns].astype(jnp.float32), blank], 0)
+        turned[columns, :] = jnp.transpose(block).astype(turned.dtype)
+
+
+def ends_kernel(here, tokens, idrow, turned, v_ref, *refs):
     width = v_ref.shape[1]
-    facts = known[...] + found[...]
+    rows, (out_ref, facts) = refs[:-2], refs[-2:]
+    place = lax.broadcasted_iota(jnp.int32, facts.shape, 0)
+    tile = jnp.zeros(facts.shape, jnp.float32)
+    for apart, row in enumerate(rows):
+        tile = jnp.where(place == lax.axis_index("uly") ^ apart, row[...], tile)
+    facts[...] = tile
     lane = lax.broadcasted_iota(jnp.int32, (HD, LANES), 1)
     place = lax.broadcasted_iota(jnp.int32, idrow.shape, 1)
     ids = idrow[...]
@@ -80,8 +59,9 @@
         weighted = []
         for head in (2 * j, 2 * j + 1):
             weight = jnp.exp(-rate_of(facts, head, here) * age)
-            keys = turned[head * HD : (head + 1) * HD, :].reshape(HD // 8, 8, LANES)
-            weighted.append((keys * weight[None]).reshape(HD, LANES))
+            keys = turned[head * HD : (head + 1) * HD, :].astype(jnp.float32)
+            keys = keys.reshape(HD // 8, 8, LANES) * weight[None]
+            weighted.append(keys.reshape(HD, LANES))
         weighted = jnp.concatenate(weighted, 0)
         high = weighted.astype(jnp.bfloat16)
         low = (weighted - high.astype(jnp.float32)).astype(jnp.bfloat16)
@@ -97,10 +77,10 @@
 
 
 def inner_kernel(
-    here, known, found, idcol, idrow, q_ref, turned, v_ref, ends, out_ref, facts, rates_ref
+    here, facts, idcol, idrow, q_ref, turned, v_ref, out_ref, tile_ref, rates_ref
 ):
     tokens, width = q_ref.shape
-    facts[...] = known[...] + found[...]
+    tile_ref[...] = facts[...]
     lane = lax.broadcasted_iota(jnp.int32, (tokens, LANES), 1)
     t = lax.broadcasted_iota(jnp.int32, (tokens, LANES), 0)
     seen = (t >= lane) & (idcol[...] == idrow[:1, :])
@@ -111,7 +91,7 @@
         zero = jnp.zeros_like(q)
         stacked = jnp.concatenate([jnp.where(lane < HD, q, zero), jnp.where(lane < HD, zero, q)], 0)
         scores = jnp.dot(
-            stacked, turned[columns, :].astype(jnp.bfloat16), preferred_element_type=jnp.float32
+            stacked, turned[columns, :], preferred_element_type=jnp.float32
         )
         rates = [rate_of(facts, 2 * j + one, here) for one in (0, 1)]
         weight = jnp.concatenate([jnp.exp(-rate * age) for rate in rates], 0)
@@ -206,57 +186,41 @@
     shape = jax.ShapeDtypeStruct
     tile = shape((members, LANES), jnp.float32)
 
-    def swapped(value, reach):
-        return lax.ppermute(value, "uly", [(u, u ^ reach) for u in range(members)])
-
-    next_rates, next_ids = swapped(decay_rate, 1), swapped(doc_ids, 1)
-    known = pl.pallas_call(
-        pair_kernel,
-        in_specs=[vmem] * 4,
-        out_specs=vmem,
-        out_shape=tile,
-        compiler_params=params,
-        name="pair",
-    )(decay_rate[None, :], doc_ids[None, :], next_rates[None, :], next_ids[None, :])
-    reach, found = 2, jnp.zeros(tile.shape, tile.dtype)
-    while reach < members:
-        known = known + found if reach > 2 else known
-        found = swapped(known, reach)
-        reach *= 2
-
+    row = jnp.pad(decay_rate, (0, LANES - here)) + jnp.pad(
+        doc_ids, (LANES - tokens, 0)
+    ).astype(jnp.float32)
+    rows_of = [row] + [
+        lax.ppermute(row, "uly", [(u, u ^ apart) for u in range(members)])
+        for apart in range(1, members)
+    ]
     turned, filled, idrow, idcol = pl.pallas_call(
         turn_kernel,
-        in_specs=[pl.BlockSpec(memory_space=pl.ANY)] * 3,
+        in_specs=[vmem] * 3,
         out_specs=[vmem] * 4,
         out_shape=[
-            shape((width, LANES), jnp.float32),
+            shape((width, LANES), jnp.bfloat16),
             shape((LANES, width), jnp.bfloat16),
             shape((8, LANES), jnp.float32),
             shape((tokens, LANES), jnp.float32),
         ],
-        scratch_shapes=[
-            pltpu.VMEM((1, tokens), jnp.int32),
-            pltpu.VMEM((tokens, width), jnp.bfloat16),
-            pltpu.SemaphoreType.DMA((6,)),
-        ],
         compiler_params=params,
         cost_estimate=pl.CostEstimate(flops=0, bytes_accessed=12_000_000, transcendentals=0),
         name="turn",
-    )(doc_ids[None, :], keys, values)
-    ends = pl.pallas_call(
+    )(row[None, :], keys, values)
+    ends, facts = pl.pallas_call(
         functools.partial(ends_kernel, here, tokens),
-        in_specs=[vmem] * 5,
-        out_specs=vmem,
-        out_shape=shape((all_pairs * HD, LANES), jnp.bfloat16),
+        in_specs=[vmem] * (3 + members),
+        out_specs=[vmem] * 2,
+        out_shape=[shape((all_pairs * HD, LANES), jnp.bfloat16), tile],
         compiler_params=params,
         name="ends",
-    )(known, found, idrow, turned, filled)
+    )(idrow, turned, filled, *[found[None, :] for found in rows_of])
     pieces = lax.all_to_all(
         ends.reshape(count, rows, LANES), axes, split_axis=0, concat_axis=0, tiled=True
     )
-    inner, facts, rates = pl.pallas_call(
+    inner, slice_facts, rates = pl.pallas_call(
         functools.partial(inner_kernel, here),
-        in_specs=[vmem] * 7 + [pl.BlockSpec(memory_space=pl.ANY)],
+        in_specs=[vmem] * 6,
         out_specs=[vmem] * 3,
         out_shape=[shape((tokens, width), jnp.float32), tile, shape((1, width), jnp.float32)],
         compiler_params=params,
@@ -264,9 +228,9 @@
             flops=8_000_000_000, bytes_accessed=4_000_000, transcendentals=600_000
         ),
         name="inner",
-    )(known, found, idcol, idrow, queries, turned, filled, ends)
+    )(facts, idcol, idrow, queries, turned, filled)
     others = [
-        lax.ppermute(facts, "ctx", [(c, (c + ahead) % slices) for c in range(slices)])
+        lax.ppermute(slice_facts, "ctx", [(c, (c + ahead) % slices) for c in range(slices)])
         for ahead in range(1, slices)
     ]
     link, before = pl.pallas_call(
@@ -277,7 +241,7 @@
         scratch_shapes=[pltpu.VMEM((count, LANES), jnp.float32)],
         compiler_params=params,
         name="link",
-    )(facts, *others)
+    )(slice_facts, *others)
     moved = pl.pallas_call(
         scan_kernel,
         in_specs=[vmem] * 2,

time: 60.7 us -> 61.6 us (1.015)
  starting transfers between devices: 12.8 us -> 20.1 us
  waiting for transfers between devices: 16.3 us -> 11 us
  local copies, waits for them, and re-layouts: 6.96 us -> 5.63 us
  other arithmetic: 0.01 us -> 0.75 us
    ppermute x7 -> x10, starting transfers between devices: 9.17 us -> 14.5 us  [the longest x7 12.5 us: local(): lax.ppermute(row, 'uly', [(u, u ^ apart) for u in range(members)])]
    ppermute x7 -> x10, waiting for transfers between devices: 8.82 us -> 3.57 us  [the longest x3 3.14 us: local(): lax.ppermute(slice_facts, 'ctx', [(c, (c + ahead) % slices) for c in rang...]
    all_to_all x1, starting transfers between devices: 3.66 us -> 5.58 us  [local(): lax.all_to_all(ends.reshape(count, rows, LANES), axes, split_axis=0, conc...]
    unnamed x20 -> x14, local copies, waits for them, and re-layouts: 6.96 us -> 5.63 us
    add x1, other arithmetic: 0.01 us -> 0.75 us  [local(): jnp.pad(decay_rate, (0, LANES - here))]
    pallas_call x3 -> x2, Pallas kernels: 2.15 us -> 1.58 us  [the longest x1 1.18 us: local(): pl.pallas_call(functools.partial(inner_kernel, here), in_specs=[vmem] * 6...]
  transfers between devices with their start and end apart: 8 -> 11, of which waited for: 5 -> 4; matrix products, arithmetic and copies ran while one was open for 0% -> 0% of each run, Pallas kernels for 4% -> 3%
where the time goes in v7:
time: 61.6 us; the launch traced here: 61.2 us
  starting transfers between devices  20.1 us (33%)
  blocking collectives  18.4 us (30%)
  waiting for transfers between devices  11 us (18%)
  local copies, waits for them, and re-layouts  5.63 us (9%)
  Pallas kernels  5.16 us (8%)
  other arithmetic  0.75 us (1%)
    all_to_all x1, blocking collectives, local(): lax.all_to_all(moved, axes, split_axis=0, concat_axis=0, tiled=True)  18.4 us
    ppermute x7, starting transfers between devices, local(): lax.ppermute(row, 'uly', [(u, u ^ apart) for u in range(members)])  12.5 us
    all_to_all x1, waiting for transfers between devices, local(): lax.all_to_all(ends.reshape(count, rows, LANES), axes, split_axis=0, conc...  7.47 us
    unnamed x14, local copies, waits for them, and re-layouts  5.63 us
    all_to_all x1, starting transfers between devices, local(): lax.all_to_all(ends.reshape(count, rows, LANES), axes, split_axis=0, conc...  5.58 us
    ppermute x3, waiting for transfers between devices, local(): lax.ppermute(slice_facts, 'ctx', [(c, (c + ahead) % slices) for c in rang...  3.14 us
    ppermute x3, starting transfers between devices, local(): lax.ppermute(slice_facts, 'ctx', [(c, (c + ahead) % slices) for c in rang...  2.08 us
    pallas_call x1, Pallas kernels, local(): pl.pallas_call(norm_kernel, in_specs=[vmem] * 7, out_specs=pl.BlockSpec(m...  1.77 us
  transfers between devices with their start and end apart: 11, of which 4 were waited for; matrix products, arithmetic and copies ran while one was open for 0% of the time, Pallas kernels for 3%

profile of v7, /device:TPU:0, one launch (start us, length us, event | category | flops | bytes accessed | tf_op | source)
XLA Modules:
  0.0 61.2 jit_solution(1563631216989890721)
XLA Ops:
  0.0 0.7 %convert_add_fusion = f32[128]{0:T(128)S(1)} fusion(s32[96]{0:T(128)} %param.9, f32[8]{0:T(128)} %param.10), kind=kLoop, calls=%fused_computation | loop fusion | flops 256 | bytes 928 | tf_op jit(solution)/shard_map/add | solution.py:189
  0.7 6.0 %collective-permute-start.6 = (f32[128]{0:T(128)S(1)}, f32[128]{0:T(128)S(1)}, u32[]{:S(2)}, u32[]{:S(2)}) collective-permute-start(f32[128]{0:T(128)S(1)} %convert_add_fusion), channel_id=1, source_target_pairs={{0,7},{1,6},{2,5},{3,4},{4,3},{5,2},{6,1},{7,0},{8,15},{9,14},{10,... | collective-permute-start | bytes 1544 | tf_op jit(solution)/shard_map/ppermute | solution.py:193
  6.9 0.8 %collective-permute-start.4 = (f32[128]{0:T(128)S(1)}, f32[128]{0:T(128)S(1)}, u32[]{:S(2)}, u32[]{:S(2)}) collective-permute-start(f32[128]{0:T(128)S(1)} %convert_add_fusion), channel_id=1, source_target_pairs={{0,5},{1,4},{2,7},{3,6},{4,1},{5,0},{6,3},{7,2},{8,13},{9,12},{10,... | collective-permute-start | bytes 1544 | tf_op jit(solution)/shard_map/ppermute | solution.py:193
  7.7 2.0 %collective-permute-start.3 = (f32[128]{0:T(128)S(1)}, f32[128]{0:T(128)S(1)}, u32[]{:S(2)}, u32[]{:S(2)}) collective-permute-start(f32[128]{0:T(128)S(1)} %convert_add_fusion), channel_id=1, source_target_pairs={{0,4},{1,5},{2,6},{3,7},{4,0},{5,1},{6,2},{7,3},{8,12},{9,13},{10,... | collective-permute-start | bytes 1544 | tf_op jit(solution)/shard_map/ppermute | solution.py:193
  9.7 2.3 %collective-permute-start.2 = (f32[128]{0:T(128)S(1)}, f32[128]{0:T(128)S(1)}, u32[]{:S(2)}, u32[]{:S(2)}) collective-permute-start(f32[128]{0:T(128)S(1)} %convert_add_fusion), channel_id=1, source_target_pairs={{0,3},{1,2},{2,1},{3,0},{4,7},{5,6},{6,5},{7,4},{8,11},{9,10},{10,... | collective-permute-start | bytes 1544 | tf_op jit(solution)/shard_map/ppermute | solution.py:193
  12.0 0.8 %collective-permute-start.1 = (f32[128]{0:T(128)S(1)}, f32[128]{0:T(128)S(1)}, u32[]{:S(2)}, u32[]{:S(2)}) collective-permute-start(f32[128]{0:T(128)S(1)} %convert_add_fusion), channel_id=1, source_target_pairs={{0,2},{1,3},{2,0},{3,1},{4,6},{5,7},{6,4},{7,5},{8,10},{9,11},{10,... | collective-permute-start | bytes 1544 | tf_op jit(solution)/shard_map/ppermute | solution.py:193
  12.8 0.4 collective-permute-start
  13.2 1.1 %copy-done.2 = bf16[96,4096]{1,0:T(8,128)(2,1)S(1)} copy-done((bf16[96,4096]{1,0:T(8,128)(2,1)S(1)}, bf16[96,4096]{1,0:T(8,128)(2,1)}, u32[]{:S(2)}) %copy-start.2) | copy-done | bytes 786456
  14.4 1.1 %copy-done.3 = bf16[96,4096]{1,0:T(8,128)(2,1)S(1)} copy-done((bf16[96,4096]{1,0:T(8,128)(2,1)S(1)}, bf16[96,4096]{1,0:T(8,128)(2,1)}, u32[]{:S(2)}) %copy-start.3) | copy-done | bytes 786456
  15.5 0.4 turn.1
  15.9 0.4 collective-permute-done
  16.3 1.6 %ends.1 = (bf16[2048,128]{1,0:T(8,128)(2,1)}, f32[8,128]{1,0:T(8,128)S(1)}) custom-call(f32[8,128]{1,0:T(8,128)S(1)} %get-tuple-element.17.idrow, bf16[4096,128]{1,0:T(8,128)(2,1)S(1)} %get-tuple-element.18.turned, bf16[128,4096]{1,0:T(8,128)(2,1)S(1)} %get-tuple-element.19.v_ref, f32[1,128]{1,0:T(1,128)S(1)} %bitcast.14, f32[1,128]{1,0:T(1,128)S(1)} %bitcast.21, ...), custom_call_target="tpu_custom_call" | custom-call | tf_op jit(solution)/shard_map/ends/pallas_call | solution.py:210
  18.0 1.0 %copy-done = bf16[128,4096]{1,0:T(8,128)(2,1)} copy-done((bf16[128,4096]{1,0:T(8,128)(2,1)}, bf16[128,4096]{1,0:T(8,128)(2,1)S(1)}, u32[]{:S(2)}) %copy-start) | copy-done | bytes 1048600
  19.0 5.6 %all-to-all-start = ((bf16[32,64,128]{2,1,0:T(8,128)(2,1)}), bf16[32,64,128]{2,1,0:T(8,128)(2,1)S(1)}, u32[]{:S(2)}, u32[]{:S(2)}) async-start(bf16[32,64,128]{2,1,0:T(8,128)(2,1)} %bitcast.8), calls=%async_computation | async-start | bytes 1048576 | tf_op jit(solution)/shard_map/all_to_all | solution.py:218
  24.6 1.2 %copy-done.1 = bf16[128,4096]{1,0:T(8,128)(2,1)S(1)} copy-done((bf16[128,4096]{1,0:T(8,128)(2,1)S(1)}, bf16[128,4096]{1,0:T(8,128)(2,1)}, u32[]{:S(2)}) %copy-start.1) | copy-done | bytes 1048600
  25.8 1.1 %copy-done.4 = bf16[96,4096]{1,0:T(8,128)(2,1)S(1)} copy-done((bf16[96,4096]{1,0:T(8,128)(2,1)S(1)}, bf16[96,4096]{1,0:T(8,128)(2,1)}, u32[]{:S(2)}) %copy-start.4) | copy-done | bytes 786456
  26.9 1.2 %inner.1 = (f32[96,4096]{1,0:T(8,128)S(1)}, f32[8,128]{1,0:T(8,128)S(1)}, f32[1,4096]{1,0:T(1,128)S(1)}) custom-call(f32[8,128]{1,0:T(8,128)S(1)} %get-tuple-element.20.facts, f32[96,128]{1,0:T(8,128)S(1)} %get-tuple-element.16.idcol, f32[8,128]{1,0:T(8,128)S(1)} %get-tuple-element.17.idrow, bf16[96,4096]{1,0:T(8,128)(2,1)S(1)} %copy-done.4, ...), custom_call_target="tpu_custom_call" | custom-call | flops 8000000000 | bytes 4000000 | tf_op jit(solution)/shard_map/inner/pallas_call | solution.py:221
  28.1 1.6 %collective-permute-start.9 = (f32[8,128]{1,0:T(8,128)S(1)}, f32[8,128]{1,0:T(8,128)S(1)}, u32[]{:S(2)}, u32[]{:S(2)}) collective-permute-start(f32[8,128]{1,0:T(8,128)S(1)} %get-tuple-element.21.facts), channel_id=1, source_target_pairs={{0,24},{8,0},{16,8},{24,16},{1,25},{9,1},{17,9},{25,17},{2,26},{10... | collective-permute-start | bytes 12296 | tf_op jit(solution)/shard_map/ppermute | solution.py:233
  29.7 0.4 collective-permute-start.8
  30.2 0.8 %collective-permute-done.9.refs_2_ = f32[8,128]{1,0:T(8,128)S(1)} collective-permute-done((f32[8,128]{1,0:T(8,128)S(1)}, f32[8,128]{1,0:T(8,128)S(1)}, u32[]{:S(2)}, u32[]{:S(2)}) %collective-permute-start.9) | collective-permute-done | bytes 4128 | tf_op jit(solution)/shard_map/ppermute | solution.py:233
  31.0 2.3 %collective-permute-done.8.refs_1_ = f32[8,128]{1,0:T(8,128)S(1)} collective-permute-done((f32[8,128]{1,0:T(8,128)S(1)}, f32[8,128]{1,0:T(8,128)S(1)}, u32[]{:S(2)}, u32[]{:S(2)}) %collective-permute-start.8) | collective-permute-done | bytes 4128 | tf_op jit(solution)/shard_map/ppermute | solution.py:233
  33.4 7.5 %all-to-all-done.in_ref = bf16[32,64,128]{2,1,0:T(8,128)(2,1)S(1)} async-done(((bf16[32,64,128]{2,1,0:T(8,128)(2,1)}), bf16[32,64,128]{2,1,0:T(8,128)(2,1)S(1)}, u32[]{:S(2)}, u32[]{:S(2)}) %all-to-all-start) | async-done | bytes 524320 | tf_op jit(solution)/shard_map/all_to_all | solution.py:218
  41.0 18.4 %all_to_all.10 = bf16[32,64,128]{2,1,0:T(8,128)(2,1)S(1)} all-to-all(bf16[32,64,128]{2,1,0:T(8,128)(2,1)S(1)} %scan.1), channel_id=1, replica_groups=mesh['ctx'=4,'uly'=8] {'ctx','uly'}, dimensions={0} | all-to-all | bytes 1048576 | tf_op jit(solution)/shard_map/all_to_all | solution.py:253
  59.4 1.8 %norm.1 = bf16[96,4096]{1,0:T(8,128)(2,1)} custom-call(f32[96,128]{1,0:T(8,128)S(1)} %get-tuple-element.16.idcol, f32[1,128]{1,0:T(1,128)S(1)} %get-tuple-element.22.before, f32[1,4096]{1,0:T(1,128)S(1)} %get-tuple-element.23.rates, bf16[96,4096]{1,0:T(8,128)(2,1)S(1)} %copy-done.5, bf16[2048,128]{1,0:T(8,128)(2,1)S(1)} %bitcast.11, ...), custom_call_target="tpu_custom_call" | custom-call | tf_op jit(solution)/shard_map/norm/pallas_call | solution.py:254
  (20 shorter events, 0.6 us)
Async XLA Ops:
  0.7 11.3 %collective-permute-start.6 = (f32[128]{0:T(128)S(1)}, f32[128]{0:T(128)S(1)}, u32[]{:S(2)}, u32[]{:S(2)}) collective-permute-start(f32[128]{0:T(128)S(1)} %convert_add_fusion), channel_id=1, source_target_pairs={{0,7},{1,6},{2,5},{3,4},{4,3},{5,2},{6,1},{7,0},{8,15},{9,14},{10,... | collective-permute-start | bytes 1544 | tf_op jit(solution)/shard_map/ppermute | solution.py:193
  6.7 6.1 %collective-permute-start.5 = (f32[128]{0:T(128)S(1)}, f32[128]{0:T(128)S(1)}, u32[]{:S(2)}, u32[]{:S(2)}) collective-permute-start(f32[128]{0:T(128)S(1)} %convert_add_fusion), channel_id=1, source_target_pairs={{0,6},{1,7},{2,4},{3,5},{4,2},{5,3},{6,0},{7,1},{8,14},{9,15},{10,... | collective-permute-start | bytes 1544 | tf_op jit(solution)/shard_map/ppermute | solution.py:193
  6.9 8.9 %collective-permute-start.4 = (f32[128]{0:T(128)S(1)}, f32[128]{0:T(128)S(1)}, u32[]{:S(2)}, u32[]{:S(2)}) collective-permute-start(f32[128]{0:T(128)S(1)} %convert_add_fusion), channel_id=1, source_target_pairs={{0,5},{1,4},{2,7},{3,6},{4,1},{5,0},{6,3},{7,2},{8,13},{9,12},{10,... | collective-permute-start | bytes 1544 | tf_op jit(solution)/shard_map/ppermute | solution.py:193
  7.7 8.2 %collective-permute-start.3 = (f32[128]{0:T(128)S(1)}, f32[128]{0:T(128)S(1)}, u32[]{:S(2)}, u32[]{:S(2)}) collective-permute-start(f32[128]{0:T(128)S(1)} %convert_add_fusion), channel_id=1, source_target_pairs={{0,4},{1,5},{2,6},{3,7},{4,0},{5,1},{6,2},{7,3},{8,12},{9,13},{10,... | collective-permute-start | bytes 1544 | tf_op jit(solution)/shard_map/ppermute | solution.py:193
  9.7 6.2 %collective-permute-start.2 = (f32[128]{0:T(128)S(1)}, f32[128]{0:T(128)S(1)}, u32[]{:S(2)}, u32[]{:S(2)}) collective-permute-start(f32[128]{0:T(128)S(1)} %convert_add_fusion), channel_id=1, source_target_pairs={{0,3},{1,2},{2,1},{3,0},{4,7},{5,6},{6,5},{7,4},{8,11},{9,10},{10,... | collective-permute-start | bytes 1544 | tf_op jit(solution)/shard_map/ppermute | solution.py:193
  12.0 3.9 %collective-permute-start.1 = (f32[128]{0:T(128)S(1)}, f32[128]{0:T(128)S(1)}, u32[]{:S(2)}, u32[]{:S(2)}) collective-permute-start(f32[128]{0:T(128)S(1)} %convert_add_fusion), channel_id=1, source_target_pairs={{0,2},{1,3},{2,0},{3,1},{4,6},{5,7},{6,4},{7,5},{8,10},{9,11},{10,... | collective-permute-start | bytes 1544 | tf_op jit(solution)/shard_map/ppermute | solution.py:193
  12.8 3.5 %collective-permute-start = (f32[128]{0:T(128)S(1)}, f32[128]{0:T(128)S(1)}, u32[]{:S(2)}, u32[]{:S(2)}) collective-permute-start(f32[128]{0:T(128)S(1)} %convert_add_fusion), channel_id=1, source_target_pairs={{0,1},{1,0},{2,3},{3,2},{4,5},{5,4},{6,7},{7,6},{8,9},{9,8},{10,11... | collective-permute-start | bytes 1544 | tf_op jit(solution)/shard_map/ppermute | solution.py:193
  13.2 1.1 %copy-start.2 = (bf16[96,4096]{1,0:T(8,128)(2,1)S(1)}, bf16[96,4096]{1,0:T(8,128)(2,1)}, u32[]{:S(2)}) copy-start(bf16[96,4096]{1,0:T(8,128)(2,1)} %k_ref.1) | copy-start | bytes 2359300
  14.3 1.1 %copy-start.3 = (bf16[96,4096]{1,0:T(8,128)(2,1)S(1)}, bf16[96,4096]{1,0:T(8,128)(2,1)}, u32[]{:S(2)}) copy-start(bf16[96,4096]{1,0:T(8,128)(2,1)} %v_ref.1) | copy-start | bytes 2359300
  18.0 1.0 %copy-start = (bf16[128,4096]{1,0:T(8,128)(2,1)}, bf16[128,4096]{1,0:T(8,128)(2,1)S(1)}, u32[]{:S(2)}) copy-start(bf16[128,4096]{1,0:T(8,128)(2,1)S(1)} %get-tuple-element.19.v_ref) | copy-start | bytes 3145732
  19.0 21.9 %all-to-all-start = ((bf16[32,64,128]{2,1,0:T(8,128)(2,1)}), bf16[32,64,128]{2,1,0:T(8,128)(2,1)S(1)}, u32[]{:S(2)}, u32[]{:S(2)}) async-start(bf16[32,64,128]{2,1,0:T(8,128)(2,1)} %bitcast.8), calls=%async_computation | async-start | bytes 1048576 | tf_op jit(solution)/shard_map/all_to_all | solution.py:218
  24.5 1.2 %copy-start.1 = (bf16[128,4096]{1,0:T(8,128)(2,1)S(1)}, bf16[128,4096]{1,0:T(8,128)(2,1)}, u32[]{:S(2)}) copy-start(bf16[128,4096]{1,0:T(8,128)(2,1)} %copy-done) | copy-start | bytes 3145732
  25.8 1.1 %copy-start.4 = (bf16[96,4096]{1,0:T(8,128)(2,1)S(1)}, bf16[96,4096]{1,0:T(8,128)(2,1)}, u32[]{:S(2)}) copy-start(bf16[96,4096]{1,0:T(8,128)(2,1)} %q_ref.3) | copy-start | bytes 2359300
  28.1 31.4 %copy-start.5 = (bf16[96,4096]{1,0:T(8,128)(2,1)S(1)}, bf16[96,4096]{1,0:T(8,128)(2,1)}, u32[]{:S(2)}) copy-start(bf16[96,4096]{1,0:T(8,128)(2,1)} %q_ref.3) | copy-start | bytes 2359300
  28.1 31.4 %copy-start.6 = (f32[4096]{0:T(1024)S(1)}, f32[4096]{0:T(1024)}, u32[]{:S(2)}) copy-start(f32[4096]{0:T(1024)} %param.11) | copy-start | bytes 49156
  28.1 2.9 %collective-permute-start.9 = (f32[8,128]{1,0:T(8,128)S(1)}, f32[8,128]{1,0:T(8,128)S(1)}, u32[]{:S(2)}, u32[]{:S(2)}) collective-permute-start(f32[8,128]{1,0:T(8,128)S(1)} %get-tuple-element.21.facts), channel_id=1, source_target_pairs={{0,24},{8,0},{16,8},{24,16},{1,25},{9,1},{17,9},{25,17},{2,26},{10... | collective-permute-start | bytes 12296 | tf_op jit(solution)/shard_map/ppermute | solution.py:233
  29.7 3.6 %collective-permute-start.8 = (f32[8,128]{1,0:T(8,128)S(1)}, f32[8,128]{1,0:T(8,128)S(1)}, u32[]{:S(2)}, u32[]{:S(2)}) collective-permute-start(f32[8,128]{1,0:T(8,128)S(1)} %get-tuple-element.21.facts), channel_id=1, source_target_pairs={{0,16},{8,24},{16,0},{24,8},{1,17},{9,25},{17,1},{25,9},{2,18},{10... | collective-permute-start | bytes 12296 | tf_op jit(solution)/shard_map/ppermute | solution.py:233
  30.0 3.3 %collective-permute-start.7 = (f32[8,128]{1,0:T(8,128)S(1)}, f32[8,128]{1,0:T(8,128)S(1)}, u32[]{:S(2)}, u32[]{:S(2)}) collective-permute-start(f32[8,128]{1,0:T(8,128)S(1)} %get-tuple-element.21.facts), channel_id=1, source_target_pairs={{0,8},{8,16},{16,24},{24,0},{1,9},{9,17},{17,25},{25,1},{2,10},{10... | collective-permute-start | bytes 12296 | tf_op jit(solution)/shard_map/ppermute | solution.py:233

commit v8 on v7

--- a/solution.py
+++ b/solution.py
@@ -30,7 +30,7 @@
 def turn_kernel(row_ref, k_ref, v_ref, turned, filled, idrow, idcol):
     tokens, width = k_ref.shape
     fill = jnp.full((1, LANES - tokens), -1.0, jnp.float32)
-    row = jnp.concatenate([row_ref[:, LANES - tokens :], fill], 1)
+    row = jnp.concatenate([row_ref[:1, LANES - tokens :], fill], 1)
     idrow[...] = jnp.broadcast_to(row, idrow.shape)
     idcol[...] = jnp.transpose(jnp.broadcast_to(row, (LANES, LANES)))[:tokens]
     filled[:tokens, :] = v_ref[...]
@@ -42,14 +42,8 @@
         turned[columns, :] = jnp.transpose(block).astype(turned.dtype)
 
 
-def ends_kernel(here, tokens, idrow, turned, v_ref, *refs):
+def ends_kernel(here, tokens, facts, idrow, turned, v_ref, out_ref):
     width = v_ref.shape[1]
-    rows, (out_ref, facts) = refs[:-2], refs[-2:]
-    place = lax.broadcasted_iota(jnp.int32, facts.shape, 0)
-    tile = jnp.zeros(facts.shape, jnp.float32)
-    for apart, row in enumerate(rows):
-        tile = jnp.where(place == lax.axis_index("uly") ^ apart, row[...], tile)
-    facts[...] = tile
     lane = lax.broadcasted_iota(jnp.int32, (HD, LANES), 1)
     place = lax.broadcasted_iota(jnp.int32, idrow.shape, 1)
     ids = idrow[...]
@@ -95,7 +89,7 @@
         )
         rates = [rate_of(facts, 2 * j + one, here) for one in (0, 1)]
         weight = jnp.concatenate([jnp.exp(-rate * age) for rate in rates], 0)
-        probs = (scores * weight).astype(jnp.bfloat16)
+        probs = (scores * weight)[:, :tokens].astype(jnp.bfloat16)
         got = jnp.dot(probs, v_ref[:, columns], preferred_element_type=jnp.float32)
         out_ref[:, columns] = jnp.where(lane < HD, got[:tokens], got[tokens:])
         rates_ref[:, columns] = jnp.where(lane[:1] < HD, rates[0], rates[1])
@@ -186,13 +180,12 @@
     shape = jax.ShapeDtypeStruct
     tile = shape((members, LANES), jnp.float32)
 
-    row = jnp.pad(decay_rate, (0, LANES - here)) + jnp.pad(
+    own = jnp.pad(decay_rate, (0, LANES - here)) + jnp.pad(
         doc_ids, (LANES - tokens, 0)
     ).astype(jnp.float32)
-    rows_of = [row] + [
-        lax.ppermute(row, "uly", [(u, u ^ apart) for u in range(members)])
-        for apart in range(1, members)
-    ]
+    facts = lax.all_to_all(
+        jnp.broadcast_to(own[None, :], tile.shape), "uly", split_axis=0, concat_axis=0, tiled=True
+    )
     turned, filled, idrow, idcol = pl.pallas_call(
         turn_kernel,
         in_specs=[vmem] * 3,
@@ -206,15 +199,15 @@
         compiler_params=params,
         cost_estimate=pl.CostEstimate(flops=0, bytes_accessed=12_000_000, transcendentals=0),
         name="turn",
-    )(row[None, :], keys, values)
-    ends, facts = pl.pallas_call(
+    )(own[None, :], keys, values)
+    ends = pl.pallas_call(
         functools.partial(ends_kernel, here, tokens),
-        in_specs=[vmem] * (3 + members),
-        out_specs=[vmem] * 2,
-        out_shape=[shape((all_pairs * HD, LANES), jnp.bfloat16), tile],
+        in_specs=[vmem] * 4,
+        out_specs=vmem,
+        out_shape=shape((all_pairs * HD, LANES), jnp.bfloat16),
         compiler_params=params,
         name="ends",
-    )(idrow, turned, filled, *[found[None, :] for found in rows_of])
+    )(facts, idrow, turned, filled)
     pieces = lax.all_to_all(
         ends.reshape(count, rows, LANES), axes, split_axis=0, concat_axis=0, tiled=True
     )
@@ -228,7 +221,7 @@
             flops=8_000_000_000, bytes_accessed=4_000_000, transcendentals=600_000
         ),
         name="inner",
-    )(facts, idcol, idrow, queries, turned, filled)
+    )(facts, idcol, idrow, queries, turned, values)
     others = [
         lax.ppermute(slice_facts, "ctx", [(c, (c + ahead) % slices) for c in range(slices)])
         for ahead in range(1, slices)

time: 61.6 us -> 56.8 us (0.922)
  starting transfers between devices: 20.1 us -> 12.4 us
  waiting for transfers between devices: 11 us -> 13.6 us
  other arithmetic: 0.75 us -> 1.49 us
    ppermute x7 -> x0, starting transfers between devices: 12.5 us -> none  [local(): lax.ppermute(row, 'uly', [(u, u ^ apart) for u in range(members)])]
    all_to_all x0 -> x1, starting transfers between devices: none -> 7.25 us  [local(): lax.all_to_all(jnp.broadcast_to(own[None, :], tile.shape), 'uly', split_a...]
    all_to_all x0 -> x1, waiting for transfers between devices: none -> 2.97 us  [local(): lax.all_to_all(jnp.broadcast_to(own[None, :], tile.shape), 'uly', split_a...]
    all_to_all x1, starting transfers between devices: 5.58 us -> 3.09 us  [local(): lax.all_to_all(ends.reshape(count, rows, LANES), axes, split_axis=0, conc...]
    unnamed x14 -> x12, local copies, waits for them, and re-layouts: 5.63 us -> 4.54 us
    broadcast_in_dim x0 -> x1, other arithmetic: none -> 0.75 us  [local(): own[None, :]]
  transfers between devices with their start and end apart: 11 -> 5, of which waited for: 4 -> 4; matrix products, arithmetic and copies ran while one was open for 0% -> 1% of each run, Pallas kernels for 3% -> 3%
where the time goes in v8:
time: 56.8 us; the launch traced here: 56.4 us
  blocking collectives  18.4 us (32%)
  waiting for transfers between devices  13.6 us (24%)
  starting transfers between devices  12.4 us (22%)
  Pallas kernels  5.23 us (9%)
  local copies, waits for them, and re-layouts  5.14 us (9%)
  other arithmetic  1.49 us (3%)
    all_to_all x1, blocking collectives, local(): lax.all_to_all(moved, axes, split_axis=0, concat_axis=0, tiled=True)  18.4 us
    all_to_all x1, waiting for transfers between devices, local(): lax.all_to_all(ends.reshape(count, rows, LANES), axes, split_axis=0, conc...  7.48 us
    all_to_all x1, starting transfers between devices, local(): lax.all_to_all(jnp.broadcast_to(own[None, :], tile.shape), 'uly', split_a...  7.25 us
    unnamed x12, local copies, waits for them, and re-layouts  4.54 us
    ppermute x3, waiting for transfers between devices, local(): lax.ppermute(slice_facts, 'ctx', [(c, (c + ahead) % slices) for c in rang...  3.14 us
    all_to_all x1, starting transfers between devices, local(): lax.all_to_all(ends.reshape(count, rows, LANES), axes, split_axis=0, conc...  3.09 us
    all_to_all x1, waiting for transfers between devices, local(): lax.all_to_all(jnp.broadcast_to(own[None, :], tile.shape), 'uly', split_a...  2.97 us
    ppermute x3, starting transfers between devices, local(): lax.ppermute(slice_facts, 'ctx', [(c, (c + ahead) % slices) for c in rang...  2.08 us
  transfers between devices with their start and end apart: 5, of which 4 were waited for; matrix products, arithmetic and copies ran while one was open for 1% of the time, Pallas kernels for 3%

profile of v8, /device:TPU:0, one launch (start us, length us, event | category | flops | bytes accessed | tf_op | source)
XLA Modules:
  0.0 56.4 jit_solution(16499181534670327457)
XLA Ops:
  0.0 0.7 %convert_add_fusion = f32[128]{0:T(128)S(1)} fusion(s32[96]{0:T(128)} %param.9, f32[8]{0:T(128)} %param.10), kind=kLoop, calls=%fused_computation | loop fusion | flops 256 | bytes 928 | tf_op jit(solution)/shard_map/add | solution.py:183
  0.7 0.6 %broadcast_in_dim.13 = f32[8,1,128]{2,1,0:T(1,128)} broadcast(f32[128]{0:T(128)S(1)} %convert_add_fusion), dimensions={2} | broadcast | bytes 4608 | tf_op jit(solution)/shard_map/broadcast_in_dim | solution.py:187
  1.3 7.3 %all-to-all-start = ((f32[8,1,128]{2,1,0:T(1,128)}), f32[8,1,128]{2,1,0:T(1,128)S(1)}, u32[]{:S(2)}, u32[]{:S(2)}) async-start(f32[8,1,128]{2,1,0:T(1,128)} %broadcast_in_dim.13), calls=%async_computation | async-start | bytes 8192 | tf_op jit(solution)/shard_map/all_to_all | solution.py:186
  8.6 0.7 %fusion.row_ref = f32[1,128]{1,0:T(1,128)S(1)} fusion(s32[96]{0:T(128)} %param.9, f32[8]{0:T(128)} %param.10), kind=kLoop, calls=%fused_computation.1 | loop fusion | flops 256 | bytes 928 | tf_op jit(solution)/shard_map/broadcast_in_dim | solution.py:202
  9.3 1.1 %copy-done = bf16[96,4096]{1,0:T(8,128)(2,1)S(1)} copy-done((bf16[96,4096]{1,0:T(8,128)(2,1)S(1)}, bf16[96,4096]{1,0:T(8,128)(2,1)}, u32[]{:S(2)}) %copy-start) | copy-done | bytes 786456
  10.5 1.1 %copy-done.1 = bf16[96,4096]{1,0:T(8,128)(2,1)S(1)} copy-done((bf16[96,4096]{1,0:T(8,128)(2,1)S(1)}, bf16[96,4096]{1,0:T(8,128)(2,1)}, u32[]{:S(2)}) %copy-start.1) | copy-done | bytes 786456
  11.6 0.4 turn.1
  12.0 3.0 %all-to-all-done = f32[8,1,128]{2,1,0:T(1,128)S(1)} async-done(((f32[8,1,128]{2,1,0:T(1,128)}), f32[8,1,128]{2,1,0:T(1,128)S(1)}, u32[]{:S(2)}, u32[]{:S(2)}) %all-to-all-start) | async-done | bytes 4128 | tf_op jit(solution)/shard_map/all_to_all | solution.py:186
  15.0 1.6 %ends.1 = bf16[2048,128]{1,0:T(8,128)(2,1)} custom-call(f32[8,128]{1,0:T(8,128)S(1)} %bitcast.8, f32[8,128]{1,0:T(8,128)S(1)} %get-tuple-element.15.idrow, bf16[4096,128]{1,0:T(8,128)(2,1)S(1)} %get-tuple-element.16.turned, bf16[128,4096]{1,0:T(8,128)(2,1)S(1)} %get-tuple-element.21.v_ref), custom_call_target="tpu_custom_call" | custom-call | tf_op jit(solution)/shard_map/ends/pallas_call | solution.py:203
  16.6 3.1 %all-to-all-start.1 = ((bf16[32,64,128]{2,1,0:T(8,128)(2,1)}), bf16[32,64,128]{2,1,0:T(8,128)(2,1)S(1)}, u32[]{:S(2)}, u32[]{:S(2)}) async-start(bf16[32,64,128]{2,1,0:T(8,128)(2,1)} %bitcast.2), calls=%async_computation.1 | async-start | bytes 1048576 | tf_op jit(solution)/shard_map/all_to_all | solution.py:211
  19.7 0.0 copy-start.2
  19.7 1.1 %copy-done.2 = bf16[96,4096]{1,0:T(8,128)(2,1)S(1)} copy-done((bf16[96,4096]{1,0:T(8,128)(2,1)S(1)}, bf16[96,4096]{1,0:T(8,128)(2,1)}, u32[]{:S(2)}) %copy-start.2) | copy-done | bytes 786456
  20.8 1.1 %copy-done.3 = bf16[96,4096]{1,0:T(8,128)(2,1)S(1)} copy-done((bf16[96,4096]{1,0:T(8,128)(2,1)S(1)}, bf16[96,4096]{1,0:T(8,128)(2,1)}, u32[]{:S(2)}) %copy-start.3) | copy-done | bytes 786456
  21.9 1.3 %inner.1 = (f32[96,4096]{1,0:T(8,128)S(1)}, f32[8,128]{1,0:T(8,128)S(1)}, f32[1,4096]{1,0:T(1,128)S(1)}) custom-call(f32[8,128]{1,0:T(8,128)S(1)} %bitcast.9, f32[96,128]{1,0:T(8,128)S(1)} %get-tuple-element.14.idcol, f32[8,128]{1,0:T(8,128)S(1)} %get-tuple-element.15.idrow, bf16[96,4096]{1,0:T(8,128)(2,1)S(1)} %copy-done.3, ...), custom_call_target="tpu_custom_call" | custom-call | flops 8000000000 | bytes 4000000 | tf_op jit(solution)/shard_map/inner/pallas_call | solution.py:214
  23.2 1.6 %collective-permute-start.2 = (f32[8,128]{1,0:T(8,128)S(1)}, f32[8,128]{1,0:T(8,128)S(1)}, u32[]{:S(2)}, u32[]{:S(2)}) collective-permute-start(f32[8,128]{1,0:T(8,128)S(1)} %get-tuple-element.17.facts), channel_id=1, source_target_pairs={{0,24},{8,0},{16,8},{24,16},{1,25},{9,1},{17,9},{25,17},{2,26},{10... | collective-permute-start | bytes 12296 | tf_op jit(solution)/shard_map/ppermute | solution.py:226
  24.8 0.4 collective-permute-start.1
  25.2 0.1 collective-permute-start
  25.3 0.8 %collective-permute-done.2.refs_2_ = f32[8,128]{1,0:T(8,128)S(1)} collective-permute-done((f32[8,128]{1,0:T(8,128)S(1)}, f32[8,128]{1,0:T(8,128)S(1)}, u32[]{:S(2)}, u32[]{:S(2)}) %collective-permute-start.2) | collective-permute-done | bytes 4128 | tf_op jit(solution)/shard_map/ppermute | solution.py:226
  26.1 2.3 %collective-permute-done.1.refs_1_ = f32[8,128]{1,0:T(8,128)S(1)} collective-permute-done((f32[8,128]{1,0:T(8,128)S(1)}, f32[8,128]{1,0:T(8,128)S(1)}, u32[]{:S(2)}, u32[]{:S(2)}) %collective-permute-start.1) | collective-permute-done | bytes 4128 | tf_op jit(solution)/shard_map/ppermute | solution.py:226
  28.5 0.1 link.1
  28.5 7.5 %all-to-all-done.1.in_ref = bf16[32,64,128]{2,1,0:T(8,128)(2,1)S(1)} async-done(((bf16[32,64,128]{2,1,0:T(8,128)(2,1)}), bf16[32,64,128]{2,1,0:T(8,128)(2,1)S(1)}, u32[]{:S(2)}, u32[]{:S(2)}) %all-to-all-start.1) | async-done | bytes 524320 | tf_op jit(solution)/shard_map/all_to_all | solution.py:211
  36.0 0.1 scan.1
  36.1 18.4 %all_to_all.18 = bf16[32,64,128]{2,1,0:T(8,128)(2,1)S(1)} all-to-all(bf16[32,64,128]{2,1,0:T(8,128)(2,1)S(1)} %scan.1), channel_id=1, replica_groups=mesh['ctx'=4,'uly'=8] {'ctx','uly'}, dimensions={0} | all-to-all | bytes 1048576 | tf_op jit(solution)/shard_map/all_to_all | solution.py:246
  54.6 1.8 %norm.1 = bf16[96,4096]{1,0:T(8,128)(2,1)} custom-call(f32[96,128]{1,0:T(8,128)S(1)} %get-tuple-element.14.idcol, f32[1,128]{1,0:T(1,128)S(1)} %get-tuple-element.18.before, f32[1,4096]{1,0:T(1,128)S(1)} %get-tuple-element.19.rates, bf16[96,4096]{1,0:T(8,128)(2,1)S(1)} %copy-done.4, bf16[2048,128]{1,0:T(8,128)(2,1)S(1)} %bitcast.6, ...), custom_call_target="tpu_custom_call" | custom-call | tf_op jit(solution)/shard_map/norm/pallas_call | solution.py:247
  (8 shorter events, 0.0 us)
Async XLA Ops:
  1.3 13.6 %all-to-all-start = ((f32[8,1,128]{2,1,0:T(1,128)}), f32[8,1,128]{2,1,0:T(1,128)S(1)}, u32[]{:S(2)}, u32[]{:S(2)}) async-start(f32[8,1,128]{2,1,0:T(1,128)} %broadcast_in_dim.13), calls=%async_computation | async-start | bytes 8192 | tf_op jit(solution)/shard_map/all_to_all | solution.py:186
  9.3 1.1 %copy-start = (bf16[96,4096]{1,0:T(8,128)(2,1)S(1)}, bf16[96,4096]{1,0:T(8,128)(2,1)}, u32[]{:S(2)}) copy-start(bf16[96,4096]{1,0:T(8,128)(2,1)} %k_ref.1) | copy-start | bytes 2359300
  10.5 1.1 %copy-start.1 = (bf16[96,4096]{1,0:T(8,128)(2,1)S(1)}, bf16[96,4096]{1,0:T(8,128)(2,1)}, u32[]{:S(2)}) copy-start(bf16[96,4096]{1,0:T(8,128)(2,1)} %v_ref.3) | copy-start | bytes 2359300
  16.6 19.4 %all-to-all-start.1 = ((bf16[32,64,128]{2,1,0:T(8,128)(2,1)}), bf16[32,64,128]{2,1,0:T(8,128)(2,1)S(1)}, u32[]{:S(2)}, u32[]{:S(2)}) async-start(bf16[32,64,128]{2,1,0:T(8,128)(2,1)} %bitcast.2), calls=%async_computation.1 | async-start | bytes 1048576 | tf_op jit(solution)/shard_map/all_to_all | solution.py:211
  19.7 1.1 %copy-start.2 = (bf16[96,4096]{1,0:T(8,128)(2,1)S(1)}, bf16[96,4096]{1,0:T(8,128)(2,1)}, u32[]{:S(2)}) copy-start(bf16[96,4096]{1,0:T(8,128)(2,1)} %v_ref.3) | copy-start | bytes 2359300
  20.8 1.1 %copy-start.3 = (bf16[96,4096]{1,0:T(8,128)(2,1)S(1)}, bf16[96,4096]{1,0:T(8,128)(2,1)}, u32[]{:S(2)}) copy-start(bf16[96,4096]{1,0:T(8,128)(2,1)} %q_ref.3) | copy-start | bytes 2359300
  23.2 31.4 %copy-start.4 = (bf16[96,4096]{1,0:T(8,128)(2,1)S(1)}, bf16[96,4096]{1,0:T(8,128)(2,1)}, u32[]{:S(2)}) copy-start(bf16[96,4096]{1,0:T(8,128)(2,1)} %q_ref.3) | copy-start | bytes 2359300
  23.2 31.4 %copy-start.5 = (f32[4096]{0:T(1024)S(1)}, f32[4096]{0:T(1024)}, u32[]{:S(2)}) copy-start(f32[4096]{0:T(1024)} %param.11) | copy-start | bytes 49156
  23.2 2.9 %collective-permute-start.2 = (f32[8,128]{1,0:T(8,128)S(1)}, f32[8,128]{1,0:T(8,128)S(1)}, u32[]{:S(2)}, u32[]{:S(2)}) collective-permute-start(f32[8,128]{1,0:T(8,128)S(1)} %get-tuple-element.17.facts), channel_id=1, source_target_pairs={{0,24},{8,0},{16,8},{24,16},{1,25},{9,1},{17,9},{25,17},{2,26},{10... | collective-permute-start | bytes 12296 | tf_op jit(solution)/shard_map/ppermute | solution.py:226
  24.8 3.6 %collective-permute-start.1 = (f32[8,128]{1,0:T(8,128)S(1)}, f32[8,128]{1,0:T(8,128)S(1)}, u32[]{:S(2)}, u32[]{:S(2)}) collective-permute-start(f32[8,128]{1,0:T(8,128)S(1)} %get-tuple-element.17.facts), channel_id=1, source_target_pairs={{0,16},{8,24},{16,0},{24,8},{1,17},{9,25},{17,1},{25,9},{2,18},{10... | collective-permute-start | bytes 12296 | tf_op jit(solution)/shard_map/ppermute | solution.py:226
  25.2 3.3 %collective-permute-start = (f32[8,128]{1,0:T(8,128)S(1)}, f32[8,128]{1,0:T(8,128)S(1)}, u32[]{:S(2)}, u32[]{:S(2)}) collective-permute-start(f32[8,128]{1,0:T(8,128)S(1)} %get-tuple-element.17.facts), channel_id=1, source_target_pairs={{0,8},{8,16},{16,24},{24,0},{1,9},{9,17},{17,25},{25,1},{2,10},{10... | collective-permute-start | bytes 12296 | tf_op jit(solution)/shard_map/ppermute | solution.py:226

commit v9 on v8

--- a/solution.py
+++ b/solution.py
@@ -95,8 +95,12 @@
         rates_ref[:, columns] = jnp.where(lane[:1] < HD, rates[0], rates[1])
 
 
-def link_kernel(here, tokens, rows, facts, *refs):
-    others, (link, before, last) = refs[:-3], refs[-3:]
+def few(count):
+    return count if count <= 8 else 1
+
+
+def link_kernel(here, tokens, chunks, facts, *refs):
+    others, (linked, through, one, half, before, last) = refs[:-6], refs[-6:]
     members, slices = facts.shape[0], len(others) + 1
     ctx, uly = lax.axis_index("ctx"), lax.axis_index("uly")
     for back, tile in enumerate((facts, *others)):
@@ -105,24 +109,63 @@
             tile[:, LANES - 1 :], (members, LANES)
         )
     me = ctx * members + uly
-    decay = jnp.exp(-pair_rate(facts, lax.div(me * rows, HD), here) * float(tokens))
     now = last[...]
     then = jnp.concatenate([now[:1], now[:-1]], 0)
-    link[...] = jnp.where(now == then, decay, 0.0)
+    end = jnp.concatenate([now[chunks - 1 :], now[: chunks - 1]], 0)
+    linked[...] = jnp.where(now == then, 1.0, 0.0)
+    through[...] = jnp.where(end == then, 1.0, 0.0)
     before[...] = jnp.where(me > 0, last[pl.ds(jnp.maximum(me - 1, 0), 1), :], -1.0)
-
-
-def scan_kernel(link, in_ref, out_ref):
-    count = in_ref.shape[0]
-    out_ref[0] = jnp.zeros(out_ref.shape[1:], out_ref.dtype)
-
-    def step(i, state):
-        state = in_ref[i].astype(jnp.float32) + link[pl.ds(i, 1), :] * state
-        out_ref[i + 1] = state.astype(out_ref.dtype)
-        return state
-
-    zero = jnp.zeros(in_ref.shape[1:], jnp.float32)
-    lax.fori_loop(0, count - 1, step, zero, unroll=min(count - 1, 31))
+    rows = one.shape[0]
+    share = min(rows, HD)
+    owner = ctx * chunks + lax.rem(uly, chunks)
+    for at in range(0, rows, share):
+        rate = pair_rate(facts, lax.div(owner * rows + at, HD), here)
+        for ref, length in ((one, tokens), (half, tokens * chunks)):
+            ref[at : at + share, :] = jnp.broadcast_to(
+                jnp.exp(-rate * float(length)), (share, LANES)
+            )
+
+
+def half_kernel(chunks, linked, one, in_ref, out_ref):
+    slices = out_ref.shape[0]
+    offset = jnp.where(lax.axis_index("uly") >= chunks, chunks, 0)
+
+    def slice_end(c, _):
+        def step(j, state):
+            keep = linked[pl.ds(c * 2 * chunks + offset + j, 1), :] * one[...]
+            return in_ref[c * chunks + j].astype(jnp.float32) + keep * state
+
+        begin = in_ref[c * chunks].astype(jnp.float32)
+        state = lax.fori_loop(1, chunks, step, begin, unroll=few(chunks - 1))
+        out_ref[c] = state.astype(out_ref.dtype)
+        return 0
+
+    lax.fori_loop(0, slices, slice_end, 0, unroll=few(slices))
+
+
+def scan_kernel(chunks, linked, through, one, half, in_ref, other, out_ref):
+    slices = other.shape[0]
+    later = lax.axis_index("uly") >= chunks
+    offset = jnp.where(later, chunks, 0)
+
+    def over_other(state, c, wanted):
+        keep = through[pl.ds(c * 2 * chunks + chunks - offset, 1), :] * half[...]
+        return jnp.where(wanted, other[c].astype(jnp.float32) + keep * state, state)
+
+    def over_slice(c, state):
+        state = over_other(state, c, later)
+
+        def step(j, state):
+            at = c * chunks + j
+            out_ref[at] = state.astype(out_ref.dtype)
+            keep = linked[pl.ds(c * 2 * chunks + offset + j, 1), :] * one[...]
+            return in_ref[at].astype(jnp.float32) + keep * state
+
+        state = lax.fori_loop(0, chunks, step, state, unroll=few(chunks))
+        return over_other(state, c, jnp.logical_not(later))
+
+    begin = jnp.zeros(in_ref.shape[1:], jnp.float32)
+    lax.fori_loop(0, slices, over_slice, begin, unroll=few(slices))
 
 
 def norm_kernel(idcol, before, rates, q_ref, s_ref, inner_ref, gain, out_ref, raw, done, sems):
@@ -173,7 +216,18 @@
     slices, members = lax.axis_size("ctx"), lax.axis_size("uly")
     count = slices * members
     all_pairs = width // LANES
-    rows = all_pairs * HD // count
+    chunks = members // 2
+    group = slices * chunks
+    rows = all_pairs * HD // group
+    groups = [
+        [c * members + half * chunks + u for c in range(slices) for u in range(chunks)]
+        for half in (0, 1)
+    ]
+    swap = [
+        (c * members + u, c * members + (u + chunks) % members)
+        for c in range(slices)
+        for u in range(members)
+    ]
 
     vmem = pl.BlockSpec(memory_space=pltpu.VMEM)
     params = pltpu.CompilerParams(vmem_limit_bytes=32 * 1024 * 1024)
@@ -209,7 +263,8 @@
         name="ends",
     )(facts, idrow, turned, filled)
     pieces = lax.all_to_all(
-        ends.reshape(count, rows, LANES), axes, split_axis=0, concat_axis=0, tiled=True
+        ends.reshape(group, rows, LANES),
+        axes, split_axis=0, concat_axis=0, axis_index_groups=groups, tiled=True,
     )
     inner, slice_facts, rates = pl.pallas_call(
         functools.partial(inner_kernel, here),
@@ -226,24 +281,37 @@
         lax.ppermute(slice_facts, "ctx", [(c, (c + ahead) % slices) for c in range(slices)])
         for ahead in range(1, slices)
     ]
-    link, before = pl.pallas_call(
-        functools.partial(link_kernel, here, tokens, rows),
+    linked, through, one, half, before = pl.pallas_call(
+        functools.partial(link_kernel, here, tokens, chunks),
         in_specs=[vmem] * slices,
-        out_specs=[vmem] * 2,
-        out_shape=[shape((count, LANES), jnp.float32), shape((1, LANES), jnp.float32)],
+        out_specs=[vmem] * 5,
+        out_shape=[shape((count, LANES), jnp.float32)] * 2
+        + [shape((rows, LANES), jnp.float32)] * 2
+        + [shape((1, LANES), jnp.float32)],
         scratch_shapes=[pltpu.VMEM((count, LANES), jnp.float32)],
         compiler_params=params,
         name="link",
     )(slice_facts, *others)
+    halves = pl.pallas_call(
+        functools.partial(half_kernel, chunks),
+        in_specs=[vmem] * 3,
+        out_specs=vmem,
+        out_shape=shape((slices, rows, LANES), jnp.bfloat16),
+        compiler_params=params,
+        name="half",
+    )(linked, one, pieces)
+    other = lax.ppermute(halves, axes, swap)
     moved = pl.pallas_call(
-        scan_kernel,
-        in_specs=[vmem] * 2,
+        functools.partial(scan_kernel, chunks),
+        in_specs=[vmem] * 6,
         out_specs=vmem,
-        out_shape=shape((count, rows, LANES), jnp.bfloat16),
+        out_shape=shape((group, rows, LANES), jnp.bfloat16),
         compiler_params=params,
         name="scan",
-    )(link, pieces)
-    states = lax.all_to_all(moved, axes, split_axis=0, concat_axis=0, tiled=True)
+    )(linked, through, one, half, pieces, other)
+    states = lax.all_to_all(
+        moved, axes, split_axis=0, concat_axis=0, axis_index_groups=groups, tiled=True
+    )
     return pl.pallas_call(
         norm_kernel,
         in_specs=[vmem] * 7,

time: 56.8 us -> 53.3 us (0.938)
  blocking collectives: 18.4 us -> 12 us
  starting transfers between devices: 12.4 us -> 14.2 us
  waiting for transfers between devices: 13.6 us -> 14.5 us
    ppermute x0 -> x1, waiting for transfers between devices: none -> 7.89 us  [local(): other = lax.ppermute(halves, axes, swap)]
    all_to_all x1, waiting for transfers between devices: 7.48 us -> 0.01 us  [local(): lax.all_to_all(ends.reshape(group, rows, LANES), axes, split_axis=0, conc...]
    all_to_all x1, blocking collectives: 18.4 us -> 12 us  [local(): lax.all_to_all(moved, axes, split_axis=0, concat_axis=0, axis_index_group...]
    ppermute x0 -> x1, starting transfers between devices: none -> 1.21 us  [local(): other = lax.ppermute(halves, axes, swap)]
  transfers between devices with their start and end apart: 5 -> 6, of which waited for: 4 -> 4; matrix products, arithmetic and copies ran while one was open for 1% -> 1% of each run, Pallas kernels for 3% -> 3%
where the time goes in v9:
time: 53.3 us; the launch traced here: 52.8 us
  waiting for transfers between devices  14.5 us (27%)
  starting transfers between devices  14.2 us (27%)
  blocking collectives  12 us (23%)
  Pallas kernels  5.5 us (10%)
  local copies, waits for them, and re-layouts  5.14 us (10%)
  other arithmetic  1.49 us (3%)
    all_to_all x1, blocking collectives, local(): lax.all_to_all(moved, axes, split_axis=0, concat_axis=0, axis_index_group...  12 us
    ppermute x1, waiting for transfers between devices, local(): other = lax.ppermute(halves, axes, swap)  7.89 us
    all_to_all x1, starting transfers between devices, local(): lax.all_to_all(jnp.broadcast_to(own[None, :], tile.shape), 'uly', split_a...  7.25 us
    unnamed x12, local copies, waits for them, and re-layouts  4.54 us
    ppermute x3, waiting for transfers between devices, local(): lax.ppermute(slice_facts, 'ctx', [(c, (c + ahead) % slices) for c in rang...  3.61 us
    all_to_all x1, starting transfers between devices, local(): lax.all_to_all(ends.reshape(group, rows, LANES), axes, split_axis=0, conc...  3.57 us
    all_to_all x1, waiting for transfers between devices, local(): lax.all_to_all(jnp.broadcast_to(own[None, :], tile.shape), 'uly', split_a...  2.97 us
    ppermute x3, starting transfers between devices, local(): lax.ppermute(slice_facts, 'ctx', [(c, (c + ahead) % slices) for c in rang...  2.15 us
  transfers between devices with their start and end apart: 6, of which 4 were waited for; matrix products, arithmetic and copies ran while one was open for 1% of the time, Pallas kernels for 3%

profile of v9, /device:TPU:0, one launch (start us, length us, event | category | flops | bytes accessed | tf_op | source)
XLA Modules:
  0.0 52.8 jit_solution(11110125039101257396)
XLA Ops:
  0.0 0.7 %convert_add_fusion = f32[128]{0:T(128)S(1)} fusion(s32[96]{0:T(128)} %param.9, f32[8]{0:T(128)} %param.10), kind=kLoop, calls=%fused_computation | loop fusion | flops 256 | bytes 928 | tf_op jit(solution)/shard_map/add | solution.py:237
  0.7 0.6 %broadcast_in_dim.13 = f32[8,1,128]{2,1,0:T(1,128)} broadcast(f32[128]{0:T(128)S(1)} %convert_add_fusion), dimensions={2} | broadcast | bytes 4608 | tf_op jit(solution)/shard_map/broadcast_in_dim | solution.py:241
  1.3 7.3 %all-to-all-start = ((f32[8,1,128]{2,1,0:T(1,128)}), f32[8,1,128]{2,1,0:T(1,128)S(1)}, u32[]{:S(2)}, u32[]{:S(2)}) async-start(f32[8,1,128]{2,1,0:T(1,128)} %broadcast_in_dim.13), calls=%async_computation | async-start | bytes 8192 | tf_op jit(solution)/shard_map/all_to_all | solution.py:240
  8.6 0.7 %fusion.row_ref = f32[1,128]{1,0:T(1,128)S(1)} fusion(s32[96]{0:T(128)} %param.9, f32[8]{0:T(128)} %param.10), kind=kLoop, calls=%fused_computation.1 | loop fusion | flops 256 | bytes 928 | tf_op jit(solution)/shard_map/broadcast_in_dim | solution.py:256
  9.3 1.1 %copy-done = bf16[96,4096]{1,0:T(8,128)(2,1)S(1)} copy-done((bf16[96,4096]{1,0:T(8,128)(2,1)S(1)}, bf16[96,4096]{1,0:T(8,128)(2,1)}, u32[]{:S(2)}) %copy-start) | copy-done | bytes 786456
  10.5 1.1 %copy-done.1 = bf16[96,4096]{1,0:T(8,128)(2,1)S(1)} copy-done((bf16[96,4096]{1,0:T(8,128)(2,1)S(1)}, bf16[96,4096]{1,0:T(8,128)(2,1)}, u32[]{:S(2)}) %copy-start.1) | copy-done | bytes 786456
  11.6 0.4 turn.1
  12.0 3.0 %all-to-all-done = f32[8,1,128]{2,1,0:T(1,128)S(1)} async-done(((f32[8,1,128]{2,1,0:T(1,128)}), f32[8,1,128]{2,1,0:T(1,128)S(1)}, u32[]{:S(2)}, u32[]{:S(2)}) %all-to-all-start) | async-done | bytes 4128 | tf_op jit(solution)/shard_map/all_to_all | solution.py:240
  15.0 1.6 %ends.1 = bf16[2048,128]{1,0:T(8,128)(2,1)} custom-call(f32[8,128]{1,0:T(8,128)S(1)} %bitcast.8, f32[8,128]{1,0:T(8,128)S(1)} %get-tuple-element.18.idrow, bf16[4096,128]{1,0:T(8,128)(2,1)S(1)} %get-tuple-element.19.turned, bf16[128,4096]{1,0:T(8,128)(2,1)S(1)} %get-tuple-element.27.v_ref), custom_call_target="tpu_custom_call" | custom-call | tf_op jit(solution)/shard_map/ends/pallas_call | solution.py:257
  16.6 3.6 %all-to-all-start.1 = ((bf16[16,128,128]{2,1,0:T(8,128)(2,1)}), bf16[16,128,128]{2,1,0:T(8,128)(2,1)S(1)}, u32[]{:S(2)}, u32[]{:S(2)}) async-start(bf16[16,128,128]{2,1,0:T(8,128)(2,1)} %bitcast.2), calls=%async_computation.1 | async-start | bytes 1048576 | tf_op jit(solution)/shard_map/all_to_all | solution.py:265
  20.2 1.1 %copy-done.2 = bf16[96,4096]{1,0:T(8,128)(2,1)S(1)} copy-done((bf16[96,4096]{1,0:T(8,128)(2,1)S(1)}, bf16[96,4096]{1,0:T(8,128)(2,1)}, u32[]{:S(2)}) %copy-start.2) | copy-done | bytes 786456
  21.3 1.1 %copy-done.3 = bf16[96,4096]{1,0:T(8,128)(2,1)S(1)} copy-done((bf16[96,4096]{1,0:T(8,128)(2,1)S(1)}, bf16[96,4096]{1,0:T(8,128)(2,1)}, u32[]{:S(2)}) %copy-start.3) | copy-done | bytes 786456
  22.4 1.3 %inner.1 = (f32[96,4096]{1,0:T(8,128)S(1)}, f32[8,128]{1,0:T(8,128)S(1)}, f32[1,4096]{1,0:T(1,128)S(1)}) custom-call(f32[8,128]{1,0:T(8,128)S(1)} %bitcast.9, f32[96,128]{1,0:T(8,128)S(1)} %get-tuple-element.17.idcol, f32[8,128]{1,0:T(8,128)S(1)} %get-tuple-element.18.idrow, bf16[96,4096]{1,0:T(8,128)(2,1)S(1)} %copy-done.3, ...), custom_call_target="tpu_custom_call" | custom-call | flops 8000000000 | bytes 4000000 | tf_op jit(solution)/shard_map/inner/pallas_call | solution.py:269
  23.7 1.7 %collective-permute-start.2 = (f32[8,128]{1,0:T(8,128)S(1)}, f32[8,128]{1,0:T(8,128)S(1)}, u32[]{:S(2)}, u32[]{:S(2)}) collective-permute-start(f32[8,128]{1,0:T(8,128)S(1)} %get-tuple-element.20.facts), channel_id=1, source_target_pairs={{0,24},{8,0},{16,8},{24,16},{1,25},{9,1},{17,9},{25,17},{2,26},{10... | collective-permute-start | bytes 12296 | tf_op jit(solution)/shard_map/ppermute | solution.py:281
  25.4 0.3 collective-permute-start.1
  25.7 0.2 collective-permute-start
  25.8 0.8 %collective-permute-done.2.refs_2_ = f32[8,128]{1,0:T(8,128)S(1)} collective-permute-done((f32[8,128]{1,0:T(8,128)S(1)}, f32[8,128]{1,0:T(8,128)S(1)}, u32[]{:S(2)}, u32[]{:S(2)}) %collective-permute-start.2) | collective-permute-done | bytes 4128 | tf_op jit(solution)/shard_map/ppermute | solution.py:281
  26.7 2.8 %collective-permute-done.1.refs_1_ = f32[8,128]{1,0:T(8,128)S(1)} collective-permute-done((f32[8,128]{1,0:T(8,128)S(1)}, f32[8,128]{1,0:T(8,128)S(1)}, u32[]{:S(2)}, u32[]{:S(2)}) %collective-permute-start.1) | collective-permute-done | bytes 4128 | tf_op jit(solution)/shard_map/ppermute | solution.py:281
  29.6 0.1 half.1
  29.8 1.2 %collective-permute-start.3 = (bf16[4,128,128]{2,1,0:T(8,128)(2,1)S(1)}, bf16[4,128,128]{2,1,0:T(8,128)(2,1)S(1)}, u32[]{:S(2)}, u32[]{:S(2)}) collective-permute-start(bf16[4,128,128]{2,1,0:T(8,128)(2,1)S(1)} %half.1), channel_id=1, source_target_pairs={{0,4},{1,5},{2,6},{3,7},{4,0},{5,1},{6,2},{7,3},{8,12},{9,13},{10,... | collective-permute-start | bytes 393224 | tf_op jit(solution)/shard_map/ppermute | solution.py:303
  31.0 7.9 %collective-permute-done.3.other = bf16[4,128,128]{2,1,0:T(8,128)(2,1)S(1)} collective-permute-done((bf16[4,128,128]{2,1,0:T(8,128)(2,1)S(1)}, bf16[4,128,128]{2,1,0:T(8,128)(2,1)S(1)}, u32[]{:S(2)}, u32[]{:S(2)}) %collective-permute-start.3) | collective-permute-done | bytes 131104 | tf_op jit(solution)/shard_map/ppermute | solution.py:303
  38.8 0.2 scan.1
  39.1 12.0 %all_to_all.18 = bf16[16,128,128]{2,1,0:T(8,128)(2,1)S(1)} all-to-all(bf16[16,128,128]{2,1,0:T(8,128)(2,1)S(1)} %scan.1), channel_id=1, replica_groups={{0,1,2,3,8,9,10,11,16,17,18,19,24,25,26,27},{4,5,6,7,12,13,14,15,20,21,..., dimensions={0} | all-to-all | bytes 1048576 | tf_op jit(solution)/shard_map/all_to_all | solution.py:312
  51.1 1.8 %norm.1 = bf16[96,4096]{1,0:T(8,128)(2,1)} custom-call(f32[96,128]{1,0:T(8,128)S(1)} %get-tuple-element.17.idcol, f32[1,128]{1,0:T(1,128)S(1)} %get-tuple-element.21.before, f32[1,4096]{1,0:T(1,128)S(1)} %get-tuple-element.22.rates, bf16[96,4096]{1,0:T(8,128)(2,1)S(1)} %copy-done.4, bf16[2048,128]{1,0:T(8,128)(2,1)S(1)} %bitcast.6, ...), custom_call_target="tpu_custom_call" | custom-call | tf_op jit(solution)/shard_map/norm/pallas_call | solution.py:315
  (11 shorter events, 0.1 us)
Async XLA Ops:
  1.3 13.6 %all-to-all-start = ((f32[8,1,128]{2,1,0:T(1,128)}), f32[8,1,128]{2,1,0:T(1,128)S(1)}, u32[]{:S(2)}, u32[]{:S(2)}) async-start(f32[8,1,128]{2,1,0:T(1,128)} %broadcast_in_dim.13), calls=%async_computation | async-start | bytes 8192 | tf_op jit(solution)/shard_map/all_to_all | solution.py:240
  9.3 1.1 %copy-start = (bf16[96,4096]{1,0:T(8,128)(2,1)S(1)}, bf16[96,4096]{1,0:T(8,128)(2,1)}, u32[]{:S(2)}) copy-start(bf16[96,4096]{1,0:T(8,128)(2,1)} %k_ref.1) | copy-start | bytes 2359300
  10.5 1.1 %copy-start.1 = (bf16[96,4096]{1,0:T(8,128)(2,1)S(1)}, bf16[96,4096]{1,0:T(8,128)(2,1)}, u32[]{:S(2)}) copy-start(bf16[96,4096]{1,0:T(8,128)(2,1)} %v_ref.3) | copy-start | bytes 2359300
  16.6 13.0 %all-to-all-start.1 = ((bf16[16,128,128]{2,1,0:T(8,128)(2,1)}), bf16[16,128,128]{2,1,0:T(8,128)(2,1)S(1)}, u32[]{:S(2)}, u32[]{:S(2)}) async-start(bf16[16,128,128]{2,1,0:T(8,128)(2,1)} %bitcast.2), calls=%async_computation.1 | async-start | bytes 1048576 | tf_op jit(solution)/shard_map/all_to_all | solution.py:265
  20.2 1.1 %copy-start.2 = (bf16[96,4096]{1,0:T(8,128)(2,1)S(1)}, bf16[96,4096]{1,0:T(8,128)(2,1)}, u32[]{:S(2)}) copy-start(bf16[96,4096]{1,0:T(8,128)(2,1)} %v_ref.3) | copy-start | bytes 2359300
  21.3 1.1 %copy-start.3 = (bf16[96,4096]{1,0:T(8,128)(2,1)S(1)}, bf16[96,4096]{1,0:T(8,128)(2,1)}, u32[]{:S(2)}) copy-start(bf16[96,4096]{1,0:T(8,128)(2,1)} %q_ref.3) | copy-start | bytes 2359300
  23.7 3.0 %collective-permute-start.2 = (f32[8,128]{1,0:T(8,128)S(1)}, f32[8,128]{1,0:T(8,128)S(1)}, u32[]{:S(2)}, u32[]{:S(2)}) collective-permute-start(f32[8,128]{1,0:T(8,128)S(1)} %get-tuple-element.20.facts), channel_id=1, source_target_pairs={{0,24},{8,0},{16,8},{24,16},{1,25},{9,1},{17,9},{25,17},{2,26},{10... | collective-permute-start | bytes 12296 | tf_op jit(solution)/shard_map/ppermute | solution.py:281
  25.4 4.1 %collective-permute-start.1 = (f32[8,128]{1,0:T(8,128)S(1)}, f32[8,128]{1,0:T(8,128)S(1)}, u32[]{:S(2)}, u32[]{:S(2)}) collective-permute-start(f32[8,128]{1,0:T(8,128)S(1)} %get-tuple-element.20.facts), channel_id=1, source_target_pairs={{0,16},{8,24},{16,0},{24,8},{1,17},{9,25},{17,1},{25,9},{2,18},{10... | collective-permute-start | bytes 12296 | tf_op jit(solution)/shard_map/ppermute | solution.py:281
  25.7 3.8 %collective-permute-start = (f32[8,128]{1,0:T(8,128)S(1)}, f32[8,128]{1,0:T(8,128)S(1)}, u32[]{:S(2)}, u32[]{:S(2)}) collective-permute-start(f32[8,128]{1,0:T(8,128)S(1)} %get-tuple-element.20.facts), channel_id=1, source_target_pairs={{0,8},{8,16},{16,24},{24,0},{1,9},{9,17},{17,25},{25,1},{2,10},{10... | collective-permute-start | bytes 12296 | tf_op jit(solution)/shard_map/ppermute | solution.py:281
  29.6 21.5 %copy-start.4 = (bf16[96,4096]{1,0:T(8,128)(2,1)S(1)}, bf16[96,4096]{1,0:T(8,128)(2,1)}, u32[]{:S(2)}) copy-start(bf16[96,4096]{1,0:T(8,128)(2,1)} %q_ref.3) | copy-start | bytes 2359300
  29.6 21.4 %copy-start.5 = (f32[4096]{0:T(1024)S(1)}, f32[4096]{0:T(1024)}, u32[]{:S(2)}) copy-start(f32[4096]{0:T(1024)} %param.11) | copy-start | bytes 49156
  29.8 9.1 %collective-permute-start.3 = (bf16[4,128,128]{2,1,0:T(8,128)(2,1)S(1)}, bf16[4,128,128]{2,1,0:T(8,128)(2,1)S(1)}, u32[]{:S(2)}, u32[]{:S(2)}) collective-permute-start(bf16[4,128,128]{2,1,0:T(8,128)(2,1)S(1)} %half.1), channel_id=1, source_target_pairs={{0,4},{1,5},{2,6},{3,7},{4,0},{5,1},{6,2},{7,3},{8,12},{9,13},{10,... | collective-permute-start | bytes 393224 | tf_op jit(solution)/shard_map/ppermute | solution.py:303

commit v10 on v9

--- a/solution.py
+++ b/solution.py
@@ -71,10 +71,9 @@
 
 
 def inner_kernel(
-    here, facts, idcol, idrow, q_ref, turned, v_ref, out_ref, tile_ref, rates_ref
+    here, facts, idcol, idrow, q_ref, turned, v_ref, after, out_ref, rates_ref
 ):
     tokens, width = q_ref.shape
-    tile_ref[...] = facts[...]
     lane = lax.broadcasted_iota(jnp.int32, (tokens, LANES), 1)
     t = lax.broadcasted_iota(jnp.int32, (tokens, LANES), 0)
     seen = (t >= lane) & (idcol[...] == idrow[:1, :])
@@ -93,6 +92,10 @@
         got = jnp.dot(probs, v_ref[:, columns], preferred_element_type=jnp.float32)
         out_ref[:, columns] = jnp.where(lane < HD, got[:tokens], got[tokens:])
         rates_ref[:, columns] = jnp.where(lane[:1] < HD, rates[0], rates[1])
+
+
+def pass_kernel(facts, after, out_ref):
+    out_ref[...] = facts[...]
 
 
 def few(count):
@@ -266,17 +269,14 @@
         ends.reshape(group, rows, LANES),
         axes, split_axis=0, concat_axis=0, axis_index_groups=groups, tiled=True,
     )
-    inner, slice_facts, rates = pl.pallas_call(
-        functools.partial(inner_kernel, here),
-        in_specs=[vmem] * 6,
-        out_specs=[vmem] * 3,
-        out_shape=[shape((tokens, width), jnp.float32), tile, shape((1, width), jnp.float32)],
-        compiler_params=params,
-        cost_estimate=pl.CostEstimate(
-            flops=8_000_000_000, bytes_accessed=4_000_000, transcendentals=600_000
-        ),
-        name="inner",
-    )(facts, idcol, idrow, queries, turned, values)
+    slice_facts = pl.pallas_call(
+        pass_kernel,
+        in_specs=[vmem, pl.BlockSpec(memory_space=pl.ANY)],
+        out_specs=vmem,
+        out_shape=tile,
+        compiler_params=params,
+        name="pass",
+    )(facts, ends)
     others = [
         lax.ppermute(slice_facts, "ctx", [(c, (c + ahead) % slices) for c in range(slices)])
         for ahead in range(1, slices)
@@ -301,6 +301,17 @@
         name="half",
     )(linked, one, pieces)
     other = lax.ppermute(halves, axes, swap)
+    inner, rates = pl.pallas_call(
+        functools.partial(inner_kernel, here),
+        in_specs=[vmem] * 6 + [pl.BlockSpec(memory_space=pl.ANY)],
+        out_specs=[vmem] * 2,
+        out_shape=[shape((tokens, width), jnp.float32), shape((1, width), jnp.float32)],
+        compiler_params=params,
+        cost_estimate=pl.CostEstimate(
+            flops=8_000_000_000, bytes_accessed=4_000_000, transcendentals=600_000
+        ),
+        name="inner",
+    )(facts, idcol, idrow, queries, turned, values, halves)
     moved = pl.pallas_call(
         functools.partial(scan_kernel, chunks),
         in_specs=[vmem] * 6,

time: 53.3 us -> 56.1 us (1.053)
  blocking collectives: 12 us -> 0 us
  waiting for transfers between devices: 14.5 us -> 23.6 us
  starting transfers between devices: 14.2 us -> 17.8 us
  local copies, waits for them, and re-layouts: 5.14 us -> 6.26 us
  Pallas kernels: 5.5 us -> 6.29 us
    all_to_all x1 -> x0, blocking collectives: 12 us -> none  [local(): lax.all_to_all(moved, axes, split_axis=0, concat_axis=0, axis_index_group...]
    all_to_all x0 -> x1, waiting for transfers between devices: none -> 5.65 us  [local(): lax.all_to_all(moved, axes, split_axis=0, concat_axis=0, axis_index_group...]
    all_to_all x0 -> x1, starting transfers between devices: none -> 3.57 us  [local(): lax.all_to_all(moved, axes, split_axis=0, concat_axis=0, axis_index_group...]
    ppermute x3, waiting for transfers between devices: 3.61 us -> 5.52 us  [local(): lax.ppermute(slice_facts, 'ctx', [(c, (c + ahead) % slices) for c in rang...]
    all_to_all x1, waiting for transfers between devices: 0.01 us -> 1.39 us  [local(): lax.all_to_all(ends.reshape(group, rows, LANES), axes, split_axis=0, conc...]
    unnamed x12, local copies, waits for them, and re-layouts: 4.54 us -> 5.66 us
    pallas_call x1, Pallas kernels: 0.23 us -> 1.02 us  [local(): pl.pallas_call(functools.partial(scan_kernel, chunks), in_specs=[vmem] *...]
  transfers between devices with their start and end apart: 6 -> 7, of which waited for: 4 -> 6; matrix products, arithmetic and copies ran while one was open for 1% -> 1% of each run, Pallas kernels for 3% -> 3%
where the time goes in v10:
time: 56.1 us; the launch traced here: 55.6 us
  waiting for transfers between devices  23.6 us (42%)
  starting transfers between devices  17.8 us (32%)
  Pallas kernels  6.29 us (11%)
  local copies, waits for them, and re-layouts  6.26 us (11%)
  other arithmetic  1.49 us (3%)
    ppermute x1, waiting for transfers between devices, local(): other = lax.ppermute(halves, axes, swap)  8.11 us
    all_to_all x1, starting transfers between devices, local(): lax.all_to_all(jnp.broadcast_to(own[None, :], tile.shape), 'uly', split_a...  7.25 us
    unnamed x12, local copies, waits for them, and re-layouts  5.66 us
    all_to_all x1, waiting for transfers between devices, local(): lax.all_to_all(moved, axes, split_axis=0, concat_axis=0, axis_index_group...  5.65 us
    ppermute x3, waiting for transfers between devices, local(): lax.ppermute(slice_facts, 'ctx', [(c, (c + ahead) % slices) for c in rang...  5.52 us
    all_to_all x1, starting transfers between devices, local(): lax.all_to_all(ends.reshape(group, rows, LANES), axes, split_axis=0, conc...  3.57 us
    all_to_all x1, starting transfers between devices, local(): lax.all_to_all(moved, axes, split_axis=0, concat_axis=0, axis_index_group...  3.57 us
    all_to_all x1, waiting for transfers between devices, local(): lax.all_to_all(jnp.broadcast_to(own[None, :], tile.shape), 'uly', split_a...  2.97 us
  transfers between devices with their start and end apart: 7, of which 6 were waited for; matrix products, arithmetic and copies ran while one was open for 1% of the time, Pallas kernels for 3%

profile of v10, /device:TPU:0, one launch (start us, length us, event | category | flops | bytes accessed | tf_op | source)
XLA Modules:
  0.0 55.6 jit_solution(4565257993172898265)
XLA Ops:
  0.0 0.7 %convert_add_fusion = f32[128]{0:T(128)S(1)} fusion(s32[96]{0:T(128)} %param.9, f32[8]{0:T(128)} %param.10), kind=kLoop, calls=%fused_computation | loop fusion | flops 256 | bytes 928 | tf_op jit(solution)/shard_map/add | solution.py:240
  0.7 0.6 %broadcast_in_dim.13 = f32[8,1,128]{2,1,0:T(1,128)} broadcast(f32[128]{0:T(128)S(1)} %convert_add_fusion), dimensions={2} | broadcast | bytes 4608 | tf_op jit(solution)/shard_map/broadcast_in_dim | solution.py:244
  1.3 7.3 %all-to-all-start = ((f32[8,1,128]{2,1,0:T(1,128)}), f32[8,1,128]{2,1,0:T(1,128)S(1)}, u32[]{:S(2)}, u32[]{:S(2)}) async-start(f32[8,1,128]{2,1,0:T(1,128)} %broadcast_in_dim.13), calls=%async_computation | async-start | bytes 8192 | tf_op jit(solution)/shard_map/all_to_all | solution.py:243
  8.6 0.7 %fusion.row_ref = f32[1,128]{1,0:T(1,128)S(1)} fusion(s32[96]{0:T(128)} %param.9, f32[8]{0:T(128)} %param.10), kind=kLoop, calls=%fused_computation.1 | loop fusion | flops 256 | bytes 928 | tf_op jit(solution)/shard_map/broadcast_in_dim | solution.py:259
  9.3 1.1 %copy-done = bf16[96,4096]{1,0:T(8,128)(2,1)S(1)} copy-done((bf16[96,4096]{1,0:T(8,128)(2,1)S(1)}, bf16[96,4096]{1,0:T(8,128)(2,1)}, u32[]{:S(2)}) %copy-start) | copy-done | bytes 786456
  10.5 1.1 %copy-done.1 = bf16[96,4096]{1,0:T(8,128)(2,1)S(1)} copy-done((bf16[96,4096]{1,0:T(8,128)(2,1)S(1)}, bf16[96,4096]{1,0:T(8,128)(2,1)}, u32[]{:S(2)}) %copy-start.1) | copy-done | bytes 786456
  11.6 0.4 turn.1
  12.0 3.0 %all-to-all-done = f32[8,1,128]{2,1,0:T(1,128)S(1)} async-done(((f32[8,1,128]{2,1,0:T(1,128)}), f32[8,1,128]{2,1,0:T(1,128)S(1)}, u32[]{:S(2)}, u32[]{:S(2)}) %all-to-all-start) | async-done | bytes 4128 | tf_op jit(solution)/shard_map/all_to_all | solution.py:243
  15.0 1.6 %ends.1.after = bf16[2048,128]{1,0:T(8,128)(2,1)} custom-call(f32[8,128]{1,0:T(8,128)S(1)} %bitcast.7, f32[8,128]{1,0:T(8,128)S(1)} %get-tuple-element.17.idrow, bf16[4096,128]{1,0:T(8,128)(2,1)S(1)} %get-tuple-element.18.turned, bf16[128,4096]{1,0:T(8,128)(2,1)S(1)} %get-tuple-element.19.v_ref), custom_call_target="tpu_custom_call" | custom-call | tf_op jit(solution)/shard_map/ends/pallas_call | solution.py:260
  16.6 3.6 %all-to-all-start.1 = ((bf16[16,128,128]{2,1,0:T(8,128)(2,1)}), bf16[16,128,128]{2,1,0:T(8,128)(2,1)S(1)}, u32[]{:S(2)}, u32[]{:S(2)}) async-start(bf16[16,128,128]{2,1,0:T(8,128)(2,1)} %bitcast.2), calls=%async_computation.1 | async-start | bytes 1048576 | tf_op jit(solution)/shard_map/all_to_all | solution.py:268
  20.2 1.7 %collective-permute-start.2 = (f32[8,128]{1,0:T(8,128)S(1)}, f32[8,128]{1,0:T(8,128)S(1)}, u32[]{:S(2)}, u32[]{:S(2)}) collective-permute-start(f32[8,128]{1,0:T(8,128)S(1)} %pass.1.facts), channel_id=1, source_target_pairs={{0,24},{8,0},{16,8},{24,16},{1,25},{9,1},{17,9},{25,17},{2,26},{10... | collective-permute-start | bytes 12296 | tf_op jit(solution)/shard_map/ppermute | solution.py:281
  22.3 2.9 %collective-permute-done.2.refs_2_ = f32[8,128]{1,0:T(8,128)S(1)} collective-permute-done((f32[8,128]{1,0:T(8,128)S(1)}, f32[8,128]{1,0:T(8,128)S(1)}, u32[]{:S(2)}, u32[]{:S(2)}) %collective-permute-start.2) | collective-permute-done | bytes 4128 | tf_op jit(solution)/shard_map/ppermute | solution.py:281
  25.2 2.7 %collective-permute-done.1.refs_1_ = f32[8,128]{1,0:T(8,128)S(1)} collective-permute-done((f32[8,128]{1,0:T(8,128)S(1)}, f32[8,128]{1,0:T(8,128)S(1)}, u32[]{:S(2)}, u32[]{:S(2)}) %collective-permute-start.1) | collective-permute-done | bytes 4128 | tf_op jit(solution)/shard_map/ppermute | solution.py:281
  28.0 1.4 %all-to-all-done.1.in_ref = bf16[16,128,128]{2,1,0:T(8,128)(2,1)S(1)} async-done(((bf16[16,128,128]{2,1,0:T(8,128)(2,1)}), bf16[16,128,128]{2,1,0:T(8,128)(2,1)S(1)}, u32[]{:S(2)}, u32[]{:S(2)}) %all-to-all-start.1) | async-done | bytes 524320 | tf_op jit(solution)/shard_map/all_to_all | solution.py:268
  29.5 1.3 %collective-permute-start.3 = (bf16[4,128,128]{2,1,0:T(8,128)(2,1)S(1)}, bf16[4,128,128]{2,1,0:T(8,128)(2,1)S(1)}, u32[]{:S(2)}, u32[]{:S(2)}) collective-permute-start(bf16[4,128,128]{2,1,0:T(8,128)(2,1)S(1)} %half.1.after), channel_id=1, source_target_pairs={{0,4},{1,5},{2,6},{3,7},{4,0},{5,1},{6,2},{7,3},{8,12},{9,13},{10,... | collective-permute-start | bytes 393224 | tf_op jit(solution)/shard_map/ppermute | solution.py:303
  30.7 8.1 %collective-permute-done.3.other = bf16[4,128,128]{2,1,0:T(8,128)(2,1)S(1)} collective-permute-done((bf16[4,128,128]{2,1,0:T(8,128)(2,1)S(1)}, bf16[4,128,128]{2,1,0:T(8,128)(2,1)S(1)}, u32[]{:S(2)}, u32[]{:S(2)}) %collective-permute-start.3) | collective-permute-done | bytes 131104 | tf_op jit(solution)/shard_map/ppermute | solution.py:303
  38.8 1.0 %scan.1 = bf16[16,128,128]{2,1,0:T(8,128)(2,1)} custom-call(f32[32,128]{1,0:T(8,128)S(1)} %get-tuple-element.21.linked, f32[32,128]{1,0:T(8,128)S(1)} %get-tuple-element.24.through, f32[128,128]{1,0:T(8,128)S(1)} %get-tuple-element.22.one, f32[128,128]{1,0:T(8,128)S(1)} %get-tuple-element.25.half, bf16[16,128,128]{2,1,0:T(8,128)(2,1)S(1)} %all-to-all-done.1.in_ref, ...), custom_call_target="tpu_custom_call" | custom-call | tf_op jit(solution)/shard_map/scan/pallas_call | solution.py:315
  39.9 3.6 %all-to-all-start.2 = ((bf16[16,128,128]{2,1,0:T(8,128)(2,1)}), bf16[16,128,128]{2,1,0:T(8,128)(2,1)S(1)}, u32[]{:S(2)}, u32[]{:S(2)}) async-start(bf16[16,128,128]{2,1,0:T(8,128)(2,1)} %scan.1), calls=%async_computation.2 | async-start | bytes 1048576 | tf_op jit(solution)/shard_map/all_to_all | solution.py:323
  43.5 1.1 %copy-done.2 = bf16[96,4096]{1,0:T(8,128)(2,1)S(1)} copy-done((bf16[96,4096]{1,0:T(8,128)(2,1)S(1)}, bf16[96,4096]{1,0:T(8,128)(2,1)}, u32[]{:S(2)}) %copy-start.2) | copy-done | bytes 786456
  44.6 1.1 %copy-done.3 = bf16[96,4096]{1,0:T(8,128)(2,1)S(1)} copy-done((bf16[96,4096]{1,0:T(8,128)(2,1)S(1)}, bf16[96,4096]{1,0:T(8,128)(2,1)}, u32[]{:S(2)}) %copy-start.3) | copy-done | bytes 786456
  45.7 1.3 %inner.1 = (f32[96,4096]{1,0:T(8,128)S(1)}, f32[1,4096]{1,0:T(1,128)S(1)}) custom-call(f32[8,128]{1,0:T(8,128)S(1)} %bitcast.9, f32[96,128]{1,0:T(8,128)S(1)} %get-tuple-element.16.idcol, f32[8,128]{1,0:T(8,128)S(1)} %get-tuple-element.17.idrow, bf16[96,4096]{1,0:T(8,128)(2,1)S(1)} %copy-done.3, bf16[4096,128]{1,0:T(8,128)(2,1)S(1)} %get-tuple-element.18.turned, ...), custom_call_target="tpu_custom_call" | custom-call | flops 8000000000 | bytes 4000000 | tf_op jit(solution)/shard_map/inner/pallas_call | solution.py:304
  47.0 5.7 %all-to-all-done.2 = bf16[16,128,128]{2,1,0:T(8,128)(2,1)S(1)} async-done(((bf16[16,128,128]{2,1,0:T(8,128)(2,1)}), bf16[16,128,128]{2,1,0:T(8,128)(2,1)S(1)}, u32[]{:S(2)}, u32[]{:S(2)}) %all-to-all-start.2) | async-done | bytes 524320 | tf_op jit(solution)/shard_map/all_to_all | solution.py:323
  52.6 1.1 %copy-done.4 = bf16[96,4096]{1,0:T(8,128)(2,1)S(1)} copy-done((bf16[96,4096]{1,0:T(8,128)(2,1)S(1)}, bf16[96,4096]{1,0:T(8,128)(2,1)}, u32[]{:S(2)}) %copy-start.4) | copy-done | bytes 786456
  53.8 1.8 %norm.1 = bf16[96,4096]{1,0:T(8,128)(2,1)} custom-call(f32[96,128]{1,0:T(8,128)S(1)} %get-tuple-element.16.idcol, f32[1,128]{1,0:T(1,128)S(1)} %get-tuple-element.20.before, f32[1,4096]{1,0:T(1,128)S(1)} %get-tuple-element.23.rates, bf16[96,4096]{1,0:T(8,128)(2,1)S(1)} %copy-done.4, bf16[2048,128]{1,0:T(8,128)(2,1)S(1)} %bitcast.6, ...), custom_call_target="tpu_custom_call" | custom-call | tf_op jit(solution)/shard_map/norm/pallas_call | solution.py:326
  (13 shorter events, 0.7 us)
Async XLA Ops:
  1.3 13.6 %all-to-all-start = ((f32[8,1,128]{2,1,0:T(1,128)}), f32[8,1,128]{2,1,0:T(1,128)S(1)}, u32[]{:S(2)}, u32[]{:S(2)}) async-start(f32[8,1,128]{2,1,0:T(1,128)} %broadcast_in_dim.13), calls=%async_computation | async-start | bytes 8192 | tf_op jit(solution)/shard_map/all_to_all | solution.py:243
  9.3 1.1 %copy-start = (bf16[96,4096]{1,0:T(8,128)(2,1)S(1)}, bf16[96,4096]{1,0:T(8,128)(2,1)}, u32[]{:S(2)}) copy-start(bf16[96,4096]{1,0:T(8,128)(2,1)} %k_ref.1) | copy-start | bytes 2359300
  10.5 1.1 %copy-start.1 = (bf16[96,4096]{1,0:T(8,128)(2,1)S(1)}, bf16[96,4096]{1,0:T(8,128)(2,1)}, u32[]{:S(2)}) copy-start(bf16[96,4096]{1,0:T(8,128)(2,1)} %v_ref.3) | copy-start | bytes 2359300
  16.6 12.8 %all-to-all-start.1 = ((bf16[16,128,128]{2,1,0:T(8,128)(2,1)}), bf16[16,128,128]{2,1,0:T(8,128)(2,1)S(1)}, u32[]{:S(2)}, u32[]{:S(2)}) async-start(bf16[16,128,128]{2,1,0:T(8,128)(2,1)} %bitcast.2), calls=%async_computation.1 | async-start | bytes 1048576 | tf_op jit(solution)/shard_map/all_to_all | solution.py:268
  20.2 5.0 %collective-permute-start.2 = (f32[8,128]{1,0:T(8,128)S(1)}, f32[8,128]{1,0:T(8,128)S(1)}, u32[]{:S(2)}, u32[]{:S(2)}) collective-permute-start(f32[8,128]{1,0:T(8,128)S(1)} %pass.1.facts), channel_id=1, source_target_pairs={{0,24},{8,0},{16,8},{24,16},{1,25},{9,1},{17,9},{25,17},{2,26},{10... | collective-permute-start | bytes 12296 | tf_op jit(solution)/shard_map/ppermute | solution.py:281
  21.8 6.0 %collective-permute-start.1 = (f32[8,128]{1,0:T(8,128)S(1)}, f32[8,128]{1,0:T(8,128)S(1)}, u32[]{:S(2)}, u32[]{:S(2)}) collective-permute-start(f32[8,128]{1,0:T(8,128)S(1)} %pass.1.facts), channel_id=1, source_target_pairs={{0,16},{8,24},{16,0},{24,8},{1,17},{9,25},{17,1},{25,9},{2,18},{10... | collective-permute-start | bytes 12296 | tf_op jit(solution)/shard_map/ppermute | solution.py:281
  22.2 5.7 %collective-permute-start = (f32[8,128]{1,0:T(8,128)S(1)}, f32[8,128]{1,0:T(8,128)S(1)}, u32[]{:S(2)}, u32[]{:S(2)}) collective-permute-start(f32[8,128]{1,0:T(8,128)S(1)} %pass.1.facts), channel_id=1, source_target_pairs={{0,8},{8,16},{16,24},{24,0},{1,9},{9,17},{17,25},{25,1},{2,10},{10... | collective-permute-start | bytes 12296 | tf_op jit(solution)/shard_map/ppermute | solution.py:281
  29.5 9.4 %collective-permute-start.3 = (bf16[4,128,128]{2,1,0:T(8,128)(2,1)S(1)}, bf16[4,128,128]{2,1,0:T(8,128)(2,1)S(1)}, u32[]{:S(2)}, u32[]{:S(2)}) collective-permute-start(bf16[4,128,128]{2,1,0:T(8,128)(2,1)S(1)} %half.1.after), channel_id=1, source_target_pairs={{0,4},{1,5},{2,6},{3,7},{4,0},{5,1},{6,2},{7,3},{8,12},{9,13},{10,... | collective-permute-start | bytes 393224 | tf_op jit(solution)/shard_map/ppermute | solution.py:303
  39.9 12.8 %all-to-all-start.2 = ((bf16[16,128,128]{2,1,0:T(8,128)(2,1)}), bf16[16,128,128]{2,1,0:T(8,128)(2,1)S(1)}, u32[]{:S(2)}, u32[]{:S(2)}) async-start(bf16[16,128,128]{2,1,0:T(8,128)(2,1)} %scan.1), calls=%async_computation.2 | async-start | bytes 1048576 | tf_op jit(solution)/shard_map/all_to_all | solution.py:323
  43.4 1.1 %copy-start.2 = (bf16[96,4096]{1,0:T(8,128)(2,1)S(1)}, bf16[96,4096]{1,0:T(8,128)(2,1)}, u32[]{:S(2)}) copy-start(bf16[96,4096]{1,0:T(8,128)(2,1)} %v_ref.3) | copy-start | bytes 2359300
  44.6 1.1 %copy-start.3 = (bf16[96,4096]{1,0:T(8,128)(2,1)S(1)}, bf16[96,4096]{1,0:T(8,128)(2,1)}, u32[]{:S(2)}) copy-start(bf16[96,4096]{1,0:T(8,128)(2,1)} %q_ref.3) | copy-start | bytes 2359300
  45.7 6.9 %copy-start.5 = (f32[4096]{0:T(1024)S(1)}, f32[4096]{0:T(1024)}, u32[]{:S(2)}) copy-start(f32[4096]{0:T(1024)} %param.11) | copy-start | bytes 49156
  52.6 1.1 %copy-start.4 = (bf16[96,4096]{1,0:T(8,128)(2,1)S(1)}, bf16[96,4096]{1,0:T(8,128)(2,1)}, u32[]{:S(2)}) copy-start(bf16[96,4096]{1,0:T(8,128)(2,1)} %q_ref.3) | copy-start | bytes 2359300

commit v11 on v10

--- a/solution.py
+++ b/solution.py
@@ -146,7 +146,7 @@
     lax.fori_loop(0, slices, slice_end, 0, unroll=few(slices))
 
 
-def scan_kernel(chunks, linked, through, one, half, in_ref, other, out_ref):
+def scan_kernel(chunks, linked, through, one, half, in_ref, other, after, out_ref):
     slices = other.shape[0]
     later = lax.axis_index("uly") >= chunks
     offset = jnp.where(later, chunks, 0)
@@ -314,12 +314,12 @@
     )(facts, idcol, idrow, queries, turned, values, halves)
     moved = pl.pallas_call(
         functools.partial(scan_kernel, chunks),
-        in_specs=[vmem] * 6,
+        in_specs=[vmem] * 6 + [pl.BlockSpec(memory_space=pl.ANY)],
         out_specs=vmem,
         out_shape=shape((group, rows, LANES), jnp.bfloat16),
         compiler_params=params,
         name="scan",
-    )(linked, through, one, half, pieces, other)
+    )(linked, through, one, half, pieces, other, rates)
     states = lax.all_to_all(
         moved, axes, split_axis=0, concat_axis=0, axis_index_groups=groups, tiled=True
     )

time: 56.1 us -> 53.4 us (0.952)
  blocking collectives: 0 us -> 12 us
  waiting for transfers between devices: 23.6 us -> 15.5 us
  local copies, waits for them, and re-layouts: 6.26 us -> 2.88 us
  starting transfers between devices: 17.8 us -> 15.6 us
  Pallas kernels: 6.29 us -> 5.52 us
    all_to_all x0 -> x1, blocking collectives: none -> 12 us  [local(): lax.all_to_all(moved, axes, split_axis=0, concat_axis=0, axis_index_group...]
    all_to_all x1 -> x0, waiting for transfers between devices: 5.65 us -> none  [local(): lax.all_to_all(moved, axes, split_axis=0, concat_axis=0, axis_index_group...]
    all_to_all x1 -> x0, starting transfers between devices: 3.57 us -> none  [local(): lax.all_to_all(moved, axes, split_axis=0, concat_axis=0, axis_index_group...]
    unnamed x12 -> x10, local copies, waits for them, and re-layouts: 5.66 us -> 2.28 us
    ppermute x3, waiting for transfers between devices: 5.52 us -> 4.21 us  [local(): lax.ppermute(slice_facts, 'ctx', [(c, (c + ahead) % slices) for c in rang...]
    ppermute x1, waiting for transfers between devices: 8.11 us -> 6.82 us  [local(): other = lax.ppermute(halves, axes, swap)]
    ppermute x3, starting transfers between devices: 2.14 us -> 3.37 us  [local(): lax.ppermute(slice_facts, 'ctx', [(c, (c + ahead) % slices) for c in rang...]
    pallas_call x1, Pallas kernels: 1.02 us -> 0.23 us  [local(): pl.pallas_call(functools.partial(scan_kernel, chunks), in_specs=[vmem] *...]
  transfers between devices with their start and end apart: 7 -> 6, of which waited for: 6 -> 5; matrix products, arithmetic and copies ran while one was open for 1% -> 1% of each run, Pallas kernels for 3% -> 3%
where the time goes in v11:
time: 53.4 us; the launch traced here: 53 us
  starting transfers between devices  15.6 us (29%)
  waiting for transfers between devices  15.5 us (29%)
  blocking collectives  12 us (22%)
  Pallas kernels  5.52 us (10%)
  local copies, waits for them, and re-layouts  2.88 us (5%)
  other arithmetic  1.49 us (3%)
    all_to_all x1, blocking collectives, local(): lax.all_to_all(moved, axes, split_axis=0, concat_axis=0, axis_index_group...  12 us
    all_to_all x1, starting transfers between devices, local(): lax.all_to_all(jnp.broadcast_to(own[None, :], tile.shape), 'uly', split_a...  7.25 us
    ppermute x1, waiting for transfers between devices, local(): other = lax.ppermute(halves, axes, swap)  6.82 us
    ppermute x3, waiting for transfers between devices, local(): lax.ppermute(slice_facts, 'ctx', [(c, (c + ahead) % slices) for c in rang...  4.21 us
    all_to_all x1, starting transfers between devices, local(): lax.all_to_all(ends.reshape(group, rows, LANES), axes, split_axis=0, conc...  3.71 us
    ppermute x3, starting transfers between devices, local(): lax.ppermute(slice_facts, 'ctx', [(c, (c + ahead) % slices) for c in rang...  3.37 us
    all_to_all x1, waiting for transfers between devices, local(): lax.all_to_all(jnp.broadcast_to(own[None, :], tile.shape), 'uly', split_a...  2.97 us
    unnamed x10, local copies, waits for them, and re-layouts  2.28 us
  transfers between devices with their start and end apart: 6, of which 5 were waited for; matrix products, arithmetic and copies ran while one was open for 1% of the time, Pallas kernels for 3%

profile of v11, /device:TPU:0, one launch (start us, length us, event | category | flops | bytes accessed | tf_op | source)
XLA Modules:
  0.0 53.0 jit_solution(10026986746563606910)
XLA Ops:
  0.0 0.7 %convert_add_fusion = f32[128]{0:T(128)S(1)} fusion(s32[96]{0:T(128)} %param.9, f32[8]{0:T(128)} %param.10), kind=kLoop, calls=%fused_computation | loop fusion | flops 256 | bytes 928 | tf_op jit(solution)/shard_map/add | solution.py:240
  0.7 0.6 %broadcast_in_dim.13 = f32[8,1,128]{2,1,0:T(1,128)} broadcast(f32[128]{0:T(128)S(1)} %convert_add_fusion), dimensions={2} | broadcast | bytes 4608 | tf_op jit(solution)/shard_map/broadcast_in_dim | solution.py:244
  1.3 7.3 %all-to-all-start = ((f32[8,1,128]{2,1,0:T(1,128)}), f32[8,1,128]{2,1,0:T(1,128)S(1)}, u32[]{:S(2)}, u32[]{:S(2)}) async-start(f32[8,1,128]{2,1,0:T(1,128)} %broadcast_in_dim.13), calls=%async_computation | async-start | bytes 8192 | tf_op jit(solution)/shard_map/all_to_all | solution.py:243
  8.6 0.7 %fusion.row_ref = f32[1,128]{1,0:T(1,128)S(1)} fusion(s32[96]{0:T(128)} %param.9, f32[8]{0:T(128)} %param.10), kind=kLoop, calls=%fused_computation.1 | loop fusion | flops 256 | bytes 928 | tf_op jit(solution)/shard_map/broadcast_in_dim | solution.py:259
  9.3 1.1 %copy-done = bf16[96,4096]{1,0:T(8,128)(2,1)S(1)} copy-done((bf16[96,4096]{1,0:T(8,128)(2,1)S(1)}, bf16[96,4096]{1,0:T(8,128)(2,1)}, u32[]{:S(2)}) %copy-start) | copy-done | bytes 786456
  10.5 1.1 %copy-done.1 = bf16[96,4096]{1,0:T(8,128)(2,1)S(1)} copy-done((bf16[96,4096]{1,0:T(8,128)(2,1)S(1)}, bf16[96,4096]{1,0:T(8,128)(2,1)}, u32[]{:S(2)}) %copy-start.1) | copy-done | bytes 786456
  11.6 0.4 turn.1
  12.0 3.0 %all-to-all-done = f32[8,1,128]{2,1,0:T(1,128)S(1)} async-done(((f32[8,1,128]{2,1,0:T(1,128)}), f32[8,1,128]{2,1,0:T(1,128)S(1)}, u32[]{:S(2)}, u32[]{:S(2)}) %all-to-all-start) | async-done | bytes 4128 | tf_op jit(solution)/shard_map/all_to_all | solution.py:243
  15.0 1.6 %ends.1.after = bf16[2048,128]{1,0:T(8,128)(2,1)} custom-call(f32[8,128]{1,0:T(8,128)S(1)} %bitcast.7, f32[8,128]{1,0:T(8,128)S(1)} %get-tuple-element.17.idrow, bf16[4096,128]{1,0:T(8,128)(2,1)S(1)} %get-tuple-element.18.turned, bf16[128,4096]{1,0:T(8,128)(2,1)S(1)} %get-tuple-element.19.v_ref), custom_call_target="tpu_custom_call" | custom-call | tf_op jit(solution)/shard_map/ends/pallas_call | solution.py:260
  16.6 3.7 %all-to-all-start.1 = ((bf16[16,128,128]{2,1,0:T(8,128)(2,1)}), bf16[16,128,128]{2,1,0:T(8,128)(2,1)S(1)}, u32[]{:S(2)}, u32[]{:S(2)}) async-start(bf16[16,128,128]{2,1,0:T(8,128)(2,1)} %bitcast.2), calls=%async_computation.1 | async-start | bytes 1048576 | tf_op jit(solution)/shard_map/all_to_all | solution.py:268
  20.3 0.4 collective-permute-start
  20.7 1.7 %collective-permute-start.1 = (f32[8,128]{1,0:T(8,128)S(1)}, f32[8,128]{1,0:T(8,128)S(1)}, u32[]{:S(2)}, u32[]{:S(2)}) collective-permute-start(f32[8,128]{1,0:T(8,128)S(1)} %pass.1.facts), channel_id=1, source_target_pairs={{0,16},{8,24},{16,0},{24,8},{1,17},{9,25},{17,1},{25,9},{2,18},{10... | collective-permute-start | bytes 12296 | tf_op jit(solution)/shard_map/ppermute | solution.py:281
  22.4 1.3 %collective-permute-start.2 = (f32[8,128]{1,0:T(8,128)S(1)}, f32[8,128]{1,0:T(8,128)S(1)}, u32[]{:S(2)}, u32[]{:S(2)}) collective-permute-start(f32[8,128]{1,0:T(8,128)S(1)} %pass.1.facts), channel_id=1, source_target_pairs={{0,24},{8,0},{16,8},{24,16},{1,25},{9,1},{17,9},{25,17},{2,26},{10... | collective-permute-start | bytes 12296 | tf_op jit(solution)/shard_map/ppermute | solution.py:281
  23.7 3.2 %collective-permute-done.refs_0_ = f32[8,128]{1,0:T(8,128)S(1)} collective-permute-done((f32[8,128]{1,0:T(8,128)S(1)}, f32[8,128]{1,0:T(8,128)S(1)}, u32[]{:S(2)}, u32[]{:S(2)}) %collective-permute-start) | collective-permute-done | bytes 4128 | tf_op jit(solution)/shard_map/ppermute | solution.py:281
  26.9 1.0 %collective-permute-done.1.refs_1_ = f32[8,128]{1,0:T(8,128)S(1)} collective-permute-done((f32[8,128]{1,0:T(8,128)S(1)}, f32[8,128]{1,0:T(8,128)S(1)}, u32[]{:S(2)}, u32[]{:S(2)}) %collective-permute-start.1) | collective-permute-done | bytes 4128 | tf_op jit(solution)/shard_map/ppermute | solution.py:281
  27.9 0.1 link.1
  28.0 1.5 %all-to-all-done.1.in_ref = bf16[16,128,128]{2,1,0:T(8,128)(2,1)S(1)} async-done(((bf16[16,128,128]{2,1,0:T(8,128)(2,1)}), bf16[16,128,128]{2,1,0:T(8,128)(2,1)S(1)}, u32[]{:S(2)}, u32[]{:S(2)}) %all-to-all-start.1) | async-done | bytes 524320 | tf_op jit(solution)/shard_map/all_to_all | solution.py:268
  29.5 0.1 half.1.after
  29.6 1.3 %collective-permute-start.3 = (bf16[4,128,128]{2,1,0:T(8,128)(2,1)S(1)}, bf16[4,128,128]{2,1,0:T(8,128)(2,1)S(1)}, u32[]{:S(2)}, u32[]{:S(2)}) collective-permute-start(bf16[4,128,128]{2,1,0:T(8,128)(2,1)S(1)} %half.1.after), channel_id=1, source_target_pairs={{0,4},{1,5},{2,6},{3,7},{4,0},{5,1},{6,2},{7,3},{8,12},{9,13},{10,... | collective-permute-start | bytes 393224 | tf_op jit(solution)/shard_map/ppermute | solution.py:303
  30.9 1.3 %inner.1 = (f32[96,4096]{1,0:T(8,128)S(1)}, f32[1,4096]{1,0:T(1,128)S(1)}) custom-call(f32[8,128]{1,0:T(8,128)S(1)} %bitcast.9, f32[96,128]{1,0:T(8,128)S(1)} %get-tuple-element.16.idcol, f32[8,128]{1,0:T(8,128)S(1)} %get-tuple-element.17.idrow, bf16[96,4096]{1,0:T(8,128)(2,1)S(1)} %copy-done.3, bf16[4096,128]{1,0:T(8,128)(2,1)S(1)} %get-tuple-element.18.turned, ...), custom_call_target="tpu_custom_call" | custom-call | flops 8000000000 | bytes 4000000 | tf_op jit(solution)/shard_map/inner/pallas_call | solution.py:304
  32.2 6.8 %collective-permute-done.3.other = bf16[4,128,128]{2,1,0:T(8,128)(2,1)S(1)} collective-permute-done((bf16[4,128,128]{2,1,0:T(8,128)(2,1)S(1)}, bf16[4,128,128]{2,1,0:T(8,128)(2,1)S(1)}, u32[]{:S(2)}, u32[]{:S(2)}) %collective-permute-start.3) | collective-permute-done | bytes 131104 | tf_op jit(solution)/shard_map/ppermute | solution.py:303
  39.0 0.2 scan.1
  39.2 12.0 %all_to_all.18 = bf16[16,128,128]{2,1,0:T(8,128)(2,1)S(1)} all-to-all(bf16[16,128,128]{2,1,0:T(8,128)(2,1)S(1)} %scan.1), channel_id=1, replica_groups={{0,1,2,3,8,9,10,11,16,17,18,19,24,25,26,27},{4,5,6,7,12,13,14,15,20,21,..., dimensions={0} | all-to-all | bytes 1048576 | tf_op jit(solution)/shard_map/all_to_all | solution.py:323
  51.2 1.8 %norm.1 = bf16[96,4096]{1,0:T(8,128)(2,1)} custom-call(f32[96,128]{1,0:T(8,128)S(1)} %get-tuple-element.16.idcol, f32[1,128]{1,0:T(1,128)S(1)} %get-tuple-element.20.before, f32[1,4096]{1,0:T(1,128)S(1)} %get-tuple-element.23.after.rates, bf16[96,4096]{1,0:T(8,128)(2,1)S(1)} %copy-done.3, bf16[2048,128]{1,0:T(8,128)(2,1)S(1)} %bitcast.6, ...), custom_call_target="tpu_custom_call" | custom-call | tf_op jit(solution)/shard_map/norm/pallas_call | solution.py:326
  (10 shorter events, 0.0 us)
Async XLA Ops:
  1.3 13.6 %all-to-all-start = ((f32[8,1,128]{2,1,0:T(1,128)}), f32[8,1,128]{2,1,0:T(1,128)S(1)}, u32[]{:S(2)}, u32[]{:S(2)}) async-start(f32[8,1,128]{2,1,0:T(1,128)} %broadcast_in_dim.13), calls=%async_computation | async-start | bytes 8192 | tf_op jit(solution)/shard_map/all_to_all | solution.py:243
  9.3 1.1 %copy-start = (bf16[96,4096]{1,0:T(8,128)(2,1)S(1)}, bf16[96,4096]{1,0:T(8,128)(2,1)}, u32[]{:S(2)}) copy-start(bf16[96,4096]{1,0:T(8,128)(2,1)} %k_ref.1) | copy-start | bytes 2359300
  10.5 1.1 %copy-start.1 = (bf16[96,4096]{1,0:T(8,128)(2,1)S(1)}, bf16[96,4096]{1,0:T(8,128)(2,1)}, u32[]{:S(2)}) copy-start(bf16[96,4096]{1,0:T(8,128)(2,1)} %v_ref.3) | copy-start | bytes 2359300
  16.6 14.3 %copy-start.2 = (bf16[96,4096]{1,0:T(8,128)(2,1)S(1)}, bf16[96,4096]{1,0:T(8,128)(2,1)}, u32[]{:S(2)}) copy-start(bf16[96,4096]{1,0:T(8,128)(2,1)} %v_ref.3) | copy-start | bytes 2359300
  16.6 14.3 %copy-start.3 = (bf16[96,4096]{1,0:T(8,128)(2,1)S(1)}, bf16[96,4096]{1,0:T(8,128)(2,1)}, u32[]{:S(2)}) copy-start(bf16[96,4096]{1,0:T(8,128)(2,1)} %q_ref.3) | copy-start | bytes 2359300
  16.6 12.9 %all-to-all-start.1 = ((bf16[16,128,128]{2,1,0:T(8,128)(2,1)}), bf16[16,128,128]{2,1,0:T(8,128)(2,1)S(1)}, u32[]{:S(2)}, u32[]{:S(2)}) async-start(bf16[16,128,128]{2,1,0:T(8,128)(2,1)} %bitcast.2), calls=%async_computation.1 | async-start | bytes 1048576 | tf_op jit(solution)/shard_map/all_to_all | solution.py:268
  20.3 6.5 %collective-permute-start = (f32[8,128]{1,0:T(8,128)S(1)}, f32[8,128]{1,0:T(8,128)S(1)}, u32[]{:S(2)}, u32[]{:S(2)}) collective-permute-start(f32[8,128]{1,0:T(8,128)S(1)} %pass.1.facts), channel_id=1, source_target_pairs={{0,8},{8,16},{16,24},{24,0},{1,9},{9,17},{17,25},{25,1},{2,10},{10... | collective-permute-start | bytes 12296 | tf_op jit(solution)/shard_map/ppermute | solution.py:281
  20.7 7.2 %collective-permute-start.1 = (f32[8,128]{1,0:T(8,128)S(1)}, f32[8,128]{1,0:T(8,128)S(1)}, u32[]{:S(2)}, u32[]{:S(2)}) collective-permute-start(f32[8,128]{1,0:T(8,128)S(1)} %pass.1.facts), channel_id=1, source_target_pairs={{0,16},{8,24},{16,0},{24,8},{1,17},{9,25},{17,1},{25,9},{2,18},{10... | collective-permute-start | bytes 12296 | tf_op jit(solution)/shard_map/ppermute | solution.py:281
  22.4 5.5 %collective-permute-start.2 = (f32[8,128]{1,0:T(8,128)S(1)}, f32[8,128]{1,0:T(8,128)S(1)}, u32[]{:S(2)}, u32[]{:S(2)}) collective-permute-start(f32[8,128]{1,0:T(8,128)S(1)} %pass.1.facts), channel_id=1, source_target_pairs={{0,24},{8,0},{16,8},{24,16},{1,25},{9,1},{17,9},{25,17},{2,26},{10... | collective-permute-start | bytes 12296 | tf_op jit(solution)/shard_map/ppermute | solution.py:281
  29.6 9.4 %collective-permute-start.3 = (bf16[4,128,128]{2,1,0:T(8,128)(2,1)S(1)}, bf16[4,128,128]{2,1,0:T(8,128)(2,1)S(1)}, u32[]{:S(2)}, u32[]{:S(2)}) collective-permute-start(bf16[4,128,128]{2,1,0:T(8,128)(2,1)S(1)} %half.1.after), channel_id=1, source_target_pairs={{0,4},{1,5},{2,6},{3,7},{4,0},{5,1},{6,2},{7,3},{8,12},{9,13},{10,... | collective-permute-start | bytes 393224 | tf_op jit(solution)/shard_map/ppermute | solution.py:303
  32.1 19.0 %copy-start.4 = (f32[4096]{0:T(1024)S(1)}, f32[4096]{0:T(1024)}, u32[]{:S(2)}) copy-start(f32[4096]{0:T(1024)} %param.11) | copy-start | bytes 49156

commit v12 on v11

--- a/solution.py
+++ b/solution.py
@@ -129,46 +129,54 @@
             )
 
 
-def half_kernel(chunks, linked, one, in_ref, out_ref):
-    slices = out_ref.shape[0]
+def half_kernel(chunks, linked, one, in_ref, early_ref, final_ref):
+    slices = early_ref.shape[0] + 1
     offset = jnp.where(lax.axis_index("uly") >= chunks, chunks, 0)
 
-    def slice_end(c, _):
+    def slice_end(c):
         def step(j, state):
             keep = linked[pl.ds(c * 2 * chunks + offset + j, 1), :] * one[...]
             return in_ref[c * chunks + j].astype(jnp.float32) + keep * state
 
         begin = in_ref[c * chunks].astype(jnp.float32)
         state = lax.fori_loop(1, chunks, step, begin, unroll=few(chunks - 1))
-        out_ref[c] = state.astype(out_ref.dtype)
+        return state.astype(early_ref.dtype)
+
+    def early(c, _):
+        early_ref[c] = slice_end(c)
         return 0
 
-    lax.fori_loop(0, slices, slice_end, 0, unroll=few(slices))
-
-
-def scan_kernel(chunks, linked, through, one, half, in_ref, other, after, out_ref):
-    slices = other.shape[0]
+    lax.fori_loop(0, slices - 1, early, 0, unroll=few(slices - 1))
+    final_ref[0] = slice_end(slices - 1)
+
+
+def scan_kernel(
+    chunks, linked, through, one, half, in_ref, early, final, after, out_ref
+):
+    slices = early.shape[0] + 1
     later = lax.axis_index("uly") >= chunks
     offset = jnp.where(later, chunks, 0)
 
-    def over_other(state, c, wanted):
+    def over_other(state, c, piece, wanted):
         keep = through[pl.ds(c * 2 * chunks + chunks - offset, 1), :] * half[...]
-        return jnp.where(wanted, other[c].astype(jnp.float32) + keep * state, state)
-
-    def over_slice(c, state):
-        state = over_other(state, c, later)
-
+        return jnp.where(wanted, piece.astype(jnp.float32) + keep * state, state)
+
+    def over_own(state, c):
         def step(j, state):
             at = c * chunks + j
             out_ref[at] = state.astype(out_ref.dtype)
             keep = linked[pl.ds(c * 2 * chunks + offset + j, 1), :] * one[...]
             return in_ref[at].astype(jnp.float32) + keep * state
 
-        state = lax.fori_loop(0, chunks, step, state, unroll=few(chunks))
-        return over_other(state, c, jnp.logical_not(later))
+        return lax.fori_loop(0, chunks, step, state, unroll=few(chunks))
+
+    def over_slice(c, state):
+        state = over_own(over_other(state, c, early[c], later), c)
+        return over_other(state, c, early[c], jnp.logical_not(later))
 
     begin = jnp.zeros(in_ref.shape[1:], jnp.float32)
-    lax.fori_loop(0, slices, over_slice, begin, unroll=few(slices))
+    state = lax.fori_loop(0, slices - 1, over_slice, begin, unroll=few(slices - 1))
+    over_own(over_other(state, slices - 1, final[0], later), slices - 1)
 
 
 def norm_kernel(idcol, before, rates, q_ref, s_ref, inner_ref, gain, out_ref, raw, done, sems):
@@ -292,15 +300,19 @@
         compiler_params=params,
         name="link",
     )(slice_facts, *others)
-    halves = pl.pallas_call(
+    early_ends, final_end = pl.pallas_call(
         functools.partial(half_kernel, chunks),
         in_specs=[vmem] * 3,
-        out_specs=vmem,
-        out_shape=shape((slices, rows, LANES), jnp.bfloat16),
+        out_specs=[vmem] * 2,
+        out_shape=[
+            shape((slices - 1, rows, LANES), jnp.bfloat16),
+            shape((1, rows, LANES), jnp.bfloat16),
+        ],
         compiler_params=params,
         name="half",
     )(linked, one, pieces)
-    other = lax.ppermute(halves, axes, swap)
+    early = lax.ppermute(early_ends, axes, swap)
+    final = lax.ppermute(final_end, axes, [(low, high) for low, high in swap if low < high])
     inner, rates = pl.pallas_call(
         functools.partial(inner_kernel, here),
         in_specs=[vmem] * 6 + [pl.BlockSpec(memory_space=pl.ANY)],
@@ -311,15 +323,15 @@
             flops=8_000_000_000, bytes_accessed=4_000_000, transcendentals=600_000
         ),
         name="inner",
-    )(facts, idcol, idrow, queries, turned, values, halves)
+    )(facts, idcol, idrow, queries, turned, values, early_ends)
     moved = pl.pallas_call(
         functools.partial(scan_kernel, chunks),
-        in_specs=[vmem] * 6 + [pl.BlockSpec(memory_space=pl.ANY)],
+        in_specs=[vmem] * 7 + [pl.BlockSpec(memory_space=pl.ANY)],
         out_specs=vmem,
         out_shape=shape((group, rows, LANES), jnp.bfloat16),
         compiler_params=params,
         name="scan",
-    )(linked, through, one, half, pieces, other, rates)
+    )(linked, through, one, half, pieces, early, final, rates)
     states = lax.all_to_all(
         moved, axes, split_axis=0, concat_axis=0, axis_index_groups=groups, tiled=True
     )

time: 53.4 us -> 52 us (0.974)
  waiting for transfers between devices: 15.5 us -> 10.4 us
  starting transfers between devices: 15.6 us -> 19.2 us
    ppermute x1 -> x2, waiting for transfers between devices: 6.82 us -> 1.77 us  [the longest x1 1.49 us: local(): early = lax.ppermute(early_ends, axes, swap)]
    ppermute x1 -> x2, starting transfers between devices: 1.26 us -> 4.88 us  [the longest x1 3.62 us: local(): lax.ppermute(final_end, axes, [(low, high) for low, high in swap if low <...]
  transfers between devices with their start and end apart: 6 -> 7, of which waited for: 5 -> 6; matrix products, arithmetic and copies ran while one was open for 1% -> 1% of each run, Pallas kernels for 3% -> 3%
where the time goes in v12:
time: 52 us; the launch traced here: 51.6 us
  starting transfers between devices  19.2 us (37%)
  blocking collectives  12 us (23%)
  waiting for transfers between devices  10.4 us (20%)
  Pallas kernels  5.53 us (11%)
  local copies, waits for them, and re-layouts  2.88 us (6%)
  other arithmetic  1.49 us (3%)
    all_to_all x1, blocking collectives, local(): lax.all_to_all(moved, axes, split_axis=0, concat_axis=0, axis_index_group...  12 us
    all_to_all x1, starting transfers between devices, local(): lax.all_to_all(jnp.broadcast_to(own[None, :], tile.shape), 'uly', split_a...  7.25 us
    ppermute x3, waiting for transfers between devices, local(): lax.ppermute(slice_facts, 'ctx', [(c, (c + ahead) % slices) for c in rang...  4.21 us
    all_to_all x1, starting transfers between devices, local(): lax.all_to_all(ends.reshape(group, rows, LANES), axes, split_axis=0, conc...  3.71 us
    ppermute x1, starting transfers between devices, local(): lax.ppermute(final_end, axes, [(low, high) for low, high in swap if low <...  3.62 us
    ppermute x3, starting transfers between devices, local(): lax.ppermute(slice_facts, 'ctx', [(c, (c + ahead) % slices) for c in rang...  3.37 us
    all_to_all x1, waiting for transfers between devices, local(): lax.all_to_all(jnp.broadcast_to(own[None, :], tile.shape), 'uly', split_a...  2.97 us
    unnamed x10, local copies, waits for them, and re-layouts  2.28 us
  transfers between devices with their start and end apart: 7, of which 6 were waited for; matrix products, arithmetic and copies ran while one was open for 1% of the time, Pallas kernels for 3%

profile of v12, /device:TPU:0, one launch (start us, length us, event | category | flops | bytes accessed | tf_op | source)
XLA Modules:
  0.0 51.6 jit_solution(16096167764897280784)
XLA Ops:
  0.0 0.7 %convert_add_fusion = f32[128]{0:T(128)S(1)} fusion(s32[96]{0:T(128)} %param.9, f32[8]{0:T(128)} %param.10), kind=kLoop, calls=%fused_computation | loop fusion | flops 256 | bytes 928 | tf_op jit(solution)/shard_map/add | solution.py:248
  0.7 0.6 %broadcast_in_dim.13 = f32[8,1,128]{2,1,0:T(1,128)} broadcast(f32[128]{0:T(128)S(1)} %convert_add_fusion), dimensions={2} | broadcast | bytes 4608 | tf_op jit(solution)/shard_map/broadcast_in_dim | solution.py:252
  1.3 7.3 %all-to-all-start = ((f32[8,1,128]{2,1,0:T(1,128)}), f32[8,1,128]{2,1,0:T(1,128)S(1)}, u32[]{:S(2)}, u32[]{:S(2)}) async-start(f32[8,1,128]{2,1,0:T(1,128)} %broadcast_in_dim.13), calls=%async_computation | async-start | bytes 8192 | tf_op jit(solution)/shard_map/all_to_all | solution.py:251
  8.6 0.7 %fusion.row_ref = f32[1,128]{1,0:T(1,128)S(1)} fusion(s32[96]{0:T(128)} %param.9, f32[8]{0:T(128)} %param.10), kind=kLoop, calls=%fused_computation.1 | loop fusion | flops 256 | bytes 928 | tf_op jit(solution)/shard_map/broadcast_in_dim | solution.py:267
  9.3 1.1 %copy-done = bf16[96,4096]{1,0:T(8,128)(2,1)S(1)} copy-done((bf16[96,4096]{1,0:T(8,128)(2,1)S(1)}, bf16[96,4096]{1,0:T(8,128)(2,1)}, u32[]{:S(2)}) %copy-start) | copy-done | bytes 786456
  10.5 1.1 %copy-done.1 = bf16[96,4096]{1,0:T(8,128)(2,1)S(1)} copy-done((bf16[96,4096]{1,0:T(8,128)(2,1)S(1)}, bf16[96,4096]{1,0:T(8,128)(2,1)}, u32[]{:S(2)}) %copy-start.1) | copy-done | bytes 786456
  11.6 0.4 turn.1
  12.0 3.0 %all-to-all-done = f32[8,1,128]{2,1,0:T(1,128)S(1)} async-done(((f32[8,1,128]{2,1,0:T(1,128)}), f32[8,1,128]{2,1,0:T(1,128)S(1)}, u32[]{:S(2)}, u32[]{:S(2)}) %all-to-all-start) | async-done | bytes 4128 | tf_op jit(solution)/shard_map/all_to_all | solution.py:251
  15.0 1.6 %ends.1.after = bf16[2048,128]{1,0:T(8,128)(2,1)} custom-call(f32[8,128]{1,0:T(8,128)S(1)} %bitcast.7, f32[8,128]{1,0:T(8,128)S(1)} %get-tuple-element.19.idrow, bf16[4096,128]{1,0:T(8,128)(2,1)S(1)} %get-tuple-element.20.turned, bf16[128,4096]{1,0:T(8,128)(2,1)S(1)} %get-tuple-element.21.v_ref), custom_call_target="tpu_custom_call" | custom-call | tf_op jit(solution)/shard_map/ends/pallas_call | solution.py:268
  16.6 3.7 %all-to-all-start.1 = ((bf16[16,128,128]{2,1,0:T(8,128)(2,1)}), bf16[16,128,128]{2,1,0:T(8,128)(2,1)S(1)}, u32[]{:S(2)}, u32[]{:S(2)}) async-start(bf16[16,128,128]{2,1,0:T(8,128)(2,1)} %bitcast.2), calls=%async_computation.1 | async-start | bytes 1048576 | tf_op jit(solution)/shard_map/all_to_all | solution.py:276
  20.3 0.4 collective-permute-start
  20.7 1.7 %collective-permute-start.1 = (f32[8,128]{1,0:T(8,128)S(1)}, f32[8,128]{1,0:T(8,128)S(1)}, u32[]{:S(2)}, u32[]{:S(2)}) collective-permute-start(f32[8,128]{1,0:T(8,128)S(1)} %pass.1.facts), channel_id=1, source_target_pairs={{0,16},{8,24},{16,0},{24,8},{1,17},{9,25},{17,1},{25,9},{2,18},{10... | collective-permute-start | bytes 12296 | tf_op jit(solution)/shard_map/ppermute | solution.py:289
  22.4 1.3 %collective-permute-start.2 = (f32[8,128]{1,0:T(8,128)S(1)}, f32[8,128]{1,0:T(8,128)S(1)}, u32[]{:S(2)}, u32[]{:S(2)}) collective-permute-start(f32[8,128]{1,0:T(8,128)S(1)} %pass.1.facts), channel_id=1, source_target_pairs={{0,24},{8,0},{16,8},{24,16},{1,25},{9,1},{17,9},{25,17},{2,26},{10... | collective-permute-start | bytes 12296 | tf_op jit(solution)/shard_map/ppermute | solution.py:289
  23.7 3.2 %collective-permute-done.refs_0_ = f32[8,128]{1,0:T(8,128)S(1)} collective-permute-done((f32[8,128]{1,0:T(8,128)S(1)}, f32[8,128]{1,0:T(8,128)S(1)}, u32[]{:S(2)}, u32[]{:S(2)}) %collective-permute-start) | collective-permute-done | bytes 4128 | tf_op jit(solution)/shard_map/ppermute | solution.py:289
  26.9 1.0 %collective-permute-done.1.refs_1_ = f32[8,128]{1,0:T(8,128)S(1)} collective-permute-done((f32[8,128]{1,0:T(8,128)S(1)}, f32[8,128]{1,0:T(8,128)S(1)}, u32[]{:S(2)}, u32[]{:S(2)}) %collective-permute-start.1) | collective-permute-done | bytes 4128 | tf_op jit(solution)/shard_map/ppermute | solution.py:289
  28.0 1.5 %all-to-all-done.1.in_ref = bf16[16,128,128]{2,1,0:T(8,128)(2,1)S(1)} async-done(((bf16[16,128,128]{2,1,0:T(8,128)(2,1)}), bf16[16,128,128]{2,1,0:T(8,128)(2,1)S(1)}, u32[]{:S(2)}, u32[]{:S(2)}) %all-to-all-start.1) | async-done | bytes 524320 | tf_op jit(solution)/shard_map/all_to_all | solution.py:276
  29.6 1.3 %collective-permute-start.3 = (bf16[3,128,128]{2,1,0:T(8,128)(2,1)S(1)}, bf16[3,128,128]{2,1,0:T(8,128)(2,1)S(1)}, u32[]{:S(2)}, u32[]{:S(2)}) collective-permute-start(bf16[3,128,128]{2,1,0:T(8,128)(2,1)S(1)} %get-tuple-element.25.after), channel_id=1, source_target_pairs={{0,4},{1,5},{2,6},{3,7},{4,0},{5,1},{6,2},{7,3},{8,12},{9,13},{10,... | collective-permute-start | bytes 294920 | tf_op jit(solution)/shard_map/ppermute | solution.py:314
  30.9 3.6 %collective-permute-start.4 = (bf16[1,128,128]{2,1,0:T(8,128)(2,1)S(1)}, bf16[1,128,128]{2,1,0:T(8,128)(2,1)S(1)}, u32[]{:S(2)}, u32[]{:S(2)}) collective-permute-start(bf16[1,128,128]{2,1,0:T(8,128)(2,1)S(1)} %get-tuple-element.29), channel_id=1, source_target_pairs={{0,4},{1,5},{2,6},{3,7},{8,12},{9,13},{10,14},{11,15},{16,20},{17,... | collective-permute-start | bytes 98312 | tf_op jit(solution)/shard_map/ppermute | solution.py:315
  34.5 1.3 %inner.1 = (f32[96,4096]{1,0:T(8,128)S(1)}, f32[1,4096]{1,0:T(1,128)S(1)}) custom-call(f32[8,128]{1,0:T(8,128)S(1)} %bitcast.9, f32[96,128]{1,0:T(8,128)S(1)} %get-tuple-element.18.idcol, f32[8,128]{1,0:T(8,128)S(1)} %get-tuple-element.19.idrow, bf16[96,4096]{1,0:T(8,128)(2,1)S(1)} %copy-done.3, bf16[4096,128]{1,0:T(8,128)(2,1)S(1)} %get-tuple-element.20.turned, ...), custom_call_target="tpu_custom_call" | custom-call | flops 8000000000 | bytes 4000000 | tf_op jit(solution)/shard_map/inner/pallas_call | solution.py:316
  35.8 0.3 collective-permute-done.4.final
  36.1 1.5 %collective-permute-done.3.early = bf16[3,128,128]{2,1,0:T(8,128)(2,1)S(1)} collective-permute-done((bf16[3,128,128]{2,1,0:T(8,128)(2,1)S(1)}, bf16[3,128,128]{2,1,0:T(8,128)(2,1)S(1)}, u32[]{:S(2)}, u32[]{:S(2)}) %collective-permute-start.3) | collective-permute-done | bytes 98336 | tf_op jit(solution)/shard_map/ppermute | solution.py:314
  37.6 0.2 scan.1
  37.8 12.0 %all_to_all.18 = bf16[16,128,128]{2,1,0:T(8,128)(2,1)S(1)} all-to-all(bf16[16,128,128]{2,1,0:T(8,128)(2,1)S(1)} %scan.1), channel_id=1, replica_groups={{0,1,2,3,8,9,10,11,16,17,18,19,24,25,26,27},{4,5,6,7,12,13,14,15,20,21,..., dimensions={0} | all-to-all | bytes 1048576 | tf_op jit(solution)/shard_map/all_to_all | solution.py:335
  49.8 1.8 %norm.1 = bf16[96,4096]{1,0:T(8,128)(2,1)} custom-call(f32[96,128]{1,0:T(8,128)S(1)} %get-tuple-element.18.idcol, f32[1,128]{1,0:T(1,128)S(1)} %get-tuple-element.22.before, f32[1,4096]{1,0:T(1,128)S(1)} %get-tuple-element.26.after.rates, bf16[96,4096]{1,0:T(8,128)(2,1)S(1)} %copy-done.3, bf16[2048,128]{1,0:T(8,128)(2,1)S(1)} %bitcast.6, ...), custom_call_target="tpu_custom_call" | custom-call | tf_op jit(solution)/shard_map/norm/pallas_call | solution.py:338
  (12 shorter events, 0.3 us)
Async XLA Ops:
  1.3 13.6 %all-to-all-start = ((f32[8,1,128]{2,1,0:T(1,128)}), f32[8,1,128]{2,1,0:T(1,128)S(1)}, u32[]{:S(2)}, u32[]{:S(2)}) async-start(f32[8,1,128]{2,1,0:T(1,128)} %broadcast_in_dim.13), calls=%async_computation | async-start | bytes 8192 | tf_op jit(solution)/shard_map/all_to_all | solution.py:251
  9.3 1.1 %copy-start = (bf16[96,4096]{1,0:T(8,128)(2,1)S(1)}, bf16[96,4096]{1,0:T(8,128)(2,1)}, u32[]{:S(2)}) copy-start(bf16[96,4096]{1,0:T(8,128)(2,1)} %k_ref.1) | copy-start | bytes 2359300
  10.5 1.1 %copy-start.1 = (bf16[96,4096]{1,0:T(8,128)(2,1)S(1)}, bf16[96,4096]{1,0:T(8,128)(2,1)}, u32[]{:S(2)}) copy-start(bf16[96,4096]{1,0:T(8,128)(2,1)} %v_ref.3) | copy-start | bytes 2359300
  16.6 17.9 %copy-start.2 = (bf16[96,4096]{1,0:T(8,128)(2,1)S(1)}, bf16[96,4096]{1,0:T(8,128)(2,1)}, u32[]{:S(2)}) copy-start(bf16[96,4096]{1,0:T(8,128)(2,1)} %v_ref.3) | copy-start | bytes 2359300
  16.6 17.9 %copy-start.3 = (bf16[96,4096]{1,0:T(8,128)(2,1)S(1)}, bf16[96,4096]{1,0:T(8,128)(2,1)}, u32[]{:S(2)}) copy-start(bf16[96,4096]{1,0:T(8,128)(2,1)} %q_ref.3) | copy-start | bytes 2359300
  16.6 12.9 %all-to-all-start.1 = ((bf16[16,128,128]{2,1,0:T(8,128)(2,1)}), bf16[16,128,128]{2,1,0:T(8,128)(2,1)S(1)}, u32[]{:S(2)}, u32[]{:S(2)}) async-start(bf16[16,128,128]{2,1,0:T(8,128)(2,1)} %bitcast.2), calls=%async_computation.1 | async-start | bytes 1048576 | tf_op jit(solution)/shard_map/all_to_all | solution.py:276
  20.3 6.5 %collective-permute-start = (f32[8,128]{1,0:T(8,128)S(1)}, f32[8,128]{1,0:T(8,128)S(1)}, u32[]{:S(2)}, u32[]{:S(2)}) collective-permute-start(f32[8,128]{1,0:T(8,128)S(1)} %pass.1.facts), channel_id=1, source_target_pairs={{0,8},{8,16},{16,24},{24,0},{1,9},{9,17},{17,25},{25,1},{2,10},{10... | collective-permute-start | bytes 12296 | tf_op jit(solution)/shard_map/ppermute | solution.py:289
  20.7 7.2 %collective-permute-start.1 = (f32[8,128]{1,0:T(8,128)S(1)}, f32[8,128]{1,0:T(8,128)S(1)}, u32[]{:S(2)}, u32[]{:S(2)}) collective-permute-start(f32[8,128]{1,0:T(8,128)S(1)} %pass.1.facts), channel_id=1, source_target_pairs={{0,16},{8,24},{16,0},{24,8},{1,17},{9,25},{17,1},{25,9},{2,18},{10... | collective-permute-start | bytes 12296 | tf_op jit(solution)/shard_map/ppermute | solution.py:289
  22.4 5.5 %collective-permute-start.2 = (f32[8,128]{1,0:T(8,128)S(1)}, f32[8,128]{1,0:T(8,128)S(1)}, u32[]{:S(2)}, u32[]{:S(2)}) collective-permute-start(f32[8,128]{1,0:T(8,128)S(1)} %pass.1.facts), channel_id=1, source_target_pairs={{0,24},{8,0},{16,8},{24,16},{1,25},{9,1},{17,9},{25,17},{2,26},{10... | collective-permute-start | bytes 12296 | tf_op jit(solution)/shard_map/ppermute | solution.py:289
  29.6 8.0 %collective-permute-start.3 = (bf16[3,128,128]{2,1,0:T(8,128)(2,1)S(1)}, bf16[3,128,128]{2,1,0:T(8,128)(2,1)S(1)}, u32[]{:S(2)}, u32[]{:S(2)}) collective-permute-start(bf16[3,128,128]{2,1,0:T(8,128)(2,1)S(1)} %get-tuple-element.25.after), channel_id=1, source_target_pairs={{0,4},{1,5},{2,6},{3,7},{4,0},{5,1},{6,2},{7,3},{8,12},{9,13},{10,... | collective-permute-start | bytes 294920 | tf_op jit(solution)/shard_map/ppermute | solution.py:314
  30.9 5.2 %collective-permute-start.4 = (bf16[1,128,128]{2,1,0:T(8,128)(2,1)S(1)}, bf16[1,128,128]{2,1,0:T(8,128)(2,1)S(1)}, u32[]{:S(2)}, u32[]{:S(2)}) collective-permute-start(bf16[1,128,128]{2,1,0:T(8,128)(2,1)S(1)} %get-tuple-element.29), channel_id=1, source_target_pairs={{0,4},{1,5},{2,6},{3,7},{8,12},{9,13},{10,14},{11,15},{16,20},{17,... | collective-permute-start | bytes 98312 | tf_op jit(solution)/shard_map/ppermute | solution.py:315
  35.8 14.0 %copy-start.4 = (f32[4096]{0:T(1024)S(1)}, f32[4096]{0:T(1024)}, u32[]{:S(2)}) copy-start(f32[4096]{0:T(1024)} %param.11) | copy-start | bytes 49156

commit v13 on v12

--- a/solution.py
+++ b/solution.py
@@ -49,9 +49,9 @@
     ids = idrow[...]
     last = ids[:, tokens - 1 : tokens]
     age = jnp.where(ids == last, (tokens - 1 - place).astype(jnp.float32), NEVER)
-    for j in range(width // LANES):
+    for j in range(0, width // LANES, 2):
         weighted = []
-        for head in (2 * j, 2 * j + 1):
+        for head in range(2 * j, 2 * j + 4):
             weight = jnp.exp(-rate_of(facts, head, here) * age)
             keys = turned[head * HD : (head + 1) * HD, :].astype(jnp.float32)
             keys = keys.reshape(HD // 8, 8, LANES) * weight[None]
@@ -59,15 +59,17 @@
         weighted = jnp.concatenate(weighted, 0)
         high = weighted.astype(jnp.bfloat16)
         low = (weighted - high.astype(jnp.float32)).astype(jnp.bfloat16)
-        v = v_ref[:, j * LANES : (j + 1) * LANES]
+        v = v_ref[:, j * LANES : (j + 2) * LANES]
         both = jnp.dot(
             jnp.concatenate([high, low], 1),
             jnp.concatenate([v, v], 0),
             preferred_element_type=jnp.float32,
         )
-        out_ref[j * HD : (j + 1) * HD, :] = jnp.where(lane < HD, both[:HD], both[HD:]).astype(
-            jnp.bfloat16
-        )
+        for one in (0, 1):
+            pair = both[one * LANES : (one + 1) * LANES, one * LANES : (one + 1) * LANES]
+            out_ref[(j + one) * HD : (j + one + 1) * HD, :] = jnp.where(
+                lane < HD, pair[:HD], pair[HD:]
+            ).astype(jnp.bfloat16)
 
 
 def inner_kernel(

time: 52 us -> 52 us (level)
  no operation moved by 1% of the time
where the time goes in v13:
time: 52 us; the launch traced here: 51.6 us
  starting transfers between devices  19.2 us (37%)
  blocking collectives  12 us (23%)
  waiting for transfers between devices  10.4 us (20%)
  Pallas kernels  5.52 us (11%)
  local copies, waits for them, and re-layouts  2.88 us (6%)
  other arithmetic  1.49 us (3%)
    all_to_all x1, blocking collectives, local(): lax.all_to_all(moved, axes, split_axis=0, concat_axis=0, axis_index_group...  12 us
    all_to_all x1, starting transfers between devices, local(): lax.all_to_all(jnp.broadcast_to(own[None, :], tile.shape), 'uly', split_a...  7.25 us
    ppermute x3, waiting for transfers between devices, local(): lax.ppermute(slice_facts, 'ctx', [(c, (c + ahead) % slices) for c in rang...  4.21 us
    all_to_all x1, starting transfers between devices, local(): lax.all_to_all(ends.reshape(group, rows, LANES), axes, split_axis=0, conc...  3.71 us
    ppermute x1, starting transfers between devices, local(): lax.ppermute(final_end, axes, [(low, high) for low, high in swap if low <...  3.63 us
    ppermute x3, starting transfers between devices, local(): lax.ppermute(slice_facts, 'ctx', [(c, (c + ahead) % slices) for c in rang...  3.37 us
    all_to_all x1, waiting for transfers between devices, local(): lax.all_to_all(jnp.broadcast_to(own[None, :], tile.shape), 'uly', split_a...  2.97 us
    unnamed x10, local copies, waits for them, and re-layouts  2.28 us
  transfers between devices with their start and end apart: 7, of which 6 were waited for; matrix products, arithmetic and copies ran while one was open for 1% of the time, Pallas kernels for 3%

profile of v13, /device:TPU:0, one launch (start us, length us, event | category | flops | bytes accessed | tf_op | source)
XLA Modules:
  0.0 51.6 jit_solution(6971741171428476575)
XLA Ops:
  0.0 0.7 %convert_add_fusion = f32[128]{0:T(128)S(1)} fusion(s32[96]{0:T(128)} %param.9, f32[8]{0:T(128)} %param.10), kind=kLoop, calls=%fused_computation | loop fusion | flops 256 | bytes 928 | tf_op jit(solution)/shard_map/add | solution.py:250
  0.7 0.6 %broadcast_in_dim.13 = f32[8,1,128]{2,1,0:T(1,128)} broadcast(f32[128]{0:T(128)S(1)} %convert_add_fusion), dimensions={2} | broadcast | bytes 4608 | tf_op jit(solution)/shard_map/broadcast_in_dim | solution.py:254
  1.3 7.3 %all-to-all-start = ((f32[8,1,128]{2,1,0:T(1,128)}), f32[8,1,128]{2,1,0:T(1,128)S(1)}, u32[]{:S(2)}, u32[]{:S(2)}) async-start(f32[8,1,128]{2,1,0:T(1,128)} %broadcast_in_dim.13), calls=%async_computation | async-start | bytes 8192 | tf_op jit(solution)/shard_map/all_to_all | solution.py:253
  8.6 0.7 %fusion.row_ref = f32[1,128]{1,0:T(1,128)S(1)} fusion(s32[96]{0:T(128)} %param.9, f32[8]{0:T(128)} %param.10), kind=kLoop, calls=%fused_computation.1 | loop fusion | flops 256 | bytes 928 | tf_op jit(solution)/shard_map/broadcast_in_dim | solution.py:269
  9.3 1.1 %copy-done = bf16[96,4096]{1,0:T(8,128)(2,1)S(1)} copy-done((bf16[96,4096]{1,0:T(8,128)(2,1)S(1)}, bf16[96,4096]{1,0:T(8,128)(2,1)}, u32[]{:S(2)}) %copy-start) | copy-done | bytes 786456
  10.5 1.1 %copy-done.1 = bf16[96,4096]{1,0:T(8,128)(2,1)S(1)} copy-done((bf16[96,4096]{1,0:T(8,128)(2,1)S(1)}, bf16[96,4096]{1,0:T(8,128)(2,1)}, u32[]{:S(2)}) %copy-start.1) | copy-done | bytes 786456
  11.6 0.4 turn.1
  12.0 3.0 %all-to-all-done = f32[8,1,128]{2,1,0:T(1,128)S(1)} async-done(((f32[8,1,128]{2,1,0:T(1,128)}), f32[8,1,128]{2,1,0:T(1,128)S(1)}, u32[]{:S(2)}, u32[]{:S(2)}) %all-to-all-start) | async-done | bytes 4128 | tf_op jit(solution)/shard_map/all_to_all | solution.py:253
  15.0 1.6 %ends.1.after = bf16[2048,128]{1,0:T(8,128)(2,1)} custom-call(f32[8,128]{1,0:T(8,128)S(1)} %bitcast.7, f32[8,128]{1,0:T(8,128)S(1)} %get-tuple-element.19.idrow, bf16[4096,128]{1,0:T(8,128)(2,1)S(1)} %get-tuple-element.20.turned, bf16[128,4096]{1,0:T(8,128)(2,1)S(1)} %get-tuple-element.21.v_ref), custom_call_target="tpu_custom_call" | custom-call | tf_op jit(solution)/shard_map/ends/pallas_call | solution.py:270
  16.6 3.7 %all-to-all-start.1 = ((bf16[16,128,128]{2,1,0:T(8,128)(2,1)}), bf16[16,128,128]{2,1,0:T(8,128)(2,1)S(1)}, u32[]{:S(2)}, u32[]{:S(2)}) async-start(bf16[16,128,128]{2,1,0:T(8,128)(2,1)} %bitcast.2), calls=%async_computation.1 | async-start | bytes 1048576 | tf_op jit(solution)/shard_map/all_to_all | solution.py:278
  20.3 0.4 collective-permute-start
  20.7 1.7 %collective-permute-start.1 = (f32[8,128]{1,0:T(8,128)S(1)}, f32[8,128]{1,0:T(8,128)S(1)}, u32[]{:S(2)}, u32[]{:S(2)}) collective-permute-start(f32[8,128]{1,0:T(8,128)S(1)} %pass.1.facts), channel_id=1, source_target_pairs={{0,16},{8,24},{16,0},{24,8},{1,17},{9,25},{17,1},{25,9},{2,18},{10... | collective-permute-start | bytes 12296 | tf_op jit(solution)/shard_map/ppermute | solution.py:291
  22.4 1.3 %collective-permute-start.2 = (f32[8,128]{1,0:T(8,128)S(1)}, f32[8,128]{1,0:T(8,128)S(1)}, u32[]{:S(2)}, u32[]{:S(2)}) collective-permute-start(f32[8,128]{1,0:T(8,128)S(1)} %pass.1.facts), channel_id=1, source_target_pairs={{0,24},{8,0},{16,8},{24,16},{1,25},{9,1},{17,9},{25,17},{2,26},{10... | collective-permute-start | bytes 12296 | tf_op jit(solution)/shard_map/ppermute | solution.py:291
  23.7 3.2 %collective-permute-done.refs_0_ = f32[8,128]{1,0:T(8,128)S(1)} collective-permute-done((f32[8,128]{1,0:T(8,128)S(1)}, f32[8,128]{1,0:T(8,128)S(1)}, u32[]{:S(2)}, u32[]{:S(2)}) %collective-permute-start) | collective-permute-done | bytes 4128 | tf_op jit(solution)/shard_map/ppermute | solution.py:291
  26.8 1.0 %collective-permute-done.1.refs_1_ = f32[8,128]{1,0:T(8,128)S(1)} collective-permute-done((f32[8,128]{1,0:T(8,128)S(1)}, f32[8,128]{1,0:T(8,128)S(1)}, u32[]{:S(2)}, u32[]{:S(2)}) %collective-permute-start.1) | collective-permute-done | bytes 4128 | tf_op jit(solution)/shard_map/ppermute | solution.py:291
  28.0 1.5 %all-to-all-done.1.in_ref = bf16[16,128,128]{2,1,0:T(8,128)(2,1)S(1)} async-done(((bf16[16,128,128]{2,1,0:T(8,128)(2,1)}), bf16[16,128,128]{2,1,0:T(8,128)(2,1)S(1)}, u32[]{:S(2)}, u32[]{:S(2)}) %all-to-all-start.1) | async-done | bytes 524320 | tf_op jit(solution)/shard_map/all_to_all | solution.py:278
  29.6 1.3 %collective-permute-start.3 = (bf16[3,128,128]{2,1,0:T(8,128)(2,1)S(1)}, bf16[3,128,128]{2,1,0:T(8,128)(2,1)S(1)}, u32[]{:S(2)}, u32[]{:S(2)}) collective-permute-start(bf16[3,128,128]{2,1,0:T(8,128)(2,1)S(1)} %get-tuple-element.25.after), channel_id=1, source_target_pairs={{0,4},{1,5},{2,6},{3,7},{4,0},{5,1},{6,2},{7,3},{8,12},{9,13},{10,... | collective-permute-start | bytes 294920 | tf_op jit(solution)/shard_map/ppermute | solution.py:316
  30.9 3.6 %collective-permute-start.4 = (bf16[1,128,128]{2,1,0:T(8,128)(2,1)S(1)}, bf16[1,128,128]{2,1,0:T(8,128)(2,1)S(1)}, u32[]{:S(2)}, u32[]{:S(2)}) collective-permute-start(bf16[1,128,128]{2,1,0:T(8,128)(2,1)S(1)} %get-tuple-element.29), channel_id=1, source_target_pairs={{0,4},{1,5},{2,6},{3,7},{8,12},{9,13},{10,14},{11,15},{16,20},{17,... | collective-permute-start | bytes 98312 | tf_op jit(solution)/shard_map/ppermute | solution.py:317
  34.5 1.3 %inner.1 = (f32[96,4096]{1,0:T(8,128)S(1)}, f32[1,4096]{1,0:T(1,128)S(1)}) custom-call(f32[8,128]{1,0:T(8,128)S(1)} %bitcast.9, f32[96,128]{1,0:T(8,128)S(1)} %get-tuple-element.18.idcol, f32[8,128]{1,0:T(8,128)S(1)} %get-tuple-element.19.idrow, bf16[96,4096]{1,0:T(8,128)(2,1)S(1)} %copy-done.3, bf16[4096,128]{1,0:T(8,128)(2,1)S(1)} %get-tuple-element.20.turned, ...), custom_call_target="tpu_custom_call" | custom-call | flops 8000000000 | bytes 4000000 | tf_op jit(solution)/shard_map/inner/pallas_call | solution.py:318
  35.8 0.3 collective-permute-done.4.final
  36.1 1.5 %collective-permute-done.3.early = bf16[3,128,128]{2,1,0:T(8,128)(2,1)S(1)} collective-permute-done((bf16[3,128,128]{2,1,0:T(8,128)(2,1)S(1)}, bf16[3,128,128]{2,1,0:T(8,128)(2,1)S(1)}, u32[]{:S(2)}, u32[]{:S(2)}) %collective-permute-start.3) | collective-permute-done | bytes 98336 | tf_op jit(solution)/shard_map/ppermute | solution.py:316
  37.6 0.2 scan.1
  37.8 12.0 %all_to_all.18 = bf16[16,128,128]{2,1,0:T(8,128)(2,1)S(1)} all-to-all(bf16[16,128,128]{2,1,0:T(8,128)(2,1)S(1)} %scan.1), channel_id=1, replica_groups={{0,1,2,3,8,9,10,11,16,17,18,19,24,25,26,27},{4,5,6,7,12,13,14,15,20,21,..., dimensions={0} | all-to-all | bytes 1048576 | tf_op jit(solution)/shard_map/all_to_all | solution.py:337
  49.8 1.8 %norm.1 = bf16[96,4096]{1,0:T(8,128)(2,1)} custom-call(f32[96,128]{1,0:T(8,128)S(1)} %get-tuple-element.18.idcol, f32[1,128]{1,0:T(1,128)S(1)} %get-tuple-element.22.before, f32[1,4096]{1,0:T(1,128)S(1)} %get-tuple-element.26.after.rates, bf16[96,4096]{1,0:T(8,128)(2,1)S(1)} %copy-done.3, bf16[2048,128]{1,0:T(8,128)(2,1)S(1)} %bitcast.6, ...), custom_call_target="tpu_custom_call" | custom-call | tf_op jit(solution)/shard_map/norm/pallas_call | solution.py:340
  (12 shorter events, 0.3 us)
Async XLA Ops:
  1.3 13.6 %all-to-all-start = ((f32[8,1,128]{2,1,0:T(1,128)}), f32[8,1,128]{2,1,0:T(1,128)S(1)}, u32[]{:S(2)}, u32[]{:S(2)}) async-start(f32[8,1,128]{2,1,0:T(1,128)} %broadcast_in_dim.13), calls=%async_computation | async-start | bytes 8192 | tf_op jit(solution)/shard_map/all_to_all | solution.py:253
  9.3 1.1 %copy-start = (bf16[96,4096]{1,0:T(8,128)(2,1)S(1)}, bf16[96,4096]{1,0:T(8,128)(2,1)}, u32[]{:S(2)}) copy-start(bf16[96,4096]{1,0:T(8,128)(2,1)} %k_ref.1) | copy-start | bytes 2359300
  10.5 1.1 %copy-start.1 = (bf16[96,4096]{1,0:T(8,128)(2,1)S(1)}, bf16[96,4096]{1,0:T(8,128)(2,1)}, u32[]{:S(2)}) copy-start(bf16[96,4096]{1,0:T(8,128)(2,1)} %v_ref.3) | copy-start | bytes 2359300
  16.6 17.9 %copy-start.2 = (bf16[96,4096]{1,0:T(8,128)(2,1)S(1)}, bf16[96,4096]{1,0:T(8,128)(2,1)}, u32[]{:S(2)}) copy-start(bf16[96,4096]{1,0:T(8,128)(2,1)} %v_ref.3) | copy-start | bytes 2359300
  16.6 17.9 %copy-start.3 = (bf16[96,4096]{1,0:T(8,128)(2,1)S(1)}, bf16[96,4096]{1,0:T(8,128)(2,1)}, u32[]{:S(2)}) copy-start(bf16[96,4096]{1,0:T(8,128)(2,1)} %q_ref.3) | copy-start | bytes 2359300
  16.6 12.9 %all-to-all-start.1 = ((bf16[16,128,128]{2,1,0:T(8,128)(2,1)}), bf16[16,128,128]{2,1,0:T(8,128)(2,1)S(1)}, u32[]{:S(2)}, u32[]{:S(2)}) async-start(bf16[16,128,128]{2,1,0:T(8,128)(2,1)} %bitcast.2), calls=%async_computation.1 | async-start | bytes 1048576 | tf_op jit(solution)/shard_map/all_to_all | solution.py:278
  20.3 6.5 %collective-permute-start = (f32[8,128]{1,0:T(8,128)S(1)}, f32[8,128]{1,0:T(8,128)S(1)}, u32[]{:S(2)}, u32[]{:S(2)}) collective-permute-start(f32[8,128]{1,0:T(8,128)S(1)} %pass.1.facts), channel_id=1, source_target_pairs={{0,8},{8,16},{16,24},{24,0},{1,9},{9,17},{17,25},{25,1},{2,10},{10... | collective-permute-start | bytes 12296 | tf_op jit(solution)/shard_map/ppermute | solution.py:291
  20.7 7.2 %collective-permute-start.1 = (f32[8,128]{1,0:T(8,128)S(1)}, f32[8,128]{1,0:T(8,128)S(1)}, u32[]{:S(2)}, u32[]{:S(2)}) collective-permute-start(f32[8,128]{1,0:T(8,128)S(1)} %pass.1.facts), channel_id=1, source_target_pairs={{0,16},{8,24},{16,0},{24,8},{1,17},{9,25},{17,1},{25,9},{2,18},{10... | collective-permute-start | bytes 12296 | tf_op jit(solution)/shard_map/ppermute | solution.py:291
  22.4 5.5 %collective-permute-start.2 = (f32[8,128]{1,0:T(8,128)S(1)}, f32[8,128]{1,0:T(8,128)S(1)}, u32[]{:S(2)}, u32[]{:S(2)}) collective-permute-start(f32[8,128]{1,0:T(8,128)S(1)} %pass.1.facts), channel_id=1, source_target_pairs={{0,24},{8,0},{16,8},{24,16},{1,25},{9,1},{17,9},{25,17},{2,26},{10... | collective-permute-start | bytes 12296 | tf_op jit(solution)/shard_map/ppermute | solution.py:291
  29.6 8.0 %collective-permute-start.3 = (bf16[3,128,128]{2,1,0:T(8,128)(2,1)S(1)}, bf16[3,128,128]{2,1,0:T(8,128)(2,1)S(1)}, u32[]{:S(2)}, u32[]{:S(2)}) collective-permute-start(bf16[3,128,128]{2,1,0:T(8,128)(2,1)S(1)} %get-tuple-element.25.after), channel_id=1, source_target_pairs={{0,4},{1,5},{2,6},{3,7},{4,0},{5,1},{6,2},{7,3},{8,12},{9,13},{10,... | collective-permute-start | bytes 294920 | tf_op jit(solution)/shard_map/ppermute | solution.py:316
  30.9 5.2 %collective-permute-start.4 = (bf16[1,128,128]{2,1,0:T(8,128)(2,1)S(1)}, bf16[1,128,128]{2,1,0:T(8,128)(2,1)S(1)}, u32[]{:S(2)}, u32[]{:S(2)}) collective-permute-start(bf16[1,128,128]{2,1,0:T(8,128)(2,1)S(1)} %get-tuple-element.29), channel_id=1, source_target_pairs={{0,4},{1,5},{2,6},{3,7},{8,12},{9,13},{10,14},{11,15},{16,20},{17,... | collective-permute-start | bytes 98312 | tf_op jit(solution)/shard_map/ppermute | solution.py:317
  35.8 14.0 %copy-start.4 = (f32[4096]{0:T(1024)S(1)}, f32[4096]{0:T(1024)}, u32[]{:S(2)}) copy-start(f32[4096]{0:T(1024)} %param.11) | copy-start | bytes 49156

commit v14 on v13

--- a/solution.py
+++ b/solution.py
@@ -42,13 +42,16 @@
         turned[columns, :] = jnp.transpose(block).astype(turned.dtype)
 
 
-def ends_kernel(here, tokens, facts, idrow, turned, v_ref, out_ref):
+def ends_kernel(here, tokens, facts, idrow, turned, v_ref, out_ref, made, sems):
     width = v_ref.shape[1]
     lane = lax.broadcasted_iota(jnp.int32, (HD, LANES), 1)
     place = lax.broadcasted_iota(jnp.int32, idrow.shape, 1)
     ids = idrow[...]
     last = ids[:, tokens - 1 : tokens]
     age = jnp.where(ids == last, (tokens - 1 - place).astype(jnp.float32), NEVER)
+    parts = sems.shape[0]
+    share = made.shape[0] // parts
+    copies = []
     for j in range(0, width // LANES, 2):
         weighted = []
         for head in range(2 * j, 2 * j + 4):
@@ -67,9 +70,16 @@
         )
         for one in (0, 1):
             pair = both[one * LANES : (one + 1) * LANES, one * LANES : (one + 1) * LANES]
-            out_ref[(j + one) * HD : (j + one + 1) * HD, :] = jnp.where(
+            made[(j + one) * HD : (j + one + 1) * HD, :] = jnp.where(
                 lane < HD, pair[:HD], pair[HD:]
             ).astype(jnp.bfloat16)
+        if (j + 2) * HD % share == 0:
+            part = (j + 2) * HD // share - 1
+            rows = slice(part * share, (part + 1) * share)
+            copies.append(pltpu.make_async_copy(made.at[rows], out_ref.at[rows], sems.at[part]))
+            copies[-1].start()
+    for copy in copies:
+        copy.wait()
 
 
 def inner_kernel(
@@ -270,8 +280,12 @@
     ends = pl.pallas_call(
         functools.partial(ends_kernel, here, tokens),
         in_specs=[vmem] * 4,
-        out_specs=vmem,
+        out_specs=pl.BlockSpec(memory_space=pl.ANY),
         out_shape=shape((all_pairs * HD, LANES), jnp.bfloat16),
+        scratch_shapes=[
+            pltpu.VMEM((all_pairs * HD, LANES), jnp.bfloat16),
+            pltpu.SemaphoreType.DMA((8,)),
+        ],
         compiler_params=params,
         name="ends",
     )(facts, idrow, turned, filled)
@@ -345,7 +359,7 @@
         scratch_shapes=[
             pltpu.VMEM((tokens, width), jnp.float32),
             pltpu.VMEM((tokens, width), jnp.bfloat16),
-            pltpu.SemaphoreType.DMA((4,)),
+            pltpu.SemaphoreType.DMA((16,)),
         ],
         compiler_params=params,
         name="norm",

time: 52 us -> 52 us (level)
  no operation moved by 1% of the time
where the time goes in v14:
time: 52 us; the launch traced here: 51.6 us
  starting transfers between devices  19.2 us (37%)
  blocking collectives  12 us (23%)
  waiting for transfers between devices  10.4 us (20%)
  Pallas kernels  5.51 us (11%)
  local copies, waits for them, and re-layouts  2.88 us (6%)
  other arithmetic  1.49 us (3%)
    all_to_all x1, blocking collectives, local(): lax.all_to_all(moved, axes, split_axis=0, concat_axis=0, axis_index_group...  12 us
    all_to_all x1, starting transfers between devices, local(): lax.all_to_all(jnp.broadcast_to(own[None, :], tile.shape), 'uly', split_a...  7.25 us
    ppermute x3, waiting for transfers between devices, local(): lax.ppermute(slice_facts, 'ctx', [(c, (c + ahead) % slices) for c in rang...  4.21 us
    all_to_all x1, starting transfers between devices, local(): lax.all_to_all(ends.reshape(group, rows, LANES), axes, split_axis=0, conc...  3.72 us
    ppermute x1, starting transfers between devices, local(): lax.ppermute(final_end, axes, [(low, high) for low, high in swap if low <...  3.63 us
    ppermute x3, starting transfers between devices, local(): lax.ppermute(slice_facts, 'ctx', [(c, (c + ahead) % slices) for c in rang...  3.37 us
    all_to_all x1, waiting for transfers between devices, local(): lax.all_to_all(jnp.broadcast_to(own[None, :], tile.shape), 'uly', split_a...  2.97 us
    unnamed x10, local copies, waits for them, and re-layouts  2.28 us
  transfers between devices with their start and end apart: 7, of which 6 were waited for; matrix products, arithmetic and copies ran while one was open for 1% of the time, Pallas kernels for 3%

profile of v14, /device:TPU:0, one launch (start us, length us, event | category | flops | bytes accessed | tf_op | source)
XLA Modules:
  0.0 51.6 jit_solution(16896538635320056306)
XLA Ops:
  0.0 0.7 %convert_add_fusion = f32[128]{0:T(128)S(1)} fusion(s32[96]{0:T(128)} %param.9, f32[8]{0:T(128)} %param.10), kind=kLoop, calls=%fused_computation | loop fusion | flops 256 | bytes 928 | tf_op jit(solution)/shard_map/add | solution.py:260
  0.7 0.6 %broadcast_in_dim.13 = f32[8,1,128]{2,1,0:T(1,128)} broadcast(f32[128]{0:T(128)S(1)} %convert_add_fusion), dimensions={2} | broadcast | bytes 4608 | tf_op jit(solution)/shard_map/broadcast_in_dim | solution.py:264
  1.3 7.3 %all-to-all-start = ((f32[8,1,128]{2,1,0:T(1,128)}), f32[8,1,128]{2,1,0:T(1,128)S(1)}, u32[]{:S(2)}, u32[]{:S(2)}) async-start(f32[8,1,128]{2,1,0:T(1,128)} %broadcast_in_dim.13), calls=%async_computation | async-start | bytes 8192 | tf_op jit(solution)/shard_map/all_to_all | solution.py:263
  8.6 0.7 %fusion.row_ref = f32[1,128]{1,0:T(1,128)S(1)} fusion(s32[96]{0:T(128)} %param.9, f32[8]{0:T(128)} %param.10), kind=kLoop, calls=%fused_computation.1 | loop fusion | flops 256 | bytes 928 | tf_op jit(solution)/shard_map/broadcast_in_dim | solution.py:279
  9.3 1.1 %copy-done = bf16[96,4096]{1,0:T(8,128)(2,1)S(1)} copy-done((bf16[96,4096]{1,0:T(8,128)(2,1)S(1)}, bf16[96,4096]{1,0:T(8,128)(2,1)}, u32[]{:S(2)}) %copy-start) | copy-done | bytes 786456
  10.5 1.1 %copy-done.1 = bf16[96,4096]{1,0:T(8,128)(2,1)S(1)} copy-done((bf16[96,4096]{1,0:T(8,128)(2,1)S(1)}, bf16[96,4096]{1,0:T(8,128)(2,1)}, u32[]{:S(2)}) %copy-start.1) | copy-done | bytes 786456
  11.6 0.4 turn.1
  12.0 3.0 %all-to-all-done = f32[8,1,128]{2,1,0:T(1,128)S(1)} async-done(((f32[8,1,128]{2,1,0:T(1,128)}), f32[8,1,128]{2,1,0:T(1,128)S(1)}, u32[]{:S(2)}, u32[]{:S(2)}) %all-to-all-start) | async-done | bytes 4128 | tf_op jit(solution)/shard_map/all_to_all | solution.py:263
  15.0 1.5 %ends.1.after = bf16[2048,128]{1,0:T(8,128)(2,1)} custom-call(f32[8,128]{1,0:T(8,128)S(1)} %bitcast.7, f32[8,128]{1,0:T(8,128)S(1)} %get-tuple-element.19.idrow, bf16[4096,128]{1,0:T(8,128)(2,1)S(1)} %get-tuple-element.20.turned, bf16[128,4096]{1,0:T(8,128)(2,1)S(1)} %get-tuple-element.21.v_ref), custom_call_target="tpu_custom_call" | custom-call | tf_op jit(solution)/shard_map/ends/pallas_call | solution.py:280
  16.5 3.7 %all-to-all-start.1 = ((bf16[16,128,128]{2,1,0:T(8,128)(2,1)}), bf16[16,128,128]{2,1,0:T(8,128)(2,1)S(1)}, u32[]{:S(2)}, u32[]{:S(2)}) async-start(bf16[16,128,128]{2,1,0:T(8,128)(2,1)} %bitcast.2), calls=%async_computation.1 | async-start | bytes 1048576 | tf_op jit(solution)/shard_map/all_to_all | solution.py:292
  20.3 0.4 collective-permute-start
  20.6 1.7 %collective-permute-start.1 = (f32[8,128]{1,0:T(8,128)S(1)}, f32[8,128]{1,0:T(8,128)S(1)}, u32[]{:S(2)}, u32[]{:S(2)}) collective-permute-start(f32[8,128]{1,0:T(8,128)S(1)} %pass.1.facts), channel_id=1, source_target_pairs={{0,16},{8,24},{16,0},{24,8},{1,17},{9,25},{17,1},{25,9},{2,18},{10... | collective-permute-start | bytes 12296 | tf_op jit(solution)/shard_map/ppermute | solution.py:305
  22.3 1.3 %collective-permute-start.2 = (f32[8,128]{1,0:T(8,128)S(1)}, f32[8,128]{1,0:T(8,128)S(1)}, u32[]{:S(2)}, u32[]{:S(2)}) collective-permute-start(f32[8,128]{1,0:T(8,128)S(1)} %pass.1.facts), channel_id=1, source_target_pairs={{0,24},{8,0},{16,8},{24,16},{1,25},{9,1},{17,9},{25,17},{2,26},{10... | collective-permute-start | bytes 12296 | tf_op jit(solution)/shard_map/ppermute | solution.py:305
  23.6 3.2 %collective-permute-done.refs_0_ = f32[8,128]{1,0:T(8,128)S(1)} collective-permute-done((f32[8,128]{1,0:T(8,128)S(1)}, f32[8,128]{1,0:T(8,128)S(1)}, u32[]{:S(2)}, u32[]{:S(2)}) %collective-permute-start) | collective-permute-done | bytes 4128 | tf_op jit(solution)/shard_map/ppermute | solution.py:305
  26.8 1.0 %collective-permute-done.1.refs_1_ = f32[8,128]{1,0:T(8,128)S(1)} collective-permute-done((f32[8,128]{1,0:T(8,128)S(1)}, f32[8,128]{1,0:T(8,128)S(1)}, u32[]{:S(2)}, u32[]{:S(2)}) %collective-permute-start.1) | collective-permute-done | bytes 4128 | tf_op jit(solution)/shard_map/ppermute | solution.py:305
  28.0 1.5 %all-to-all-done.1.in_ref = bf16[16,128,128]{2,1,0:T(8,128)(2,1)S(1)} async-done(((bf16[16,128,128]{2,1,0:T(8,128)(2,1)}), bf16[16,128,128]{2,1,0:T(8,128)(2,1)S(1)}, u32[]{:S(2)}, u32[]{:S(2)}) %all-to-all-start.1) | async-done | bytes 524320 | tf_op jit(solution)/shard_map/all_to_all | solution.py:292
  29.6 1.3 %collective-permute-start.3 = (bf16[3,128,128]{2,1,0:T(8,128)(2,1)S(1)}, bf16[3,128,128]{2,1,0:T(8,128)(2,1)S(1)}, u32[]{:S(2)}, u32[]{:S(2)}) collective-permute-start(bf16[3,128,128]{2,1,0:T(8,128)(2,1)S(1)} %get-tuple-element.25.after), channel_id=1, source_target_pairs={{0,4},{1,5},{2,6},{3,7},{4,0},{5,1},{6,2},{7,3},{8,12},{9,13},{10,... | collective-permute-start | bytes 294920 | tf_op jit(solution)/shard_map/ppermute | solution.py:330
  30.8 3.6 %collective-permute-start.4 = (bf16[1,128,128]{2,1,0:T(8,128)(2,1)S(1)}, bf16[1,128,128]{2,1,0:T(8,128)(2,1)S(1)}, u32[]{:S(2)}, u32[]{:S(2)}) collective-permute-start(bf16[1,128,128]{2,1,0:T(8,128)(2,1)S(1)} %get-tuple-element.29), channel_id=1, source_target_pairs={{0,4},{1,5},{2,6},{3,7},{8,12},{9,13},{10,14},{11,15},{16,20},{17,... | collective-permute-start | bytes 98312 | tf_op jit(solution)/shard_map/ppermute | solution.py:331
  34.5 1.3 %inner.1 = (f32[96,4096]{1,0:T(8,128)S(1)}, f32[1,4096]{1,0:T(1,128)S(1)}) custom-call(f32[8,128]{1,0:T(8,128)S(1)} %bitcast.9, f32[96,128]{1,0:T(8,128)S(1)} %get-tuple-element.18.idcol, f32[8,128]{1,0:T(8,128)S(1)} %get-tuple-element.19.idrow, bf16[96,4096]{1,0:T(8,128)(2,1)S(1)} %copy-done.3, bf16[4096,128]{1,0:T(8,128)(2,1)S(1)} %get-tuple-element.20.turned, ...), custom_call_target="tpu_custom_call" | custom-call | flops 8000000000 | bytes 4000000 | tf_op jit(solution)/shard_map/inner/pallas_call | solution.py:332
  35.8 0.3 collective-permute-done.4.final
  36.0 1.5 %collective-permute-done.3.early = bf16[3,128,128]{2,1,0:T(8,128)(2,1)S(1)} collective-permute-done((bf16[3,128,128]{2,1,0:T(8,128)(2,1)S(1)}, bf16[3,128,128]{2,1,0:T(8,128)(2,1)S(1)}, u32[]{:S(2)}, u32[]{:S(2)}) %collective-permute-start.3) | collective-permute-done | bytes 98336 | tf_op jit(solution)/shard_map/ppermute | solution.py:330
  37.5 0.2 scan.1
  37.8 12.0 %all_to_all.18 = bf16[16,128,128]{2,1,0:T(8,128)(2,1)S(1)} all-to-all(bf16[16,128,128]{2,1,0:T(8,128)(2,1)S(1)} %scan.1), channel_id=1, replica_groups={{0,1,2,3,8,9,10,11,16,17,18,19,24,25,26,27},{4,5,6,7,12,13,14,15,20,21,..., dimensions={0} | all-to-all | bytes 1048576 | tf_op jit(solution)/shard_map/all_to_all | solution.py:351
  49.7 1.9 %norm.1 = bf16[96,4096]{1,0:T(8,128)(2,1)} custom-call(f32[96,128]{1,0:T(8,128)S(1)} %get-tuple-element.18.idcol, f32[1,128]{1,0:T(1,128)S(1)} %get-tuple-element.22.before, f32[1,4096]{1,0:T(1,128)S(1)} %get-tuple-element.26.after.rates, bf16[96,4096]{1,0:T(8,128)(2,1)S(1)} %copy-done.3, bf16[2048,128]{1,0:T(8,128)(2,1)S(1)} %bitcast.6, ...), custom_call_target="tpu_custom_call" | custom-call | tf_op jit(solution)/shard_map/norm/pallas_call | solution.py:354
  (12 shorter events, 0.3 us)
Async XLA Ops:
  1.3 13.6 %all-to-all-start = ((f32[8,1,128]{2,1,0:T(1,128)}), f32[8,1,128]{2,1,0:T(1,128)S(1)}, u32[]{:S(2)}, u32[]{:S(2)}) async-start(f32[8,1,128]{2,1,0:T(1,128)} %broadcast_in_dim.13), calls=%async_computation | async-start | bytes 8192 | tf_op jit(solution)/shard_map/all_to_all | solution.py:263
  9.3 1.1 %copy-start = (bf16[96,4096]{1,0:T(8,128)(2,1)S(1)}, bf16[96,4096]{1,0:T(8,128)(2,1)}, u32[]{:S(2)}) copy-start(bf16[96,4096]{1,0:T(8,128)(2,1)} %k_ref.1) | copy-start | bytes 2359300
  10.5 1.1 %copy-start.1 = (bf16[96,4096]{1,0:T(8,128)(2,1)S(1)}, bf16[96,4096]{1,0:T(8,128)(2,1)}, u32[]{:S(2)}) copy-start(bf16[96,4096]{1,0:T(8,128)(2,1)} %v_ref.3) | copy-start | bytes 2359300
  16.5 18.0 %copy-start.2 = (bf16[96,4096]{1,0:T(8,128)(2,1)S(1)}, bf16[96,4096]{1,0:T(8,128)(2,1)}, u32[]{:S(2)}) copy-start(bf16[96,4096]{1,0:T(8,128)(2,1)} %v_ref.3) | copy-start | bytes 2359300
  16.5 18.0 %copy-start.3 = (bf16[96,4096]{1,0:T(8,128)(2,1)S(1)}, bf16[96,4096]{1,0:T(8,128)(2,1)}, u32[]{:S(2)}) copy-start(bf16[96,4096]{1,0:T(8,128)(2,1)} %q_ref.3) | copy-start | bytes 2359300
  16.5 12.9 %all-to-all-start.1 = ((bf16[16,128,128]{2,1,0:T(8,128)(2,1)}), bf16[16,128,128]{2,1,0:T(8,128)(2,1)S(1)}, u32[]{:S(2)}, u32[]{:S(2)}) async-start(bf16[16,128,128]{2,1,0:T(8,128)(2,1)} %bitcast.2), calls=%async_computation.1 | async-start | bytes 1048576 | tf_op jit(solution)/shard_map/all_to_all | solution.py:292
  20.3 6.5 %collective-permute-start = (f32[8,128]{1,0:T(8,128)S(1)}, f32[8,128]{1,0:T(8,128)S(1)}, u32[]{:S(2)}, u32[]{:S(2)}) collective-permute-start(f32[8,128]{1,0:T(8,128)S(1)} %pass.1.facts), channel_id=1, source_target_pairs={{0,8},{8,16},{16,24},{24,0},{1,9},{9,17},{17,25},{25,1},{2,10},{10... | collective-permute-start | bytes 12296 | tf_op jit(solution)/shard_map/ppermute | solution.py:305
  20.6 7.2 %collective-permute-start.1 = (f32[8,128]{1,0:T(8,128)S(1)}, f32[8,128]{1,0:T(8,128)S(1)}, u32[]{:S(2)}, u32[]{:S(2)}) collective-permute-start(f32[8,128]{1,0:T(8,128)S(1)} %pass.1.facts), channel_id=1, source_target_pairs={{0,16},{8,24},{16,0},{24,8},{1,17},{9,25},{17,1},{25,9},{2,18},{10... | collective-permute-start | bytes 12296 | tf_op jit(solution)/shard_map/ppermute | solution.py:305
  22.3 5.5 %collective-permute-start.2 = (f32[8,128]{1,0:T(8,128)S(1)}, f32[8,128]{1,0:T(8,128)S(1)}, u32[]{:S(2)}, u32[]{:S(2)}) collective-permute-start(f32[8,128]{1,0:T(8,128)S(1)} %pass.1.facts), channel_id=1, source_target_pairs={{0,24},{8,0},{16,8},{24,16},{1,25},{9,1},{17,9},{25,17},{2,26},{10... | collective-permute-start | bytes 12296 | tf_op jit(solution)/shard_map/ppermute | solution.py:305
  29.6 8.0 %collective-permute-start.3 = (bf16[3,128,128]{2,1,0:T(8,128)(2,1)S(1)}, bf16[3,128,128]{2,1,0:T(8,128)(2,1)S(1)}, u32[]{:S(2)}, u32[]{:S(2)}) collective-permute-start(bf16[3,128,128]{2,1,0:T(8,128)(2,1)S(1)} %get-tuple-element.25.after), channel_id=1, source_target_pairs={{0,4},{1,5},{2,6},{3,7},{4,0},{5,1},{6,2},{7,3},{8,12},{9,13},{10,... | collective-permute-start | bytes 294920 | tf_op jit(solution)/shard_map/ppermute | solution.py:330
  30.8 5.2 %collective-permute-start.4 = (bf16[1,128,128]{2,1,0:T(8,128)(2,1)S(1)}, bf16[1,128,128]{2,1,0:T(8,128)(2,1)S(1)}, u32[]{:S(2)}, u32[]{:S(2)}) collective-permute-start(bf16[1,128,128]{2,1,0:T(8,128)(2,1)S(1)} %get-tuple-element.29), channel_id=1, source_target_pairs={{0,4},{1,5},{2,6},{3,7},{8,12},{9,13},{10,14},{11,15},{16,20},{17,... | collective-permute-start | bytes 98312 | tf_op jit(solution)/shard_map/ppermute | solution.py:331
  35.7 14.0 %copy-start.4 = (f32[4096]{0:T(1024)S(1)}, f32[4096]{0:T(1024)}, u32[]{:S(2)}) copy-start(f32[4096]{0:T(1024)} %param.11) | copy-start | bytes 49156

commit v15 on v14

--- a/solution.py
+++ b/solution.py
@@ -77,7 +77,7 @@
             part = (j + 2) * HD // share - 1
             rows = slice(part * share, (part + 1) * share)
             copies.append(pltpu.make_async_copy(made.at[rows], out_ref.at[rows], sems.at[part]))
-            copies[-1].start()
+            copies[-1].start(priority=part % 2)
     for copy in copies:
         copy.wait()
 
@@ -227,7 +227,7 @@
         copies.append(
             pltpu.make_async_copy(done.at[:, columns], out_ref.at[:, columns], sems.at[part])
         )
-        copies[-1].start()
+        copies[-1].start(priority=part % 2)
     for copy in copies:
         copy.wait()
 

time: 52 us -> 52 us (level)
  no operation moved by 1% of the time
where the time goes in v15:
time: 52 us; the launch traced here: 51.6 us
  starting transfers between devices  19.2 us (37%)
  blocking collectives  12 us (23%)
  waiting for transfers between devices  10.4 us (20%)
  Pallas kernels  5.51 us (11%)
  local copies, waits for them, and re-layouts  2.88 us (6%)
  other arithmetic  1.49 us (3%)
    all_to_all x1, blocking collectives, local(): lax.all_to_all(moved, axes, split_axis=0, concat_axis=0, axis_index_group...  12 us
    all_to_all x1, starting transfers between devices, local(): lax.all_to_all(jnp.broadcast_to(own[None, :], tile.shape), 'uly', split_a...  7.25 us
    ppermute x3, waiting for transfers between devices, local(): lax.ppermute(slice_facts, 'ctx', [(c, (c + ahead) % slices) for c in rang...  4.21 us
    all_to_all x1, starting transfers between devices, local(): lax.all_to_all(ends.reshape(group, rows, LANES), axes, split_axis=0, conc...  3.72 us
    ppermute x1, starting transfers between devices, local(): lax.ppermute(final_end, axes, [(low, high) for low, high in swap if low <...  3.63 us
    ppermute x3, starting transfers between devices, local(): lax.ppermute(slice_facts, 'ctx', [(c, (c + ahead) % slices) for c in rang...  3.37 us
    all_to_all x1, waiting for transfers between devices, local(): lax.all_to_all(jnp.broadcast_to(own[None, :], tile.shape), 'uly', split_a...  2.97 us
    unnamed x10, local copies, waits for them, and re-layouts  2.28 us
  transfers between devices with their start and end apart: 7, of which 6 were waited for; matrix products, arithmetic and copies ran while one was open for 1% of the time, Pallas kernels for 3%

profile of v15, /device:TPU:0, one launch (start us, length us, event | category | flops | bytes accessed | tf_op | source)
XLA Modules:
  0.0 51.6 jit_solution(772110508036438683)
XLA Ops:
  0.0 0.7 %convert_add_fusion = f32[128]{0:T(128)S(1)} fusion(s32[96]{0:T(128)} %param.9, f32[8]{0:T(128)} %param.10), kind=kLoop, calls=%fused_computation | loop fusion | flops 256 | bytes 928 | tf_op jit(solution)/shard_map/add | solution.py:260
  0.7 0.6 %broadcast_in_dim.13 = f32[8,1,128]{2,1,0:T(1,128)} broadcast(f32[128]{0:T(128)S(1)} %convert_add_fusion), dimensions={2} | broadcast | bytes 4608 | tf_op jit(solution)/shard_map/broadcast_in_dim | solution.py:264
  1.3 7.3 %all-to-all-start = ((f32[8,1,128]{2,1,0:T(1,128)}), f32[8,1,128]{2,1,0:T(1,128)S(1)}, u32[]{:S(2)}, u32[]{:S(2)}) async-start(f32[8,1,128]{2,1,0:T(1,128)} %broadcast_in_dim.13), calls=%async_computation | async-start | bytes 8192 | tf_op jit(solution)/shard_map/all_to_all | solution.py:263
  8.6 0.7 %fusion.row_ref = f32[1,128]{1,0:T(1,128)S(1)} fusion(s32[96]{0:T(128)} %param.9, f32[8]{0:T(128)} %param.10), kind=kLoop, calls=%fused_computation.1 | loop fusion | flops 256 | bytes 928 | tf_op jit(solution)/shard_map/broadcast_in_dim | solution.py:279
  9.3 1.1 %copy-done = bf16[96,4096]{1,0:T(8,128)(2,1)S(1)} copy-done((bf16[96,4096]{1,0:T(8,128)(2,1)S(1)}, bf16[96,4096]{1,0:T(8,128)(2,1)}, u32[]{:S(2)}) %copy-start) | copy-done | bytes 786456
  10.5 1.1 %copy-done.1 = bf16[96,4096]{1,0:T(8,128)(2,1)S(1)} copy-done((bf16[96,4096]{1,0:T(8,128)(2,1)S(1)}, bf16[96,4096]{1,0:T(8,128)(2,1)}, u32[]{:S(2)}) %copy-start.1) | copy-done | bytes 786456
  11.6 0.4 turn.1
  12.0 3.0 %all-to-all-done = f32[8,1,128]{2,1,0:T(1,128)S(1)} async-done(((f32[8,1,128]{2,1,0:T(1,128)}), f32[8,1,128]{2,1,0:T(1,128)S(1)}, u32[]{:S(2)}, u32[]{:S(2)}) %all-to-all-start) | async-done | bytes 4128 | tf_op jit(solution)/shard_map/all_to_all | solution.py:263
  15.0 1.5 %ends.1.after = bf16[2048,128]{1,0:T(8,128)(2,1)} custom-call(f32[8,128]{1,0:T(8,128)S(1)} %bitcast.7, f32[8,128]{1,0:T(8,128)S(1)} %get-tuple-element.19.idrow, bf16[4096,128]{1,0:T(8,128)(2,1)S(1)} %get-tuple-element.20.turned, bf16[128,4096]{1,0:T(8,128)(2,1)S(1)} %get-tuple-element.21.v_ref), custom_call_target="tpu_custom_call" | custom-call | tf_op jit(solution)/shard_map/ends/pallas_call | solution.py:280
  16.5 3.7 %all-to-all-start.1 = ((bf16[16,128,128]{2,1,0:T(8,128)(2,1)}), bf16[16,128,128]{2,1,0:T(8,128)(2,1)S(1)}, u32[]{:S(2)}, u32[]{:S(2)}) async-start(bf16[16,128,128]{2,1,0:T(8,128)(2,1)} %bitcast.2), calls=%async_computation.1 | async-start | bytes 1048576 | tf_op jit(solution)/shard_map/all_to_all | solution.py:292
  20.3 0.4 collective-permute-start
  20.6 1.7 %collective-permute-start.1 = (f32[8,128]{1,0:T(8,128)S(1)}, f32[8,128]{1,0:T(8,128)S(1)}, u32[]{:S(2)}, u32[]{:S(2)}) collective-permute-start(f32[8,128]{1,0:T(8,128)S(1)} %pass.1.facts), channel_id=1, source_target_pairs={{0,16},{8,24},{16,0},{24,8},{1,17},{9,25},{17,1},{25,9},{2,18},{10... | collective-permute-start | bytes 12296 | tf_op jit(solution)/shard_map/ppermute | solution.py:305
  22.3 1.3 %collective-permute-start.2 = (f32[8,128]{1,0:T(8,128)S(1)}, f32[8,128]{1,0:T(8,128)S(1)}, u32[]{:S(2)}, u32[]{:S(2)}) collective-permute-start(f32[8,128]{1,0:T(8,128)S(1)} %pass.1.facts), channel_id=1, source_target_pairs={{0,24},{8,0},{16,8},{24,16},{1,25},{9,1},{17,9},{25,17},{2,26},{10... | collective-permute-start | bytes 12296 | tf_op jit(solution)/shard_map/ppermute | solution.py:305
  23.6 3.2 %collective-permute-done.refs_0_ = f32[8,128]{1,0:T(8,128)S(1)} collective-permute-done((f32[8,128]{1,0:T(8,128)S(1)}, f32[8,128]{1,0:T(8,128)S(1)}, u32[]{:S(2)}, u32[]{:S(2)}) %collective-permute-start) | collective-permute-done | bytes 4128 | tf_op jit(solution)/shard_map/ppermute | solution.py:305
  26.8 1.0 %collective-permute-done.1.refs_1_ = f32[8,128]{1,0:T(8,128)S(1)} collective-permute-done((f32[8,128]{1,0:T(8,128)S(1)}, f32[8,128]{1,0:T(8,128)S(1)}, u32[]{:S(2)}, u32[]{:S(2)}) %collective-permute-start.1) | collective-permute-done | bytes 4128 | tf_op jit(solution)/shard_map/ppermute | solution.py:305
  28.0 1.5 %all-to-all-done.1.in_ref = bf16[16,128,128]{2,1,0:T(8,128)(2,1)S(1)} async-done(((bf16[16,128,128]{2,1,0:T(8,128)(2,1)}), bf16[16,128,128]{2,1,0:T(8,128)(2,1)S(1)}, u32[]{:S(2)}, u32[]{:S(2)}) %all-to-all-start.1) | async-done | bytes 524320 | tf_op jit(solution)/shard_map/all_to_all | solution.py:292
  29.6 1.3 %collective-permute-start.3 = (bf16[3,128,128]{2,1,0:T(8,128)(2,1)S(1)}, bf16[3,128,128]{2,1,0:T(8,128)(2,1)S(1)}, u32[]{:S(2)}, u32[]{:S(2)}) collective-permute-start(bf16[3,128,128]{2,1,0:T(8,128)(2,1)S(1)} %get-tuple-element.25.after), channel_id=1, source_target_pairs={{0,4},{1,5},{2,6},{3,7},{4,0},{5,1},{6,2},{7,3},{8,12},{9,13},{10,... | collective-permute-start | bytes 294920 | tf_op jit(solution)/shard_map/ppermute | solution.py:330
  30.8 3.6 %collective-permute-start.4 = (bf16[1,128,128]{2,1,0:T(8,128)(2,1)S(1)}, bf16[1,128,128]{2,1,0:T(8,128)(2,1)S(1)}, u32[]{:S(2)}, u32[]{:S(2)}) collective-permute-start(bf16[1,128,128]{2,1,0:T(8,128)(2,1)S(1)} %get-tuple-element.29), channel_id=1, source_target_pairs={{0,4},{1,5},{2,6},{3,7},{8,12},{9,13},{10,14},{11,15},{16,20},{17,... | collective-permute-start | bytes 98312 | tf_op jit(solution)/shard_map/ppermute | solution.py:331
  34.5 1.3 %inner.1 = (f32[96,4096]{1,0:T(8,128)S(1)}, f32[1,4096]{1,0:T(1,128)S(1)}) custom-call(f32[8,128]{1,0:T(8,128)S(1)} %bitcast.9, f32[96,128]{1,0:T(8,128)S(1)} %get-tuple-element.18.idcol, f32[8,128]{1,0:T(8,128)S(1)} %get-tuple-element.19.idrow, bf16[96,4096]{1,0:T(8,128)(2,1)S(1)} %copy-done.3, bf16[4096,128]{1,0:T(8,128)(2,1)S(1)} %get-tuple-element.20.turned, ...), custom_call_target="tpu_custom_call" | custom-call | flops 8000000000 | bytes 4000000 | tf_op jit(solution)/shard_map/inner/pallas_call | solution.py:332
  35.8 0.3 collective-permute-done.4.final
  36.0 1.5 %collective-permute-done.3.early = bf16[3,128,128]{2,1,0:T(8,128)(2,1)S(1)} collective-permute-done((bf16[3,128,128]{2,1,0:T(8,128)(2,1)S(1)}, bf16[3,128,128]{2,1,0:T(8,128)(2,1)S(1)}, u32[]{:S(2)}, u32[]{:S(2)}) %collective-permute-start.3) | collective-permute-done | bytes 98336 | tf_op jit(solution)/shard_map/ppermute | solution.py:330
  37.5 0.2 scan.1
  37.8 12.0 %all_to_all.18 = bf16[16,128,128]{2,1,0:T(8,128)(2,1)S(1)} all-to-all(bf16[16,128,128]{2,1,0:T(8,128)(2,1)S(1)} %scan.1), channel_id=1, replica_groups={{0,1,2,3,8,9,10,11,16,17,18,19,24,25,26,27},{4,5,6,7,12,13,14,15,20,21,..., dimensions={0} | all-to-all | bytes 1048576 | tf_op jit(solution)/shard_map/all_to_all | solution.py:351
  49.7 1.9 %norm.1 = bf16[96,4096]{1,0:T(8,128)(2,1)} custom-call(f32[96,128]{1,0:T(8,128)S(1)} %get-tuple-element.18.idcol, f32[1,128]{1,0:T(1,128)S(1)} %get-tuple-element.22.before, f32[1,4096]{1,0:T(1,128)S(1)} %get-tuple-element.26.after.rates, bf16[96,4096]{1,0:T(8,128)(2,1)S(1)} %copy-done.3, bf16[2048,128]{1,0:T(8,128)(2,1)S(1)} %bitcast.6, ...), custom_call_target="tpu_custom_call" | custom-call | tf_op jit(solution)/shard_map/norm/pallas_call | solution.py:354
  (12 shorter events, 0.3 us)
Async XLA Ops:
  1.3 13.6 %all-to-all-start = ((f32[8,1,128]{2,1,0:T(1,128)}), f32[8,1,128]{2,1,0:T(1,128)S(1)}, u32[]{:S(2)}, u32[]{:S(2)}) async-start(f32[8,1,128]{2,1,0:T(1,128)} %broadcast_in_dim.13), calls=%async_computation | async-start | bytes 8192 | tf_op jit(solution)/shard_map/all_to_all | solution.py:263
  9.3 1.1 %copy-start = (bf16[96,4096]{1,0:T(8,128)(2,1)S(1)}, bf16[96,4096]{1,0:T(8,128)(2,1)}, u32[]{:S(2)}) copy-start(bf16[96,4096]{1,0:T(8,128)(2,1)} %k_ref.1) | copy-start | bytes 2359300
  10.5 1.1 %copy-start.1 = (bf16[96,4096]{1,0:T(8,128)(2,1)S(1)}, bf16[96,4096]{1,0:T(8,128)(2,1)}, u32[]{:S(2)}) copy-start(bf16[96,4096]{1,0:T(8,128)(2,1)} %v_ref.3) | copy-start | bytes 2359300
  16.5 18.0 %copy-start.2 = (bf16[96,4096]{1,0:T(8,128)(2,1)S(1)}, bf16[96,4096]{1,0:T(8,128)(2,1)}, u32[]{:S(2)}) copy-start(bf16[96,4096]{1,0:T(8,128)(2,1)} %v_ref.3) | copy-start | bytes 2359300
  16.5 18.0 %copy-start.3 = (bf16[96,4096]{1,0:T(8,128)(2,1)S(1)}, bf16[96,4096]{1,0:T(8,128)(2,1)}, u32[]{:S(2)}) copy-start(bf16[96,4096]{1,0:T(8,128)(2,1)} %q_ref.3) | copy-start | bytes 2359300
  16.5 12.9 %all-to-all-start.1 = ((bf16[16,128,128]{2,1,0:T(8,128)(2,1)}), bf16[16,128,128]{2,1,0:T(8,128)(2,1)S(1)}, u32[]{:S(2)}, u32[]{:S(2)}) async-start(bf16[16,128,128]{2,1,0:T(8,128)(2,1)} %bitcast.2), calls=%async_computation.1 | async-start | bytes 1048576 | tf_op jit(solution)/shard_map/all_to_all | solution.py:292
  20.3 6.5 %collective-permute-start = (f32[8,128]{1,0:T(8,128)S(1)}, f32[8,128]{1,0:T(8,128)S(1)}, u32[]{:S(2)}, u32[]{:S(2)}) collective-permute-start(f32[8,128]{1,0:T(8,128)S(1)} %pass.1.facts), channel_id=1, source_target_pairs={{0,8},{8,16},{16,24},{24,0},{1,9},{9,17},{17,25},{25,1},{2,10},{10... | collective-permute-start | bytes 12296 | tf_op jit(solution)/shard_map/ppermute | solution.py:305
  20.6 7.2 %collective-permute-start.1 = (f32[8,128]{1,0:T(8,128)S(1)}, f32[8,128]{1,0:T(8,128)S(1)}, u32[]{:S(2)}, u32[]{:S(2)}) collective-permute-start(f32[8,128]{1,0:T(8,128)S(1)} %pass.1.facts), channel_id=1, source_target_pairs={{0,16},{8,24},{16,0},{24,8},{1,17},{9,25},{17,1},{25,9},{2,18},{10... | collective-permute-start | bytes 12296 | tf_op jit(solution)/shard_map/ppermute | solution.py:305
  22.3 5.5 %collective-permute-start.2 = (f32[8,128]{1,0:T(8,128)S(1)}, f32[8,128]{1,0:T(8,128)S(1)}, u32[]{:S(2)}, u32[]{:S(2)}) collective-permute-start(f32[8,128]{1,0:T(8,128)S(1)} %pass.1.facts), channel_id=1, source_target_pairs={{0,24},{8,0},{16,8},{24,16},{1,25},{9,1},{17,9},{25,17},{2,26},{10... | collective-permute-start | bytes 12296 | tf_op jit(solution)/shard_map/ppermute | solution.py:305
  29.6 8.0 %collective-permute-start.3 = (bf16[3,128,128]{2,1,0:T(8,128)(2,1)S(1)}, bf16[3,128,128]{2,1,0:T(8,128)(2,1)S(1)}, u32[]{:S(2)}, u32[]{:S(2)}) collective-permute-start(bf16[3,128,128]{2,1,0:T(8,128)(2,1)S(1)} %get-tuple-element.25.after), channel_id=1, source_target_pairs={{0,4},{1,5},{2,6},{3,7},{4,0},{5,1},{6,2},{7,3},{8,12},{9,13},{10,... | collective-permute-start | bytes 294920 | tf_op jit(solution)/shard_map/ppermute | solution.py:330
  30.8 5.2 %collective-permute-start.4 = (bf16[1,128,128]{2,1,0:T(8,128)(2,1)S(1)}, bf16[1,128,128]{2,1,0:T(8,128)(2,1)S(1)}, u32[]{:S(2)}, u32[]{:S(2)}) collective-permute-start(bf16[1,128,128]{2,1,0:T(8,128)(2,1)S(1)} %get-tuple-element.29), channel_id=1, source_target_pairs={{0,4},{1,5},{2,6},{3,7},{8,12},{9,13},{10,14},{11,15},{16,20},{17,... | collective-permute-start | bytes 98312 | tf_op jit(solution)/shard_map/ppermute | solution.py:331
  35.7 14.0 %copy-start.4 = (f32[4096]{0:T(1024)S(1)}, f32[4096]{0:T(1024)}, u32[]{:S(2)}) copy-start(f32[4096]{0:T(1024)} %param.11) | copy-start | bytes 49156

commit v16 on v12

--- a/solution.py
+++ b/solution.py
@@ -42,32 +42,58 @@
         turned[columns, :] = jnp.transpose(block).astype(turned.dtype)
 
 
-def ends_kernel(here, tokens, facts, idrow, turned, v_ref, out_ref):
+def ends_kernel(here, tokens, facts, idrow, turned, v_ref, out_ref, made, sems):
     width = v_ref.shape[1]
     lane = lax.broadcasted_iota(jnp.int32, (HD, LANES), 1)
     place = lax.broadcasted_iota(jnp.int32, idrow.shape, 1)
     ids = idrow[...]
     last = ids[:, tokens - 1 : tokens]
     age = jnp.where(ids == last, (tokens - 1 - place).astype(jnp.float32), NEVER)
-    for j in range(width // LANES):
-        weighted = []
-        for head in (2 * j, 2 * j + 1):
-            weight = jnp.exp(-rate_of(facts, head, here) * age)
-            keys = turned[head * HD : (head + 1) * HD, :].astype(jnp.float32)
-            keys = keys.reshape(HD // 8, 8, LANES) * weight[None]
-            weighted.append(keys.reshape(HD, LANES))
-        weighted = jnp.concatenate(weighted, 0)
-        high = weighted.astype(jnp.bfloat16)
-        low = (weighted - high.astype(jnp.float32)).astype(jnp.bfloat16)
-        v = v_ref[:, j * LANES : (j + 1) * LANES]
-        both = jnp.dot(
-            jnp.concatenate([high, low], 1),
-            jnp.concatenate([v, v], 0),
-            preferred_element_type=jnp.float32,
-        )
-        out_ref[j * HD : (j + 1) * HD, :] = jnp.where(lane < HD, both[:HD], both[HD:]).astype(
-            jnp.bfloat16
-        )
+    parts = sems.shape[0]
+    wide = width // parts
+    tall = made.shape[0] // parts
+
+    def copy_of(part):
+        rows = pl.ds(pl.multiple_of(part * tall, tall), tall)
+        return pltpu.make_async_copy(made.at[rows], out_ref.at[rows], sems.at[part])
+
+    def make(part, _):
+        for quad in range(wide // (2 * LANES)):
+            weighted = []
+            for head in range(4 * quad, 4 * quad + 4):
+                row = part * (wide // HD // here) + head // here
+                rate = facts[pl.ds(row, 1), head % here : head % here + 1]
+                weight = jnp.exp(-rate * age)
+                at = pl.multiple_of(part * wide + head * HD, HD)
+                keys = turned[pl.ds(at, HD), :].astype(jnp.float32)
+                keys = keys.reshape(HD // 8, 8, LANES) * weight[None]
+                weighted.append(keys.reshape(HD, LANES))
+            weighted = jnp.concatenate(weighted, 0)
+            high = weighted.astype(jnp.bfloat16)
+            low = (weighted - high.astype(jnp.float32)).astype(jnp.bfloat16)
+            at = pl.multiple_of(part * wide + quad * 2 * LANES, 2 * LANES)
+            v = v_ref[:, pl.ds(at, 2 * LANES)]
+            both = jnp.dot(
+                jnp.concatenate([high, low], 1),
+                jnp.concatenate([v, v], 0),
+                preferred_element_type=jnp.float32,
+            )
+            for one in (0, 1):
+                pair = both[one * LANES : (one + 1) * LANES, one * LANES : (one + 1) * LANES]
+                at = pl.multiple_of(part * tall + (2 * quad + one) * HD, HD)
+                made[pl.ds(at, HD), :] = jnp.where(lane < HD, pair[:HD], pair[HD:]).astype(
+                    jnp.bfloat16
+                )
+        copy_of(part).start()
+        return 0
+
+    lax.fori_loop(0, parts, make, 0)
+
+    def finish(part, _):
+        copy_of(part).wait()
+        return 0
+
+    lax.fori_loop(0, parts, finish, 0)
 
 
 def inner_kernel(
@@ -185,39 +211,51 @@
     place = lax.broadcasted_iota(jnp.int32, (tokens, LANES), 0)
     age = jnp.where(idcol[...] == before[...], (place + 1).astype(jnp.float32), NEVER)
     zero = jnp.zeros((HD, LANES), s_ref.dtype)
-    total = jnp.zeros((tokens, LANES), jnp.float32)
-    for j in range(0, width // LANES, 2):
+
+    def join(quad, total):
         square = []
         for one in (0, 1):
-            state = s_ref[(j + one) * HD : (j + one + 1) * HD, :]
+            at = pl.multiple_of((2 * quad + one) * HD, HD)
+            state = s_ref[pl.ds(at, HD), :]
             for half in (jnp.where(lane < HD, state, zero), jnp.where(lane < HD, zero, state)):
                 square.append(jnp.concatenate([zero, half] if one else [half, zero], 1))
-        columns = slice(j * LANES, (j + 2) * LANES)
+        columns = pl.ds(pl.multiple_of(quad * 2 * LANES, 2 * LANES), 2 * LANES)
         outer = jnp.dot(
             q_ref[:, columns], jnp.concatenate(square, 0), preferred_element_type=jnp.float32
         )
         for one in (0, 1):
-            columns = slice((j + one) * LANES, (j + one + 1) * LANES)
+            columns = pl.ds(pl.multiple_of((2 * quad + one) * LANES, LANES), LANES)
             fade = jnp.exp(-rates[:, columns] * age)
             value = inner_ref[:, columns] + outer[:, one * LANES : (one + 1) * LANES] * fade
             total += value * value
             raw[:, columns] = value
+        return total
+
+    total = jnp.zeros((tokens, LANES), jnp.float32)
+    total = lax.fori_loop(0, width // (2 * LANES), join, total, unroll=2)
     mean = jnp.sum(total, axis=1, keepdims=True) / float(width)
     scale = jnp.broadcast_to(lax.rsqrt(mean + 1e-06), (tokens, LANES))
     parts = sems.shape[0]
     share = width // parts
-    copies = []
-    for part in range(parts):
-        for at in range(part * share, (part + 1) * share, LANES):
-            columns = slice(at, at + LANES)
+
+    def copy_of(part):
+        columns = pl.ds(pl.multiple_of(part * share, share), share)
+        return pltpu.make_async_copy(done.at[:, columns], out_ref.at[:, columns], sems.at[part])
+
+    def send(part, _):
+        for at in range(0, share, LANES):
+            columns = pl.ds(pl.multiple_of(part * share + at, LANES), LANES)
             done[:, columns] = (raw[:, columns] * scale * gain[:, columns]).astype(jnp.bfloat16)
-        columns = slice(part * share, (part + 1) * share)
-        copies.append(
-            pltpu.make_async_copy(done.at[:, columns], out_ref.at[:, columns], sems.at[part])
-        )
-        copies[-1].start()
-    for copy in copies:
-        copy.wait()
+        copy_of(part).start()
+        return 0
+
+    lax.fori_loop(0, parts, send, 0, unroll=2)
+
+    def finish(part, _):
+        copy_of(part).wait()
+        return 0
+
+    lax.fori_loop(0, parts, finish, 0)
 
 
 def local(queries, keys, values, doc_ids, decay_rate, norm_gain):
@@ -268,8 +306,12 @@
     ends = pl.pallas_call(
         functools.partial(ends_kernel, here, tokens),
         in_specs=[vmem] * 4,
-        out_specs=vmem,
+        out_specs=pl.BlockSpec(memory_space=pl.ANY),
         out_shape=shape((all_pairs * HD, LANES), jnp.bfloat16),
+        scratch_shapes=[
+            pltpu.VMEM((all_pairs * HD, LANES), jnp.bfloat16),
+            pltpu.SemaphoreType.DMA((8,)),
+        ],
         compiler_params=params,
         name="ends",
     )(facts, idrow, turned, filled)
@@ -343,7 +385,7 @@
         scratch_shapes=[
             pltpu.VMEM((tokens, width), jnp.float32),
             pltpu.VMEM((tokens, width), jnp.bfloat16),
-            pltpu.SemaphoreType.DMA((4,)),
+            pltpu.SemaphoreType.DMA((8,)),
         ],
         compiler_params=params,
         name="norm",

time: 52 us -> 54.8 us (1.054)
  Pallas kernels: 5.53 us -> 8.32 us
    pallas_call x1, Pallas kernels: 1.59 us -> 3.36 us  [local(): pl.pallas_call(functools.partial(ends_kernel, here, tokens), in_specs=[vm...]
    pallas_call x1, Pallas kernels: 1.81 us -> 2.82 us  [local(): pl.pallas_call(norm_kernel, in_specs=[vmem] * 7, out_specs=pl.BlockSpec(m...]
where the time goes in v16:
time: 54.8 us; the launch traced here: 54.4 us
  starting transfers between devices  19.2 us (35%)
  blocking collectives  12 us (22%)
  waiting for transfers between devices  10.4 us (19%)
  Pallas kernels  8.32 us (15%)
  local copies, waits for them, and re-layouts  2.88 us (5%)
  other arithmetic  1.49 us (3%)
    all_to_all x1, blocking collectives, local(): lax.all_to_all(moved, axes, split_axis=0, concat_axis=0, axis_index_group...  12 us
    all_to_all x1, starting transfers between devices, local(): lax.all_to_all(jnp.broadcast_to(own[None, :], tile.shape), 'uly', split_a...  7.25 us
    ppermute x3, waiting for transfers between devices, local(): lax.ppermute(slice_facts, 'ctx', [(c, (c + ahead) % slices) for c in rang...  4.21 us
    all_to_all x1, starting transfers between devices, local(): lax.all_to_all(ends.reshape(group, rows, LANES), axes, split_axis=0, conc...  3.72 us
    ppermute x1, starting transfers between devices, local(): lax.ppermute(final_end, axes, [(low, high) for low, high in swap if low <...  3.63 us
    ppermute x3, starting transfers between devices, local(): lax.ppermute(slice_facts, 'ctx', [(c, (c + ahead) % slices) for c in rang...  3.37 us
    pallas_call x1, Pallas kernels, local(): pl.pallas_call(functools.partial(ends_kernel, here, tokens), in_specs=[vm...  3.36 us
    all_to_all x1, waiting for transfers between devices, local(): lax.all_to_all(jnp.broadcast_to(own[None, :], tile.shape), 'uly', split_a...  2.97 us
  transfers between devices with their start and end apart: 7, of which 6 were waited for; matrix products, arithmetic and copies ran while one was open for 1% of the time, Pallas kernels for 3%

profile of v16, /device:TPU:0, one launch (start us, length us, event | category | flops | bytes accessed | tf_op | source)
XLA Modules:
  0.0 54.4 jit_solution(7900440596288623428)
XLA Ops:
  0.0 0.7 %convert_add_fusion = f32[128]{0:T(128)S(1)} fusion(s32[96]{0:T(128)} %param.9, f32[8]{0:T(128)} %param.10), kind=kLoop, calls=%fused_computation | loop fusion | flops 256 | bytes 928 | tf_op jit(solution)/shard_map/add | solution.py:286
  0.7 0.6 %broadcast_in_dim.13 = f32[8,1,128]{2,1,0:T(1,128)} broadcast(f32[128]{0:T(128)S(1)} %convert_add_fusion), dimensions={2} | broadcast | bytes 4608 | tf_op jit(solution)/shard_map/broadcast_in_dim | solution.py:290
  1.3 7.3 %all-to-all-start = ((f32[8,1,128]{2,1,0:T(1,128)}), f32[8,1,128]{2,1,0:T(1,128)S(1)}, u32[]{:S(2)}, u32[]{:S(2)}) async-start(f32[8,1,128]{2,1,0:T(1,128)} %broadcast_in_dim.13), calls=%async_computation | async-start | bytes 8192 | tf_op jit(solution)/shard_map/all_to_all | solution.py:289
  8.6 0.7 %fusion.row_ref = f32[1,128]{1,0:T(1,128)S(1)} fusion(s32[96]{0:T(128)} %param.9, f32[8]{0:T(128)} %param.10), kind=kLoop, calls=%fused_computation.1 | loop fusion | flops 256 | bytes 928 | tf_op jit(solution)/shard_map/broadcast_in_dim | solution.py:305
  9.3 1.1 %copy-done = bf16[96,4096]{1,0:T(8,128)(2,1)S(1)} copy-done((bf16[96,4096]{1,0:T(8,128)(2,1)S(1)}, bf16[96,4096]{1,0:T(8,128)(2,1)}, u32[]{:S(2)}) %copy-start) | copy-done | bytes 786456
  10.5 1.1 %copy-done.1 = bf16[96,4096]{1,0:T(8,128)(2,1)S(1)} copy-done((bf16[96,4096]{1,0:T(8,128)(2,1)S(1)}, bf16[96,4096]{1,0:T(8,128)(2,1)}, u32[]{:S(2)}) %copy-start.1) | copy-done | bytes 786456
  11.6 0.4 turn.1
  12.0 3.0 %all-to-all-done = f32[8,1,128]{2,1,0:T(1,128)S(1)} async-done(((f32[8,1,128]{2,1,0:T(1,128)}), f32[8,1,128]{2,1,0:T(1,128)S(1)}, u32[]{:S(2)}, u32[]{:S(2)}) %all-to-all-start) | async-done | bytes 4128 | tf_op jit(solution)/shard_map/all_to_all | solution.py:289
  15.0 3.4 %ends.1.after = bf16[2048,128]{1,0:T(8,128)(2,1)} custom-call(f32[8,128]{1,0:T(8,128)S(1)} %bitcast.7, f32[8,128]{1,0:T(8,128)S(1)} %get-tuple-element.19.idrow, bf16[4096,128]{1,0:T(8,128)(2,1)S(1)} %get-tuple-element.20.turned, bf16[128,4096]{1,0:T(8,128)(2,1)S(1)} %get-tuple-element.21.v_ref), custom_call_target="tpu_custom_call" | custom-call | tf_op jit(solution)/shard_map/ends/pallas_call | solution.py:306
  18.4 3.7 %all-to-all-start.1 = ((bf16[16,128,128]{2,1,0:T(8,128)(2,1)}), bf16[16,128,128]{2,1,0:T(8,128)(2,1)S(1)}, u32[]{:S(2)}, u32[]{:S(2)}) async-start(bf16[16,128,128]{2,1,0:T(8,128)(2,1)} %bitcast.2), calls=%async_computation.1 | async-start | bytes 1048576 | tf_op jit(solution)/shard_map/all_to_all | solution.py:318
  22.1 0.4 collective-permute-start
  22.5 1.7 %collective-permute-start.1 = (f32[8,128]{1,0:T(8,128)S(1)}, f32[8,128]{1,0:T(8,128)S(1)}, u32[]{:S(2)}, u32[]{:S(2)}) collective-permute-start(f32[8,128]{1,0:T(8,128)S(1)} %pass.1.facts), channel_id=1, source_target_pairs={{0,16},{8,24},{16,0},{24,8},{1,17},{9,25},{17,1},{25,9},{2,18},{10... | collective-permute-start | bytes 12296 | tf_op jit(solution)/shard_map/ppermute | solution.py:331
  24.2 1.3 %collective-permute-start.2 = (f32[8,128]{1,0:T(8,128)S(1)}, f32[8,128]{1,0:T(8,128)S(1)}, u32[]{:S(2)}, u32[]{:S(2)}) collective-permute-start(f32[8,128]{1,0:T(8,128)S(1)} %pass.1.facts), channel_id=1, source_target_pairs={{0,24},{8,0},{16,8},{24,16},{1,25},{9,1},{17,9},{25,17},{2,26},{10... | collective-permute-start | bytes 12296 | tf_op jit(solution)/shard_map/ppermute | solution.py:331
  25.5 3.2 %collective-permute-done.refs_0_ = f32[8,128]{1,0:T(8,128)S(1)} collective-permute-done((f32[8,128]{1,0:T(8,128)S(1)}, f32[8,128]{1,0:T(8,128)S(1)}, u32[]{:S(2)}, u32[]{:S(2)}) %collective-permute-start) | collective-permute-done | bytes 4128 | tf_op jit(solution)/shard_map/ppermute | solution.py:331
  28.7 1.0 %collective-permute-done.1.refs_1_ = f32[8,128]{1,0:T(8,128)S(1)} collective-permute-done((f32[8,128]{1,0:T(8,128)S(1)}, f32[8,128]{1,0:T(8,128)S(1)}, u32[]{:S(2)}, u32[]{:S(2)}) %collective-permute-start.1) | collective-permute-done | bytes 4128 | tf_op jit(solution)/shard_map/ppermute | solution.py:331
  29.8 1.5 %all-to-all-done.1.in_ref = bf16[16,128,128]{2,1,0:T(8,128)(2,1)S(1)} async-done(((bf16[16,128,128]{2,1,0:T(8,128)(2,1)}), bf16[16,128,128]{2,1,0:T(8,128)(2,1)S(1)}, u32[]{:S(2)}, u32[]{:S(2)}) %all-to-all-start.1) | async-done | bytes 524320 | tf_op jit(solution)/shard_map/all_to_all | solution.py:318
  31.4 1.3 %collective-permute-start.3 = (bf16[3,128,128]{2,1,0:T(8,128)(2,1)S(1)}, bf16[3,128,128]{2,1,0:T(8,128)(2,1)S(1)}, u32[]{:S(2)}, u32[]{:S(2)}) collective-permute-start(bf16[3,128,128]{2,1,0:T(8,128)(2,1)S(1)} %get-tuple-element.25.after), channel_id=1, source_target_pairs={{0,4},{1,5},{2,6},{3,7},{4,0},{5,1},{6,2},{7,3},{8,12},{9,13},{10,... | collective-permute-start | bytes 294920 | tf_op jit(solution)/shard_map/ppermute | solution.py:356
  32.7 3.6 %collective-permute-start.4 = (bf16[1,128,128]{2,1,0:T(8,128)(2,1)S(1)}, bf16[1,128,128]{2,1,0:T(8,128)(2,1)S(1)}, u32[]{:S(2)}, u32[]{:S(2)}) collective-permute-start(bf16[1,128,128]{2,1,0:T(8,128)(2,1)S(1)} %get-tuple-element.29), channel_id=1, source_target_pairs={{0,4},{1,5},{2,6},{3,7},{8,12},{9,13},{10,14},{11,15},{16,20},{17,... | collective-permute-start | bytes 98312 | tf_op jit(solution)/shard_map/ppermute | solution.py:357
  36.3 1.3 %inner.1 = (f32[96,4096]{1,0:T(8,128)S(1)}, f32[1,4096]{1,0:T(1,128)S(1)}) custom-call(f32[8,128]{1,0:T(8,128)S(1)} %bitcast.9, f32[96,128]{1,0:T(8,128)S(1)} %get-tuple-element.18.idcol, f32[8,128]{1,0:T(8,128)S(1)} %get-tuple-element.19.idrow, bf16[96,4096]{1,0:T(8,128)(2,1)S(1)} %copy-done.3, bf16[4096,128]{1,0:T(8,128)(2,1)S(1)} %get-tuple-element.20.turned, ...), custom_call_target="tpu_custom_call" | custom-call | flops 8000000000 | bytes 4000000 | tf_op jit(solution)/shard_map/inner/pallas_call | solution.py:358
  37.6 0.3 collective-permute-done.4.final
  37.9 1.5 %collective-permute-done.3.early = bf16[3,128,128]{2,1,0:T(8,128)(2,1)S(1)} collective-permute-done((bf16[3,128,128]{2,1,0:T(8,128)(2,1)S(1)}, bf16[3,128,128]{2,1,0:T(8,128)(2,1)S(1)}, u32[]{:S(2)}, u32[]{:S(2)}) %collective-permute-start.3) | collective-permute-done | bytes 98336 | tf_op jit(solution)/shard_map/ppermute | solution.py:356
  39.4 0.2 scan.1
  39.6 12.0 %all_to_all.18 = bf16[16,128,128]{2,1,0:T(8,128)(2,1)S(1)} all-to-all(bf16[16,128,128]{2,1,0:T(8,128)(2,1)S(1)} %scan.1), channel_id=1, replica_groups={{0,1,2,3,8,9,10,11,16,17,18,19,24,25,26,27},{4,5,6,7,12,13,14,15,20,21,..., dimensions={0} | all-to-all | bytes 1048576 | tf_op jit(solution)/shard_map/all_to_all | solution.py:377
  51.6 2.8 %norm.1 = bf16[96,4096]{1,0:T(8,128)(2,1)} custom-call(f32[96,128]{1,0:T(8,128)S(1)} %get-tuple-element.18.idcol, f32[1,128]{1,0:T(1,128)S(1)} %get-tuple-element.22.before, f32[1,4096]{1,0:T(1,128)S(1)} %get-tuple-element.26.after.rates, bf16[96,4096]{1,0:T(8,128)(2,1)S(1)} %copy-done.3, bf16[2048,128]{1,0:T(8,128)(2,1)S(1)} %bitcast.6, ...), custom_call_target="tpu_custom_call" | custom-call | tf_op jit(solution)/shard_map/norm/pallas_call | solution.py:380
  (12 shorter events, 0.3 us)
Async XLA Ops:
  1.3 13.6 %all-to-all-start = ((f32[8,1,128]{2,1,0:T(1,128)}), f32[8,1,128]{2,1,0:T(1,128)S(1)}, u32[]{:S(2)}, u32[]{:S(2)}) async-start(f32[8,1,128]{2,1,0:T(1,128)} %broadcast_in_dim.13), calls=%async_computation | async-start | bytes 8192 | tf_op jit(solution)/shard_map/all_to_all | solution.py:289
  9.3 1.1 %copy-start = (bf16[96,4096]{1,0:T(8,128)(2,1)S(1)}, bf16[96,4096]{1,0:T(8,128)(2,1)}, u32[]{:S(2)}) copy-start(bf16[96,4096]{1,0:T(8,128)(2,1)} %k_ref.1) | copy-start | bytes 2359300
  10.5 1.1 %copy-start.1 = (bf16[96,4096]{1,0:T(8,128)(2,1)S(1)}, bf16[96,4096]{1,0:T(8,128)(2,1)}, u32[]{:S(2)}) copy-start(bf16[96,4096]{1,0:T(8,128)(2,1)} %v_ref.3) | copy-start | bytes 2359300
  18.4 18.0 %copy-start.2 = (bf16[96,4096]{1,0:T(8,128)(2,1)S(1)}, bf16[96,4096]{1,0:T(8,128)(2,1)}, u32[]{:S(2)}) copy-start(bf16[96,4096]{1,0:T(8,128)(2,1)} %v_ref.3) | copy-start | bytes 2359300
  18.4 18.0 %copy-start.3 = (bf16[96,4096]{1,0:T(8,128)(2,1)S(1)}, bf16[96,4096]{1,0:T(8,128)(2,1)}, u32[]{:S(2)}) copy-start(bf16[96,4096]{1,0:T(8,128)(2,1)} %q_ref.3) | copy-start | bytes 2359300
  18.4 12.9 %all-to-all-start.1 = ((bf16[16,128,128]{2,1,0:T(8,128)(2,1)}), bf16[16,128,128]{2,1,0:T(8,128)(2,1)S(1)}, u32[]{:S(2)}, u32[]{:S(2)}) async-start(bf16[16,128,128]{2,1,0:T(8,128)(2,1)} %bitcast.2), calls=%async_computation.1 | async-start | bytes 1048576 | tf_op jit(solution)/shard_map/all_to_all | solution.py:318
  22.1 6.5 %collective-permute-start = (f32[8,128]{1,0:T(8,128)S(1)}, f32[8,128]{1,0:T(8,128)S(1)}, u32[]{:S(2)}, u32[]{:S(2)}) collective-permute-start(f32[8,128]{1,0:T(8,128)S(1)} %pass.1.facts), channel_id=1, source_target_pairs={{0,8},{8,16},{16,24},{24,0},{1,9},{9,17},{17,25},{25,1},{2,10},{10... | collective-permute-start | bytes 12296 | tf_op jit(solution)/shard_map/ppermute | solution.py:331
  22.5 7.2 %collective-permute-start.1 = (f32[8,128]{1,0:T(8,128)S(1)}, f32[8,128]{1,0:T(8,128)S(1)}, u32[]{:S(2)}, u32[]{:S(2)}) collective-permute-start(f32[8,128]{1,0:T(8,128)S(1)} %pass.1.facts), channel_id=1, source_target_pairs={{0,16},{8,24},{16,0},{24,8},{1,17},{9,25},{17,1},{25,9},{2,18},{10... | collective-permute-start | bytes 12296 | tf_op jit(solution)/shard_map/ppermute | solution.py:331
  24.2 5.5 %collective-permute-start.2 = (f32[8,128]{1,0:T(8,128)S(1)}, f32[8,128]{1,0:T(8,128)S(1)}, u32[]{:S(2)}, u32[]{:S(2)}) collective-permute-start(f32[8,128]{1,0:T(8,128)S(1)} %pass.1.facts), channel_id=1, source_target_pairs={{0,24},{8,0},{16,8},{24,16},{1,25},{9,1},{17,9},{25,17},{2,26},{10... | collective-permute-start | bytes 12296 | tf_op jit(solution)/shard_map/ppermute | solution.py:331
  31.4 8.0 %collective-permute-start.3 = (bf16[3,128,128]{2,1,0:T(8,128)(2,1)S(1)}, bf16[3,128,128]{2,1,0:T(8,128)(2,1)S(1)}, u32[]{:S(2)}, u32[]{:S(2)}) collective-permute-start(bf16[3,128,128]{2,1,0:T(8,128)(2,1)S(1)} %get-tuple-element.25.after), channel_id=1, source_target_pairs={{0,4},{1,5},{2,6},{3,7},{4,0},{5,1},{6,2},{7,3},{8,12},{9,13},{10,... | collective-permute-start | bytes 294920 | tf_op jit(solution)/shard_map/ppermute | solution.py:356
  32.7 5.2 %collective-permute-start.4 = (bf16[1,128,128]{2,1,0:T(8,128)(2,1)S(1)}, bf16[1,128,128]{2,1,0:T(8,128)(2,1)S(1)}, u32[]{:S(2)}, u32[]{:S(2)}) collective-permute-start(bf16[1,128,128]{2,1,0:T(8,128)(2,1)S(1)} %get-tuple-element.29), channel_id=1, source_target_pairs={{0,4},{1,5},{2,6},{3,7},{8,12},{9,13},{10,14},{11,15},{16,20},{17,... | collective-permute-start | bytes 98312 | tf_op jit(solution)/shard_map/ppermute | solution.py:357
  37.6 14.0 %copy-start.4 = (f32[4096]{0:T(1024)S(1)}, f32[4096]{0:T(1024)}, u32[]{:S(2)}) copy-start(f32[4096]{0:T(1024)} %param.11) | copy-start | bytes 49156

commit v17 on v14

--- a/solution.py
+++ b/solution.py
@@ -132,7 +132,7 @@
     before[...] = jnp.where(me > 0, last[pl.ds(jnp.maximum(me - 1, 0), 1), :], -1.0)
     rows = one.shape[0]
     share = min(rows, HD)
-    owner = ctx * chunks + lax.rem(uly, chunks)
+    owner = lax.rem(ctx, slices // 2) * chunks + lax.rem(uly, chunks)
     for at in range(0, rows, share):
         rate = pair_rate(facts, lax.div(owner * rows + at, HD), here)
         for ref, length in ((one, tokens), (half, tokens * chunks)):
@@ -141,43 +141,53 @@
             )
 
 
-def half_kernel(chunks, linked, one, in_ref, early_ref, final_ref):
-    slices = early_ref.shape[0] + 1
-    offset = jnp.where(lax.axis_index("uly") >= chunks, chunks, 0)
-
-    def slice_end(c):
+def half_kernel(chunks, linked, through, one, half, in_ref, early_ref, final_ref, sum_ref):
+    span = early_ref.shape[0] + 1
+    later = lax.axis_index("uly") >= chunks
+    offset = jnp.where(later, chunks, 0)
+    base = jnp.where(lax.axis_index("ctx") >= span, span, 0) * 2 * chunks
+
+    def slice_end(c, total):
+        start = base + c * 2 * chunks
+
         def step(j, state):
-            keep = linked[pl.ds(c * 2 * chunks + offset + j, 1), :] * one[...]
+            keep = linked[pl.ds(start + offset + j, 1), :] * one[...]
             return in_ref[c * chunks + j].astype(jnp.float32) + keep * state
 
         begin = in_ref[c * chunks].astype(jnp.float32)
         state = lax.fori_loop(1, chunks, step, begin, unroll=few(chunks - 1))
-        return state.astype(early_ref.dtype)
-
-    def early(c, _):
-        early_ref[c] = slice_end(c)
-        return 0
-
-    lax.fori_loop(0, slices - 1, early, 0, unroll=few(slices - 1))
-    final_ref[0] = slice_end(slices - 1)
+        low = through[pl.ds(start, 1), :] * half[...]
+        high = through[pl.ds(start + chunks, 1), :] * half[...]
+        total = jnp.where(later, 1.0, high) * state + low * high * total
+        return state.astype(early_ref.dtype), total
+
+    def early(c, total):
+        early_ref[c], total = slice_end(c, total)
+        return total
+
+    total = jnp.zeros(in_ref.shape[1:], jnp.float32)
+    total = lax.fori_loop(0, span - 1, early, total, unroll=few(span - 1))
+    final_ref[0], total = slice_end(span - 1, total)
+    sum_ref[...] = total.astype(sum_ref.dtype)
 
 
 def scan_kernel(
-    chunks, linked, through, one, half, in_ref, early, final, after, out_ref
+    chunks, linked, through, one, half, in_ref, early, final, straight, across, after, out_ref
 ):
-    slices = early.shape[0] + 1
+    span = early.shape[0] + 1
     later = lax.axis_index("uly") >= chunks
     offset = jnp.where(later, chunks, 0)
+    base = jnp.where(lax.axis_index("ctx") >= span, span, 0) * 2 * chunks
 
     def over_other(state, c, piece, wanted):
-        keep = through[pl.ds(c * 2 * chunks + chunks - offset, 1), :] * half[...]
+        keep = through[pl.ds(base + c * 2 * chunks + chunks - offset, 1), :] * half[...]
         return jnp.where(wanted, piece.astype(jnp.float32) + keep * state, state)
 
     def over_own(state, c):
         def step(j, state):
             at = c * chunks + j
             out_ref[at] = state.astype(out_ref.dtype)
-            keep = linked[pl.ds(c * 2 * chunks + offset + j, 1), :] * one[...]
+            keep = linked[pl.ds(base + c * 2 * chunks + offset + j, 1), :] * one[...]
             return in_ref[at].astype(jnp.float32) + keep * state
 
         return lax.fori_loop(0, chunks, step, state, unroll=few(chunks))
@@ -186,9 +196,9 @@
         state = over_own(over_other(state, c, early[c], later), c)
         return over_other(state, c, early[c], jnp.logical_not(later))
 
-    begin = jnp.zeros(in_ref.shape[1:], jnp.float32)
-    state = lax.fori_loop(0, slices - 1, over_slice, begin, unroll=few(slices - 1))
-    over_own(over_other(state, slices - 1, final[0], later), slices - 1)
+    state = straight[...].astype(jnp.float32) + across[...].astype(jnp.float32)
+    state = lax.fori_loop(0, span - 1, over_slice, state, unroll=few(span - 1))
+    over_own(over_other(state, span - 1, final[0], later), span - 1)
 
 
 def norm_kernel(idcol, before, rates, q_ref, s_ref, inner_ref, gain, out_ref, raw, done, sems):
@@ -240,17 +250,21 @@
     count = slices * members
     all_pairs = width // LANES
     chunks = members // 2
-    group = slices * chunks
+    span = slices // 2
+    group = span * chunks
     rows = all_pairs * HD // group
+    device = lambda c, u: c * members + u
     groups = [
-        [c * members + half * chunks + u for c in range(slices) for u in range(chunks)]
-        for half in (0, 1)
+        [device(first + c, half + u) for c in range(span) for u in range(chunks)]
+        for first in (0, span)
+        for half in (0, chunks)
     ]
-    swap = [
-        (c * members + u, c * members + (u + chunks) % members)
-        for c in range(slices)
-        for u in range(members)
-    ]
+    opposite = lambda u: (u + chunks) % members
+    every = [(c, u) for c in range(slices) for u in range(members)]
+    swap = [(device(c, u), device(c, opposite(u))) for c, u in every]
+    upward = [(device(c, u), device(c, opposite(u))) for c, u in every if u < chunks]
+    onward = [(device(c, u), device(c + span, u)) for c, u in every if c < span]
+    onward_across = [(device(c, u), device(c + span, opposite(u))) for c, u in every if c < span]
 
     vmem = pl.BlockSpec(memory_space=pltpu.VMEM)
     params = pltpu.CompilerParams(vmem_limit_bytes=32 * 1024 * 1024)
@@ -316,19 +330,23 @@
         compiler_params=params,
         name="link",
     )(slice_facts, *others)
-    early_ends, final_end = pl.pallas_call(
+    block = shape((rows, LANES), jnp.bfloat16)
+    early_ends, final_end, left = pl.pallas_call(
         functools.partial(half_kernel, chunks),
-        in_specs=[vmem] * 3,
-        out_specs=[vmem] * 2,
+        in_specs=[vmem] * 5,
+        out_specs=[vmem] * 3,
         out_shape=[
-            shape((slices - 1, rows, LANES), jnp.bfloat16),
+            shape((span - 1, rows, LANES), jnp.bfloat16),
             shape((1, rows, LANES), jnp.bfloat16),
+            block,
         ],
         compiler_params=params,
         name="half",
-    )(linked, one, pieces)
+    )(linked, through, one, half, pieces)
     early = lax.ppermute(early_ends, axes, swap)
-    final = lax.ppermute(final_end, axes, [(low, high) for low, high in swap if low < high])
+    final = lax.ppermute(final_end, axes, upward)
+    straight = lax.ppermute(left, axes, onward)
+    across = lax.ppermute(left, axes, onward_across)
     inner, rates = pl.pallas_call(
         functools.partial(inner_kernel, here),
         in_specs=[vmem] * 6 + [pl.BlockSpec(memory_space=pl.ANY)],
@@ -342,12 +360,12 @@
     )(facts, idcol, idrow, queries, turned, values, early_ends)
     moved = pl.pallas_call(
         functools.partial(scan_kernel, chunks),
-        in_specs=[vmem] * 7 + [pl.BlockSpec(memory_space=pl.ANY)],
+        in_specs=[vmem] * 9 + [pl.BlockSpec(memory_space=pl.ANY)],
         out_specs=vmem,
         out_shape=shape((group, rows, LANES), jnp.bfloat16),
         compiler_params=params,
         name="scan",
-    )(linked, through, one, half, pieces, early, final, rates)
+    )(linked, through, one, half, pieces, early, final, straight, across, rates)
     states = lax.all_to_all(
         moved, axes, split_axis=0, concat_axis=0, axis_index_groups=groups, tiled=True
     )

time: 52 us -> 57.3 us (1.10)
  starting transfers between devices: 19.2 us -> 23.5 us
  waiting for transfers between devices: 10.4 us -> 11.4 us
    ppermute x1 -> x3, starting transfers between devices: 3.63 us -> 7.18 us  [the longest x1 3.42 us: local(): straight = lax.ppermute(left, axes, onward)]
    all_to_all x1, waiting for transfers between devices: 1.47 us -> 4.66 us  [local(): lax.all_to_all(ends.reshape(group, rows, LANES), axes, split_axis=0, conc...]
    ppermute x3, waiting for transfers between devices: 4.21 us -> 1.33 us  [local(): lax.ppermute(slice_facts, 'ctx', [(c, (c + ahead) % slices) for c in rang...]
    ppermute x1, starting transfers between devices: 1.25 us -> 2.43 us  [local(): early = lax.ppermute(early_ends, axes, swap)]
    ppermute x1, waiting for transfers between devices: 1.49 us -> 2.43 us  [local(): early = lax.ppermute(early_ends, axes, swap)]
  transfers between devices with their start and end apart: 7 -> 9, of which waited for: 6 -> 5; matrix products, arithmetic and copies ran while one was open for 1% -> 1% of each run, Pallas kernels for 3% -> 3%
where the time goes in v17:
time: 57.3 us; the launch traced here: 56.8 us
  starting transfers between devices  23.5 us (41%)
  blocking collectives  11.8 us (21%)
  waiting for transfers between devices  11.4 us (20%)
  Pallas kernels  5.59 us (10%)
  local copies, waits for them, and re-layouts  2.88 us (5%)
  other arithmetic  1.49 us (3%)
    all_to_all x1, blocking collectives, local(): lax.all_to_all(moved, axes, split_axis=0, concat_axis=0, axis_index_group...  11.8 us
    all_to_all x1, starting transfers between devices, local(): lax.all_to_all(jnp.broadcast_to(own[None, :], tile.shape), 'uly', split_a...  7.25 us
    all_to_all x1, waiting for transfers between devices, local(): lax.all_to_all(ends.reshape(group, rows, LANES), axes, split_axis=0, conc...  4.66 us
    all_to_all x1, starting transfers between devices, local(): lax.all_to_all(ends.reshape(group, rows, LANES), axes, split_axis=0, conc...  3.64 us
    ppermute x1, starting transfers between devices, local(): straight = lax.ppermute(left, axes, onward)  3.42 us
    ppermute x3, starting transfers between devices, local(): lax.ppermute(slice_facts, 'ctx', [(c, (c + ahead) % slices) for c in rang...  3.03 us
    all_to_all x1, waiting for transfers between devices, local(): lax.all_to_all(jnp.broadcast_to(own[None, :], tile.shape), 'uly', split_a...  2.97 us
    ppermute x1, starting transfers between devices, local(): final = lax.ppermute(final_end, axes, upward)  2.46 us
  transfers between devices with their start and end apart: 9, of which 5 were waited for; matrix products, arithmetic and copies ran while one was open for 1% of the time, Pallas kernels for 3%

profile of v17, /device:TPU:0, one launch (start us, length us, event | category | flops | bytes accessed | tf_op | source)
XLA Modules:
  0.0 56.8 jit_solution(9528432403402652765)
XLA Ops:
  0.0 0.7 %convert_add_fusion = f32[128]{0:T(128)S(1)} fusion(s32[96]{0:T(128)} %param.9, f32[8]{0:T(128)} %param.10), kind=kLoop, calls=%fused_computation | loop fusion | flops 256 | bytes 928 | tf_op jit(solution)/shard_map/add | solution.py:274
  0.7 0.6 %broadcast_in_dim.13 = f32[8,1,128]{2,1,0:T(1,128)} broadcast(f32[128]{0:T(128)S(1)} %convert_add_fusion), dimensions={2} | broadcast | bytes 4608 | tf_op jit(solution)/shard_map/broadcast_in_dim | solution.py:278
  1.3 7.3 %all-to-all-start = ((f32[8,1,128]{2,1,0:T(1,128)}), f32[8,1,128]{2,1,0:T(1,128)S(1)}, u32[]{:S(2)}, u32[]{:S(2)}) async-start(f32[8,1,128]{2,1,0:T(1,128)} %broadcast_in_dim.13), calls=%async_computation | async-start | bytes 8192 | tf_op jit(solution)/shard_map/all_to_all | solution.py:277
  8.6 0.7 %fusion.row_ref = f32[1,128]{1,0:T(1,128)S(1)} fusion(s32[96]{0:T(128)} %param.9, f32[8]{0:T(128)} %param.10), kind=kLoop, calls=%fused_computation.1 | loop fusion | flops 256 | bytes 928 | tf_op jit(solution)/shard_map/broadcast_in_dim | solution.py:293
  9.3 1.1 %copy-done = bf16[96,4096]{1,0:T(8,128)(2,1)S(1)} copy-done((bf16[96,4096]{1,0:T(8,128)(2,1)S(1)}, bf16[96,4096]{1,0:T(8,128)(2,1)}, u32[]{:S(2)}) %copy-start) | copy-done | bytes 786456
  10.5 1.1 %copy-done.1 = bf16[96,4096]{1,0:T(8,128)(2,1)S(1)} copy-done((bf16[96,4096]{1,0:T(8,128)(2,1)S(1)}, bf16[96,4096]{1,0:T(8,128)(2,1)}, u32[]{:S(2)}) %copy-start.1) | copy-done | bytes 786456
  11.6 0.4 turn.1
  12.0 3.0 %all-to-all-done = f32[8,1,128]{2,1,0:T(1,128)S(1)} async-done(((f32[8,1,128]{2,1,0:T(1,128)}), f32[8,1,128]{2,1,0:T(1,128)S(1)}, u32[]{:S(2)}, u32[]{:S(2)}) %all-to-all-start) | async-done | bytes 4128 | tf_op jit(solution)/shard_map/all_to_all | solution.py:277
  15.0 1.5 %ends.1.after = bf16[2048,128]{1,0:T(8,128)(2,1)} custom-call(f32[8,128]{1,0:T(8,128)S(1)} %bitcast.7, f32[8,128]{1,0:T(8,128)S(1)} %get-tuple-element.20.idrow, bf16[4096,128]{1,0:T(8,128)(2,1)S(1)} %get-tuple-element.21.turned, bf16[128,4096]{1,0:T(8,128)(2,1)S(1)} %get-tuple-element.22.v_ref), custom_call_target="tpu_custom_call" | custom-call | tf_op jit(solution)/shard_map/ends/pallas_call | solution.py:294
  16.5 3.6 %all-to-all-start.1 = ((bf16[8,256,128]{2,1,0:T(8,128)(2,1)}), bf16[8,256,128]{2,1,0:T(8,128)(2,1)S(1)}, u32[]{:S(2)}, u32[]{:S(2)}) async-start(bf16[8,256,128]{2,1,0:T(8,128)(2,1)} %bitcast.2), calls=%async_computation.1 | async-start | bytes 1048576 | tf_op jit(solution)/shard_map/all_to_all | solution.py:306
  20.2 0.4 collective-permute-start
  20.6 1.5 %collective-permute-start.1 = (f32[8,128]{1,0:T(8,128)S(1)}, f32[8,128]{1,0:T(8,128)S(1)}, u32[]{:S(2)}, u32[]{:S(2)}) collective-permute-start(f32[8,128]{1,0:T(8,128)S(1)} %pass.1.facts), channel_id=1, source_target_pairs={{0,16},{8,24},{16,0},{24,8},{1,17},{9,25},{17,1},{25,9},{2,18},{10... | collective-permute-start | bytes 12296 | tf_op jit(solution)/shard_map/ppermute | solution.py:319
  22.1 1.1 %collective-permute-start.2 = (f32[8,128]{1,0:T(8,128)S(1)}, f32[8,128]{1,0:T(8,128)S(1)}, u32[]{:S(2)}, u32[]{:S(2)}) collective-permute-start(f32[8,128]{1,0:T(8,128)S(1)} %pass.1.facts), channel_id=1, source_target_pairs={{0,24},{8,0},{16,8},{24,16},{1,25},{9,1},{17,9},{25,17},{2,26},{10... | collective-permute-start | bytes 12296 | tf_op jit(solution)/shard_map/ppermute | solution.py:319
  23.3 0.9 %collective-permute-done.1.refs_1_ = f32[8,128]{1,0:T(8,128)S(1)} collective-permute-done((f32[8,128]{1,0:T(8,128)S(1)}, f32[8,128]{1,0:T(8,128)S(1)}, u32[]{:S(2)}, u32[]{:S(2)}) %collective-permute-start.1) | collective-permute-done | bytes 4128 | tf_op jit(solution)/shard_map/ppermute | solution.py:319
  24.2 0.3 collective-permute-done.2.refs_2_
  24.7 4.7 %all-to-all-done.1.in_ref = bf16[8,256,128]{2,1,0:T(8,128)(2,1)S(1)} async-done(((bf16[8,256,128]{2,1,0:T(8,128)(2,1)}), bf16[8,256,128]{2,1,0:T(8,128)(2,1)S(1)}, u32[]{:S(2)}, u32[]{:S(2)}) %all-to-all-start.1) | async-done | bytes 524320 | tf_op jit(solution)/shard_map/all_to_all | solution.py:306
  29.5 3.4 %collective-permute-start.5 = (bf16[256,128]{1,0:T(8,128)(2,1)S(1)}, bf16[256,128]{1,0:T(8,128)(2,1)S(1)}, u32[]{:S(2)}, u32[]{:S(2)}) collective-permute-start(bf16[256,128]{1,0:T(8,128)(2,1)S(1)} %get-tuple-element.31), channel_id=1, source_target_pairs={{0,16},{1,17},{2,18},{3,19},{4,20},{5,21},{6,22},{7,23},{8,24},{9,... | collective-permute-start | bytes 196616 | tf_op jit(solution)/shard_map/ppermute | solution.py:348
  33.0 1.3 %collective-permute-start.6 = (bf16[256,128]{1,0:T(8,128)(2,1)S(1)}, bf16[256,128]{1,0:T(8,128)(2,1)S(1)}, u32[]{:S(2)}, u32[]{:S(2)}) collective-permute-start(bf16[256,128]{1,0:T(8,128)(2,1)S(1)} %get-tuple-element.31), channel_id=1, source_target_pairs={{0,20},{1,21},{2,22},{3,23},{4,16},{5,17},{6,18},{7,19},{8,28},{9,... | collective-permute-start | bytes 196616 | tf_op jit(solution)/shard_map/ppermute | solution.py:349
  34.3 2.4 %collective-permute-start.3 = (bf16[1,256,128]{2,1,0:T(8,128)(2,1)S(1)}, bf16[1,256,128]{2,1,0:T(8,128)(2,1)S(1)}, u32[]{:S(2)}, u32[]{:S(2)}) collective-permute-start(bf16[1,256,128]{2,1,0:T(8,128)(2,1)S(1)} %get-tuple-element.28.after), channel_id=1, source_target_pairs={{0,4},{1,5},{2,6},{3,7},{4,0},{5,1},{6,2},{7,3},{8,12},{9,13},{10,... | collective-permute-start | bytes 196616 | tf_op jit(solution)/shard_map/ppermute | solution.py:346
  36.7 2.5 %collective-permute-start.4 = (bf16[1,256,128]{2,1,0:T(8,128)(2,1)S(1)}, bf16[1,256,128]{2,1,0:T(8,128)(2,1)S(1)}, u32[]{:S(2)}, u32[]{:S(2)}) collective-permute-start(bf16[1,256,128]{2,1,0:T(8,128)(2,1)S(1)} %get-tuple-element.30), channel_id=1, source_target_pairs={{0,4},{1,5},{2,6},{3,7},{8,12},{9,13},{10,14},{11,15},{16,20},{17,... | collective-permute-start | bytes 196616 | tf_op jit(solution)/shard_map/ppermute | solution.py:347
  39.2 1.3 %inner.1 = (f32[96,4096]{1,0:T(8,128)S(1)}, f32[1,4096]{1,0:T(1,128)S(1)}) custom-call(f32[8,128]{1,0:T(8,128)S(1)} %bitcast.9, f32[96,128]{1,0:T(8,128)S(1)} %get-tuple-element.19.idcol, f32[8,128]{1,0:T(8,128)S(1)} %get-tuple-element.20.idrow, bf16[96,4096]{1,0:T(8,128)(2,1)S(1)} %copy-done.3, bf16[4096,128]{1,0:T(8,128)(2,1)S(1)} %get-tuple-element.21.turned, ...), custom_call_target="tpu_custom_call" | custom-call | flops 8000000000 | bytes 4000000 | tf_op jit(solution)/shard_map/inner/pallas_call | solution.py:350
  40.5 2.4 %collective-permute-done.3.early = bf16[1,256,128]{2,1,0:T(8,128)(2,1)S(1)} collective-permute-done((bf16[1,256,128]{2,1,0:T(8,128)(2,1)S(1)}, bf16[1,256,128]{2,1,0:T(8,128)(2,1)S(1)}, u32[]{:S(2)}, u32[]{:S(2)}) %collective-permute-start.3) | collective-permute-done | bytes 65568 | tf_op jit(solution)/shard_map/ppermute | solution.py:346
  43.1 11.8 %all_to_all.18 = bf16[8,256,128]{2,1,0:T(8,128)(2,1)S(1)} all-to-all(bf16[8,256,128]{2,1,0:T(8,128)(2,1)S(1)} %scan.1), channel_id=1, replica_groups={{0,1,2,3,8,9,10,11},{4,5,6,7,12,13,14,15},{16,17,18,19,24,25,26,27},{20..., dimensions={0} | all-to-all | bytes 1048576 | tf_op jit(solution)/shard_map/all_to_all | solution.py:369
  54.9 1.9 %norm.1 = bf16[96,4096]{1,0:T(8,128)(2,1)} custom-call(f32[96,128]{1,0:T(8,128)S(1)} %get-tuple-element.19.idcol, f32[1,128]{1,0:T(1,128)S(1)} %get-tuple-element.23.before, f32[1,4096]{1,0:T(1,128)S(1)} %get-tuple-element.29.after.rates, bf16[96,4096]{1,0:T(8,128)(2,1)S(1)} %copy-done.3, bf16[2048,128]{1,0:T(8,128)(2,1)S(1)} %bitcast.6, ...), custom_call_target="tpu_custom_call" | custom-call | tf_op jit(solution)/shard_map/norm/pallas_call | solution.py:372
  (16 shorter events, 0.6 us)
Async XLA Ops:
  1.3 13.6 %all-to-all-start = ((f32[8,1,128]{2,1,0:T(1,128)}), f32[8,1,128]{2,1,0:T(1,128)S(1)}, u32[]{:S(2)}, u32[]{:S(2)}) async-start(f32[8,1,128]{2,1,0:T(1,128)} %broadcast_in_dim.13), calls=%async_computation | async-start | bytes 8192 | tf_op jit(solution)/shard_map/all_to_all | solution.py:277
  9.3 1.1 %copy-start = (bf16[96,4096]{1,0:T(8,128)(2,1)S(1)}, bf16[96,4096]{1,0:T(8,128)(2,1)}, u32[]{:S(2)}) copy-start(bf16[96,4096]{1,0:T(8,128)(2,1)} %k_ref.1) | copy-start | bytes 2359300
  10.5 1.1 %copy-start.1 = (bf16[96,4096]{1,0:T(8,128)(2,1)S(1)}, bf16[96,4096]{1,0:T(8,128)(2,1)}, u32[]{:S(2)}) copy-start(bf16[96,4096]{1,0:T(8,128)(2,1)} %v_ref.3) | copy-start | bytes 2359300
  16.5 22.7 %copy-start.2 = (bf16[96,4096]{1,0:T(8,128)(2,1)S(1)}, bf16[96,4096]{1,0:T(8,128)(2,1)}, u32[]{:S(2)}) copy-start(bf16[96,4096]{1,0:T(8,128)(2,1)} %v_ref.3) | copy-start | bytes 2359300
  16.5 22.7 %copy-start.3 = (bf16[96,4096]{1,0:T(8,128)(2,1)S(1)}, bf16[96,4096]{1,0:T(8,128)(2,1)}, u32[]{:S(2)}) copy-start(bf16[96,4096]{1,0:T(8,128)(2,1)} %q_ref.3) | copy-start | bytes 2359300
  16.5 12.8 %all-to-all-start.1 = ((bf16[8,256,128]{2,1,0:T(8,128)(2,1)}), bf16[8,256,128]{2,1,0:T(8,128)(2,1)S(1)}, u32[]{:S(2)}, u32[]{:S(2)}) async-start(bf16[8,256,128]{2,1,0:T(8,128)(2,1)} %bitcast.2), calls=%async_computation.1 | async-start | bytes 1048576 | tf_op jit(solution)/shard_map/all_to_all | solution.py:306
  20.2 3.1 %collective-permute-start = (f32[8,128]{1,0:T(8,128)S(1)}, f32[8,128]{1,0:T(8,128)S(1)}, u32[]{:S(2)}, u32[]{:S(2)}) collective-permute-start(f32[8,128]{1,0:T(8,128)S(1)} %pass.1.facts), channel_id=1, source_target_pairs={{0,8},{8,16},{16,24},{24,0},{1,9},{9,17},{17,25},{25,1},{2,10},{10... | collective-permute-start | bytes 12296 | tf_op jit(solution)/shard_map/ppermute | solution.py:319
  20.6 3.6 %collective-permute-start.1 = (f32[8,128]{1,0:T(8,128)S(1)}, f32[8,128]{1,0:T(8,128)S(1)}, u32[]{:S(2)}, u32[]{:S(2)}) collective-permute-start(f32[8,128]{1,0:T(8,128)S(1)} %pass.1.facts), channel_id=1, source_target_pairs={{0,16},{8,24},{16,0},{24,8},{1,17},{9,25},{17,1},{25,9},{2,18},{10... | collective-permute-start | bytes 12296 | tf_op jit(solution)/shard_map/ppermute | solution.py:319
  22.1 2.4 %collective-permute-start.2 = (f32[8,128]{1,0:T(8,128)S(1)}, f32[8,128]{1,0:T(8,128)S(1)}, u32[]{:S(2)}, u32[]{:S(2)}) collective-permute-start(f32[8,128]{1,0:T(8,128)S(1)} %pass.1.facts), channel_id=1, source_target_pairs={{0,24},{8,0},{16,8},{24,16},{1,25},{9,1},{17,9},{25,17},{2,26},{10... | collective-permute-start | bytes 12296 | tf_op jit(solution)/shard_map/ppermute | solution.py:319
  29.5 13.4 %collective-permute-start.5 = (bf16[256,128]{1,0:T(8,128)(2,1)S(1)}, bf16[256,128]{1,0:T(8,128)(2,1)S(1)}, u32[]{:S(2)}, u32[]{:S(2)}) collective-permute-start(bf16[256,128]{1,0:T(8,128)(2,1)S(1)} %get-tuple-element.31), channel_id=1, source_target_pairs={{0,16},{1,17},{2,18},{3,19},{4,20},{5,21},{6,22},{7,23},{8,24},{9,... | collective-permute-start | bytes 196616 | tf_op jit(solution)/shard_map/ppermute | solution.py:348
  33.0 9.9 %collective-permute-start.6 = (bf16[256,128]{1,0:T(8,128)(2,1)S(1)}, bf16[256,128]{1,0:T(8,128)(2,1)S(1)}, u32[]{:S(2)}, u32[]{:S(2)}) collective-permute-start(bf16[256,128]{1,0:T(8,128)(2,1)S(1)} %get-tuple-element.31), channel_id=1, source_target_pairs={{0,20},{1,21},{2,22},{3,23},{4,16},{5,17},{6,18},{7,19},{8,28},{9,... | collective-permute-start | bytes 196616 | tf_op jit(solution)/shard_map/ppermute | solution.py:349
  34.3 8.6 %collective-permute-start.3 = (bf16[1,256,128]{2,1,0:T(8,128)(2,1)S(1)}, bf16[1,256,128]{2,1,0:T(8,128)(2,1)S(1)}, u32[]{:S(2)}, u32[]{:S(2)}) collective-permute-start(bf16[1,256,128]{2,1,0:T(8,128)(2,1)S(1)} %get-tuple-element.28.after), channel_id=1, source_target_pairs={{0,4},{1,5},{2,6},{3,7},{4,0},{5,1},{6,2},{7,3},{8,12},{9,13},{10,... | collective-permute-start | bytes 196616 | tf_op jit(solution)/shard_map/ppermute | solution.py:346
  36.7 6.2 %collective-permute-start.4 = (bf16[1,256,128]{2,1,0:T(8,128)(2,1)S(1)}, bf16[1,256,128]{2,1,0:T(8,128)(2,1)S(1)}, u32[]{:S(2)}, u32[]{:S(2)}) collective-permute-start(bf16[1,256,128]{2,1,0:T(8,128)(2,1)S(1)} %get-tuple-element.30), channel_id=1, source_target_pairs={{0,4},{1,5},{2,6},{3,7},{8,12},{9,13},{10,14},{11,15},{16,20},{17,... | collective-permute-start | bytes 196616 | tf_op jit(solution)/shard_map/ppermute | solution.py:347
  40.5 14.5 %copy-start.4 = (f32[4096]{0:T(1024)S(1)}, f32[4096]{0:T(1024)}, u32[]{:S(2)}) copy-start(f32[4096]{0:T(1024)} %param.11) | copy-start | bytes 49156

commit v18 on v14

--- a/solution.py
+++ b/solution.py
@@ -42,8 +42,11 @@
         turned[columns, :] = jnp.transpose(block).astype(turned.dtype)
 
 
-def ends_kernel(here, tokens, facts, idrow, turned, v_ref, out_ref, made, sems):
+def ends_kernel(here, tokens, stored, idrow, turned, v_ref, out_ref, facts, made, sems):
     width = v_ref.shape[1]
+    members = facts.shape[0]
+    for u in range(members):
+        facts[u : u + 1, :] = stored[members - 1 - u : members - u, :]
     lane = lax.broadcasted_iota(jnp.int32, (HD, LANES), 1)
     place = lax.broadcasted_iota(jnp.int32, idrow.shape, 1)
     ids = idrow[...]
@@ -55,7 +58,7 @@
     for j in range(0, width // LANES, 2):
         weighted = []
         for head in range(2 * j, 2 * j + 4):
-            weight = jnp.exp(-rate_of(facts, head, here) * age)
+            weight = jnp.exp(-rate_of(stored, (members - 1) * here + 2 * (head % here) - head, here) * age)
             keys = turned[head * HD : (head + 1) * HD, :].astype(jnp.float32)
             keys = keys.reshape(HD // 8, 8, LANES) * weight[None]
             weighted.append(keys.reshape(HD, LANES))
@@ -260,8 +263,10 @@
     own = jnp.pad(decay_rate, (0, LANES - here)) + jnp.pad(
         doc_ids, (LANES - tokens, 0)
     ).astype(jnp.float32)
-    facts = lax.all_to_all(
-        jnp.broadcast_to(own[None, :], tile.shape), "uly", split_axis=0, concat_axis=0, tiled=True
+    backward = [list(range(members))[::-1]]
+    stored = lax.all_to_all(
+        jnp.broadcast_to(own[None, :], tile.shape),
+        "uly", split_axis=0, concat_axis=0, axis_index_groups=backward, tiled=True,
     )
     turned, filled, idrow, idcol = pl.pallas_call(
         turn_kernel,
@@ -277,18 +282,18 @@
         cost_estimate=pl.CostEstimate(flops=0, bytes_accessed=12_000_000, transcendentals=0),
         name="turn",
     )(own[None, :], keys, values)
-    ends = pl.pallas_call(
+    ends, facts = pl.pallas_call(
         functools.partial(ends_kernel, here, tokens),
         in_specs=[vmem] * 4,
-        out_specs=pl.BlockSpec(memory_space=pl.ANY),
-        out_shape=shape((all_pairs * HD, LANES), jnp.bfloat16),
+        out_specs=[pl.BlockSpec(memory_space=pl.ANY), vmem],
+        out_shape=[shape((all_pairs * HD, LANES), jnp.bfloat16), tile],
         scratch_shapes=[
             pltpu.VMEM((all_pairs * HD, LANES), jnp.bfloat16),
             pltpu.SemaphoreType.DMA((8,)),
         ],
         compiler_params=params,
         name="ends",
-    )(facts, idrow, turned, filled)
+    )(stored, idrow, turned, filled)
     pieces = lax.all_to_all(
         ends.reshape(group, rows, LANES),
         axes, split_axis=0, concat_axis=0, axis_index_groups=groups, tiled=True,

time: 52 us -> 52 us (level)
  waiting for transfers between devices: 10.4 us -> 7.46 us
  starting transfers between devices: 19.2 us -> 21.2 us
  blocking collectives: 12 us -> 12.9 us
    all_to_all x1, waiting for transfers between devices: 2.97 us -> 0.01 us  [local(): lax.all_to_all(jnp.broadcast_to(own[None, :], tile.shape), 'uly', split_a...]
    all_to_all x1, starting transfers between devices: 7.25 us -> 9.23 us  [local(): lax.all_to_all(jnp.broadcast_to(own[None, :], tile.shape), 'uly', split_a...]
    ppermute x1, starting transfers between devices: 1.25 us -> 2.43 us  [local(): early = lax.ppermute(early_ends, axes, swap)]
    ppermute x1, starting transfers between devices: 3.63 us -> 2.45 us  [local(): lax.ppermute(final_end, axes, [(low, high) for low, high in swap if low <...]
    all_to_all x1, blocking collectives: 12 us -> 12.9 us  [local(): lax.all_to_all(moved, axes, split_axis=0, concat_axis=0, axis_index_group...]
  transfers between devices with their start and end apart: 7 -> 7, of which waited for: 6 -> 5; matrix products, arithmetic and copies ran while one was open for 1% -> 1% of each run, Pallas kernels for 3% -> 3%
where the time goes in v18:
time: 52 us; the launch traced here: 51.5 us
  starting transfers between devices  21.2 us (41%)
  blocking collectives  12.9 us (25%)
  waiting for transfers between devices  7.46 us (14%)
  Pallas kernels  5.5 us (11%)
  local copies, waits for them, and re-layouts  2.88 us (6%)
  other arithmetic  1.49 us (3%)
    all_to_all x1, blocking collectives, local(): lax.all_to_all(moved, axes, split_axis=0, concat_axis=0, axis_index_group...  12.9 us
    all_to_all x1, starting transfers between devices, local(): lax.all_to_all(jnp.broadcast_to(own[None, :], tile.shape), 'uly', split_a...  9.23 us
    ppermute x3, waiting for transfers between devices, local(): lax.ppermute(slice_facts, 'ctx', [(c, (c + ahead) % slices) for c in rang...  4.21 us
    all_to_all x1, starting transfers between devices, local(): lax.all_to_all(ends.reshape(group, rows, LANES), axes, split_axis=0, conc...  3.72 us
    ppermute x3, starting transfers between devices, local(): lax.ppermute(slice_facts, 'ctx', [(c, (c + ahead) % slices) for c in rang...  3.37 us
    ppermute x1, starting transfers between devices, local(): lax.ppermute(final_end, axes, [(low, high) for low, high in swap if low <...  2.45 us
    ppermute x1, starting transfers between devices, local(): early = lax.ppermute(early_ends, axes, swap)  2.43 us
    unnamed x10, local copies, waits for them, and re-layouts  2.28 us
  transfers between devices with their start and end apart: 7, of which 5 were waited for; matrix products, arithmetic and copies ran while one was open for 1% of the time, Pallas kernels for 3%

profile of v18, /device:TPU:0, one launch (start us, length us, event | category | flops | bytes accessed | tf_op | source)
XLA Modules:
  0.0 51.5 jit_solution(10941405405959472628)
XLA Ops:
  0.0 0.7 %convert_add_fusion = f32[128]{0:T(128)S(1)} fusion(s32[96]{0:T(128)} %param.9, f32[8]{0:T(128)} %param.10), kind=kLoop, calls=%fused_computation | loop fusion | flops 256 | bytes 928 | tf_op jit(solution)/shard_map/add | solution.py:263
  0.7 0.6 %broadcast_in_dim.13 = f32[8,1,128]{2,1,0:T(1,128)} broadcast(f32[128]{0:T(128)S(1)} %convert_add_fusion), dimensions={2} | broadcast | bytes 4608 | tf_op jit(solution)/shard_map/broadcast_in_dim | solution.py:268
  1.3 9.2 %all-to-all-start = ((f32[8,1,128]{2,1,0:T(1,128)}), f32[8,1,128]{2,1,0:T(1,128)S(1)}, u32[]{:S(2)}, u32[]{:S(2)}) async-start(f32[8,1,128]{2,1,0:T(1,128)} %broadcast_in_dim.13), calls=%async_computation | async-start | bytes 8192 | tf_op jit(solution)/shard_map/all_to_all | solution.py:267
  10.6 0.7 %fusion.row_ref = f32[1,128]{1,0:T(1,128)S(1)} fusion(s32[96]{0:T(128)} %param.9, f32[8]{0:T(128)} %param.10), kind=kLoop, calls=%fused_computation.1 | loop fusion | flops 256 | bytes 928 | tf_op jit(solution)/shard_map/broadcast_in_dim | solution.py:284
  11.3 1.1 %copy-done = bf16[96,4096]{1,0:T(8,128)(2,1)S(1)} copy-done((bf16[96,4096]{1,0:T(8,128)(2,1)S(1)}, bf16[96,4096]{1,0:T(8,128)(2,1)}, u32[]{:S(2)}) %copy-start) | copy-done | bytes 786456
  12.5 1.1 %copy-done.1 = bf16[96,4096]{1,0:T(8,128)(2,1)S(1)} copy-done((bf16[96,4096]{1,0:T(8,128)(2,1)S(1)}, bf16[96,4096]{1,0:T(8,128)(2,1)}, u32[]{:S(2)}) %copy-start.1) | copy-done | bytes 786456
  13.6 0.4 turn.1
  14.0 1.5 %ends.1 = (bf16[2048,128]{1,0:T(8,128)(2,1)}, f32[8,128]{1,0:T(8,128)S(1)}) custom-call(f32[8,128]{1,0:T(8,128)S(1)} %bitcast.8, f32[8,128]{1,0:T(8,128)S(1)} %get-tuple-element.21.idrow, bf16[4096,128]{1,0:T(8,128)(2,1)S(1)} %get-tuple-element.22.turned, bf16[128,4096]{1,0:T(8,128)(2,1)S(1)} %get-tuple-element.23.v_ref), custom_call_target="tpu_custom_call" | custom-call | tf_op jit(solution)/shard_map/ends/pallas_call | solution.py:285
  15.5 3.7 %all-to-all-start.1 = ((bf16[16,128,128]{2,1,0:T(8,128)(2,1)}), bf16[16,128,128]{2,1,0:T(8,128)(2,1)S(1)}, u32[]{:S(2)}, u32[]{:S(2)}) async-start(bf16[16,128,128]{2,1,0:T(8,128)(2,1)} %bitcast.2), calls=%async_computation.1 | async-start | bytes 1048576 | tf_op jit(solution)/shard_map/all_to_all | solution.py:297
  19.3 0.4 collective-permute-start
  19.6 1.7 %collective-permute-start.1 = (f32[8,128]{1,0:T(8,128)S(1)}, f32[8,128]{1,0:T(8,128)S(1)}, u32[]{:S(2)}, u32[]{:S(2)}) collective-permute-start(f32[8,128]{1,0:T(8,128)S(1)} %pass.1.facts), channel_id=1, source_target_pairs={{0,16},{8,24},{16,0},{24,8},{1,17},{9,25},{17,1},{25,9},{2,18},{10... | collective-permute-start | bytes 12296 | tf_op jit(solution)/shard_map/ppermute | solution.py:310
  21.3 1.3 %collective-permute-start.2 = (f32[8,128]{1,0:T(8,128)S(1)}, f32[8,128]{1,0:T(8,128)S(1)}, u32[]{:S(2)}, u32[]{:S(2)}) collective-permute-start(f32[8,128]{1,0:T(8,128)S(1)} %pass.1.facts), channel_id=1, source_target_pairs={{0,24},{8,0},{16,8},{24,16},{1,25},{9,1},{17,9},{25,17},{2,26},{10... | collective-permute-start | bytes 12296 | tf_op jit(solution)/shard_map/ppermute | solution.py:310
  22.6 3.2 %collective-permute-done.refs_0_ = f32[8,128]{1,0:T(8,128)S(1)} collective-permute-done((f32[8,128]{1,0:T(8,128)S(1)}, f32[8,128]{1,0:T(8,128)S(1)}, u32[]{:S(2)}, u32[]{:S(2)}) %collective-permute-start) | collective-permute-done | bytes 4128 | tf_op jit(solution)/shard_map/ppermute | solution.py:310
  25.8 1.0 %collective-permute-done.1.refs_1_ = f32[8,128]{1,0:T(8,128)S(1)} collective-permute-done((f32[8,128]{1,0:T(8,128)S(1)}, f32[8,128]{1,0:T(8,128)S(1)}, u32[]{:S(2)}, u32[]{:S(2)}) %collective-permute-start.1) | collective-permute-done | bytes 4128 | tf_op jit(solution)/shard_map/ppermute | solution.py:310
  27.0 1.5 %all-to-all-done.1.in_ref = bf16[16,128,128]{2,1,0:T(8,128)(2,1)S(1)} async-done(((bf16[16,128,128]{2,1,0:T(8,128)(2,1)}), bf16[16,128,128]{2,1,0:T(8,128)(2,1)S(1)}, u32[]{:S(2)}, u32[]{:S(2)}) %all-to-all-start.1) | async-done | bytes 524320 | tf_op jit(solution)/shard_map/all_to_all | solution.py:297
  28.5 0.1 half.1
  28.6 2.4 %collective-permute-start.3 = (bf16[3,128,128]{2,1,0:T(8,128)(2,1)S(1)}, bf16[3,128,128]{2,1,0:T(8,128)(2,1)S(1)}, u32[]{:S(2)}, u32[]{:S(2)}) collective-permute-start(bf16[3,128,128]{2,1,0:T(8,128)(2,1)S(1)} %get-tuple-element.29.after), channel_id=1, source_target_pairs={{0,4},{1,5},{2,6},{3,7},{4,0},{5,1},{6,2},{7,3},{8,12},{9,13},{10,... | collective-permute-start | bytes 294920 | tf_op jit(solution)/shard_map/ppermute | solution.py:335
  31.0 2.5 %collective-permute-start.4 = (bf16[1,128,128]{2,1,0:T(8,128)(2,1)S(1)}, bf16[1,128,128]{2,1,0:T(8,128)(2,1)S(1)}, u32[]{:S(2)}, u32[]{:S(2)}) collective-permute-start(bf16[1,128,128]{2,1,0:T(8,128)(2,1)S(1)} %get-tuple-element.33), channel_id=1, source_target_pairs={{0,4},{1,5},{2,6},{3,7},{8,12},{9,13},{10,14},{11,15},{16,20},{17,... | collective-permute-start | bytes 98312 | tf_op jit(solution)/shard_map/ppermute | solution.py:336
  33.5 1.3 %inner.1 = (f32[96,4096]{1,0:T(8,128)S(1)}, f32[1,4096]{1,0:T(1,128)S(1)}) custom-call(f32[8,128]{1,0:T(8,128)S(1)} %get-tuple-element.24.facts, f32[96,128]{1,0:T(8,128)S(1)} %get-tuple-element.20.idcol, f32[8,128]{1,0:T(8,128)S(1)} %get-tuple-element.21.idrow, bf16[96,4096]{1,0:T(8,128)(2,1)S(1)} %copy-done.3, ...), custom_call_target="tpu_custom_call" | custom-call | flops 8000000000 | bytes 4000000 | tf_op jit(solution)/shard_map/inner/pallas_call | solution.py:337
  34.8 0.3 collective-permute-done.4.final
  35.1 1.5 %collective-permute-done.3.early = bf16[3,128,128]{2,1,0:T(8,128)(2,1)S(1)} collective-permute-done((bf16[3,128,128]{2,1,0:T(8,128)(2,1)S(1)}, bf16[3,128,128]{2,1,0:T(8,128)(2,1)S(1)}, u32[]{:S(2)}, u32[]{:S(2)}) %collective-permute-start.3) | collective-permute-done | bytes 98336 | tf_op jit(solution)/shard_map/ppermute | solution.py:335
  36.5 0.2 scan.1
  36.8 12.9 %all_to_all.18 = bf16[16,128,128]{2,1,0:T(8,128)(2,1)S(1)} all-to-all(bf16[16,128,128]{2,1,0:T(8,128)(2,1)S(1)} %scan.1), channel_id=1, replica_groups={{0,1,2,3,8,9,10,11,16,17,18,19,24,25,26,27},{4,5,6,7,12,13,14,15,20,21,..., dimensions={0} | all-to-all | bytes 1048576 | tf_op jit(solution)/shard_map/all_to_all | solution.py:356
  49.7 1.9 %norm.1 = bf16[96,4096]{1,0:T(8,128)(2,1)} custom-call(f32[96,128]{1,0:T(8,128)S(1)} %get-tuple-element.20.idcol, f32[1,128]{1,0:T(1,128)S(1)} %get-tuple-element.26.before, f32[1,4096]{1,0:T(1,128)S(1)} %get-tuple-element.30.after.rates, bf16[96,4096]{1,0:T(8,128)(2,1)S(1)} %copy-done.3, bf16[2048,128]{1,0:T(8,128)(2,1)S(1)} %bitcast.6, ...), custom_call_target="tpu_custom_call" | custom-call | tf_op jit(solution)/shard_map/norm/pallas_call | solution.py:359
  (12 shorter events, 0.1 us)
Async XLA Ops:
  1.3 12.7 %all-to-all-start = ((f32[8,1,128]{2,1,0:T(1,128)}), f32[8,1,128]{2,1,0:T(1,128)S(1)}, u32[]{:S(2)}, u32[]{:S(2)}) async-start(f32[8,1,128]{2,1,0:T(1,128)} %broadcast_in_dim.13), calls=%async_computation | async-start | bytes 8192 | tf_op jit(solution)/shard_map/all_to_all | solution.py:267
  11.3 1.1 %copy-start = (bf16[96,4096]{1,0:T(8,128)(2,1)S(1)}, bf16[96,4096]{1,0:T(8,128)(2,1)}, u32[]{:S(2)}) copy-start(bf16[96,4096]{1,0:T(8,128)(2,1)} %k_ref.1) | copy-start | bytes 2359300
  12.5 1.1 %copy-start.1 = (bf16[96,4096]{1,0:T(8,128)(2,1)S(1)}, bf16[96,4096]{1,0:T(8,128)(2,1)}, u32[]{:S(2)}) copy-start(bf16[96,4096]{1,0:T(8,128)(2,1)} %v_ref.3) | copy-start | bytes 2359300
  15.5 18.0 %copy-start.2 = (bf16[96,4096]{1,0:T(8,128)(2,1)S(1)}, bf16[96,4096]{1,0:T(8,128)(2,1)}, u32[]{:S(2)}) copy-start(bf16[96,4096]{1,0:T(8,128)(2,1)} %v_ref.3) | copy-start | bytes 2359300
  15.5 18.0 %copy-start.3 = (bf16[96,4096]{1,0:T(8,128)(2,1)S(1)}, bf16[96,4096]{1,0:T(8,128)(2,1)}, u32[]{:S(2)}) copy-start(bf16[96,4096]{1,0:T(8,128)(2,1)} %q_ref.3) | copy-start | bytes 2359300
  15.5 12.9 %all-to-all-start.1 = ((bf16[16,128,128]{2,1,0:T(8,128)(2,1)}), bf16[16,128,128]{2,1,0:T(8,128)(2,1)S(1)}, u32[]{:S(2)}, u32[]{:S(2)}) async-start(bf16[16,128,128]{2,1,0:T(8,128)(2,1)} %bitcast.2), calls=%async_computation.1 | async-start | bytes 1048576 | tf_op jit(solution)/shard_map/all_to_all | solution.py:297
  19.3 6.5 %collective-permute-start = (f32[8,128]{1,0:T(8,128)S(1)}, f32[8,128]{1,0:T(8,128)S(1)}, u32[]{:S(2)}, u32[]{:S(2)}) collective-permute-start(f32[8,128]{1,0:T(8,128)S(1)} %pass.1.facts), channel_id=1, source_target_pairs={{0,8},{8,16},{16,24},{24,0},{1,9},{9,17},{17,25},{25,1},{2,10},{10... | collective-permute-start | bytes 12296 | tf_op jit(solution)/shard_map/ppermute | solution.py:310
  19.6 7.2 %collective-permute-start.1 = (f32[8,128]{1,0:T(8,128)S(1)}, f32[8,128]{1,0:T(8,128)S(1)}, u32[]{:S(2)}, u32[]{:S(2)}) collective-permute-start(f32[8,128]{1,0:T(8,128)S(1)} %pass.1.facts), channel_id=1, source_target_pairs={{0,16},{8,24},{16,0},{24,8},{1,17},{9,25},{17,1},{25,9},{2,18},{10... | collective-permute-start | bytes 12296 | tf_op jit(solution)/shard_map/ppermute | solution.py:310
  21.3 5.5 %collective-permute-start.2 = (f32[8,128]{1,0:T(8,128)S(1)}, f32[8,128]{1,0:T(8,128)S(1)}, u32[]{:S(2)}, u32[]{:S(2)}) collective-permute-start(f32[8,128]{1,0:T(8,128)S(1)} %pass.1.facts), channel_id=1, source_target_pairs={{0,24},{8,0},{16,8},{24,16},{1,25},{9,1},{17,9},{25,17},{2,26},{10... | collective-permute-start | bytes 12296 | tf_op jit(solution)/shard_map/ppermute | solution.py:310
  28.6 7.9 %collective-permute-start.3 = (bf16[3,128,128]{2,1,0:T(8,128)(2,1)S(1)}, bf16[3,128,128]{2,1,0:T(8,128)(2,1)S(1)}, u32[]{:S(2)}, u32[]{:S(2)}) collective-permute-start(bf16[3,128,128]{2,1,0:T(8,128)(2,1)S(1)} %get-tuple-element.29.after), channel_id=1, source_target_pairs={{0,4},{1,5},{2,6},{3,7},{4,0},{5,1},{6,2},{7,3},{8,12},{9,13},{10,... | collective-permute-start | bytes 294920 | tf_op jit(solution)/shard_map/ppermute | solution.py:335
  31.0 4.0 %collective-permute-start.4 = (bf16[1,128,128]{2,1,0:T(8,128)(2,1)S(1)}, bf16[1,128,128]{2,1,0:T(8,128)(2,1)S(1)}, u32[]{:S(2)}, u32[]{:S(2)}) collective-permute-start(bf16[1,128,128]{2,1,0:T(8,128)(2,1)S(1)} %get-tuple-element.33), channel_id=1, source_target_pairs={{0,4},{1,5},{2,6},{3,7},{8,12},{9,13},{10,14},{11,15},{16,20},{17,... | collective-permute-start | bytes 98312 | tf_op jit(solution)/shard_map/ppermute | solution.py:336
  34.8 14.9 %copy-start.4 = (f32[4096]{0:T(1024)S(1)}, f32[4096]{0:T(1024)}, u32[]{:S(2)}) copy-start(f32[4096]{0:T(1024)} %param.11) | copy-start | bytes 49156

commit v19 on v14

--- a/solution.py
+++ b/solution.py
@@ -27,12 +27,8 @@
     return jnp.where(lane < HD, rates[0], rates[1])
 
 
-def turn_kernel(row_ref, k_ref, v_ref, turned, filled, idrow, idcol):
+def turn_kernel(k_ref, v_ref, turned, filled):
     tokens, width = k_ref.shape
-    fill = jnp.full((1, LANES - tokens), -1.0, jnp.float32)
-    row = jnp.concatenate([row_ref[:1, LANES - tokens :], fill], 1)
-    idrow[...] = jnp.broadcast_to(row, idrow.shape)
-    idcol[...] = jnp.transpose(jnp.broadcast_to(row, (LANES, LANES)))[:tokens]
     filled[:tokens, :] = v_ref[...]
     filled[tokens:, :] = jnp.zeros((LANES - tokens, width), filled.dtype)
     blank = jnp.zeros((LANES - tokens, LANES), jnp.float32)
@@ -42,20 +38,29 @@
         turned[columns, :] = jnp.transpose(block).astype(turned.dtype)
 
 
-def ends_kernel(here, tokens, facts, idrow, turned, v_ref, out_ref, made, sems):
+def own_ids(stored, tokens):
+    at = stored.shape[0] - 1 - lax.axis_index("uly")
+    row = stored[pl.ds(at, 1), :]
+    fill = jnp.full((1, LANES - tokens), -1.0, jnp.float32)
+    return jnp.concatenate([row[:, LANES - tokens :], fill], 1)
+
+
+def ends_kernel(here, tokens, group, stored, turned, v_ref, out_ref, made, sems):
     width = v_ref.shape[1]
+    members = stored.shape[0]
     lane = lax.broadcasted_iota(jnp.int32, (HD, LANES), 1)
-    place = lax.broadcasted_iota(jnp.int32, idrow.shape, 1)
-    ids = idrow[...]
+    ids = jnp.broadcast_to(own_ids(stored, tokens), (8, LANES))
+    place = lax.broadcasted_iota(jnp.int32, ids.shape, 1)
     last = ids[:, tokens - 1 : tokens]
     age = jnp.where(ids == last, (tokens - 1 - place).astype(jnp.float32), NEVER)
+    rows_each = made.shape[0] // group
     parts = sems.shape[0]
     share = made.shape[0] // parts
     copies = []
     for j in range(0, width // LANES, 2):
         weighted = []
         for head in range(2 * j, 2 * j + 4):
-            weight = jnp.exp(-rate_of(facts, head, here) * age)
+            weight = jnp.exp(-rate_of(stored, (members - 1) * here + 2 * (head % here) - head, here) * age)
             keys = turned[head * HD : (head + 1) * HD, :].astype(jnp.float32)
             keys = keys.reshape(HD // 8, 8, LANES) * weight[None]
             weighted.append(keys.reshape(HD, LANES))
@@ -70,11 +75,14 @@
         )
         for one in (0, 1):
             pair = both[one * LANES : (one + 1) * LANES, one * LANES : (one + 1) * LANES]
-            made[(j + one) * HD : (j + one + 1) * HD, :] = jnp.where(
-                lane < HD, pair[:HD], pair[HD:]
-            ).astype(jnp.bfloat16)
+            state = jnp.where(lane < HD, pair[:HD], pair[HD:])
+            size = min(rows_each, HD)
+            for at in range(0, HD, size):
+                owner, start = divmod((j + one) * HD + at, rows_each)
+                start += (group - 1 - owner) * rows_each
+                made[start : start + size, :] = state[at : at + size].astype(jnp.bfloat16)
         if (j + 2) * HD % share == 0:
-            part = (j + 2) * HD // share - 1
+            part = parts - (j + 2) * HD // share
             rows = slice(part * share, (part + 1) * share)
             copies.append(pltpu.make_async_copy(made.at[rows], out_ref.at[rows], sems.at[part]))
             copies[-1].start()
@@ -106,8 +114,13 @@
         rates_ref[:, columns] = jnp.where(lane[:1] < HD, rates[0], rates[1])
 
 
-def pass_kernel(facts, after, out_ref):
-    out_ref[...] = facts[...]
+def pass_kernel(stored, after, facts, idrow, idcol):
+    members, tokens = stored.shape[0], idcol.shape[0]
+    for u in range(members):
+        facts[u : u + 1, :] = stored[members - 1 - u : members - u, :]
+    row = own_ids(stored, tokens)
+    idrow[...] = jnp.broadcast_to(row, idrow.shape)
+    idcol[...] = jnp.transpose(jnp.broadcast_to(row, (LANES, LANES)))[:tokens]
 
 
 def few(count):
@@ -142,15 +155,15 @@
 
 
 def half_kernel(chunks, linked, one, in_ref, early_ref, final_ref):
-    slices = early_ref.shape[0] + 1
+    slices, newest = early_ref.shape[0] + 1, in_ref.shape[0] - 1
     offset = jnp.where(lax.axis_index("uly") >= chunks, chunks, 0)
 
     def slice_end(c):
         def step(j, state):
             keep = linked[pl.ds(c * 2 * chunks + offset + j, 1), :] * one[...]
-            return in_ref[c * chunks + j].astype(jnp.float32) + keep * state
-
-        begin = in_ref[c * chunks].astype(jnp.float32)
+            return in_ref[newest - c * chunks - j].astype(jnp.float32) + keep * state
+
+        begin = in_ref[newest - c * chunks].astype(jnp.float32)
         state = lax.fori_loop(1, chunks, step, begin, unroll=few(chunks - 1))
         return state.astype(early_ref.dtype)
 
@@ -165,7 +178,7 @@
 def scan_kernel(
     chunks, linked, through, one, half, in_ref, early, final, after, out_ref
 ):
-    slices = early.shape[0] + 1
+    slices, newest = early.shape[0] + 1, in_ref.shape[0] - 1
     later = lax.axis_index("uly") >= chunks
     offset = jnp.where(later, chunks, 0)
 
@@ -178,7 +191,7 @@
             at = c * chunks + j
             out_ref[at] = state.astype(out_ref.dtype)
             keep = linked[pl.ds(c * 2 * chunks + offset + j, 1), :] * one[...]
-            return in_ref[at].astype(jnp.float32) + keep * state
+            return in_ref[newest - at].astype(jnp.float32) + keep * state
 
         return lax.fori_loop(0, chunks, step, state, unroll=few(chunks))
 
@@ -260,26 +273,23 @@
     own = jnp.pad(decay_rate, (0, LANES - here)) + jnp.pad(
         doc_ids, (LANES - tokens, 0)
     ).astype(jnp.float32)
-    facts = lax.all_to_all(
-        jnp.broadcast_to(own[None, :], tile.shape), "uly", split_axis=0, concat_axis=0, tiled=True
+    backward = [list(range(members))[::-1]]
+    stored = lax.all_to_all(
+        jnp.broadcast_to(own[None, :], tile.shape),
+        "uly", split_axis=0, concat_axis=0, axis_index_groups=backward, tiled=True,
     )
-    turned, filled, idrow, idcol = pl.pallas_call(
+    turned, filled = pl.pallas_call(
         turn_kernel,
-        in_specs=[vmem] * 3,
-        out_specs=[vmem] * 4,
-        out_shape=[
-            shape((width, LANES), jnp.bfloat16),
-            shape((LANES, width), jnp.bfloat16),
-            shape((8, LANES), jnp.float32),
-            shape((tokens, LANES), jnp.float32),
-        ],
+        in_specs=[vmem] * 2,
+        out_specs=[vmem] * 2,
+        out_shape=[shape((width, LANES), jnp.bfloat16), shape((LANES, width), jnp.bfloat16)],
         compiler_params=params,
         cost_estimate=pl.CostEstimate(flops=0, bytes_accessed=12_000_000, transcendentals=0),
         name="turn",
-    )(own[None, :], keys, values)
+    )(keys, values)
     ends = pl.pallas_call(
-        functools.partial(ends_kernel, here, tokens),
-        in_specs=[vmem] * 4,
+        functools.partial(ends_kernel, here, tokens, group),
+        in_specs=[vmem] * 3,
         out_specs=pl.BlockSpec(memory_space=pl.ANY),
         out_shape=shape((all_pairs * HD, LANES), jnp.bfloat16),
         scratch_shapes=[
@@ -288,21 +298,22 @@
         ],
         compiler_params=params,
         name="ends",
-    )(facts, idrow, turned, filled)
+    )(stored, turned, filled)
     pieces = lax.all_to_all(
         ends.reshape(group, rows, LANES),
-        axes, split_axis=0, concat_axis=0, axis_index_groups=groups, tiled=True,
+        axes, split_axis=0, concat_axis=0, tiled=True,
+        axis_index_groups=[members_of[::-1] for members_of in groups],
     )
-    slice_facts = pl.pallas_call(
+    facts, idrow, idcol = pl.pallas_call(
         pass_kernel,
         in_specs=[vmem, pl.BlockSpec(memory_space=pl.ANY)],
-        out_specs=vmem,
-        out_shape=tile,
+        out_specs=[vmem] * 3,
+        out_shape=[tile, shape((8, LANES), jnp.float32), shape((tokens, LANES), jnp.float32)],
         compiler_params=params,
         name="pass",
-    )(facts, ends)
+    )(stored, ends)
     others = [
-        lax.ppermute(slice_facts, "ctx", [(c, (c + ahead) % slices) for c in range(slices)])
+        lax.ppermute(facts, "ctx", [(c, (c + ahead) % slices) for c in range(slices)])
         for ahead in range(1, slices)
     ]
     linked, through, one, half, before = pl.pallas_call(
@@ -315,7 +326,7 @@
         scratch_shapes=[pltpu.VMEM((count, LANES), jnp.float32)],
         compiler_params=params,
         name="link",
-    )(slice_facts, *others)
+    )(facts, *others)
     early_ends, final_end = pl.pallas_call(
         functools.partial(half_kernel, chunks),
         in_specs=[vmem] * 3,

time: 52 us -> 50.4 us (0.969)
  waiting for transfers between devices: 10.4 us -> 6.9 us
  starting transfers between devices: 19.2 us -> 21.3 us
  other arithmetic: 1.49 us -> 0.75 us
    all_to_all x1, waiting for transfers between devices: 2.97 us -> 0.01 us  [local(): lax.all_to_all(jnp.broadcast_to(own[None, :], tile.shape), 'uly', split_a...]
    all_to_all x1, starting transfers between devices: 7.25 us -> 9.23 us  [local(): lax.all_to_all(jnp.broadcast_to(own[None, :], tile.shape), 'uly', split_a...]
    all_to_all x1, waiting for transfers between devices: 1.47 us -> 0.01 us  [local(): lax.all_to_all(ends.reshape(group, rows, LANES), axes, split_axis=0, conc...]
    all_to_all x1, starting transfers between devices: 3.72 us -> 5.07 us  [local(): lax.all_to_all(ends.reshape(group, rows, LANES), axes, split_axis=0, conc...]
    ppermute x3, starting transfers between devices: 3.37 us -> 2.08 us  [local(): lax.ppermute(facts, 'ctx', [(c, (c + ahead) % slices) for c in range(slic...]
    ppermute x3, waiting for transfers between devices: 4.21 us -> 5.21 us  [local(): lax.ppermute(facts, 'ctx', [(c, (c + ahead) % slices) for c in range(slic...]
    ppermute x1, starting transfers between devices: 3.63 us -> 2.78 us  [local(): lax.ppermute(final_end, axes, [(low, high) for low, high in swap if low <...]
    ppermute x1, starting transfers between devices: 1.25 us -> 2.11 us  [local(): early = lax.ppermute(early_ends, axes, swap)]
  transfers between devices with their start and end apart: 7 -> 7, of which waited for: 6 -> 4; matrix products, arithmetic and copies ran while one was open for 1% -> 0% of each run, Pallas kernels for 3% -> 4%
where the time goes in v19:
time: 50.4 us; the launch traced here: 50 us
  starting transfers between devices  21.3 us (42%)
  blocking collectives  12.4 us (25%)
  waiting for transfers between devices  6.9 us (14%)
  Pallas kernels  5.71 us (11%)
  local copies, waits for them, and re-layouts  2.88 us (6%)
  other arithmetic  0.75 us (1%)
    all_to_all x1, blocking collectives, local(): lax.all_to_all(moved, axes, split_axis=0, concat_axis=0, axis_index_group...  12.4 us
    all_to_all x1, starting transfers between devices, local(): lax.all_to_all(jnp.broadcast_to(own[None, :], tile.shape), 'uly', split_a...  9.23 us
    ppermute x3, waiting for transfers between devices, local(): lax.ppermute(facts, 'ctx', [(c, (c + ahead) % slices) for c in range(slic...  5.21 us
    all_to_all x1, starting transfers between devices, local(): lax.all_to_all(ends.reshape(group, rows, LANES), axes, split_axis=0, conc...  5.07 us
    ppermute x1, starting transfers between devices, local(): lax.ppermute(final_end, axes, [(low, high) for low, high in swap if low <...  2.78 us
    unnamed x10, local copies, waits for them, and re-layouts  2.28 us
    ppermute x1, starting transfers between devices, local(): early = lax.ppermute(early_ends, axes, swap)  2.11 us
    ppermute x3, starting transfers between devices, local(): lax.ppermute(facts, 'ctx', [(c, (c + ahead) % slices) for c in range(slic...  2.08 us
  transfers between devices with their start and end apart: 7, of which 4 were waited for; matrix products, arithmetic and copies ran while one was open for 0% of the time, Pallas kernels for 4%

profile of v19, /device:TPU:0, one launch (start us, length us, event | category | flops | bytes accessed | tf_op | source)
XLA Modules:
  0.0 50.0 jit_solution(11153435092248509218)
XLA Ops:
  0.0 0.7 %convert_add_fusion = f32[128]{0:T(128)S(1)} fusion(s32[96]{0:T(128)} %param.9, f32[8]{0:T(128)} %param.10), kind=kLoop, calls=%fused_computation | loop fusion | flops 256 | bytes 928 | tf_op jit(solution)/shard_map/add | solution.py:273
  0.7 0.6 %broadcast_in_dim.4 = f32[8,1,128]{2,1,0:T(1,128)} broadcast(f32[128]{0:T(128)S(1)} %convert_add_fusion), dimensions={2} | broadcast | bytes 4608 | tf_op jit(solution)/shard_map/broadcast_in_dim | solution.py:278
  1.3 9.2 %all-to-all-start = ((f32[8,1,128]{2,1,0:T(1,128)}), f32[8,1,128]{2,1,0:T(1,128)S(1)}, u32[]{:S(2)}, u32[]{:S(2)}) async-start(f32[8,1,128]{2,1,0:T(1,128)} %broadcast_in_dim.4), calls=%async_computation | async-start | bytes 8192 | tf_op jit(solution)/shard_map/all_to_all | solution.py:277
  10.6 1.1 %copy-done = bf16[96,4096]{1,0:T(8,128)(2,1)S(1)} copy-done((bf16[96,4096]{1,0:T(8,128)(2,1)S(1)}, bf16[96,4096]{1,0:T(8,128)(2,1)}, u32[]{:S(2)}) %copy-start) | copy-done | bytes 786456
  11.7 1.1 %copy-done.1 = bf16[96,4096]{1,0:T(8,128)(2,1)S(1)} copy-done((bf16[96,4096]{1,0:T(8,128)(2,1)S(1)}, bf16[96,4096]{1,0:T(8,128)(2,1)}, u32[]{:S(2)}) %copy-start.1) | copy-done | bytes 786456
  12.8 0.4 turn.1
  13.2 1.6 %ends.1.after = bf16[2048,128]{1,0:T(8,128)(2,1)} custom-call(f32[8,128]{1,0:T(8,128)S(1)} %bitcast.5, bf16[4096,128]{1,0:T(8,128)(2,1)S(1)} %get-tuple-element.19.turned, bf16[128,4096]{1,0:T(8,128)(2,1)S(1)} %get-tuple-element.20.v_ref), custom_call_target="tpu_custom_call" | custom-call | tf_op jit(solution)/shard_map/ends/pallas_call | solution.py:290
  14.8 5.1 %all-to-all-start.1 = ((bf16[16,128,128]{2,1,0:T(8,128)(2,1)}), bf16[16,128,128]{2,1,0:T(8,128)(2,1)S(1)}, u32[]{:S(2)}, u32[]{:S(2)}) async-start(bf16[16,128,128]{2,1,0:T(8,128)(2,1)} %bitcast.1), calls=%async_computation.1 | async-start | bytes 1048576 | tf_op jit(solution)/shard_map/all_to_all | solution.py:302
  19.9 0.2 pass.1
  20.1 0.1 collective-permute-start
  20.2 0.6 %collective-permute-start.1 = (f32[8,128]{1,0:T(8,128)S(1)}, f32[8,128]{1,0:T(8,128)S(1)}, u32[]{:S(2)}, u32[]{:S(2)}) collective-permute-start(f32[8,128]{1,0:T(8,128)S(1)} %get-tuple-element.22.facts), channel_id=1, source_target_pairs={{0,16},{8,24},{16,0},{24,8},{1,17},{9,25},{17,1},{25,9},{2,18},{10... | collective-permute-start | bytes 12296 | tf_op jit(solution)/shard_map/ppermute | solution.py:316
  20.8 1.4 %collective-permute-start.2 = (f32[8,128]{1,0:T(8,128)S(1)}, f32[8,128]{1,0:T(8,128)S(1)}, u32[]{:S(2)}, u32[]{:S(2)}) collective-permute-start(f32[8,128]{1,0:T(8,128)S(1)} %get-tuple-element.22.facts), channel_id=1, source_target_pairs={{0,24},{8,0},{16,8},{24,16},{1,25},{9,1},{17,9},{25,17},{2,26},{10... | collective-permute-start | bytes 12296 | tf_op jit(solution)/shard_map/ppermute | solution.py:316
  22.1 4.5 %collective-permute-done.refs_0_ = f32[8,128]{1,0:T(8,128)S(1)} collective-permute-done((f32[8,128]{1,0:T(8,128)S(1)}, f32[8,128]{1,0:T(8,128)S(1)}, u32[]{:S(2)}, u32[]{:S(2)}) %collective-permute-start) | collective-permute-done | bytes 4128 | tf_op jit(solution)/shard_map/ppermute | solution.py:316
  26.7 0.7 %collective-permute-done.1.refs_1_ = f32[8,128]{1,0:T(8,128)S(1)} collective-permute-done((f32[8,128]{1,0:T(8,128)S(1)}, f32[8,128]{1,0:T(8,128)S(1)}, u32[]{:S(2)}, u32[]{:S(2)}) %collective-permute-start.1) | collective-permute-done | bytes 4128 | tf_op jit(solution)/shard_map/ppermute | solution.py:316
  27.4 0.1 link.1
  27.5 0.1 half.1
  27.6 2.1 %collective-permute-start.3 = (bf16[3,128,128]{2,1,0:T(8,128)(2,1)S(1)}, bf16[3,128,128]{2,1,0:T(8,128)(2,1)S(1)}, u32[]{:S(2)}, u32[]{:S(2)}) collective-permute-start(bf16[3,128,128]{2,1,0:T(8,128)(2,1)S(1)} %get-tuple-element.27.after), channel_id=1, source_target_pairs={{0,4},{1,5},{2,6},{3,7},{4,0},{5,1},{6,2},{7,3},{8,12},{9,13},{10,... | collective-permute-start | bytes 294920 | tf_op jit(solution)/shard_map/ppermute | solution.py:341
  29.7 2.8 %collective-permute-start.4 = (bf16[1,128,128]{2,1,0:T(8,128)(2,1)S(1)}, bf16[1,128,128]{2,1,0:T(8,128)(2,1)S(1)}, u32[]{:S(2)}, u32[]{:S(2)}) collective-permute-start(bf16[1,128,128]{2,1,0:T(8,128)(2,1)S(1)} %get-tuple-element.31), channel_id=1, source_target_pairs={{0,4},{1,5},{2,6},{3,7},{8,12},{9,13},{10,14},{11,15},{16,20},{17,... | collective-permute-start | bytes 98312 | tf_op jit(solution)/shard_map/ppermute | solution.py:342
  32.5 1.3 %inner.1 = (f32[96,4096]{1,0:T(8,128)S(1)}, f32[1,4096]{1,0:T(1,128)S(1)}) custom-call(f32[8,128]{1,0:T(8,128)S(1)} %get-tuple-element.22.facts, f32[96,128]{1,0:T(8,128)S(1)} %get-tuple-element.21.idcol, f32[8,128]{1,0:T(8,128)S(1)} %get-tuple-element.24.idrow, bf16[96,4096]{1,0:T(8,128)(2,1)S(1)} %copy-done.3, ...), custom_call_target="tpu_custom_call" | custom-call | flops 8000000000 | bytes 4000000 | tf_op jit(solution)/shard_map/inner/pallas_call | solution.py:343
  33.8 0.3 collective-permute-done.4.final
  34.1 1.4 %collective-permute-done.3.early = bf16[3,128,128]{2,1,0:T(8,128)(2,1)S(1)} collective-permute-done((bf16[3,128,128]{2,1,0:T(8,128)(2,1)S(1)}, bf16[3,128,128]{2,1,0:T(8,128)(2,1)S(1)}, u32[]{:S(2)}, u32[]{:S(2)}) %collective-permute-start.3) | collective-permute-done | bytes 98336 | tf_op jit(solution)/shard_map/ppermute | solution.py:341
  35.5 0.2 scan.1
  35.7 12.4 %all_to_all.18 = bf16[16,128,128]{2,1,0:T(8,128)(2,1)S(1)} all-to-all(bf16[16,128,128]{2,1,0:T(8,128)(2,1)S(1)} %scan.1), channel_id=1, replica_groups={{0,1,2,3,8,9,10,11,16,17,18,19,24,25,26,27},{4,5,6,7,12,13,14,15,20,21,..., dimensions={0} | all-to-all | bytes 1048576 | tf_op jit(solution)/shard_map/all_to_all | solution.py:362
  48.2 1.9 %norm.1 = bf16[96,4096]{1,0:T(8,128)(2,1)} custom-call(f32[96,128]{1,0:T(8,128)S(1)} %get-tuple-element.21.idcol, f32[1,128]{1,0:T(1,128)S(1)} %get-tuple-element.23.before, f32[1,4096]{1,0:T(1,128)S(1)} %get-tuple-element.28.after.rates, bf16[96,4096]{1,0:T(8,128)(2,1)S(1)} %copy-done.3, bf16[2048,128]{1,0:T(8,128)(2,1)S(1)} %bitcast.4, ...), custom_call_target="tpu_custom_call" | custom-call | tf_op jit(solution)/shard_map/norm/pallas_call | solution.py:365
  (11 shorter events, 0.0 us)
Async XLA Ops:
  1.3 11.9 %all-to-all-start = ((f32[8,1,128]{2,1,0:T(1,128)}), f32[8,1,128]{2,1,0:T(1,128)S(1)}, u32[]{:S(2)}, u32[]{:S(2)}) async-start(f32[8,1,128]{2,1,0:T(1,128)} %broadcast_in_dim.4), calls=%async_computation | async-start | bytes 8192 | tf_op jit(solution)/shard_map/all_to_all | solution.py:277
  10.6 1.1 %copy-start = (bf16[96,4096]{1,0:T(8,128)(2,1)S(1)}, bf16[96,4096]{1,0:T(8,128)(2,1)}, u32[]{:S(2)}) copy-start(bf16[96,4096]{1,0:T(8,128)(2,1)} %k_ref.1) | copy-start | bytes 2359300
  11.7 1.1 %copy-start.1 = (bf16[96,4096]{1,0:T(8,128)(2,1)S(1)}, bf16[96,4096]{1,0:T(8,128)(2,1)}, u32[]{:S(2)}) copy-start(bf16[96,4096]{1,0:T(8,128)(2,1)} %v_ref.3) | copy-start | bytes 2359300
  14.8 17.7 %copy-start.2 = (bf16[96,4096]{1,0:T(8,128)(2,1)S(1)}, bf16[96,4096]{1,0:T(8,128)(2,1)}, u32[]{:S(2)}) copy-start(bf16[96,4096]{1,0:T(8,128)(2,1)} %v_ref.3) | copy-start | bytes 2359300
  14.8 17.7 %copy-start.3 = (bf16[96,4096]{1,0:T(8,128)(2,1)S(1)}, bf16[96,4096]{1,0:T(8,128)(2,1)}, u32[]{:S(2)}) copy-start(bf16[96,4096]{1,0:T(8,128)(2,1)} %q_ref.3) | copy-start | bytes 2359300
  14.8 12.6 %all-to-all-start.1 = ((bf16[16,128,128]{2,1,0:T(8,128)(2,1)}), bf16[16,128,128]{2,1,0:T(8,128)(2,1)S(1)}, u32[]{:S(2)}, u32[]{:S(2)}) async-start(bf16[16,128,128]{2,1,0:T(8,128)(2,1)} %bitcast.1), calls=%async_computation.1 | async-start | bytes 1048576 | tf_op jit(solution)/shard_map/all_to_all | solution.py:302
  20.1 6.6 %collective-permute-start = (f32[8,128]{1,0:T(8,128)S(1)}, f32[8,128]{1,0:T(8,128)S(1)}, u32[]{:S(2)}, u32[]{:S(2)}) collective-permute-start(f32[8,128]{1,0:T(8,128)S(1)} %get-tuple-element.22.facts), channel_id=1, source_target_pairs={{0,8},{8,16},{16,24},{24,0},{1,9},{9,17},{17,25},{25,1},{2,10},{10... | collective-permute-start | bytes 12296 | tf_op jit(solution)/shard_map/ppermute | solution.py:316
  20.2 7.1 %collective-permute-start.1 = (f32[8,128]{1,0:T(8,128)S(1)}, f32[8,128]{1,0:T(8,128)S(1)}, u32[]{:S(2)}, u32[]{:S(2)}) collective-permute-start(f32[8,128]{1,0:T(8,128)S(1)} %get-tuple-element.22.facts), channel_id=1, source_target_pairs={{0,16},{8,24},{16,0},{24,8},{1,17},{9,25},{17,1},{25,9},{2,18},{10... | collective-permute-start | bytes 12296 | tf_op jit(solution)/shard_map/ppermute | solution.py:316
  20.8 6.6 %collective-permute-start.2 = (f32[8,128]{1,0:T(8,128)S(1)}, f32[8,128]{1,0:T(8,128)S(1)}, u32[]{:S(2)}, u32[]{:S(2)}) collective-permute-start(f32[8,128]{1,0:T(8,128)S(1)} %get-tuple-element.22.facts), channel_id=1, source_target_pairs={{0,24},{8,0},{16,8},{24,16},{1,25},{9,1},{17,9},{25,17},{2,26},{10... | collective-permute-start | bytes 12296 | tf_op jit(solution)/shard_map/ppermute | solution.py:316
  27.6 7.9 %collective-permute-start.3 = (bf16[3,128,128]{2,1,0:T(8,128)(2,1)S(1)}, bf16[3,128,128]{2,1,0:T(8,128)(2,1)S(1)}, u32[]{:S(2)}, u32[]{:S(2)}) collective-permute-start(bf16[3,128,128]{2,1,0:T(8,128)(2,1)S(1)} %get-tuple-element.27.after), channel_id=1, source_target_pairs={{0,4},{1,5},{2,6},{3,7},{4,0},{5,1},{6,2},{7,3},{8,12},{9,13},{10,... | collective-permute-start | bytes 294920 | tf_op jit(solution)/shard_map/ppermute | solution.py:341
  29.7 4.4 %collective-permute-start.4 = (bf16[1,128,128]{2,1,0:T(8,128)(2,1)S(1)}, bf16[1,128,128]{2,1,0:T(8,128)(2,1)S(1)}, u32[]{:S(2)}, u32[]{:S(2)}) collective-permute-start(bf16[1,128,128]{2,1,0:T(8,128)(2,1)S(1)} %get-tuple-element.31), channel_id=1, source_target_pairs={{0,4},{1,5},{2,6},{3,7},{8,12},{9,13},{10,14},{11,15},{16,20},{17,... | collective-permute-start | bytes 98312 | tf_op jit(solution)/shard_map/ppermute | solution.py:342
  33.8 14.3 %copy-start.4 = (f32[4096]{0:T(1024)S(1)}, f32[4096]{0:T(1024)}, u32[]{:S(2)}) copy-start(f32[4096]{0:T(1024)} %param.11) | copy-start | bytes 49156

commit v20 on v19

--- a/solution.py
+++ b/solution.py
@@ -39,7 +39,8 @@
 
 
 def own_ids(stored, tokens):
-    at = stored.shape[0] - 1 - lax.axis_index("uly")
+    members = stored.shape[0]
+    at = lax.rem(lax.axis_index("uly") + members // 2, members)
     row = stored[pl.ds(at, 1), :]
     fill = jnp.full((1, LANES - tokens), -1.0, jnp.float32)
     return jnp.concatenate([row[:, LANES - tokens :], fill], 1)
@@ -60,7 +61,7 @@
     for j in range(0, width // LANES, 2):
         weighted = []
         for head in range(2 * j, 2 * j + 4):
-            weight = jnp.exp(-rate_of(stored, (members - 1) * here + 2 * (head % here) - head, here) * age)
+            weight = jnp.exp(-rate_of(stored, (head + members // 2 * here) % (members * here), here) * age)
             keys = turned[head * HD : (head + 1) * HD, :].astype(jnp.float32)
             keys = keys.reshape(HD // 8, 8, LANES) * weight[None]
             weighted.append(keys.reshape(HD, LANES))
@@ -117,7 +118,8 @@
 def pass_kernel(stored, after, facts, idrow, idcol):
     members, tokens = stored.shape[0], idcol.shape[0]
     for u in range(members):
-        facts[u : u + 1, :] = stored[members - 1 - u : members - u, :]
+        at = (u + members // 2) % members
+        facts[u : u + 1, :] = stored[at : at + 1, :]
     row = own_ids(stored, tokens)
     idrow[...] = jnp.broadcast_to(row, idrow.shape)
     idcol[...] = jnp.transpose(jnp.broadcast_to(row, (LANES, LANES)))[:tokens]
@@ -273,10 +275,10 @@
     own = jnp.pad(decay_rate, (0, LANES - here)) + jnp.pad(
         doc_ids, (LANES - tokens, 0)
     ).astype(jnp.float32)
-    backward = [list(range(members))[::-1]]
+    turned_round = [[(u + members // 2) % members for u in range(members)]]
     stored = lax.all_to_all(
         jnp.broadcast_to(own[None, :], tile.shape),
-        "uly", split_axis=0, concat_axis=0, axis_index_groups=backward, tiled=True,
+        "uly", split_axis=0, concat_axis=0, axis_index_groups=turned_round, tiled=True,
     )
     turned, filled = pl.pallas_call(
         turn_kernel,

time: 50.4 us -> 49.9 us (0.990)
  starting transfers between devices: 21.3 us -> 19.8 us
  waiting for transfers between devices: 6.9 us -> 8.29 us
    all_to_all x1, starting transfers between devices: 9.23 us -> 7.81 us  [local(): lax.all_to_all(jnp.broadcast_to(own[None, :], tile.shape), 'uly', split_a...]
    all_to_all x1, waiting for transfers between devices: 0.01 us -> 1.4 us  [local(): lax.all_to_all(jnp.broadcast_to(own[None, :], tile.shape), 'uly', split_a...]
    ppermute x1, starting transfers between devices: 2.78 us -> 3.36 us  [local(): lax.ppermute(final_end, axes, [(low, high) for low, high in swap if low <...]
    ppermute x1, starting transfers between devices: 2.11 us -> 1.52 us  [local(): early = lax.ppermute(early_ends, axes, swap)]
  transfers between devices with their start and end apart: 7 -> 7, of which waited for: 4 -> 5; matrix products, arithmetic and copies ran while one was open for 0% -> 0% of each run, Pallas kernels for 4% -> 4%
where the time goes in v20:
time: 49.9 us; the launch traced here: 49.5 us
  starting transfers between devices  19.8 us (40%)
  blocking collectives  11.9 us (24%)
  waiting for transfers between devices  8.29 us (17%)
  Pallas kernels  5.72 us (11%)
  local copies, waits for them, and re-layouts  2.88 us (6%)
  other arithmetic  0.75 us (2%)
    all_to_all x1, blocking collectives, local(): lax.all_to_all(moved, axes, split_axis=0, concat_axis=0, axis_index_group...  11.9 us
    all_to_all x1, starting transfers between devices, local(): lax.all_to_all(jnp.broadcast_to(own[None, :], tile.shape), 'uly', split_a...  7.81 us
    ppermute x3, waiting for transfers between devices, local(): lax.ppermute(facts, 'ctx', [(c, (c + ahead) % slices) for c in range(slic...  5.2 us
    all_to_all x1, starting transfers between devices, local(): lax.all_to_all(ends.reshape(group, rows, LANES), axes, split_axis=0, conc...  5.07 us
    ppermute x1, starting transfers between devices, local(): lax.ppermute(final_end, axes, [(low, high) for low, high in swap if low <...  3.36 us
    unnamed x10, local copies, waits for them, and re-layouts  2.28 us
    ppermute x3, starting transfers between devices, local(): lax.ppermute(facts, 'ctx', [(c, (c + ahead) % slices) for c in range(slic...  2.08 us
    pallas_call x1, Pallas kernels, local(): pl.pallas_call(norm_kernel, in_specs=[vmem] * 7, out_specs=pl.BlockSpec(m...  1.88 us
  transfers between devices with their start and end apart: 7, of which 5 were waited for; matrix products, arithmetic and copies ran while one was open for 0% of the time, Pallas kernels for 4%

profile of v20, /device:TPU:0, one launch (start us, length us, event | category | flops | bytes accessed | tf_op | source)
XLA Modules:
  0.0 49.5 jit_solution(13665260037850284291)
XLA Ops:
  0.0 0.7 %convert_add_fusion = f32[128]{0:T(128)S(1)} fusion(s32[96]{0:T(128)} %param.9, f32[8]{0:T(128)} %param.10), kind=kLoop, calls=%fused_computation | loop fusion | flops 256 | bytes 928 | tf_op jit(solution)/shard_map/add | solution.py:275
  0.7 0.6 %broadcast_in_dim.4 = f32[8,1,128]{2,1,0:T(1,128)} broadcast(f32[128]{0:T(128)S(1)} %convert_add_fusion), dimensions={2} | broadcast | bytes 4608 | tf_op jit(solution)/shard_map/broadcast_in_dim | solution.py:280
  1.3 7.8 %all-to-all-start = ((f32[8,1,128]{2,1,0:T(1,128)}), f32[8,1,128]{2,1,0:T(1,128)S(1)}, u32[]{:S(2)}, u32[]{:S(2)}) async-start(f32[8,1,128]{2,1,0:T(1,128)} %broadcast_in_dim.4), calls=%async_computation | async-start | bytes 8192 | tf_op jit(solution)/shard_map/all_to_all | solution.py:279
  9.2 1.1 %copy-done = bf16[96,4096]{1,0:T(8,128)(2,1)S(1)} copy-done((bf16[96,4096]{1,0:T(8,128)(2,1)S(1)}, bf16[96,4096]{1,0:T(8,128)(2,1)}, u32[]{:S(2)}) %copy-start) | copy-done | bytes 786456
  10.3 1.1 %copy-done.1 = bf16[96,4096]{1,0:T(8,128)(2,1)S(1)} copy-done((bf16[96,4096]{1,0:T(8,128)(2,1)S(1)}, bf16[96,4096]{1,0:T(8,128)(2,1)}, u32[]{:S(2)}) %copy-start.1) | copy-done | bytes 786456
  11.4 0.4 turn.1
  11.8 1.4 %all-to-all-done = f32[8,1,128]{2,1,0:T(1,128)S(1)} async-done(((f32[8,1,128]{2,1,0:T(1,128)}), f32[8,1,128]{2,1,0:T(1,128)S(1)}, u32[]{:S(2)}, u32[]{:S(2)}) %all-to-all-start) | async-done | bytes 4128 | tf_op jit(solution)/shard_map/all_to_all | solution.py:279
  13.2 1.6 %ends.1.after = bf16[2048,128]{1,0:T(8,128)(2,1)} custom-call(f32[8,128]{1,0:T(8,128)S(1)} %bitcast.5, bf16[4096,128]{1,0:T(8,128)(2,1)S(1)} %get-tuple-element.19.turned, bf16[128,4096]{1,0:T(8,128)(2,1)S(1)} %get-tuple-element.20.v_ref), custom_call_target="tpu_custom_call" | custom-call | tf_op jit(solution)/shard_map/ends/pallas_call | solution.py:292
  14.8 5.1 %all-to-all-start.1 = ((bf16[16,128,128]{2,1,0:T(8,128)(2,1)}), bf16[16,128,128]{2,1,0:T(8,128)(2,1)S(1)}, u32[]{:S(2)}, u32[]{:S(2)}) async-start(bf16[16,128,128]{2,1,0:T(8,128)(2,1)} %bitcast.1), calls=%async_computation.1 | async-start | bytes 1048576 | tf_op jit(solution)/shard_map/all_to_all | solution.py:304
  19.9 0.2 pass.1
  20.0 0.1 collective-permute-start
  20.2 0.6 %collective-permute-start.1 = (f32[8,128]{1,0:T(8,128)S(1)}, f32[8,128]{1,0:T(8,128)S(1)}, u32[]{:S(2)}, u32[]{:S(2)}) collective-permute-start(f32[8,128]{1,0:T(8,128)S(1)} %get-tuple-element.22.facts), channel_id=1, source_target_pairs={{0,16},{8,24},{16,0},{24,8},{1,17},{9,25},{17,1},{25,9},{2,18},{10... | collective-permute-start | bytes 12296 | tf_op jit(solution)/shard_map/ppermute | solution.py:318
  20.7 1.4 %collective-permute-start.2 = (f32[8,128]{1,0:T(8,128)S(1)}, f32[8,128]{1,0:T(8,128)S(1)}, u32[]{:S(2)}, u32[]{:S(2)}) collective-permute-start(f32[8,128]{1,0:T(8,128)S(1)} %get-tuple-element.22.facts), channel_id=1, source_target_pairs={{0,24},{8,0},{16,8},{24,16},{1,25},{9,1},{17,9},{25,17},{2,26},{10... | collective-permute-start | bytes 12296 | tf_op jit(solution)/shard_map/ppermute | solution.py:318
  22.1 4.8 %collective-permute-done.refs_0_ = f32[8,128]{1,0:T(8,128)S(1)} collective-permute-done((f32[8,128]{1,0:T(8,128)S(1)}, f32[8,128]{1,0:T(8,128)S(1)}, u32[]{:S(2)}, u32[]{:S(2)}) %collective-permute-start) | collective-permute-done | bytes 4128 | tf_op jit(solution)/shard_map/ppermute | solution.py:318
  26.9 0.4 collective-permute-done.1.refs_1_
  27.5 0.1 half.1
  27.6 1.5 %collective-permute-start.3 = (bf16[3,128,128]{2,1,0:T(8,128)(2,1)S(1)}, bf16[3,128,128]{2,1,0:T(8,128)(2,1)S(1)}, u32[]{:S(2)}, u32[]{:S(2)}) collective-permute-start(bf16[3,128,128]{2,1,0:T(8,128)(2,1)S(1)} %get-tuple-element.27.after), channel_id=1, source_target_pairs={{0,4},{1,5},{2,6},{3,7},{4,0},{5,1},{6,2},{7,3},{8,12},{9,13},{10,... | collective-permute-start | bytes 294920 | tf_op jit(solution)/shard_map/ppermute | solution.py:343
  29.1 3.4 %collective-permute-start.4 = (bf16[1,128,128]{2,1,0:T(8,128)(2,1)S(1)}, bf16[1,128,128]{2,1,0:T(8,128)(2,1)S(1)}, u32[]{:S(2)}, u32[]{:S(2)}) collective-permute-start(bf16[1,128,128]{2,1,0:T(8,128)(2,1)S(1)} %get-tuple-element.31), channel_id=1, source_target_pairs={{0,4},{1,5},{2,6},{3,7},{8,12},{9,13},{10,14},{11,15},{16,20},{17,... | collective-permute-start | bytes 98312 | tf_op jit(solution)/shard_map/ppermute | solution.py:344
  32.5 1.3 %inner.1 = (f32[96,4096]{1,0:T(8,128)S(1)}, f32[1,4096]{1,0:T(1,128)S(1)}) custom-call(f32[8,128]{1,0:T(8,128)S(1)} %get-tuple-element.22.facts, f32[96,128]{1,0:T(8,128)S(1)} %get-tuple-element.21.idcol, f32[8,128]{1,0:T(8,128)S(1)} %get-tuple-element.24.idrow, bf16[96,4096]{1,0:T(8,128)(2,1)S(1)} %copy-done.3, ...), custom_call_target="tpu_custom_call" | custom-call | flops 8000000000 | bytes 4000000 | tf_op jit(solution)/shard_map/inner/pallas_call | solution.py:345
  33.8 0.3 collective-permute-done.4.final
  34.1 1.4 %collective-permute-done.3.early = bf16[3,128,128]{2,1,0:T(8,128)(2,1)S(1)} collective-permute-done((bf16[3,128,128]{2,1,0:T(8,128)(2,1)S(1)}, bf16[3,128,128]{2,1,0:T(8,128)(2,1)S(1)}, u32[]{:S(2)}, u32[]{:S(2)}) %collective-permute-start.3) | collective-permute-done | bytes 98336 | tf_op jit(solution)/shard_map/ppermute | solution.py:343
  35.5 0.2 scan.1
  35.7 11.9 %all_to_all.18 = bf16[16,128,128]{2,1,0:T(8,128)(2,1)S(1)} all-to-all(bf16[16,128,128]{2,1,0:T(8,128)(2,1)S(1)} %scan.1), channel_id=1, replica_groups={{0,1,2,3,8,9,10,11,16,17,18,19,24,25,26,27},{4,5,6,7,12,13,14,15,20,21,..., dimensions={0} | all-to-all | bytes 1048576 | tf_op jit(solution)/shard_map/all_to_all | solution.py:364
  47.7 1.9 %norm.1 = bf16[96,4096]{1,0:T(8,128)(2,1)} custom-call(f32[96,128]{1,0:T(8,128)S(1)} %get-tuple-element.21.idcol, f32[1,128]{1,0:T(1,128)S(1)} %get-tuple-element.23.before, f32[1,4096]{1,0:T(1,128)S(1)} %get-tuple-element.28.after.rates, bf16[96,4096]{1,0:T(8,128)(2,1)S(1)} %copy-done.3, bf16[2048,128]{1,0:T(8,128)(2,1)S(1)} %bitcast.4, ...), custom_call_target="tpu_custom_call" | custom-call | tf_op jit(solution)/shard_map/norm/pallas_call | solution.py:367
  (11 shorter events, 0.1 us)
Async XLA Ops:
  1.3 11.8 %all-to-all-start = ((f32[8,1,128]{2,1,0:T(1,128)}), f32[8,1,128]{2,1,0:T(1,128)S(1)}, u32[]{:S(2)}, u32[]{:S(2)}) async-start(f32[8,1,128]{2,1,0:T(1,128)} %broadcast_in_dim.4), calls=%async_computation | async-start | bytes 8192 | tf_op jit(solution)/shard_map/all_to_all | solution.py:279
  9.2 1.1 %copy-start = (bf16[96,4096]{1,0:T(8,128)(2,1)S(1)}, bf16[96,4096]{1,0:T(8,128)(2,1)}, u32[]{:S(2)}) copy-start(bf16[96,4096]{1,0:T(8,128)(2,1)} %k_ref.1) | copy-start | bytes 2359300
  10.3 1.1 %copy-start.1 = (bf16[96,4096]{1,0:T(8,128)(2,1)S(1)}, bf16[96,4096]{1,0:T(8,128)(2,1)}, u32[]{:S(2)}) copy-start(bf16[96,4096]{1,0:T(8,128)(2,1)} %v_ref.3) | copy-start | bytes 2359300
  14.8 17.7 %copy-start.2 = (bf16[96,4096]{1,0:T(8,128)(2,1)S(1)}, bf16[96,4096]{1,0:T(8,128)(2,1)}, u32[]{:S(2)}) copy-start(bf16[96,4096]{1,0:T(8,128)(2,1)} %v_ref.3) | copy-start | bytes 2359300
  14.8 17.7 %copy-start.3 = (bf16[96,4096]{1,0:T(8,128)(2,1)S(1)}, bf16[96,4096]{1,0:T(8,128)(2,1)}, u32[]{:S(2)}) copy-start(bf16[96,4096]{1,0:T(8,128)(2,1)} %q_ref.3) | copy-start | bytes 2359300
  14.8 12.6 %all-to-all-start.1 = ((bf16[16,128,128]{2,1,0:T(8,128)(2,1)}), bf16[16,128,128]{2,1,0:T(8,128)(2,1)S(1)}, u32[]{:S(2)}, u32[]{:S(2)}) async-start(bf16[16,128,128]{2,1,0:T(8,128)(2,1)} %bitcast.1), calls=%async_computation.1 | async-start | bytes 1048576 | tf_op jit(solution)/shard_map/all_to_all | solution.py:304
  20.0 6.8 %collective-permute-start = (f32[8,128]{1,0:T(8,128)S(1)}, f32[8,128]{1,0:T(8,128)S(1)}, u32[]{:S(2)}, u32[]{:S(2)}) collective-permute-start(f32[8,128]{1,0:T(8,128)S(1)} %get-tuple-element.22.facts), channel_id=1, source_target_pairs={{0,8},{8,16},{16,24},{24,0},{1,9},{9,17},{17,25},{25,1},{2,10},{10... | collective-permute-start | bytes 12296 | tf_op jit(solution)/shard_map/ppermute | solution.py:318
  20.2 7.1 %collective-permute-start.1 = (f32[8,128]{1,0:T(8,128)S(1)}, f32[8,128]{1,0:T(8,128)S(1)}, u32[]{:S(2)}, u32[]{:S(2)}) collective-permute-start(f32[8,128]{1,0:T(8,128)S(1)} %get-tuple-element.22.facts), channel_id=1, source_target_pairs={{0,16},{8,24},{16,0},{24,8},{1,17},{9,25},{17,1},{25,9},{2,18},{10... | collective-permute-start | bytes 12296 | tf_op jit(solution)/shard_map/ppermute | solution.py:318
  20.7 6.6 %collective-permute-start.2 = (f32[8,128]{1,0:T(8,128)S(1)}, f32[8,128]{1,0:T(8,128)S(1)}, u32[]{:S(2)}, u32[]{:S(2)}) collective-permute-start(f32[8,128]{1,0:T(8,128)S(1)} %get-tuple-element.22.facts), channel_id=1, source_target_pairs={{0,24},{8,0},{16,8},{24,16},{1,25},{9,1},{17,9},{25,17},{2,26},{10... | collective-permute-start | bytes 12296 | tf_op jit(solution)/shard_map/ppermute | solution.py:318
  27.6 7.9 %collective-permute-start.3 = (bf16[3,128,128]{2,1,0:T(8,128)(2,1)S(1)}, bf16[3,128,128]{2,1,0:T(8,128)(2,1)S(1)}, u32[]{:S(2)}, u32[]{:S(2)}) collective-permute-start(bf16[3,128,128]{2,1,0:T(8,128)(2,1)S(1)} %get-tuple-element.27.after), channel_id=1, source_target_pairs={{0,4},{1,5},{2,6},{3,7},{4,0},{5,1},{6,2},{7,3},{8,12},{9,13},{10,... | collective-permute-start | bytes 294920 | tf_op jit(solution)/shard_map/ppermute | solution.py:343
  29.1 4.9 %collective-permute-start.4 = (bf16[1,128,128]{2,1,0:T(8,128)(2,1)S(1)}, bf16[1,128,128]{2,1,0:T(8,128)(2,1)S(1)}, u32[]{:S(2)}, u32[]{:S(2)}) collective-permute-start(bf16[1,128,128]{2,1,0:T(8,128)(2,1)S(1)} %get-tuple-element.31), channel_id=1, source_target_pairs={{0,4},{1,5},{2,6},{3,7},{8,12},{9,13},{10,14},{11,15},{16,20},{17,... | collective-permute-start | bytes 98312 | tf_op jit(solution)/shard_map/ppermute | solution.py:344
  33.8 13.9 %copy-start.4 = (f32[4096]{0:T(1024)S(1)}, f32[4096]{0:T(1024)}, u32[]{:S(2)}) copy-start(f32[4096]{0:T(1024)} %param.11) | copy-start | bytes 49156

commit v21 on v20

--- a/solution.py
+++ b/solution.py
@@ -191,7 +191,7 @@
     def over_own(state, c):
         def step(j, state):
             at = c * chunks + j
-            out_ref[at] = state.astype(out_ref.dtype)
+            out_ref[lax.rem(at + out_ref.shape[0] // 2, out_ref.shape[0])] = state.astype(out_ref.dtype)
             keep = linked[pl.ds(c * 2 * chunks + offset + j, 1), :] * one[...]
             return in_ref[newest - at].astype(jnp.float32) + keep * state
 
@@ -216,7 +216,8 @@
     for j in range(0, width // LANES, 2):
         square = []
         for one in (0, 1):
-            state = s_ref[(j + one) * HD : (j + one + 1) * HD, :]
+            at = ((j + one) * HD + s_ref.shape[0] // 2) % s_ref.shape[0]
+            state = s_ref[at : at + HD, :]
             for half in (jnp.where(lane < HD, state, zero), jnp.where(lane < HD, zero, state)):
                 square.append(jnp.concatenate([zero, half] if one else [half, zero], 1))
         columns = slice(j * LANES, (j + 2) * LANES)
@@ -362,7 +363,9 @@
         name="scan",
     )(linked, through, one, half, pieces, early, final, rates)
     states = lax.all_to_all(
-        moved, axes, split_axis=0, concat_axis=0, axis_index_groups=groups, tiled=True
+        moved,
+        axes, split_axis=0, concat_axis=0, tiled=True,
+        axis_index_groups=[members_of[group // 2 :] + members_of[: group // 2] for members_of in groups],
     )
     return pl.pallas_call(
         norm_kernel,

time: 49.9 us -> 50.8 us (1.018)
  blocking collectives: 11.9 us -> 12.8 us
    all_to_all x1, blocking collectives: 11.9 us -> 12.8 us  [local(): lax.all_to_all(moved, axes, split_axis=0, concat_axis=0, tiled=True, axis...]
where the time goes in v21:
time: 50.8 us; the launch traced here: 50.4 us
  starting transfers between devices  19.8 us (39%)
  blocking collectives  12.8 us (25%)
  waiting for transfers between devices  8.29 us (16%)
  Pallas kernels  5.71 us (11%)
  local copies, waits for them, and re-layouts  2.88 us (6%)
  other arithmetic  0.75 us (1%)
    all_to_all x1, blocking collectives, local(): lax.all_to_all(moved, axes, split_axis=0, concat_axis=0, tiled=True, axis...  12.8 us
    all_to_all x1, starting transfers between devices, local(): lax.all_to_all(jnp.broadcast_to(own[None, :], tile.shape), 'uly', split_a...  7.81 us
    ppermute x3, waiting for transfers between devices, local(): lax.ppermute(facts, 'ctx', [(c, (c + ahead) % slices) for c in range(slic...  5.2 us
    all_to_all x1, starting transfers between devices, local(): lax.all_to_all(ends.reshape(group, rows, LANES), axes, split_axis=0, conc...  5.07 us
    ppermute x1, starting transfers between devices, local(): lax.ppermute(final_end, axes, [(low, high) for low, high in swap if low <...  3.36 us
    unnamed x10, local copies, waits for them, and re-layouts  2.28 us
    ppermute x3, starting transfers between devices, local(): lax.ppermute(facts, 'ctx', [(c, (c + ahead) % slices) for c in range(slic...  2.08 us
    pallas_call x1, Pallas kernels, local(): pl.pallas_call(norm_kernel, in_specs=[vmem] * 7, out_specs=pl.BlockSpec(m...  1.88 us
  transfers between devices with their start and end apart: 7, of which 5 were waited for; matrix products, arithmetic and copies ran while one was open for 0% of the time, Pallas kernels for 4%

profile of v21, /device:TPU:0, one launch (start us, length us, event | category | flops | bytes accessed | tf_op | source)
XLA Modules:
  0.0 50.4 jit_solution(7676305165169868524)
XLA Ops:
  0.0 0.7 %convert_add_fusion = f32[128]{0:T(128)S(1)} fusion(s32[96]{0:T(128)} %param.9, f32[8]{0:T(128)} %param.10), kind=kLoop, calls=%fused_computation | loop fusion | flops 256 | bytes 928 | tf_op jit(solution)/shard_map/add | solution.py:276
  0.7 0.6 %broadcast_in_dim.4 = f32[8,1,128]{2,1,0:T(1,128)} broadcast(f32[128]{0:T(128)S(1)} %convert_add_fusion), dimensions={2} | broadcast | bytes 4608 | tf_op jit(solution)/shard_map/broadcast_in_dim | solution.py:281
  1.3 7.8 %all-to-all-start = ((f32[8,1,128]{2,1,0:T(1,128)}), f32[8,1,128]{2,1,0:T(1,128)S(1)}, u32[]{:S(2)}, u32[]{:S(2)}) async-start(f32[8,1,128]{2,1,0:T(1,128)} %broadcast_in_dim.4), calls=%async_computation | async-start | bytes 8192 | tf_op jit(solution)/shard_map/all_to_all | solution.py:280
  9.2 1.1 %copy-done = bf16[96,4096]{1,0:T(8,128)(2,1)S(1)} copy-done((bf16[96,4096]{1,0:T(8,128)(2,1)S(1)}, bf16[96,4096]{1,0:T(8,128)(2,1)}, u32[]{:S(2)}) %copy-start) | copy-done | bytes 786456
  10.3 1.1 %copy-done.1 = bf16[96,4096]{1,0:T(8,128)(2,1)S(1)} copy-done((bf16[96,4096]{1,0:T(8,128)(2,1)S(1)}, bf16[96,4096]{1,0:T(8,128)(2,1)}, u32[]{:S(2)}) %copy-start.1) | copy-done | bytes 786456
  11.4 0.4 turn.1
  11.8 1.4 %all-to-all-done = f32[8,1,128]{2,1,0:T(1,128)S(1)} async-done(((f32[8,1,128]{2,1,0:T(1,128)}), f32[8,1,128]{2,1,0:T(1,128)S(1)}, u32[]{:S(2)}, u32[]{:S(2)}) %all-to-all-start) | async-done | bytes 4128 | tf_op jit(solution)/shard_map/all_to_all | solution.py:280
  13.2 1.6 %ends.1.after = bf16[2048,128]{1,0:T(8,128)(2,1)} custom-call(f32[8,128]{1,0:T(8,128)S(1)} %bitcast.5, bf16[4096,128]{1,0:T(8,128)(2,1)S(1)} %get-tuple-element.19.turned, bf16[128,4096]{1,0:T(8,128)(2,1)S(1)} %get-tuple-element.20.v_ref), custom_call_target="tpu_custom_call" | custom-call | tf_op jit(solution)/shard_map/ends/pallas_call | solution.py:293
  14.8 5.1 %all-to-all-start.1 = ((bf16[16,128,128]{2,1,0:T(8,128)(2,1)}), bf16[16,128,128]{2,1,0:T(8,128)(2,1)S(1)}, u32[]{:S(2)}, u32[]{:S(2)}) async-start(bf16[16,128,128]{2,1,0:T(8,128)(2,1)} %bitcast.1), calls=%async_computation.1 | async-start | bytes 1048576 | tf_op jit(solution)/shard_map/all_to_all | solution.py:305
  19.9 0.2 pass.1
  20.0 0.1 collective-permute-start
  20.2 0.6 %collective-permute-start.1 = (f32[8,128]{1,0:T(8,128)S(1)}, f32[8,128]{1,0:T(8,128)S(1)}, u32[]{:S(2)}, u32[]{:S(2)}) collective-permute-start(f32[8,128]{1,0:T(8,128)S(1)} %get-tuple-element.22.facts), channel_id=1, source_target_pairs={{0,16},{8,24},{16,0},{24,8},{1,17},{9,25},{17,1},{25,9},{2,18},{10... | collective-permute-start | bytes 12296 | tf_op jit(solution)/shard_map/ppermute | solution.py:319
  20.7 1.4 %collective-permute-start.2 = (f32[8,128]{1,0:T(8,128)S(1)}, f32[8,128]{1,0:T(8,128)S(1)}, u32[]{:S(2)}, u32[]{:S(2)}) collective-permute-start(f32[8,128]{1,0:T(8,128)S(1)} %get-tuple-element.22.facts), channel_id=1, source_target_pairs={{0,24},{8,0},{16,8},{24,16},{1,25},{9,1},{17,9},{25,17},{2,26},{10... | collective-permute-start | bytes 12296 | tf_op jit(solution)/shard_map/ppermute | solution.py:319
  22.1 4.8 %collective-permute-done.refs_0_ = f32[8,128]{1,0:T(8,128)S(1)} collective-permute-done((f32[8,128]{1,0:T(8,128)S(1)}, f32[8,128]{1,0:T(8,128)S(1)}, u32[]{:S(2)}, u32[]{:S(2)}) %collective-permute-start) | collective-permute-done | bytes 4128 | tf_op jit(solution)/shard_map/ppermute | solution.py:319
  26.9 0.4 collective-permute-done.1.refs_1_
  27.5 0.1 half.1
  27.6 1.5 %collective-permute-start.3 = (bf16[3,128,128]{2,1,0:T(8,128)(2,1)S(1)}, bf16[3,128,128]{2,1,0:T(8,128)(2,1)S(1)}, u32[]{:S(2)}, u32[]{:S(2)}) collective-permute-start(bf16[3,128,128]{2,1,0:T(8,128)(2,1)S(1)} %get-tuple-element.27.after), channel_id=1, source_target_pairs={{0,4},{1,5},{2,6},{3,7},{4,0},{5,1},{6,2},{7,3},{8,12},{9,13},{10,... | collective-permute-start | bytes 294920 | tf_op jit(solution)/shard_map/ppermute | solution.py:344
  29.1 3.4 %collective-permute-start.4 = (bf16[1,128,128]{2,1,0:T(8,128)(2,1)S(1)}, bf16[1,128,128]{2,1,0:T(8,128)(2,1)S(1)}, u32[]{:S(2)}, u32[]{:S(2)}) collective-permute-start(bf16[1,128,128]{2,1,0:T(8,128)(2,1)S(1)} %get-tuple-element.31), channel_id=1, source_target_pairs={{0,4},{1,5},{2,6},{3,7},{8,12},{9,13},{10,14},{11,15},{16,20},{17,... | collective-permute-start | bytes 98312 | tf_op jit(solution)/shard_map/ppermute | solution.py:345
  32.5 1.3 %inner.1 = (f32[96,4096]{1,0:T(8,128)S(1)}, f32[1,4096]{1,0:T(1,128)S(1)}) custom-call(f32[8,128]{1,0:T(8,128)S(1)} %get-tuple-element.22.facts, f32[96,128]{1,0:T(8,128)S(1)} %get-tuple-element.21.idcol, f32[8,128]{1,0:T(8,128)S(1)} %get-tuple-element.24.idrow, bf16[96,4096]{1,0:T(8,128)(2,1)S(1)} %copy-done.3, ...), custom_call_target="tpu_custom_call" | custom-call | flops 8000000000 | bytes 4000000 | tf_op jit(solution)/shard_map/inner/pallas_call | solution.py:346
  33.8 0.3 collective-permute-done.4.final
  34.1 1.4 %collective-permute-done.3.early = bf16[3,128,128]{2,1,0:T(8,128)(2,1)S(1)} collective-permute-done((bf16[3,128,128]{2,1,0:T(8,128)(2,1)S(1)}, bf16[3,128,128]{2,1,0:T(8,128)(2,1)S(1)}, u32[]{:S(2)}, u32[]{:S(2)}) %collective-permute-start.3) | collective-permute-done | bytes 98336 | tf_op jit(solution)/shard_map/ppermute | solution.py:344
  35.5 0.2 scan.1
  35.7 12.8 %all_to_all.18 = bf16[16,128,128]{2,1,0:T(8,128)(2,1)S(1)} all-to-all(bf16[16,128,128]{2,1,0:T(8,128)(2,1)S(1)} %scan.1), channel_id=1, replica_groups={{16,17,18,19,24,25,26,27,0,1,2,3,8,9,10,11},{20,21,22,23,28,29,30,31,4,..., dimensions={0} | all-to-all | bytes 1048576 | tf_op jit(solution)/shard_map/all_to_all | solution.py:365
  48.5 1.9 %norm.1 = bf16[96,4096]{1,0:T(8,128)(2,1)} custom-call(f32[96,128]{1,0:T(8,128)S(1)} %get-tuple-element.21.idcol, f32[1,128]{1,0:T(1,128)S(1)} %get-tuple-element.23.before, f32[1,4096]{1,0:T(1,128)S(1)} %get-tuple-element.28.after.rates, bf16[96,4096]{1,0:T(8,128)(2,1)S(1)} %copy-done.3, bf16[2048,128]{1,0:T(8,128)(2,1)S(1)} %bitcast.4, ...), custom_call_target="tpu_custom_call" | custom-call | tf_op jit(solution)/shard_map/norm/pallas_call | solution.py:370
  (11 shorter events, 0.1 us)
Async XLA Ops:
  1.3 11.8 %all-to-all-start = ((f32[8,1,128]{2,1,0:T(1,128)}), f32[8,1,128]{2,1,0:T(1,128)S(1)}, u32[]{:S(2)}, u32[]{:S(2)}) async-start(f32[8,1,128]{2,1,0:T(1,128)} %broadcast_in_dim.4), calls=%async_computation | async-start | bytes 8192 | tf_op jit(solution)/shard_map/all_to_all | solution.py:280
  9.2 1.1 %copy-start = (bf16[96,4096]{1,0:T(8,128)(2,1)S(1)}, bf16[96,4096]{1,0:T(8,128)(2,1)}, u32[]{:S(2)}) copy-start(bf16[96,4096]{1,0:T(8,128)(2,1)} %k_ref.1) | copy-start | bytes 2359300
  10.3 1.1 %copy-start.1 = (bf16[96,4096]{1,0:T(8,128)(2,1)S(1)}, bf16[96,4096]{1,0:T(8,128)(2,1)}, u32[]{:S(2)}) copy-start(bf16[96,4096]{1,0:T(8,128)(2,1)} %v_ref.3) | copy-start | bytes 2359300
  14.8 17.7 %copy-start.2 = (bf16[96,4096]{1,0:T(8,128)(2,1)S(1)}, bf16[96,4096]{1,0:T(8,128)(2,1)}, u32[]{:S(2)}) copy-start(bf16[96,4096]{1,0:T(8,128)(2,1)} %v_ref.3) | copy-start | bytes 2359300
  14.8 17.7 %copy-start.3 = (bf16[96,4096]{1,0:T(8,128)(2,1)S(1)}, bf16[96,4096]{1,0:T(8,128)(2,1)}, u32[]{:S(2)}) copy-start(bf16[96,4096]{1,0:T(8,128)(2,1)} %q_ref.3) | copy-start | bytes 2359300
  14.8 12.6 %all-to-all-start.1 = ((bf16[16,128,128]{2,1,0:T(8,128)(2,1)}), bf16[16,128,128]{2,1,0:T(8,128)(2,1)S(1)}, u32[]{:S(2)}, u32[]{:S(2)}) async-start(bf16[16,128,128]{2,1,0:T(8,128)(2,1)} %bitcast.1), calls=%async_computation.1 | async-start | bytes 1048576 | tf_op jit(solution)/shard_map/all_to_all | solution.py:305
  20.0 6.8 %collective-permute-start = (f32[8,128]{1,0:T(8,128)S(1)}, f32[8,128]{1,0:T(8,128)S(1)}, u32[]{:S(2)}, u32[]{:S(2)}) collective-permute-start(f32[8,128]{1,0:T(8,128)S(1)} %get-tuple-element.22.facts), channel_id=1, source_target_pairs={{0,8},{8,16},{16,24},{24,0},{1,9},{9,17},{17,25},{25,1},{2,10},{10... | collective-permute-start | bytes 12296 | tf_op jit(solution)/shard_map/ppermute | solution.py:319
  20.2 7.1 %collective-permute-start.1 = (f32[8,128]{1,0:T(8,128)S(1)}, f32[8,128]{1,0:T(8,128)S(1)}, u32[]{:S(2)}, u32[]{:S(2)}) collective-permute-start(f32[8,128]{1,0:T(8,128)S(1)} %get-tuple-element.22.facts), channel_id=1, source_target_pairs={{0,16},{8,24},{16,0},{24,8},{1,17},{9,25},{17,1},{25,9},{2,18},{10... | collective-permute-start | bytes 12296 | tf_op jit(solution)/shard_map/ppermute | solution.py:319
  20.7 6.6 %collective-permute-start.2 = (f32[8,128]{1,0:T(8,128)S(1)}, f32[8,128]{1,0:T(8,128)S(1)}, u32[]{:S(2)}, u32[]{:S(2)}) collective-permute-start(f32[8,128]{1,0:T(8,128)S(1)} %get-tuple-element.22.facts), channel_id=1, source_target_pairs={{0,24},{8,0},{16,8},{24,16},{1,25},{9,1},{17,9},{25,17},{2,26},{10... | collective-permute-start | bytes 12296 | tf_op jit(solution)/shard_map/ppermute | solution.py:319
  27.6 7.9 %collective-permute-start.3 = (bf16[3,128,128]{2,1,0:T(8,128)(2,1)S(1)}, bf16[3,128,128]{2,1,0:T(8,128)(2,1)S(1)}, u32[]{:S(2)}, u32[]{:S(2)}) collective-permute-start(bf16[3,128,128]{2,1,0:T(8,128)(2,1)S(1)} %get-tuple-element.27.after), channel_id=1, source_target_pairs={{0,4},{1,5},{2,6},{3,7},{4,0},{5,1},{6,2},{7,3},{8,12},{9,13},{10,... | collective-permute-start | bytes 294920 | tf_op jit(solution)/shard_map/ppermute | solution.py:344
  29.1 4.9 %collective-permute-start.4 = (bf16[1,128,128]{2,1,0:T(8,128)(2,1)S(1)}, bf16[1,128,128]{2,1,0:T(8,128)(2,1)S(1)}, u32[]{:S(2)}, u32[]{:S(2)}) collective-permute-start(bf16[1,128,128]{2,1,0:T(8,128)(2,1)S(1)} %get-tuple-element.31), channel_id=1, source_target_pairs={{0,4},{1,5},{2,6},{3,7},{8,12},{9,13},{10,14},{11,15},{16,20},{17,... | collective-permute-start | bytes 98312 | tf_op jit(solution)/shard_map/ppermute | solution.py:345
  33.8 14.7 %copy-start.4 = (f32[4096]{0:T(1024)S(1)}, f32[4096]{0:T(1024)}, u32[]{:S(2)}) copy-start(f32[4096]{0:T(1024)} %param.11) | copy-start | bytes 49156

commit v22 on v20

--- a/solution.py
+++ b/solution.py
@@ -232,16 +232,16 @@
     mean = jnp.sum(total, axis=1, keepdims=True) / float(width)
     scale = jnp.broadcast_to(lax.rsqrt(mean + 1e-06), (tokens, LANES))
     parts = sems.shape[0]
-    share = width // parts
+    share = tokens // parts
     copies = []
     for part in range(parts):
-        for at in range(part * share, (part + 1) * share, LANES):
+        rows = slice(part * share, (part + 1) * share)
+        for at in range(0, width, LANES):
             columns = slice(at, at + LANES)
-            done[:, columns] = (raw[:, columns] * scale * gain[:, columns]).astype(jnp.bfloat16)
-        columns = slice(part * share, (part + 1) * share)
-        copies.append(
-            pltpu.make_async_copy(done.at[:, columns], out_ref.at[:, columns], sems.at[part])
-        )
+            done[rows, columns] = (raw[rows, columns] * scale[rows] * gain[:, columns]).astype(
+                jnp.bfloat16
+            )
+        copies.append(pltpu.make_async_copy(done.at[rows], out_ref.at[rows], sems.at[part]))
         copies[-1].start()
     for copy in copies:
         copy.wait()
@@ -372,7 +372,7 @@
         scratch_shapes=[
             pltpu.VMEM((tokens, width), jnp.float32),
             pltpu.VMEM((tokens, width), jnp.bfloat16),
-            pltpu.SemaphoreType.DMA((16,)),
+            pltpu.SemaphoreType.DMA((tokens // 16,)),
         ],
         compiler_params=params,
         name="norm",

time: 49.9 us -> 49.8 us (level)
  no operation moved by 1% of the time
where the time goes in v22:
time: 49.8 us; the launch traced here: 49.3 us
  starting transfers between devices  19.8 us (40%)
  blocking collectives  11.9 us (24%)
  waiting for transfers between devices  8.29 us (17%)
  Pallas kernels  5.52 us (11%)
  local copies, waits for them, and re-layouts  2.88 us (6%)
  other arithmetic  0.75 us (2%)
    all_to_all x1, blocking collectives, local(): lax.all_to_all(moved, axes, split_axis=0, concat_axis=0, axis_index_group...  11.9 us
    all_to_all x1, starting transfers between devices, local(): lax.all_to_all(jnp.broadcast_to(own[None, :], tile.shape), 'uly', split_a...  7.81 us
    ppermute x3, waiting for transfers between devices, local(): lax.ppermute(facts, 'ctx', [(c, (c + ahead) % slices) for c in range(slic...  5.2 us
    all_to_all x1, starting transfers between devices, local(): lax.all_to_all(ends.reshape(group, rows, LANES), axes, split_axis=0, conc...  5.07 us
    ppermute x1, starting transfers between devices, local(): lax.ppermute(final_end, axes, [(low, high) for low, high in swap if low <...  3.36 us
    unnamed x10, local copies, waits for them, and re-layouts  2.28 us
    ppermute x3, starting transfers between devices, local(): lax.ppermute(facts, 'ctx', [(c, (c + ahead) % slices) for c in range(slic...  2.08 us
    pallas_call x1, Pallas kernels, local(): pl.pallas_call(norm_kernel, in_specs=[vmem] * 7, out_specs=pl.BlockSpec(m...  1.68 us
  transfers between devices with their start and end apart: 7, of which 5 were waited for; matrix products, arithmetic and copies ran while one was open for 0% of the time, Pallas kernels for 4%

profile of v22, /device:TPU:0, one launch (start us, length us, event | category | flops | bytes accessed | tf_op | source)
XLA Modules:
  0.0 49.3 jit_solution(14888413621244057135)
XLA Ops:
  0.0 0.7 %convert_add_fusion = f32[128]{0:T(128)S(1)} fusion(s32[96]{0:T(128)} %param.9, f32[8]{0:T(128)} %param.10), kind=kLoop, calls=%fused_computation | loop fusion | flops 256 | bytes 928 | tf_op jit(solution)/shard_map/add | solution.py:275
  0.7 0.6 %broadcast_in_dim.4 = f32[8,1,128]{2,1,0:T(1,128)} broadcast(f32[128]{0:T(128)S(1)} %convert_add_fusion), dimensions={2} | broadcast | bytes 4608 | tf_op jit(solution)/shard_map/broadcast_in_dim | solution.py:280
  1.3 7.8 %all-to-all-start = ((f32[8,1,128]{2,1,0:T(1,128)}), f32[8,1,128]{2,1,0:T(1,128)S(1)}, u32[]{:S(2)}, u32[]{:S(2)}) async-start(f32[8,1,128]{2,1,0:T(1,128)} %broadcast_in_dim.4), calls=%async_computation | async-start | bytes 8192 | tf_op jit(solution)/shard_map/all_to_all | solution.py:279
  9.2 1.1 %copy-done = bf16[96,4096]{1,0:T(8,128)(2,1)S(1)} copy-done((bf16[96,4096]{1,0:T(8,128)(2,1)S(1)}, bf16[96,4096]{1,0:T(8,128)(2,1)}, u32[]{:S(2)}) %copy-start) | copy-done | bytes 786456
  10.3 1.1 %copy-done.1 = bf16[96,4096]{1,0:T(8,128)(2,1)S(1)} copy-done((bf16[96,4096]{1,0:T(8,128)(2,1)S(1)}, bf16[96,4096]{1,0:T(8,128)(2,1)}, u32[]{:S(2)}) %copy-start.1) | copy-done | bytes 786456
  11.4 0.4 turn.1
  11.8 1.4 %all-to-all-done = f32[8,1,128]{2,1,0:T(1,128)S(1)} async-done(((f32[8,1,128]{2,1,0:T(1,128)}), f32[8,1,128]{2,1,0:T(1,128)S(1)}, u32[]{:S(2)}, u32[]{:S(2)}) %all-to-all-start) | async-done | bytes 4128 | tf_op jit(solution)/shard_map/all_to_all | solution.py:279
  13.2 1.6 %ends.1.after = bf16[2048,128]{1,0:T(8,128)(2,1)} custom-call(f32[8,128]{1,0:T(8,128)S(1)} %bitcast.5, bf16[4096,128]{1,0:T(8,128)(2,1)S(1)} %get-tuple-element.19.turned, bf16[128,4096]{1,0:T(8,128)(2,1)S(1)} %get-tuple-element.20.v_ref), custom_call_target="tpu_custom_call" | custom-call | tf_op jit(solution)/shard_map/ends/pallas_call | solution.py:292
  14.8 5.1 %all-to-all-start.1 = ((bf16[16,128,128]{2,1,0:T(8,128)(2,1)}), bf16[16,128,128]{2,1,0:T(8,128)(2,1)S(1)}, u32[]{:S(2)}, u32[]{:S(2)}) async-start(bf16[16,128,128]{2,1,0:T(8,128)(2,1)} %bitcast.1), calls=%async_computation.1 | async-start | bytes 1048576 | tf_op jit(solution)/shard_map/all_to_all | solution.py:304
  19.9 0.2 pass.1
  20.0 0.1 collective-permute-start
  20.2 0.6 %collective-permute-start.1 = (f32[8,128]{1,0:T(8,128)S(1)}, f32[8,128]{1,0:T(8,128)S(1)}, u32[]{:S(2)}, u32[]{:S(2)}) collective-permute-start(f32[8,128]{1,0:T(8,128)S(1)} %get-tuple-element.22.facts), channel_id=1, source_target_pairs={{0,16},{8,24},{16,0},{24,8},{1,17},{9,25},{17,1},{25,9},{2,18},{10... | collective-permute-start | bytes 12296 | tf_op jit(solution)/shard_map/ppermute | solution.py:318
  20.7 1.4 %collective-permute-start.2 = (f32[8,128]{1,0:T(8,128)S(1)}, f32[8,128]{1,0:T(8,128)S(1)}, u32[]{:S(2)}, u32[]{:S(2)}) collective-permute-start(f32[8,128]{1,0:T(8,128)S(1)} %get-tuple-element.22.facts), channel_id=1, source_target_pairs={{0,24},{8,0},{16,8},{24,16},{1,25},{9,1},{17,9},{25,17},{2,26},{10... | collective-permute-start | bytes 12296 | tf_op jit(solution)/shard_map/ppermute | solution.py:318
  22.1 4.8 %collective-permute-done.refs_0_ = f32[8,128]{1,0:T(8,128)S(1)} collective-permute-done((f32[8,128]{1,0:T(8,128)S(1)}, f32[8,128]{1,0:T(8,128)S(1)}, u32[]{:S(2)}, u32[]{:S(2)}) %collective-permute-start) | collective-permute-done | bytes 4128 | tf_op jit(solution)/shard_map/ppermute | solution.py:318
  26.9 0.4 collective-permute-done.1.refs_1_
  27.5 0.1 half.1
  27.6 1.5 %collective-permute-start.3 = (bf16[3,128,128]{2,1,0:T(8,128)(2,1)S(1)}, bf16[3,128,128]{2,1,0:T(8,128)(2,1)S(1)}, u32[]{:S(2)}, u32[]{:S(2)}) collective-permute-start(bf16[3,128,128]{2,1,0:T(8,128)(2,1)S(1)} %get-tuple-element.27.after), channel_id=1, source_target_pairs={{0,4},{1,5},{2,6},{3,7},{4,0},{5,1},{6,2},{7,3},{8,12},{9,13},{10,... | collective-permute-start | bytes 294920 | tf_op jit(solution)/shard_map/ppermute | solution.py:343
  29.1 3.4 %collective-permute-start.4 = (bf16[1,128,128]{2,1,0:T(8,128)(2,1)S(1)}, bf16[1,128,128]{2,1,0:T(8,128)(2,1)S(1)}, u32[]{:S(2)}, u32[]{:S(2)}) collective-permute-start(bf16[1,128,128]{2,1,0:T(8,128)(2,1)S(1)} %get-tuple-element.31), channel_id=1, source_target_pairs={{0,4},{1,5},{2,6},{3,7},{8,12},{9,13},{10,14},{11,15},{16,20},{17,... | collective-permute-start | bytes 98312 | tf_op jit(solution)/shard_map/ppermute | solution.py:344
  32.5 1.3 %inner.1 = (f32[96,4096]{1,0:T(8,128)S(1)}, f32[1,4096]{1,0:T(1,128)S(1)}) custom-call(f32[8,128]{1,0:T(8,128)S(1)} %get-tuple-element.22.facts, f32[96,128]{1,0:T(8,128)S(1)} %get-tuple-element.21.idcol, f32[8,128]{1,0:T(8,128)S(1)} %get-tuple-element.24.idrow, bf16[96,4096]{1,0:T(8,128)(2,1)S(1)} %copy-done.3, ...), custom_call_target="tpu_custom_call" | custom-call | flops 8000000000 | bytes 4000000 | tf_op jit(solution)/shard_map/inner/pallas_call | solution.py:345
  33.8 0.3 collective-permute-done.4.final
  34.1 1.4 %collective-permute-done.3.early = bf16[3,128,128]{2,1,0:T(8,128)(2,1)S(1)} collective-permute-done((bf16[3,128,128]{2,1,0:T(8,128)(2,1)S(1)}, bf16[3,128,128]{2,1,0:T(8,128)(2,1)S(1)}, u32[]{:S(2)}, u32[]{:S(2)}) %collective-permute-start.3) | collective-permute-done | bytes 98336 | tf_op jit(solution)/shard_map/ppermute | solution.py:343
  35.5 0.2 scan.1
  35.7 11.9 %all_to_all.18 = bf16[16,128,128]{2,1,0:T(8,128)(2,1)S(1)} all-to-all(bf16[16,128,128]{2,1,0:T(8,128)(2,1)S(1)} %scan.1), channel_id=1, replica_groups={{0,1,2,3,8,9,10,11,16,17,18,19,24,25,26,27},{4,5,6,7,12,13,14,15,20,21,..., dimensions={0} | all-to-all | bytes 1048576 | tf_op jit(solution)/shard_map/all_to_all | solution.py:364
  47.7 1.7 %norm.1 = bf16[96,4096]{1,0:T(8,128)(2,1)} custom-call(f32[96,128]{1,0:T(8,128)S(1)} %get-tuple-element.21.idcol, f32[1,128]{1,0:T(1,128)S(1)} %get-tuple-element.23.before, f32[1,4096]{1,0:T(1,128)S(1)} %get-tuple-element.28.after.rates, bf16[96,4096]{1,0:T(8,128)(2,1)S(1)} %copy-done.3, bf16[2048,128]{1,0:T(8,128)(2,1)S(1)} %bitcast.4, ...), custom_call_target="tpu_custom_call" | custom-call | tf_op jit(solution)/shard_map/norm/pallas_call | solution.py:367
  (11 shorter events, 0.1 us)
Async XLA Ops:
  1.3 11.8 %all-to-all-start = ((f32[8,1,128]{2,1,0:T(1,128)}), f32[8,1,128]{2,1,0:T(1,128)S(1)}, u32[]{:S(2)}, u32[]{:S(2)}) async-start(f32[8,1,128]{2,1,0:T(1,128)} %broadcast_in_dim.4), calls=%async_computation | async-start | bytes 8192 | tf_op jit(solution)/shard_map/all_to_all | solution.py:279
  9.2 1.1 %copy-start = (bf16[96,4096]{1,0:T(8,128)(2,1)S(1)}, bf16[96,4096]{1,0:T(8,128)(2,1)}, u32[]{:S(2)}) copy-start(bf16[96,4096]{1,0:T(8,128)(2,1)} %k_ref.1) | copy-start | bytes 2359300
  10.3 1.1 %copy-start.1 = (bf16[96,4096]{1,0:T(8,128)(2,1)S(1)}, bf16[96,4096]{1,0:T(8,128)(2,1)}, u32[]{:S(2)}) copy-start(bf16[96,4096]{1,0:T(8,128)(2,1)} %v_ref.3) | copy-start | bytes 2359300
  14.8 17.7 %copy-start.2 = (bf16[96,4096]{1,0:T(8,128)(2,1)S(1)}, bf16[96,4096]{1,0:T(8,128)(2,1)}, u32[]{:S(2)}) copy-start(bf16[96,4096]{1,0:T(8,128)(2,1)} %v_ref.3) | copy-start | bytes 2359300
  14.8 17.7 %copy-start.3 = (bf16[96,4096]{1,0:T(8,128)(2,1)S(1)}, bf16[96,4096]{1,0:T(8,128)(2,1)}, u32[]{:S(2)}) copy-start(bf16[96,4096]{1,0:T(8,128)(2,1)} %q_ref.3) | copy-start | bytes 2359300
  14.8 12.6 %all-to-all-start.1 = ((bf16[16,128,128]{2,1,0:T(8,128)(2,1)}), bf16[16,128,128]{2,1,0:T(8,128)(2,1)S(1)}, u32[]{:S(2)}, u32[]{:S(2)}) async-start(bf16[16,128,128]{2,1,0:T(8,128)(2,1)} %bitcast.1), calls=%async_computation.1 | async-start | bytes 1048576 | tf_op jit(solution)/shard_map/all_to_all | solution.py:304
  20.0 6.8 %collective-permute-start = (f32[8,128]{1,0:T(8,128)S(1)}, f32[8,128]{1,0:T(8,128)S(1)}, u32[]{:S(2)}, u32[]{:S(2)}) collective-permute-start(f32[8,128]{1,0:T(8,128)S(1)} %get-tuple-element.22.facts), channel_id=1, source_target_pairs={{0,8},{8,16},{16,24},{24,0},{1,9},{9,17},{17,25},{25,1},{2,10},{10... | collective-permute-start | bytes 12296 | tf_op jit(solution)/shard_map/ppermute | solution.py:318
  20.2 7.1 %collective-permute-start.1 = (f32[8,128]{1,0:T(8,128)S(1)}, f32[8,128]{1,0:T(8,128)S(1)}, u32[]{:S(2)}, u32[]{:S(2)}) collective-permute-start(f32[8,128]{1,0:T(8,128)S(1)} %get-tuple-element.22.facts), channel_id=1, source_target_pairs={{0,16},{8,24},{16,0},{24,8},{1,17},{9,25},{17,1},{25,9},{2,18},{10... | collective-permute-start | bytes 12296 | tf_op jit(solution)/shard_map/ppermute | solution.py:318
  20.7 6.6 %collective-permute-start.2 = (f32[8,128]{1,0:T(8,128)S(1)}, f32[8,128]{1,0:T(8,128)S(1)}, u32[]{:S(2)}, u32[]{:S(2)}) collective-permute-start(f32[8,128]{1,0:T(8,128)S(1)} %get-tuple-element.22.facts), channel_id=1, source_target_pairs={{0,24},{8,0},{16,8},{24,16},{1,25},{9,1},{17,9},{25,17},{2,26},{10... | collective-permute-start | bytes 12296 | tf_op jit(solution)/shard_map/ppermute | solution.py:318
  27.6 7.9 %collective-permute-start.3 = (bf16[3,128,128]{2,1,0:T(8,128)(2,1)S(1)}, bf16[3,128,128]{2,1,0:T(8,128)(2,1)S(1)}, u32[]{:S(2)}, u32[]{:S(2)}) collective-permute-start(bf16[3,128,128]{2,1,0:T(8,128)(2,1)S(1)} %get-tuple-element.27.after), channel_id=1, source_target_pairs={{0,4},{1,5},{2,6},{3,7},{4,0},{5,1},{6,2},{7,3},{8,12},{9,13},{10,... | collective-permute-start | bytes 294920 | tf_op jit(solution)/shard_map/ppermute | solution.py:343
  29.1 4.9 %collective-permute-start.4 = (bf16[1,128,128]{2,1,0:T(8,128)(2,1)S(1)}, bf16[1,128,128]{2,1,0:T(8,128)(2,1)S(1)}, u32[]{:S(2)}, u32[]{:S(2)}) collective-permute-start(bf16[1,128,128]{2,1,0:T(8,128)(2,1)S(1)} %get-tuple-element.31), channel_id=1, source_target_pairs={{0,4},{1,5},{2,6},{3,7},{8,12},{9,13},{10,14},{11,15},{16,20},{17,... | collective-permute-start | bytes 98312 | tf_op jit(solution)/shard_map/ppermute | solution.py:344
  33.8 13.9 %copy-start.4 = (f32[4096]{0:T(1024)S(1)}, f32[4096]{0:T(1024)}, u32[]{:S(2)}) copy-start(f32[4096]{0:T(1024)} %param.11) | copy-start | bytes 49156

commit v23 on v22

--- a/solution.py
+++ b/solution.py
@@ -25,6 +25,24 @@
             jnp.sum(jnp.where(lane == lax.rem(head, here), row, 0.0), axis=1, keepdims=True)
         )
     return jnp.where(lane < HD, rates[0], rates[1])
+
+
+def own_kernel(rates, ids, out_ref, rates_here, ids_here, rows, sems):
+    here, tokens = rates.shape[1], ids.shape[1]
+    copies = [
+        pltpu.make_async_copy(rates, rates_here, sems.at[0]),
+        pltpu.make_async_copy(ids, ids_here, sems.at[1]),
+    ]
+    for copy in copies:
+        copy.start()
+    for copy in copies:
+        copy.wait()
+    blank = jnp.zeros((1, LANES - tokens - here), jnp.float32)
+    row = jnp.concatenate([rates_here[...], blank, ids_here[...].astype(jnp.float32)], 1)
+    rows[...] = jnp.broadcast_to(row, rows.shape)
+    done = pltpu.make_async_copy(rows, out_ref, sems.at[2])
+    done.start()
+    done.wait()
 
 
 def turn_kernel(k_ref, v_ref, turned, filled):
@@ -272,12 +290,23 @@
     shape = jax.ShapeDtypeStruct
     tile = shape((members, LANES), jnp.float32)
 
-    own = jnp.pad(decay_rate, (0, LANES - here)) + jnp.pad(
-        doc_ids, (LANES - tokens, 0)
-    ).astype(jnp.float32)
+    own = pl.pallas_call(
+        own_kernel,
+        in_specs=[pl.BlockSpec(memory_space=pl.ANY)] * 2,
+        out_specs=pl.BlockSpec(memory_space=pl.ANY),
+        out_shape=tile,
+        scratch_shapes=[
+            pltpu.VMEM((1, here), jnp.float32),
+            pltpu.VMEM((1, tokens), jnp.int32),
+            pltpu.VMEM(tile.shape, jnp.float32),
+            pltpu.SemaphoreType.DMA((3,)),
+        ],
+        compiler_params=pltpu.CompilerParams(vmem_limit_bytes=62 * 1024 * 1024),
+        name="own",
+    )(decay_rate[None, :], doc_ids[None, :])
     turned_round = [[(u + members // 2) % members for u in range(members)]]
     stored = lax.all_to_all(
-        jnp.broadcast_to(own[None, :], tile.shape),
+        own,
         "uly", split_axis=0, concat_axis=0, axis_index_groups=turned_round, tiled=True,
     )
     turned, filled = pl.pallas_call(

time: 49.8 us -> 49.7 us (level)
  Pallas kernels: 5.52 us -> 6.82 us
  other arithmetic: 0.75 us -> 0 us
  local copies, waits for them, and re-layouts: 2.88 us -> 2.28 us
    pallas_call x0 -> x1, Pallas kernels: none -> 1.36 us  [local(): pl.pallas_call(own_kernel, in_specs=[pl.BlockSpec(memory_space=pl.ANY)] *...]
    add x1 -> x0, other arithmetic: 0.75 us -> none  [local(): jnp.pad(decay_rate, (0, LANES - here))]
    broadcast_in_dim x1 -> x0, local copies, waits for them, and re-layouts: 0.6 us -> none  [local(): jnp.broadcast_to(own[None, :], tile.shape)]
where the time goes in v23:
time: 49.7 us; the launch traced here: 49.3 us
  starting transfers between devices  19.9 us (40%)
  blocking collectives  11.9 us (24%)
  waiting for transfers between devices  8.29 us (17%)
  Pallas kernels  6.82 us (14%)
  local copies, waits for them, and re-layouts  2.28 us (5%)
    all_to_all x1, blocking collectives, local(): lax.all_to_all(moved, axes, split_axis=0, concat_axis=0, axis_index_group...  11.9 us
    all_to_all x1, starting transfers between devices, local(): lax.all_to_all(own, 'uly', split_axis=0, concat_axis=0, axis_index_groups...  7.83 us
    ppermute x3, waiting for transfers between devices, local(): lax.ppermute(facts, 'ctx', [(c, (c + ahead) % slices) for c in range(slic...  5.2 us
    all_to_all x1, starting transfers between devices, local(): lax.all_to_all(ends.reshape(group, rows, LANES), axes, split_axis=0, conc...  5.07 us
    ppermute x1, starting transfers between devices, local(): lax.ppermute(final_end, axes, [(low, high) for low, high in swap if low <...  3.36 us
    unnamed x10, local copies, waits for them, and re-layouts  2.28 us
    ppermute x3, starting transfers between devices, local(): lax.ppermute(facts, 'ctx', [(c, (c + ahead) % slices) for c in range(slic...  2.08 us
    pallas_call x1, Pallas kernels, local(): pl.pallas_call(norm_kernel, in_specs=[vmem] * 7, out_specs=pl.BlockSpec(m...  1.62 us
  transfers between devices with their start and end apart: 7, of which 5 were waited for; matrix products, arithmetic and copies ran while one was open for 0% of the time, Pallas kernels for 4%

profile of v23, /device:TPU:0, one launch (start us, length us, event | category | flops | bytes accessed | tf_op | source)
XLA Modules:
  0.0 49.3 jit_solution(16112511013538000572)
XLA Ops:
  0.0 1.4 %own.1 = f32[8,128]{1,0:T(8,128)} custom-call(f32[1,8]{1,0:T(1,128)} %bitcast.14, s32[1,96]{1,0:T(1,128)} %bitcast.15), custom_call_target="tpu_custom_call" | custom-call | tf_op jit(solution)/shard_map/own/pallas_call | solution.py:293
  1.4 7.8 %all-to-all-start = ((f32[8,1,128]{2,1,0:T(1,128)}), f32[8,1,128]{2,1,0:T(1,128)S(1)}, u32[]{:S(2)}, u32[]{:S(2)}) async-start(f32[8,1,128]{2,1,0:T(1,128)} %bitcast.13), calls=%async_computation | async-start | bytes 8192 | tf_op jit(solution)/shard_map/all_to_all | solution.py:308
  9.2 1.1 %copy-done = bf16[96,4096]{1,0:T(8,128)(2,1)S(1)} copy-done((bf16[96,4096]{1,0:T(8,128)(2,1)S(1)}, bf16[96,4096]{1,0:T(8,128)(2,1)}, u32[]{:S(2)}) %copy-start) | copy-done | bytes 786456
  10.3 1.1 %copy-done.1 = bf16[96,4096]{1,0:T(8,128)(2,1)S(1)} copy-done((bf16[96,4096]{1,0:T(8,128)(2,1)S(1)}, bf16[96,4096]{1,0:T(8,128)(2,1)}, u32[]{:S(2)}) %copy-start.1) | copy-done | bytes 786456
  11.5 0.4 turn.1
  11.8 1.4 %all-to-all-done = f32[8,1,128]{2,1,0:T(1,128)S(1)} async-done(((f32[8,1,128]{2,1,0:T(1,128)}), f32[8,1,128]{2,1,0:T(1,128)S(1)}, u32[]{:S(2)}, u32[]{:S(2)}) %all-to-all-start) | async-done | bytes 4128 | tf_op jit(solution)/shard_map/all_to_all | solution.py:308
  13.2 1.6 %ends.1.after = bf16[2048,128]{1,0:T(8,128)(2,1)} custom-call(f32[8,128]{1,0:T(8,128)S(1)} %bitcast.10, bf16[4096,128]{1,0:T(8,128)(2,1)S(1)} %get-tuple-element.19.turned, bf16[128,4096]{1,0:T(8,128)(2,1)S(1)} %get-tuple-element.20.v_ref), custom_call_target="tpu_custom_call" | custom-call | tf_op jit(solution)/shard_map/ends/pallas_call | solution.py:321
  14.8 5.1 %all-to-all-start.1 = ((bf16[16,128,128]{2,1,0:T(8,128)(2,1)}), bf16[16,128,128]{2,1,0:T(8,128)(2,1)S(1)}, u32[]{:S(2)}, u32[]{:S(2)}) async-start(bf16[16,128,128]{2,1,0:T(8,128)(2,1)} %bitcast.5), calls=%async_computation.1 | async-start | bytes 1048576 | tf_op jit(solution)/shard_map/all_to_all | solution.py:333
  19.9 0.2 pass.1
  20.1 0.1 collective-permute-start
  20.2 0.6 %collective-permute-start.1 = (f32[8,128]{1,0:T(8,128)S(1)}, f32[8,128]{1,0:T(8,128)S(1)}, u32[]{:S(2)}, u32[]{:S(2)}) collective-permute-start(f32[8,128]{1,0:T(8,128)S(1)} %get-tuple-element.22.facts), channel_id=1, source_target_pairs={{0,16},{8,24},{16,0},{24,8},{1,17},{9,25},{17,1},{25,9},{2,18},{10... | collective-permute-start | bytes 12296 | tf_op jit(solution)/shard_map/ppermute | solution.py:347
  20.8 1.4 %collective-permute-start.2 = (f32[8,128]{1,0:T(8,128)S(1)}, f32[8,128]{1,0:T(8,128)S(1)}, u32[]{:S(2)}, u32[]{:S(2)}) collective-permute-start(f32[8,128]{1,0:T(8,128)S(1)} %get-tuple-element.22.facts), channel_id=1, source_target_pairs={{0,24},{8,0},{16,8},{24,16},{1,25},{9,1},{17,9},{25,17},{2,26},{10... | collective-permute-start | bytes 12296 | tf_op jit(solution)/shard_map/ppermute | solution.py:347
  22.2 4.8 %collective-permute-done.refs_0_ = f32[8,128]{1,0:T(8,128)S(1)} collective-permute-done((f32[8,128]{1,0:T(8,128)S(1)}, f32[8,128]{1,0:T(8,128)S(1)}, u32[]{:S(2)}, u32[]{:S(2)}) %collective-permute-start) | collective-permute-done | bytes 4128 | tf_op jit(solution)/shard_map/ppermute | solution.py:347
  26.9 0.4 collective-permute-done.1.refs_1_
  27.4 0.1 link.1
  27.5 0.1 half.1
  27.6 1.5 %collective-permute-start.3 = (bf16[3,128,128]{2,1,0:T(8,128)(2,1)S(1)}, bf16[3,128,128]{2,1,0:T(8,128)(2,1)S(1)}, u32[]{:S(2)}, u32[]{:S(2)}) collective-permute-start(bf16[3,128,128]{2,1,0:T(8,128)(2,1)S(1)} %get-tuple-element.27.after), channel_id=1, source_target_pairs={{0,4},{1,5},{2,6},{3,7},{4,0},{5,1},{6,2},{7,3},{8,12},{9,13},{10,... | collective-permute-start | bytes 294920 | tf_op jit(solution)/shard_map/ppermute | solution.py:372
  29.2 3.4 %collective-permute-start.4 = (bf16[1,128,128]{2,1,0:T(8,128)(2,1)S(1)}, bf16[1,128,128]{2,1,0:T(8,128)(2,1)S(1)}, u32[]{:S(2)}, u32[]{:S(2)}) collective-permute-start(bf16[1,128,128]{2,1,0:T(8,128)(2,1)S(1)} %get-tuple-element.31), channel_id=1, source_target_pairs={{0,4},{1,5},{2,6},{3,7},{8,12},{9,13},{10,14},{11,15},{16,20},{17,... | collective-permute-start | bytes 98312 | tf_op jit(solution)/shard_map/ppermute | solution.py:373
  32.5 1.3 %inner.1 = (f32[96,4096]{1,0:T(8,128)S(1)}, f32[1,4096]{1,0:T(1,128)S(1)}) custom-call(f32[8,128]{1,0:T(8,128)S(1)} %get-tuple-element.22.facts, f32[96,128]{1,0:T(8,128)S(1)} %get-tuple-element.21.idcol, f32[8,128]{1,0:T(8,128)S(1)} %get-tuple-element.24.idrow, bf16[96,4096]{1,0:T(8,128)(2,1)S(1)} %copy-done.3, ...), custom_call_target="tpu_custom_call" | custom-call | flops 8000000000 | bytes 4000000 | tf_op jit(solution)/shard_map/inner/pallas_call | solution.py:374
  33.8 0.3 collective-permute-done.4.final
  34.1 1.4 %collective-permute-done.3.early = bf16[3,128,128]{2,1,0:T(8,128)(2,1)S(1)} collective-permute-done((bf16[3,128,128]{2,1,0:T(8,128)(2,1)S(1)}, bf16[3,128,128]{2,1,0:T(8,128)(2,1)S(1)}, u32[]{:S(2)}, u32[]{:S(2)}) %collective-permute-start.3) | collective-permute-done | bytes 98336 | tf_op jit(solution)/shard_map/ppermute | solution.py:372
  35.5 0.2 scan.1
  35.7 11.9 %all_to_all.21 = bf16[16,128,128]{2,1,0:T(8,128)(2,1)S(1)} all-to-all(bf16[16,128,128]{2,1,0:T(8,128)(2,1)S(1)} %scan.1), channel_id=1, replica_groups={{0,1,2,3,8,9,10,11,16,17,18,19,24,25,26,27},{4,5,6,7,12,13,14,15,20,21,..., dimensions={0} | all-to-all | bytes 1048576 | tf_op jit(solution)/shard_map/all_to_all | solution.py:393
  47.7 1.6 %norm.1 = bf16[96,4096]{1,0:T(8,128)(2,1)} custom-call(f32[96,128]{1,0:T(8,128)S(1)} %get-tuple-element.21.idcol, f32[1,128]{1,0:T(1,128)S(1)} %get-tuple-element.23.before, f32[1,4096]{1,0:T(1,128)S(1)} %get-tuple-element.28.after.rates, bf16[96,4096]{1,0:T(8,128)(2,1)S(1)} %copy-done.3, bf16[2048,128]{1,0:T(8,128)(2,1)S(1)} %bitcast.9, ...), custom_call_target="tpu_custom_call" | custom-call | tf_op jit(solution)/shard_map/norm/pallas_call | solution.py:396
  (10 shorter events, 0.0 us)
Async XLA Ops:
  1.4 11.9 %all-to-all-start = ((f32[8,1,128]{2,1,0:T(1,128)}), f32[8,1,128]{2,1,0:T(1,128)S(1)}, u32[]{:S(2)}, u32[]{:S(2)}) async-start(f32[8,1,128]{2,1,0:T(1,128)} %bitcast.13), calls=%async_computation | async-start | bytes 8192 | tf_op jit(solution)/shard_map/all_to_all | solution.py:308
  9.2 1.1 %copy-start = (bf16[96,4096]{1,0:T(8,128)(2,1)S(1)}, bf16[96,4096]{1,0:T(8,128)(2,1)}, u32[]{:S(2)}) copy-start(bf16[96,4096]{1,0:T(8,128)(2,1)} %k_ref.1) | copy-start | bytes 2359300
  10.3 1.1 %copy-start.1 = (bf16[96,4096]{1,0:T(8,128)(2,1)S(1)}, bf16[96,4096]{1,0:T(8,128)(2,1)}, u32[]{:S(2)}) copy-start(bf16[96,4096]{1,0:T(8,128)(2,1)} %v_ref.3) | copy-start | bytes 2359300
  14.8 17.7 %copy-start.2 = (bf16[96,4096]{1,0:T(8,128)(2,1)S(1)}, bf16[96,4096]{1,0:T(8,128)(2,1)}, u32[]{:S(2)}) copy-start(bf16[96,4096]{1,0:T(8,128)(2,1)} %v_ref.3) | copy-start | bytes 2359300
  14.8 17.7 %copy-start.3 = (bf16[96,4096]{1,0:T(8,128)(2,1)S(1)}, bf16[96,4096]{1,0:T(8,128)(2,1)}, u32[]{:S(2)}) copy-start(bf16[96,4096]{1,0:T(8,128)(2,1)} %q_ref.3) | copy-start | bytes 2359300
  14.8 12.6 %all-to-all-start.1 = ((bf16[16,128,128]{2,1,0:T(8,128)(2,1)}), bf16[16,128,128]{2,1,0:T(8,128)(2,1)S(1)}, u32[]{:S(2)}, u32[]{:S(2)}) async-start(bf16[16,128,128]{2,1,0:T(8,128)(2,1)} %bitcast.5), calls=%async_computation.1 | async-start | bytes 1048576 | tf_op jit(solution)/shard_map/all_to_all | solution.py:333
  20.1 6.8 %collective-permute-start = (f32[8,128]{1,0:T(8,128)S(1)}, f32[8,128]{1,0:T(8,128)S(1)}, u32[]{:S(2)}, u32[]{:S(2)}) collective-permute-start(f32[8,128]{1,0:T(8,128)S(1)} %get-tuple-element.22.facts), channel_id=1, source_target_pairs={{0,8},{8,16},{16,24},{24,0},{1,9},{9,17},{17,25},{25,1},{2,10},{10... | collective-permute-start | bytes 12296 | tf_op jit(solution)/shard_map/ppermute | solution.py:347
  20.2 7.1 %collective-permute-start.1 = (f32[8,128]{1,0:T(8,128)S(1)}, f32[8,128]{1,0:T(8,128)S(1)}, u32[]{:S(2)}, u32[]{:S(2)}) collective-permute-start(f32[8,128]{1,0:T(8,128)S(1)} %get-tuple-element.22.facts), channel_id=1, source_target_pairs={{0,16},{8,24},{16,0},{24,8},{1,17},{9,25},{17,1},{25,9},{2,18},{10... | collective-permute-start | bytes 12296 | tf_op jit(solution)/shard_map/ppermute | solution.py:347
  20.8 6.6 %collective-permute-start.2 = (f32[8,128]{1,0:T(8,128)S(1)}, f32[8,128]{1,0:T(8,128)S(1)}, u32[]{:S(2)}, u32[]{:S(2)}) collective-permute-start(f32[8,128]{1,0:T(8,128)S(1)} %get-tuple-element.22.facts), channel_id=1, source_target_pairs={{0,24},{8,0},{16,8},{24,16},{1,25},{9,1},{17,9},{25,17},{2,26},{10... | collective-permute-start | bytes 12296 | tf_op jit(solution)/shard_map/ppermute | solution.py:347
  27.6 7.9 %collective-permute-start.3 = (bf16[3,128,128]{2,1,0:T(8,128)(2,1)S(1)}, bf16[3,128,128]{2,1,0:T(8,128)(2,1)S(1)}, u32[]{:S(2)}, u32[]{:S(2)}) collective-permute-start(bf16[3,128,128]{2,1,0:T(8,128)(2,1)S(1)} %get-tuple-element.27.after), channel_id=1, source_target_pairs={{0,4},{1,5},{2,6},{3,7},{4,0},{5,1},{6,2},{7,3},{8,12},{9,13},{10,... | collective-permute-start | bytes 294920 | tf_op jit(solution)/shard_map/ppermute | solution.py:372
  29.2 4.9 %collective-permute-start.4 = (bf16[1,128,128]{2,1,0:T(8,128)(2,1)S(1)}, bf16[1,128,128]{2,1,0:T(8,128)(2,1)S(1)}, u32[]{:S(2)}, u32[]{:S(2)}) collective-permute-start(bf16[1,128,128]{2,1,0:T(8,128)(2,1)S(1)} %get-tuple-element.31), channel_id=1, source_target_pairs={{0,4},{1,5},{2,6},{3,7},{8,12},{9,13},{10,14},{11,15},{16,20},{17,... | collective-permute-start | bytes 98312 | tf_op jit(solution)/shard_map/ppermute | solution.py:373
  33.8 13.9 %copy-start.4 = (f32[4096]{0:T(1024)S(1)}, f32[4096]{0:T(1024)}, u32[]{:S(2)}) copy-start(f32[4096]{0:T(1024)} %param.11) | copy-start | bytes 49156

commit v24 on v22

v24 whole, which is shorter than its diff:
```python
import functools

import jax
import jax.numpy as jnp
from jax import lax
from jax.experimental import pallas as pl
from jax.experimental.pallas import tpu as pltpu
from jax.sharding import PartitionSpec as P

HD = 64
LANES = 2 * HD
NEVER = 1e9
MARK = 8


def rate_of(facts, head, here):
    return facts[head // here : head // here + 1, head % here : head % here + 1]


def pair_rate(stored, pair, here):
    members = stored.shape[0]
    lane = lax.broadcasted_iota(jnp.int32, (1, LANES), 1)
    rates = []
    for head in (2 * pair, 2 * pair + 1):
        at = lax.rem(lax.div(head, here) + members // 2, members)
        row = stored[pl.ds(at, 1), :]
        rates.append(
            jnp.sum(jnp.where(lane == lax.rem(head, here), row, 0.0), axis=1, keepdims=True)
        )
    return jnp.where(lane < HD, rates[0], rates[1])


def own_ids(stored, tokens):
    members = stored.shape[0]
    at = lax.rem(lax.axis_index("uly") + members // 2, members)
    row = stored[pl.ds(at, 1), :]
    fill = jnp.full((1, LANES - tokens), -1.0, jnp.float32)
    return jnp.concatenate([row[:, LANES - tokens :], fill], 1)


def turn_kernel(k_ref, v_ref, turned, filled):
    tokens, width = k_ref.shape
    filled[:tokens, :] = v_ref[...]
    filled[tokens:, :] = jnp.zeros((LANES - tokens, width), filled.dtype)
    blank = jnp.zeros((LANES - tokens, LANES), jnp.float32)
    for j in range(width // LANES):
        columns = slice(j * LANES, (j + 1) * LANES)
        block = jnp.concatenate([k_ref[:, columns].astype(jnp.float32), blank], 0)
        turned[columns, :] = jnp.transpose(block).astype(turned.dtype)


def ends_kernel(here, tokens, stored, turned, v_ref, out_ref):
    width = v_ref.shape[1]
    members = stored.shape[0]
    group, rows = out_ref.shape[0], out_ref.shape[1] - MARK
    lane = lax.broadcasted_iota(jnp.int32, (HD, LANES), 1)
    ids = jnp.broadcast_to(own_ids(stored, tokens), (8, LANES))
    place = lax.broadcasted_iota(jnp.int32, ids.shape, 1)
    last = ids[:, tokens - 1 : tokens]
    age = jnp.where(ids == last, (tokens - 1 - place).astype(jnp.float32), NEVER)
    mark = jnp.broadcast_to(last[:1], (MARK, LANES)).astype(jnp.bfloat16)
    for owner in range(group):
        out_ref[owner, rows:, :] = mark
    for j in range(0, width // LANES, 2):
        weighted = []
        for head in range(2 * j, 2 * j + 4):
            weight = jnp.exp(-rate_of(stored, (head + members // 2 * here) % (members * here), here) * age)
            keys = turned[head * HD : (head + 1) * HD, :].astype(jnp.float32)
            keys = keys.reshape(HD // 8, 8, LANES) * weight[None]
            weighted.append(keys.reshape(HD, LANES))
        weighted = jnp.concatenate(weighted, 0)
        high = weighted.astype(jnp.bfloat16)
        low = (weighted - high.astype(jnp.float32)).astype(jnp.bfloat16)
        v = v_ref[:, j * LANES : (j + 2) * LANES]
        both = jnp.dot(
            jnp.concatenate([high, low], 1),
            jnp.concatenate([v, v], 0),
            preferred_element_type=jnp.float32,
        )
        for one in (0, 1):
            pair = both[one * LANES : (one + 1) * LANES, one * LANES : (one + 1) * LANES]
            state = jnp.where(lane < HD, pair[:HD], pair[HD:])
            size = min(rows, HD)
            for at in range(0, HD, size):
                owner, start = divmod((j + one) * HD + at, rows)
                out_ref[group - 1 - owner, start : start + size, :] = state[at : at + size].astype(
                    jnp.bfloat16
                )


def inner_kernel(here, stored, q_ref, turned, v_ref, after, out_ref, rates_ref, idcol):
    tokens, width = q_ref.shape
    members = stored.shape[0]
    row = own_ids(stored, tokens)
    column = jnp.transpose(jnp.broadcast_to(row, (LANES, LANES)))[:tokens]
    idcol[...] = column
    lane = lax.broadcasted_iota(jnp.int32, (tokens, LANES), 1)
    t = lax.broadcasted_iota(jnp.int32, (tokens, LANES), 0)
    seen = (t >= lane) & (column == row)
    age = jnp.where(seen, (t - lane).astype(jnp.float32), NEVER)
    for j in range(width // LANES):
        columns = slice(j * LANES, (j + 1) * LANES)
        q = q_ref[:, columns]
        zero = jnp.zeros_like(q)
        stacked = jnp.concatenate([jnp.where(lane < HD, q, zero), jnp.where(lane < HD, zero, q)], 0)
        scores = jnp.dot(
            stacked, turned[columns, :], preferred_element_type=jnp.float32
        )
        rates = [
            rate_of(stored, (2 * j + one + members // 2 * here) % (members * here), here)
            for one in (0, 1)
        ]
        weight = jnp.concatenate([jnp.exp(-rate * age) for rate in rates], 0)
        probs = (scores * weight)[:, :tokens].astype(jnp.bfloat16)
        got = jnp.dot(probs, v_ref[:, columns], preferred_element_type=jnp.float32)
        out_ref[:, columns] = jnp.where(lane < HD, got[:tokens], got[tokens:])
        rates_ref[:, columns] = jnp.where(lane[:1] < HD, rates[0], rates[1])


def few(count):
    return count if count <= 8 else 1


def split(piece, rows):
    return piece[:rows].astype(jnp.float32), piece[rows : rows + 1].astype(jnp.float32)


def half_kernel(here, tokens, chunks, stored, in_ref, early_ref, final_ref, one, half, mine):
    slices, newest = early_ref.shape[0] + 1, in_ref.shape[0] - 1
    rows = one.shape[0]
    owner = lax.axis_index("ctx") * chunks + lax.rem(lax.axis_index("uly"), chunks)
    share = min(rows, HD)
    for at in range(0, rows, share):
        rate = pair_rate(stored, lax.div(owner * rows + at, HD), here)
        for ref, length in ((one, tokens), (half, tokens * chunks)):
            ref[at : at + share, :] = jnp.broadcast_to(
                jnp.exp(-rate * float(length)), (share, LANES)
            )
    last = own_ids(stored, tokens)[:, tokens - 1 : tokens]
    mine[...] = jnp.broadcast_to(last, mine.shape)

    def slice_end(c, ref, at):
        def step(j, carry):
            state, last = carry
            fresh, own = split(in_ref[newest - c * chunks - j], rows)
            return fresh + jnp.where(own == last, one[...], 0.0) * state, own

        begin = split(in_ref[newest - c * chunks], rows)
        state, _ = lax.fori_loop(1, chunks, step, begin, unroll=few(chunks - 1))
        ref[at, :rows, :] = state.astype(ref.dtype)
        ref[at, rows:, :] = in_ref[newest - c * chunks - chunks + 1][rows:]

    def early(c, _):
        slice_end(c, early_ref, c)
        return 0

    lax.fori_loop(0, slices - 1, early, 0, unroll=few(slices - 1))
    slice_end(slices - 1, final_ref, 0)


def scan_kernel(chunks, one, half, in_ref, early, final, after, out_ref):
    slices, newest = early.shape[0] + 1, in_ref.shape[0] - 1
    rows = one.shape[0]
    later = lax.axis_index("uly") >= chunks

    def over_other(carry, piece, wanted):
        state, last = carry
        fresh, own = split(piece, rows)
        moved = fresh + jnp.where(own == last, half[...], 0.0) * state
        return jnp.where(wanted, moved, state), jnp.where(wanted, own, last)

    def over_own(carry, c):
        def step(j, carry):
            state, last = carry
            at = c * chunks + j
            out_ref[at] = state.astype(out_ref.dtype)
            fresh, own = split(in_ref[newest - at], rows)
            return fresh + jnp.where(own == last, one[...], 0.0) * state, own

        return lax.fori_loop(0, chunks, step, carry, unroll=few(chunks))

    def over_slice(c, carry):
        carry = over_own(over_other(carry, early[c], later), c)
        return over_other(carry, early[c], jnp.logical_not(later))

    begin = (jnp.zeros((rows, LANES), jnp.float32), jnp.full((1, LANES), -1.0, jnp.float32))
    carry = lax.fori_loop(0, slices - 1, over_slice, begin, unroll=few(slices - 1))
    over_own(over_other(carry, final[0], later), slices - 1)


def norm_kernel(idcol, stored, earlier, rates, q_ref, s_ref, inner_ref, gain, out_ref, raw, done, sems):
    tokens, width = q_ref.shape
    lane = lax.broadcasted_iota(jnp.int32, (HD, LANES), 1)
    place = lax.broadcasted_iota(jnp.int32, (tokens, LANES), 0)
    ctx, uly = lax.axis_index("ctx"), lax.axis_index("uly")
    members = stored.shape[0]
    at = lax.rem(uly + members - 1 + members // 2, members)
    before = jnp.where(uly > 0, stored[pl.ds(at, 1), LANES - 1 :], earlier[:1, :1])
    before = jnp.where(ctx + uly > 0, before, -1.0)
    age = jnp.where(idcol[...] == before, (place + 1).astype(jnp.float32), NEVER)
    zero = jnp.zeros((HD, LANES), s_ref.dtype)
    total = jnp.zeros((tokens, LANES), jnp.float32)
    for j in range(0, width // LANES, 2):
        square = []
        for one in (0, 1):
            state = s_ref[(j + one) * HD : (j + one + 1) * HD, :]
            for half in (jnp.where(lane < HD, state, zero), jnp.where(lane < HD, zero, state)):
                square.append(jnp.concatenate([zero, half] if one else [half, zero], 1))
        columns = slice(j * LANES, (j + 2) * LANES)
        outer = jnp.dot(
            q_ref[:, columns], jnp.concatenate(square, 0), preferred_element_type=jnp.float32
        )
        for one in (0, 1):
            columns = slice((j + one) * LANES, (j + one + 1) * LANES)
            fade = jnp.exp(-rates[:, columns] * age)
            value = inner_ref[:, columns] + outer[:, one * LANES : (one + 1) * LANES] * fade
            total += value * value
            raw[:, columns] = value
    mean = jnp.sum(total, axis=1, keepdims=True) / float(width)
    scale = jnp.broadcast_to(lax.rsqrt(mean + 1e-06), (tokens, LANES))
    parts = sems.shape[0]
    share = tokens // parts
    copies = []
    for part in range(parts):
        rows = slice(part * share, (part + 1) * share)
        for at in range(0, width, LANES):
            columns = slice(at, at + LANES)
            done[rows, columns] = (raw[rows, columns] * scale[rows] * gain[:, columns]).astype(
                jnp.bfloat16
            )
        copies.append(pltpu.make_async_copy(done.at[rows], out_ref.at[rows], sems.at[part]))
        copies[-1].start()
    for copy in copies:
        copy.wait()


def local(queries, keys, values, doc_ids, decay_rate, norm_gain):
    tokens, width = queries.shape
    here = decay_rate.shape[0]
    axes = ("ctx", "uly")
    slices, members = lax.axis_size("ctx"), lax.axis_size("uly")
    count = slices * members
    all_pairs = width // LANES
    chunks = members // 2
    group = slices * chunks
    rows = all_pairs * HD // group
    groups = [
        [c * members + half * chunks + u for c in range(slices) for u in range(chunks)]
        for half in (0, 1)
    ]
    swap = [
        (c * members + u, c * members + (u + chunks) % members)
        for c in range(slices)
        for u in range(members)
    ]

    vmem = pl.BlockSpec(memory_space=pltpu.VMEM)
    params = pltpu.CompilerParams(vmem_limit_bytes=32 * 1024 * 1024)
    shape = jax.ShapeDtypeStruct
    tile = shape((members, LANES), jnp.float32)

    own = jnp.pad(decay_rate, (0, LANES - here)) + jnp.pad(
        doc_ids, (LANES - tokens, 0)
    ).astype(jnp.float32)
    turned_round = [[(u + members // 2) % members for u in range(members)]]
    stored = lax.all_to_all(
        jnp.broadcast_to(own[None, :], tile.shape),
        "uly", split_axis=0, concat_axis=0, axis_index_groups=turned_round, tiled=True,
    )
    turned, filled = pl.pallas_call(
        turn_kernel,
        in_specs=[vmem] * 2,
        out_specs=[vmem] * 2,
        out_shape=[shape((width, LANES), jnp.bfloat16), shape((LANES, width), jnp.bfloat16)],
        compiler_params=params,
        cost_estimate=pl.CostEstimate(flops=0, bytes_accessed=12_000_000, transcendentals=0),
        name="turn",
    )(keys, values)
    ends = pl.pallas_call(
        functools.partial(ends_kernel, here, tokens),
        in_specs=[vmem] * 3,
        out_specs=vmem,
        out_shape=shape((group, rows + MARK, LANES), jnp.bfloat16),
        compiler_params=params,
        name="ends",
    )(stored, turned, filled)
    pieces = lax.all_to_all(
        ends,
        axes, split_axis=0, concat_axis=0, tiled=True,
        axis_index_groups=[members_of[::-1] for members_of in groups],
    )
    early_ends, final_end, one, half, mine = pl.pallas_call(
        functools.partial(half_kernel, here, tokens, chunks),
        in_specs=[vmem] * 2,
        out_specs=[vmem] * 5,
        out_shape=[
            shape((slices - 1, rows + MARK, LANES), jnp.bfloat16),
            shape((1, rows + MARK, LANES), jnp.bfloat16),
            shape((rows, LANES), jnp.float32),
            shape((rows, LANES), jnp.float32),
            shape((8, LANES), jnp.float32),
        ],
        compiler_params=params,
        name="half",
    )(stored, pieces)
    early = lax.ppermute(early_ends, axes, swap)
    final = lax.ppermute(final_end, axes, [(low, high) for low, high in swap if low < high])
    earlier = lax.ppermute(
        mine, axes, [(c * members - 1, c * members) for c in range(1, slices)]
    )
    inner, rates, idcol = pl.pallas_call(
        functools.partial(inner_kernel, here),
        in_specs=[vmem] * 4 + [pl.BlockSpec(memory_space=pl.ANY)],
        out_specs=[vmem] * 3,
        out_shape=[
            shape((tokens, width), jnp.float32),
            shape((1, width), jnp.float32),
            shape((tokens, LANES), jnp.float32),
        ],
        compiler_params=params,
        cost_estimate=pl.CostEstimate(
            flops=8_000_000_000, bytes_accessed=4_000_000, transcendentals=600_000
        ),
        name="inner",
    )(stored, queries, turned, values, early_ends)
    moved = pl.pallas_call(
        functools.partial(scan_kernel, chunks),
        in_specs=[vmem] * 5 + [pl.BlockSpec(memory_space=pl.ANY)],
        out_specs=vmem,
        out_shape=shape((group, rows, LANES), jnp.bfloat16),
        compiler_params=params,
        name="scan",
    )(one, half, pieces, early, final, rates)
    states = lax.all_to_all(
        moved, axes, split_axis=0, concat_axis=0, axis_index_groups=groups, tiled=True
    )
    return pl.pallas_call(
        norm_kernel,
        in_specs=[vmem] * 8,
        out_specs=pl.BlockSpec(memory_space=pl.ANY),
        out_shape=shape((tokens, width), jnp.bfloat16),
        scratch_shapes=[
            pltpu.VMEM((tokens, width), jnp.float32),
            pltpu.VMEM((tokens, width), jnp.bfloat16),
            pltpu.SemaphoreType.DMA((tokens // 16,)),
        ],
        compiler_params=params,
        name="norm",
    )(idcol, stored, earlier, rates, queries, states.reshape(all_pairs * HD, LANES), inner, norm_gain[None, :])


def solution(mesh):
    in_specs = (
        P(("ctx", "uly"), None),
        P(("ctx", "uly"), None),
        P(("ctx", "uly"), None),
        P(("ctx", "uly")),
        P("uly"),
        P(),
    )
    out_specs = P(("ctx", "uly"), None)
    return jax.shard_map(local, mesh=mesh, in_specs=in_specs, out_specs=out_specs, check_vma=False)
```

time: 49.8 us -> 53.8 us (1.080)
  the two profiles are of different devices: /device:TPU:0 before, /device:TPU:1 now
where the time goes in v24:
time: 53.8 us; the launch traced here: 53.4 us
  starting transfers between devices  17.3 us (32%)
  blocking collectives  14.1 us (26%)
  waiting for transfers between devices  12.8 us (24%)
  Pallas kernels  5.45 us (10%)
  local copies, waits for them, and re-layouts  2.88 us (5%)
  other arithmetic  0.75 us (1%)
    all_to_all x1, blocking collectives, local(): lax.all_to_all(ends, axes, split_axis=0, concat_axis=0, tiled=True, axis_...  14.1 us
    ppermute x1, waiting for transfers between devices, local(): lax.ppermute(mine, axes, [(c * members - 1, c * members) for c in range(1...  10.7 us
    all_to_all x1, starting transfers between devices, local(): lax.all_to_all(jnp.broadcast_to(own[None, :], tile.shape), 'uly', split_a...  6.64 us
    all_to_all x1, starting transfers between devices, local(): lax.all_to_all(moved, axes, split_axis=0, concat_axis=0, axis_index_group...  5.1 us
    ppermute x1, starting transfers between devices, local(): lax.ppermute(final_end, axes, [(low, high) for low, high in swap if low <...  3.08 us
    unnamed x12, local copies, waits for them, and re-layouts  2.29 us
    pallas_call x1, Pallas kernels, local(): pl.pallas_call(norm_kernel, in_specs=[vmem] * 8, out_specs=pl.BlockSpec(m...  1.67 us
    ppermute x1, waiting for transfers between devices, local(): early = lax.ppermute(early_ends, axes, swap)  1.59 us
  transfers between devices with their start and end apart: 5, of which 3 were waited for; matrix products, arithmetic and copies ran while one was open for 0% of the time, Pallas kernels for 3%

profile of v24, /device:TPU:1, one launch (start us, length us, event | category | flops | bytes accessed | tf_op | source)
XLA Modules:
  0.0 53.4 jit_solution(17999284742257197442)
XLA Ops:
  0.0 0.7 %convert_add_fusion = f32[128]{0:T(128)S(1)} fusion(s32[96]{0:T(128)} %param.9, f32[8]{0:T(128)} %param.10), kind=kLoop, calls=%fused_computation | loop fusion | flops 256 | bytes 928 | tf_op jit(solution)/shard_map/add | solution.py:262
  0.7 0.6 %broadcast_in_dim.4 = f32[8,1,128]{2,1,0:T(1,128)} broadcast(f32[128]{0:T(128)S(1)} %convert_add_fusion), dimensions={2} | broadcast | bytes 4608 | tf_op jit(solution)/shard_map/broadcast_in_dim | solution.py:267
  1.3 6.6 %all-to-all-start = ((f32[8,1,128]{2,1,0:T(1,128)}), f32[8,1,128]{2,1,0:T(1,128)S(1)}, u32[]{:S(2)}, u32[]{:S(2)}) async-start(f32[8,1,128]{2,1,0:T(1,128)} %broadcast_in_dim.4), calls=%async_computation | async-start | bytes 8192 | tf_op jit(solution)/shard_map/all_to_all | solution.py:266
  8.0 1.1 %copy-done.2 = bf16[96,4096]{1,0:T(8,128)(2,1)S(1)} copy-done((bf16[96,4096]{1,0:T(8,128)(2,1)S(1)}, bf16[96,4096]{1,0:T(8,128)(2,1)}, u32[]{:S(2)}) %copy-start.2) | copy-done | bytes 786456
  9.1 1.1 %copy-done.3 = bf16[96,4096]{1,0:T(8,128)(2,1)S(1)} copy-done((bf16[96,4096]{1,0:T(8,128)(2,1)S(1)}, bf16[96,4096]{1,0:T(8,128)(2,1)}, u32[]{:S(2)}) %copy-start.3) | copy-done | bytes 786456
  10.2 0.4 turn.1
  10.6 0.5 all-to-all-done
  11.1 0.9 %ends.1 = bf16[16,136,128]{2,1,0:T(8,128)(2,1)S(1)} custom-call(f32[8,128]{1,0:T(8,128)S(1)} %bitcast.4, bf16[4096,128]{1,0:T(8,128)(2,1)S(1)} %get-tuple-element.15.turned, bf16[128,4096]{1,0:T(8,128)(2,1)S(1)} %get-tuple-element.16.v_ref), custom_call_target="tpu_custom_call" | custom-call | tf_op jit(solution)/shard_map/ends/pallas_call | solution.py:279
  12.0 14.1 %all_to_all.18.in_ref = bf16[16,136,128]{2,1,0:T(8,128)(2,1)S(1)} all-to-all(bf16[16,136,128]{2,1,0:T(8,128)(2,1)S(1)} %ends.1), channel_id=1, replica_groups={{27,26,25,24,19,18,17,16,11,10,9,8,3,2,1,0},{31,30,29,28,23,22,21,20,15..., dimensions={0} | all-to-all | bytes 1114112 | tf_op jit(solution)/shard_map/all_to_all | solution.py:287
  26.1 0.2 half.1
  26.4 1.2 %collective-permute-start.1 = (bf16[3,136,128]{2,1,0:T(8,128)(2,1)S(1)}, bf16[3,136,128]{2,1,0:T(8,128)(2,1)S(1)}, u32[]{:S(2)}, u32[]{:S(2)}) collective-permute-start(bf16[3,136,128]{2,1,0:T(8,128)(2,1)S(1)} %get-tuple-element.17.after), channel_id=1, source_target_pairs={{0,4},{1,5},{2,6},{3,7},{4,0},{5,1},{6,2},{7,3},{8,12},{9,13},{10,... | collective-permute-start | bytes 313352 | tf_op jit(solution)/shard_map/ppermute | solution.py:306
  27.6 3.1 %collective-permute-start.2 = (bf16[1,136,128]{2,1,0:T(8,128)(2,1)S(1)}, bf16[1,136,128]{2,1,0:T(8,128)(2,1)S(1)}, u32[]{:S(2)}, u32[]{:S(2)}) collective-permute-start(bf16[1,136,128]{2,1,0:T(8,128)(2,1)S(1)} %get-tuple-element.23), channel_id=1, source_target_pairs={{0,4},{1,5},{2,6},{3,7},{8,12},{9,13},{10,14},{11,15},{16,20},{17,... | collective-permute-start | bytes 104456 | tf_op jit(solution)/shard_map/ppermute | solution.py:307
  30.7 1.2 %inner.1 = (f32[96,4096]{1,0:T(8,128)S(1)}, f32[1,4096]{1,0:T(1,128)S(1)}, f32[96,128]{1,0:T(8,128)S(1)}) custom-call(f32[8,128]{1,0:T(8,128)S(1)} %bitcast.6, bf16[96,4096]{1,0:T(8,128)(2,1)S(1)} %copy-done, bf16[4096,128]{1,0:T(8,128)(2,1)S(1)} %get-tuple-element.15.turned, bf16[96,4096]{1,0:T(8,128)(2,1)S(1)} %copy-done.4, ...), custom_call_target="tpu_custom_call" | custom-call | flops 8000000000 | bytes 4000000 | tf_op jit(solution)/shard_map/inner/pallas_call | solution.py:311
  32.0 0.0 copy-start.1
  32.0 0.0 copy-start.5
  32.0 0.0 collective-permute-done.2.final
  32.0 1.6 %collective-permute-done.1.early = bf16[3,136,128]{2,1,0:T(8,128)(2,1)S(1)} collective-permute-done((bf16[3,136,128]{2,1,0:T(8,128)(2,1)S(1)}, bf16[3,136,128]{2,1,0:T(8,128)(2,1)S(1)}, u32[]{:S(2)}, u32[]{:S(2)}) %collective-permute-start.1) | collective-permute-done | bytes 104480 | tf_op jit(solution)/shard_map/ppermute | solution.py:306
  33.6 1.0 %scan.1 = bf16[16,128,128]{2,1,0:T(8,128)(2,1)} custom-call(f32[128,128]{1,0:T(8,128)S(1)} %get-tuple-element.21.one, f32[128,128]{1,0:T(8,128)S(1)} %get-tuple-element.22.half, bf16[16,136,128]{2,1,0:T(8,128)(2,1)S(1)} %all_to_all.18.in_ref, bf16[3,136,128]{2,1,0:T(8,128)(2,1)S(1)} %collective-permute-done.1.early, ...), custom_call_target="tpu_custom_call" | custom-call | tf_op jit(solution)/shard_map/scan/pallas_call | solution.py:326
  34.7 5.1 %all-to-all-start.2 = ((bf16[16,128,128]{2,1,0:T(8,128)(2,1)}), bf16[16,128,128]{2,1,0:T(8,128)(2,1)S(1)}, u32[]{:S(2)}, u32[]{:S(2)}) async-start(bf16[16,128,128]{2,1,0:T(8,128)(2,1)} %scan.1), calls=%async_computation.2 | async-start | bytes 1048576 | tf_op jit(solution)/shard_map/all_to_all | solution.py:334
  39.8 1.3 %collective-permute-start = (f32[8,128]{1,0:T(8,128)S(1)}, f32[8,128]{1,0:T(8,128)S(1)}, u32[]{:S(2)}, u32[]{:S(2)}) collective-permute-start(f32[8,128]{1,0:T(8,128)S(1)} %get-tuple-element.19), channel_id=1, source_target_pairs={{7,8},{15,16},{23,24}} | collective-permute-start | bytes 12296 | tf_op jit(solution)/shard_map/ppermute | solution.py:308
  41.1 10.7 %collective-permute-done.earlier = f32[8,128]{1,0:T(8,128)S(1)} collective-permute-done((f32[8,128]{1,0:T(8,128)S(1)}, f32[8,128]{1,0:T(8,128)S(1)}, u32[]{:S(2)}, u32[]{:S(2)}) %collective-permute-start) | collective-permute-done | bytes 4128 | tf_op jit(solution)/shard_map/ppermute | solution.py:308
  51.7 0.0 all-to-all-done.2
  51.7 0.0 copy-done.5
  51.7 1.7 %norm.1 = bf16[96,4096]{1,0:T(8,128)(2,1)} custom-call(f32[96,128]{1,0:T(8,128)S(1)} %get-tuple-element.18.idcol, f32[8,128]{1,0:T(8,128)S(1)} %bitcast.7, f32[8,128]{1,0:T(8,128)S(1)} %collective-permute-done.earlier, f32[1,4096]{1,0:T(1,128)S(1)} %get-tuple-element.20.after.rates, bf16[96,4096]{1,0:T(8,128)(2,1)S(1)} %copy-done.1, ...), custom_call_target="tpu_custom_call" | custom-call | tf_op jit(solution)/shard_map/norm/pallas_call | solution.py:337
  (7 shorter events, 0.0 us)
Async XLA Ops:
  1.3 9.8 %all-to-all-start = ((f32[8,1,128]{2,1,0:T(1,128)}), f32[8,1,128]{2,1,0:T(1,128)S(1)}, u32[]{:S(2)}, u32[]{:S(2)}) async-start(f32[8,1,128]{2,1,0:T(1,128)} %broadcast_in_dim.4), calls=%async_computation | async-start | bytes 8192 | tf_op jit(solution)/shard_map/all_to_all | solution.py:266
  8.0 1.1 %copy-start.2 = (bf16[96,4096]{1,0:T(8,128)(2,1)S(1)}, bf16[96,4096]{1,0:T(8,128)(2,1)}, u32[]{:S(2)}) copy-start(bf16[96,4096]{1,0:T(8,128)(2,1)} %k_ref.1) | copy-start | bytes 2359300
  9.1 1.1 %copy-start.3 = (bf16[96,4096]{1,0:T(8,128)(2,1)S(1)}, bf16[96,4096]{1,0:T(8,128)(2,1)}, u32[]{:S(2)}) copy-start(bf16[96,4096]{1,0:T(8,128)(2,1)} %v_ref.3) | copy-start | bytes 2359300
  11.1 19.6 %copy-start = (bf16[96,4096]{1,0:T(8,128)(2,1)S(1)}, bf16[96,4096]{1,0:T(8,128)(2,1)}, u32[]{:S(2)}) copy-start(bf16[96,4096]{1,0:T(8,128)(2,1)} %q_ref.3) | copy-start | bytes 2359300
  11.1 19.6 %copy-start.4 = (bf16[96,4096]{1,0:T(8,128)(2,1)S(1)}, bf16[96,4096]{1,0:T(8,128)(2,1)}, u32[]{:S(2)}) copy-start(bf16[96,4096]{1,0:T(8,128)(2,1)} %v_ref.3) | copy-start | bytes 2359300
  26.4 7.2 %collective-permute-start.1 = (bf16[3,136,128]{2,1,0:T(8,128)(2,1)S(1)}, bf16[3,136,128]{2,1,0:T(8,128)(2,1)S(1)}, u32[]{:S(2)}, u32[]{:S(2)}) collective-permute-start(bf16[3,136,128]{2,1,0:T(8,128)(2,1)S(1)} %get-tuple-element.17.after), channel_id=1, source_target_pairs={{0,4},{1,5},{2,6},{3,7},{4,0},{5,1},{6,2},{7,3},{8,12},{9,13},{10,... | collective-permute-start | bytes 313352 | tf_op jit(solution)/shard_map/ppermute | solution.py:306
  27.6 4.4 %collective-permute-start.2 = (bf16[1,136,128]{2,1,0:T(8,128)(2,1)S(1)}, bf16[1,136,128]{2,1,0:T(8,128)(2,1)S(1)}, u32[]{:S(2)}, u32[]{:S(2)}) collective-permute-start(bf16[1,136,128]{2,1,0:T(8,128)(2,1)S(1)} %get-tuple-element.23), channel_id=1, source_target_pairs={{0,4},{1,5},{2,6},{3,7},{8,12},{9,13},{10,14},{11,15},{16,20},{17,... | collective-permute-start | bytes 104456 | tf_op jit(solution)/shard_map/ppermute | solution.py:307
  32.0 19.7 %copy-start.1 = (bf16[96,4096]{1,0:T(8,128)(2,1)S(1)}, bf16[96,4096]{1,0:T(8,128)(2,1)}, u32[]{:S(2)}) copy-start(bf16[96,4096]{1,0:T(8,128)(2,1)} %q_ref.3) | copy-start | bytes 2359300
  32.0 19.7 %copy-start.5 = (f32[4096]{0:T(1024)S(1)}, f32[4096]{0:T(1024)}, u32[]{:S(2)}) copy-start(f32[4096]{0:T(1024)} %param.11) | copy-start | bytes 49156
  34.7 17.1 %all-to-all-start.2 = ((bf16[16,128,128]{2,1,0:T(8,128)(2,1)}), bf16[16,128,128]{2,1,0:T(8,128)(2,1)S(1)}, u32[]{:S(2)}, u32[]{:S(2)}) async-start(bf16[16,128,128]{2,1,0:T(8,128)(2,1)} %scan.1), calls=%async_computation.2 | async-start | bytes 1048576 | tf_op jit(solution)/shard_map/all_to_all | solution.py:334
  39.8 12.0 %collective-permute-start = (f32[8,128]{1,0:T(8,128)S(1)}, f32[8,128]{1,0:T(8,128)S(1)}, u32[]{:S(2)}, u32[]{:S(2)}) collective-permute-start(f32[8,128]{1,0:T(8,128)S(1)} %get-tuple-element.19), channel_id=1, source_target_pairs={{7,8},{15,16},{23,24}} | collective-permute-start | bytes 12296 | tf_op jit(solution)/shard_map/ppermute | solution.py:308

commit v25 on v24

--- a/solution.py
+++ b/solution.py
@@ -158,7 +158,7 @@
     slice_end(slices - 1, final_ref, 0)
 
 
-def scan_kernel(chunks, one, half, in_ref, early, final, after, out_ref):
+def scan_kernel(chunks, one, half, in_ref, early, final, after, earlier, out_ref):
     slices, newest = early.shape[0] + 1, in_ref.shape[0] - 1
     rows = one.shape[0]
     later = lax.axis_index("uly") >= chunks
@@ -325,12 +325,12 @@
     )(stored, queries, turned, values, early_ends)
     moved = pl.pallas_call(
         functools.partial(scan_kernel, chunks),
-        in_specs=[vmem] * 5 + [pl.BlockSpec(memory_space=pl.ANY)],
+        in_specs=[vmem] * 5 + [pl.BlockSpec(memory_space=pl.ANY)] * 2,
         out_specs=vmem,
         out_shape=shape((group, rows, LANES), jnp.bfloat16),
         compiler_params=params,
         name="scan",
-    )(one, half, pieces, early, final, rates)
+    )(one, half, pieces, early, final, rates, earlier)
     states = lax.all_to_all(
         moved, axes, split_axis=0, concat_axis=0, axis_index_groups=groups, tiled=True
     )

time: 53.8 us -> 52 us (0.967)
  the two profiles are of different devices: /device:TPU:1 before, /device:TPU:0 now
where the time goes in v25:
time: 52 us; the launch traced here: 51.7 us
  blocking collectives  27.3 us (52%)
  starting transfers between devices  13.4 us (26%)
  Pallas kernels  4.69 us (9%)
  local copies, waits for them, and re-layouts  2.88 us (6%)
  waiting for transfers between devices  2.61 us (5%)
  other arithmetic  0.75 us (1%)
    all_to_all x1, blocking collectives, local(): lax.all_to_all(moved, axes, split_axis=0, concat_axis=0, axis_index_group...  14.8 us
    all_to_all x1, blocking collectives, local(): lax.all_to_all(ends, axes, split_axis=0, concat_axis=0, tiled=True, axis_...  12.5 us
    all_to_all x1, starting transfers between devices, local(): lax.all_to_all(jnp.broadcast_to(own[None, :], tile.shape), 'uly', split_a...  7.81 us
    ppermute x1, starting transfers between devices, local(): lax.ppermute(final_end, axes, [(low, high) for low, high in swap if low <...  3.37 us
    unnamed x10, local copies, waits for them, and re-layouts  2.28 us
    pallas_call x1, Pallas kernels, local(): pl.pallas_call(norm_kernel, in_specs=[vmem] * 8, out_specs=pl.BlockSpec(m...  1.71 us
    ppermute x1, starting transfers between devices, local(): early = lax.ppermute(early_ends, axes, swap)  1.52 us
    all_to_all x1, waiting for transfers between devices, local(): lax.all_to_all(jnp.broadcast_to(own[None, :], tile.shape), 'uly', split_a...  1.4 us
  transfers between devices with their start and end apart: 4, of which 3 were waited for; matrix products, arithmetic and copies ran while one was open for 0% of the time, Pallas kernels for 3%

profile of v25, /device:TPU:0, one launch (start us, length us, event | category | flops | bytes accessed | tf_op | source)
XLA Modules:
  0.0 51.7 jit_solution(14720749691034763240)
XLA Ops:
  0.0 0.7 %convert_add_fusion = f32[128]{0:T(128)S(1)} fusion(s32[96]{0:T(128)} %param.9, f32[8]{0:T(128)} %param.10), kind=kLoop, calls=%fused_computation | loop fusion | flops 256 | bytes 928 | tf_op jit(solution)/shard_map/add | solution.py:262
  0.7 0.6 %broadcast_in_dim.4 = f32[8,1,128]{2,1,0:T(1,128)} broadcast(f32[128]{0:T(128)S(1)} %convert_add_fusion), dimensions={2} | broadcast | bytes 4608 | tf_op jit(solution)/shard_map/broadcast_in_dim | solution.py:267
  1.3 7.8 %all-to-all-start = ((f32[8,1,128]{2,1,0:T(1,128)}), f32[8,1,128]{2,1,0:T(1,128)S(1)}, u32[]{:S(2)}, u32[]{:S(2)}) async-start(f32[8,1,128]{2,1,0:T(1,128)} %broadcast_in_dim.4), calls=%async_computation | async-start | bytes 8192 | tf_op jit(solution)/shard_map/all_to_all | solution.py:266
  9.2 1.1 %copy-done.1 = bf16[96,4096]{1,0:T(8,128)(2,1)S(1)} copy-done((bf16[96,4096]{1,0:T(8,128)(2,1)S(1)}, bf16[96,4096]{1,0:T(8,128)(2,1)}, u32[]{:S(2)}) %copy-start.1) | copy-done | bytes 786456
  10.3 1.1 %copy-done.2 = bf16[96,4096]{1,0:T(8,128)(2,1)S(1)} copy-done((bf16[96,4096]{1,0:T(8,128)(2,1)S(1)}, bf16[96,4096]{1,0:T(8,128)(2,1)}, u32[]{:S(2)}) %copy-start.2) | copy-done | bytes 786456
  11.4 0.4 turn.1
  11.8 1.4 %all-to-all-done = f32[8,1,128]{2,1,0:T(1,128)S(1)} async-done(((f32[8,1,128]{2,1,0:T(1,128)}), f32[8,1,128]{2,1,0:T(1,128)S(1)}, u32[]{:S(2)}, u32[]{:S(2)}) %all-to-all-start) | async-done | bytes 4128 | tf_op jit(solution)/shard_map/all_to_all | solution.py:266
  13.2 0.9 %ends.1 = bf16[16,136,128]{2,1,0:T(8,128)(2,1)S(1)} custom-call(f32[8,128]{1,0:T(8,128)S(1)} %bitcast.4, bf16[4096,128]{1,0:T(8,128)(2,1)S(1)} %get-tuple-element.15.turned, bf16[128,4096]{1,0:T(8,128)(2,1)S(1)} %get-tuple-element.16.v_ref), custom_call_target="tpu_custom_call" | custom-call | tf_op jit(solution)/shard_map/ends/pallas_call | solution.py:279
  14.1 12.5 %all_to_all.18.in_ref = bf16[16,136,128]{2,1,0:T(8,128)(2,1)S(1)} all-to-all(bf16[16,136,128]{2,1,0:T(8,128)(2,1)S(1)} %ends.1), channel_id=1, replica_groups={{27,26,25,24,19,18,17,16,11,10,9,8,3,2,1,0},{31,30,29,28,23,22,21,20,15..., dimensions={0} | all-to-all | bytes 1114112 | tf_op jit(solution)/shard_map/all_to_all | solution.py:287
  26.6 0.2 half.1
  26.8 1.5 %collective-permute-start.1 = (bf16[3,136,128]{2,1,0:T(8,128)(2,1)S(1)}, bf16[3,136,128]{2,1,0:T(8,128)(2,1)S(1)}, u32[]{:S(2)}, u32[]{:S(2)}) collective-permute-start(bf16[3,136,128]{2,1,0:T(8,128)(2,1)S(1)} %get-tuple-element.17.after), channel_id=1, source_target_pairs={{0,4},{1,5},{2,6},{3,7},{4,0},{5,1},{6,2},{7,3},{8,12},{9,13},{10,... | collective-permute-start | bytes 313352 | tf_op jit(solution)/shard_map/ppermute | solution.py:306
  28.3 0.6 %collective-permute-start = (f32[8,128]{1,0:T(8,128)S(1)}, f32[8,128]{1,0:T(8,128)S(1)}, u32[]{:S(2)}, u32[]{:S(2)}) collective-permute-start(f32[8,128]{1,0:T(8,128)S(1)} %get-tuple-element.19), channel_id=1, source_target_pairs={{7,8},{15,16},{23,24}} | collective-permute-start | bytes 12296 | tf_op jit(solution)/shard_map/ppermute | solution.py:308
  29.0 3.4 %collective-permute-start.2 = (bf16[1,136,128]{2,1,0:T(8,128)(2,1)S(1)}, bf16[1,136,128]{2,1,0:T(8,128)(2,1)S(1)}, u32[]{:S(2)}, u32[]{:S(2)}) collective-permute-start(bf16[1,136,128]{2,1,0:T(8,128)(2,1)S(1)} %get-tuple-element.23), channel_id=1, source_target_pairs={{0,4},{1,5},{2,6},{3,7},{8,12},{9,13},{10,14},{11,15},{16,20},{17,... | collective-permute-start | bytes 104456 | tf_op jit(solution)/shard_map/ppermute | solution.py:307
  32.4 0.0 copy-done
  32.4 0.0 copy-done.3
  32.4 1.2 %inner.1 = (f32[96,4096]{1,0:T(8,128)S(1)}, f32[1,4096]{1,0:T(1,128)S(1)}, f32[96,128]{1,0:T(8,128)S(1)}) custom-call(f32[8,128]{1,0:T(8,128)S(1)} %bitcast.6, bf16[96,4096]{1,0:T(8,128)(2,1)S(1)} %copy-done, bf16[4096,128]{1,0:T(8,128)(2,1)S(1)} %get-tuple-element.15.turned, bf16[96,4096]{1,0:T(8,128)(2,1)S(1)} %copy-done.3, ...), custom_call_target="tpu_custom_call" | custom-call | flops 8000000000 | bytes 4000000 | tf_op jit(solution)/shard_map/inner/pallas_call | solution.py:311
  33.6 0.0 copy-start.4
  33.7 0.0 collective-permute-done.earlier
  33.7 0.3 collective-permute-done.2.final
  34.0 0.9 %collective-permute-done.1.early = bf16[3,136,128]{2,1,0:T(8,128)(2,1)S(1)} collective-permute-done((bf16[3,136,128]{2,1,0:T(8,128)(2,1)S(1)}, bf16[3,136,128]{2,1,0:T(8,128)(2,1)S(1)}, u32[]{:S(2)}, u32[]{:S(2)}) %collective-permute-start.1) | collective-permute-done | bytes 104480 | tf_op jit(solution)/shard_map/ppermute | solution.py:306
  34.9 0.3 scan.1
  35.1 14.8 %all_to_all.19 = bf16[16,128,128]{2,1,0:T(8,128)(2,1)S(1)} all-to-all(bf16[16,128,128]{2,1,0:T(8,128)(2,1)S(1)} %scan.1), channel_id=1, replica_groups={{0,1,2,3,8,9,10,11,16,17,18,19,24,25,26,27},{4,5,6,7,12,13,14,15,20,21,..., dimensions={0} | all-to-all | bytes 1048576 | tf_op jit(solution)/shard_map/all_to_all | solution.py:334
  50.0 0.0 copy-done.4
  50.0 1.7 %norm.1 = bf16[96,4096]{1,0:T(8,128)(2,1)} custom-call(f32[96,128]{1,0:T(8,128)S(1)} %get-tuple-element.18.idcol, f32[8,128]{1,0:T(8,128)S(1)} %bitcast.7, f32[8,128]{1,0:T(8,128)S(1)} %collective-permute-done.earlier, f32[1,4096]{1,0:T(1,128)S(1)} %get-tuple-element.20.after.rates, bf16[96,4096]{1,0:T(8,128)(2,1)S(1)} %copy-done, ...), custom_call_target="tpu_custom_call" | custom-call | tf_op jit(solution)/shard_map/norm/pallas_call | solution.py:337
  (4 shorter events, 0.0 us)
Async XLA Ops:
  1.3 11.8 %all-to-all-start = ((f32[8,1,128]{2,1,0:T(1,128)}), f32[8,1,128]{2,1,0:T(1,128)S(1)}, u32[]{:S(2)}, u32[]{:S(2)}) async-start(f32[8,1,128]{2,1,0:T(1,128)} %broadcast_in_dim.4), calls=%async_computation | async-start | bytes 8192 | tf_op jit(solution)/shard_map/all_to_all | solution.py:266
  9.2 1.1 %copy-start.1 = (bf16[96,4096]{1,0:T(8,128)(2,1)S(1)}, bf16[96,4096]{1,0:T(8,128)(2,1)}, u32[]{:S(2)}) copy-start(bf16[96,4096]{1,0:T(8,128)(2,1)} %k_ref.1) | copy-start | bytes 2359300
  10.3 1.1 %copy-start.2 = (bf16[96,4096]{1,0:T(8,128)(2,1)S(1)}, bf16[96,4096]{1,0:T(8,128)(2,1)}, u32[]{:S(2)}) copy-start(bf16[96,4096]{1,0:T(8,128)(2,1)} %v_ref.3) | copy-start | bytes 2359300
  13.2 19.2 %copy-start = (bf16[96,4096]{1,0:T(8,128)(2,1)S(1)}, bf16[96,4096]{1,0:T(8,128)(2,1)}, u32[]{:S(2)}) copy-start(bf16[96,4096]{1,0:T(8,128)(2,1)} %q_ref.3) | copy-start | bytes 2359300
  13.2 19.2 %copy-start.3 = (bf16[96,4096]{1,0:T(8,128)(2,1)S(1)}, bf16[96,4096]{1,0:T(8,128)(2,1)}, u32[]{:S(2)}) copy-start(bf16[96,4096]{1,0:T(8,128)(2,1)} %v_ref.3) | copy-start | bytes 2359300
  26.8 8.1 %collective-permute-start.1 = (bf16[3,136,128]{2,1,0:T(8,128)(2,1)S(1)}, bf16[3,136,128]{2,1,0:T(8,128)(2,1)S(1)}, u32[]{:S(2)}, u32[]{:S(2)}) collective-permute-start(bf16[3,136,128]{2,1,0:T(8,128)(2,1)S(1)} %get-tuple-element.17.after), channel_id=1, source_target_pairs={{0,4},{1,5},{2,6},{3,7},{4,0},{5,1},{6,2},{7,3},{8,12},{9,13},{10,... | collective-permute-start | bytes 313352 | tf_op jit(solution)/shard_map/ppermute | solution.py:306
  28.3 5.3 %collective-permute-start = (f32[8,128]{1,0:T(8,128)S(1)}, f32[8,128]{1,0:T(8,128)S(1)}, u32[]{:S(2)}, u32[]{:S(2)}) collective-permute-start(f32[8,128]{1,0:T(8,128)S(1)} %get-tuple-element.19), channel_id=1, source_target_pairs={{7,8},{15,16},{23,24}} | collective-permute-start | bytes 12296 | tf_op jit(solution)/shard_map/ppermute | solution.py:308
  29.0 5.0 %collective-permute-start.2 = (bf16[1,136,128]{2,1,0:T(8,128)(2,1)S(1)}, bf16[1,136,128]{2,1,0:T(8,128)(2,1)S(1)}, u32[]{:S(2)}, u32[]{:S(2)}) collective-permute-start(bf16[1,136,128]{2,1,0:T(8,128)(2,1)S(1)} %get-tuple-element.23), channel_id=1, source_target_pairs={{0,4},{1,5},{2,6},{3,7},{8,12},{9,13},{10,14},{11,15},{16,20},{17,... | collective-permute-start | bytes 104456 | tf_op jit(solution)/shard_map/ppermute | solution.py:307
  33.6 16.3 %copy-start.4 = (f32[4096]{0:T(1024)S(1)}, f32[4096]{0:T(1024)}, u32[]{:S(2)}) copy-start(f32[4096]{0:T(1024)} %param.11) | copy-start | bytes 49156

commit v26 on v25

--- a/solution.py
+++ b/solution.py
@@ -125,7 +125,7 @@
     return piece[:rows].astype(jnp.float32), piece[rows : rows + 1].astype(jnp.float32)
 
 
-def half_kernel(here, tokens, chunks, stored, in_ref, early_ref, final_ref, one, half, mine):
+def half_kernel(here, tokens, chunks, stored, in_ref, early_ref, final_ref, one, half):
     slices, newest = early_ref.shape[0] + 1, in_ref.shape[0] - 1
     rows = one.shape[0]
     owner = lax.axis_index("ctx") * chunks + lax.rem(lax.axis_index("uly"), chunks)
@@ -136,8 +136,6 @@
             ref[at : at + share, :] = jnp.broadcast_to(
                 jnp.exp(-rate * float(length)), (share, LANES)
             )
-    last = own_ids(stored, tokens)[:, tokens - 1 : tokens]
-    mine[...] = jnp.broadcast_to(last, mine.shape)
 
     def slice_end(c, ref, at):
         def step(j, carry):
@@ -158,10 +156,16 @@
     slice_end(slices - 1, final_ref, 0)
 
 
-def scan_kernel(chunks, one, half, in_ref, early, final, after, earlier, out_ref):
+def scan_kernel(chunks, stored, one, half, in_ref, early, final, after, out_ref, before):
     slices, newest = early.shape[0] + 1, in_ref.shape[0] - 1
     rows = one.shape[0]
-    later = lax.axis_index("uly") >= chunks
+    ctx, uly = lax.axis_index("ctx"), lax.axis_index("uly")
+    later = uly >= chunks
+    members = stored.shape[0]
+    at = lax.rem(uly + members - 1 + members // 2, members)
+    _, slice_before = split(early[jnp.maximum(ctx - 1, 0)], rows)
+    first = jnp.where(ctx > 0, slice_before, -1.0)
+    before[...] = jnp.where(uly > 0, stored[pl.ds(at, 1), LANES - 1 :], first)
 
     def over_other(carry, piece, wanted):
         state, last = carry
@@ -188,16 +192,11 @@
     over_own(over_other(carry, final[0], later), slices - 1)
 
 
-def norm_kernel(idcol, stored, earlier, rates, q_ref, s_ref, inner_ref, gain, out_ref, raw, done, sems):
+def norm_kernel(idcol, before, rates, q_ref, s_ref, inner_ref, gain, out_ref, raw, done, sems):
     tokens, width = q_ref.shape
     lane = lax.broadcasted_iota(jnp.int32, (HD, LANES), 1)
     place = lax.broadcasted_iota(jnp.int32, (tokens, LANES), 0)
-    ctx, uly = lax.axis_index("ctx"), lax.axis_index("uly")
-    members = stored.shape[0]
-    at = lax.rem(uly + members - 1 + members // 2, members)
-    before = jnp.where(uly > 0, stored[pl.ds(at, 1), LANES - 1 :], earlier[:1, :1])
-    before = jnp.where(ctx + uly > 0, before, -1.0)
-    age = jnp.where(idcol[...] == before, (place + 1).astype(jnp.float32), NEVER)
+    age = jnp.where(idcol[...] == before[...], (place + 1).astype(jnp.float32), NEVER)
     zero = jnp.zeros((HD, LANES), s_ref.dtype)
     total = jnp.zeros((tokens, LANES), jnp.float32)
     for j in range(0, width // LANES, 2):
@@ -289,25 +288,21 @@
         axes, split_axis=0, concat_axis=0, tiled=True,
         axis_index_groups=[members_of[::-1] for members_of in groups],
     )
-    early_ends, final_end, one, half, mine = pl.pallas_call(
+    early_ends, final_end, one, half = pl.pallas_call(
         functools.partial(half_kernel, here, tokens, chunks),
         in_specs=[vmem] * 2,
-        out_specs=[vmem] * 5,
+        out_specs=[vmem] * 4,
         out_shape=[
             shape((slices - 1, rows + MARK, LANES), jnp.bfloat16),
             shape((1, rows + MARK, LANES), jnp.bfloat16),
             shape((rows, LANES), jnp.float32),
             shape((rows, LANES), jnp.float32),
-            shape((8, LANES), jnp.float32),
         ],
         compiler_params=params,
         name="half",
     )(stored, pieces)
     early = lax.ppermute(early_ends, axes, swap)
     final = lax.ppermute(final_end, axes, [(low, high) for low, high in swap if low < high])
-    earlier = lax.ppermute(
-        mine, axes, [(c * members - 1, c * members) for c in range(1, slices)]
-    )
     inner, rates, idcol = pl.pallas_call(
         functools.partial(inner_kernel, here),
         in_specs=[vmem] * 4 + [pl.BlockSpec(memory_space=pl.ANY)],
@@ -323,20 +318,23 @@
         ),
         name="inner",
     )(stored, queries, turned, values, early_ends)
-    moved = pl.pallas_call(
+    moved, before = pl.pallas_call(
         functools.partial(scan_kernel, chunks),
-        in_specs=[vmem] * 5 + [pl.BlockSpec(memory_space=pl.ANY)] * 2,
-        out_specs=vmem,
-        out_shape=shape((group, rows, LANES), jnp.bfloat16),
+        in_specs=[vmem] * 6 + [pl.BlockSpec(memory_space=pl.ANY)],
+        out_specs=[vmem] * 2,
+        out_shape=[
+            shape((group, rows, LANES), jnp.bfloat16),
+            shape((1, LANES), jnp.float32),
+        ],
         compiler_params=params,
         name="scan",
-    )(one, half, pieces, early, final, rates, earlier)
+    )(stored, one, half, pieces, early, final, rates)
     states = lax.all_to_all(
         moved, axes, split_axis=0, concat_axis=0, axis_index_groups=groups, tiled=True
     )
     return pl.pallas_call(
         norm_kernel,
-        in_specs=[vmem] * 8,
+        in_specs=[vmem] * 7,
         out_specs=pl.BlockSpec(memory_space=pl.ANY),
         out_shape=shape((tokens, width), jnp.bfloat16),
         scratch_shapes=[
@@ -346,7 +344,7 @@
         ],
         compiler_params=params,
         name="norm",
-    )(idcol, stored, earlier, rates, queries, states.reshape(all_pairs * HD, LANES), inner, norm_gain[None, :])
+    )(idcol, before, rates, queries, states.reshape(all_pairs * HD, LANES), inner, norm_gain[None, :])
 
 
 def solution(mesh):

time: 52 us -> 50.1 us (0.963)
  blocking collectives: 27.3 us -> 25.4 us
  starting transfers between devices: 13.4 us -> 12.7 us
  waiting for transfers between devices: 2.61 us -> 3.29 us
    all_to_all x1, blocking collectives: 14.8 us -> 13 us  [local(): lax.all_to_all(moved, axes, split_axis=0, concat_axis=0, axis_index_group...]
    ppermute x1, waiting for transfers between devices: 0.9 us -> 1.57 us  [local(): early = lax.ppermute(early_ends, axes, swap)]
    ppermute x1 -> x0, starting transfers between devices: 0.65 us -> none  [local(): lax.ppermute(mine, axes, [(c * members - 1, c * members) for c in range(1...]
  transfers between devices with their start and end apart: 4 -> 3, of which waited for: 3 -> 3; matrix products, arithmetic and copies ran while one was open for 0% -> 0% of each run, Pallas kernels for 3% -> 3%
where the time goes in v26:
time: 50.1 us; the launch traced here: 49.8 us
  blocking collectives  25.4 us (51%)
  starting transfers between devices  12.7 us (25%)
  Pallas kernels  4.66 us (9%)
  waiting for transfers between devices  3.29 us (7%)
  local copies, waits for them, and re-layouts  2.88 us (6%)
  other arithmetic  0.75 us (1%)
    all_to_all x1, blocking collectives, local(): lax.all_to_all(moved, axes, split_axis=0, concat_axis=0, axis_index_group...  13 us
    all_to_all x1, blocking collectives, local(): lax.all_to_all(ends, axes, split_axis=0, concat_axis=0, tiled=True, axis_...  12.5 us
    all_to_all x1, starting transfers between devices, local(): lax.all_to_all(jnp.broadcast_to(own[None, :], tile.shape), 'uly', split_a...  7.81 us
    ppermute x1, starting transfers between devices, local(): lax.ppermute(final_end, axes, [(low, high) for low, high in swap if low <...  3.36 us
    unnamed x10, local copies, waits for them, and re-layouts  2.28 us
    pallas_call x1, Pallas kernels, local(): pl.pallas_call(norm_kernel, in_specs=[vmem] * 7, out_specs=pl.BlockSpec(m...  1.67 us
    ppermute x1, waiting for transfers between devices, local(): early = lax.ppermute(early_ends, axes, swap)  1.57 us
    ppermute x1, starting transfers between devices, local(): early = lax.ppermute(early_ends, axes, swap)  1.52 us
  transfers between devices with their start and end apart: 3, of which 3 were waited for; matrix products, arithmetic and copies ran while one was open for 0% of the time, Pallas kernels for 3%

profile of v26, /device:TPU:0, one launch (start us, length us, event | category | flops | bytes accessed | tf_op | source)
XLA Modules:
  0.0 49.8 jit_solution(10193685000693992080)
XLA Ops:
  0.0 0.7 %convert_add_fusion = f32[128]{0:T(128)S(1)} fusion(s32[96]{0:T(128)} %param.9, f32[8]{0:T(128)} %param.10), kind=kLoop, calls=%fused_computation | loop fusion | flops 256 | bytes 928 | tf_op jit(solution)/shard_map/add | solution.py:261
  0.7 0.6 %broadcast_in_dim.4 = f32[8,1,128]{2,1,0:T(1,128)} broadcast(f32[128]{0:T(128)S(1)} %convert_add_fusion), dimensions={2} | broadcast | bytes 4608 | tf_op jit(solution)/shard_map/broadcast_in_dim | solution.py:266
  1.3 7.8 %all-to-all-start = ((f32[8,1,128]{2,1,0:T(1,128)}), f32[8,1,128]{2,1,0:T(1,128)S(1)}, u32[]{:S(2)}, u32[]{:S(2)}) async-start(f32[8,1,128]{2,1,0:T(1,128)} %broadcast_in_dim.4), calls=%async_computation | async-start | bytes 8192 | tf_op jit(solution)/shard_map/all_to_all | solution.py:265
  9.2 0.0 copy-start
  9.2 1.1 %copy-done = bf16[96,4096]{1,0:T(8,128)(2,1)S(1)} copy-done((bf16[96,4096]{1,0:T(8,128)(2,1)S(1)}, bf16[96,4096]{1,0:T(8,128)(2,1)}, u32[]{:S(2)}) %copy-start) | copy-done | bytes 786456
  10.3 0.0 copy-start.1
  10.3 1.1 %copy-done.1 = bf16[96,4096]{1,0:T(8,128)(2,1)S(1)} copy-done((bf16[96,4096]{1,0:T(8,128)(2,1)S(1)}, bf16[96,4096]{1,0:T(8,128)(2,1)}, u32[]{:S(2)}) %copy-start.1) | copy-done | bytes 786456
  11.4 0.4 turn.1
  11.8 1.4 %all-to-all-done = f32[8,1,128]{2,1,0:T(1,128)S(1)} async-done(((f32[8,1,128]{2,1,0:T(1,128)}), f32[8,1,128]{2,1,0:T(1,128)S(1)}, u32[]{:S(2)}, u32[]{:S(2)}) %all-to-all-start) | async-done | bytes 4128 | tf_op jit(solution)/shard_map/all_to_all | solution.py:265
  13.2 0.9 %ends.1 = bf16[16,136,128]{2,1,0:T(8,128)(2,1)S(1)} custom-call(f32[8,128]{1,0:T(8,128)S(1)} %bitcast.4, bf16[4096,128]{1,0:T(8,128)(2,1)S(1)} %get-tuple-element.16.turned, bf16[128,4096]{1,0:T(8,128)(2,1)S(1)} %get-tuple-element.17.v_ref), custom_call_target="tpu_custom_call" | custom-call | tf_op jit(solution)/shard_map/ends/pallas_call | solution.py:278
  14.1 12.5 %all_to_all.18.in_ref = bf16[16,136,128]{2,1,0:T(8,128)(2,1)S(1)} all-to-all(bf16[16,136,128]{2,1,0:T(8,128)(2,1)S(1)} %ends.1), channel_id=1, replica_groups={{27,26,25,24,19,18,17,16,11,10,9,8,3,2,1,0},{31,30,29,28,23,22,21,20,15..., dimensions={0} | all-to-all | bytes 1114112 | tf_op jit(solution)/shard_map/all_to_all | solution.py:286
  26.6 0.2 half.1
  26.8 1.5 %collective-permute-start = (bf16[3,136,128]{2,1,0:T(8,128)(2,1)S(1)}, bf16[3,136,128]{2,1,0:T(8,128)(2,1)S(1)}, u32[]{:S(2)}, u32[]{:S(2)}) collective-permute-start(bf16[3,136,128]{2,1,0:T(8,128)(2,1)S(1)} %get-tuple-element.18.after), channel_id=1, source_target_pairs={{0,4},{1,5},{2,6},{3,7},{4,0},{5,1},{6,2},{7,3},{8,12},{9,13},{10,... | collective-permute-start | bytes 313352 | tf_op jit(solution)/shard_map/ppermute | solution.py:304
  28.3 3.4 %collective-permute-start.1 = (bf16[1,136,128]{2,1,0:T(8,128)(2,1)S(1)}, bf16[1,136,128]{2,1,0:T(8,128)(2,1)S(1)}, u32[]{:S(2)}, u32[]{:S(2)}) collective-permute-start(bf16[1,136,128]{2,1,0:T(8,128)(2,1)S(1)} %get-tuple-element.22), channel_id=1, source_target_pairs={{0,4},{1,5},{2,6},{3,7},{8,12},{9,13},{10,14},{11,15},{16,20},{17,... | collective-permute-start | bytes 104456 | tf_op jit(solution)/shard_map/ppermute | solution.py:305
  31.7 0.0 copy-done.2
  31.7 0.0 copy-done.3
  31.7 1.2 %inner.1 = (f32[96,4096]{1,0:T(8,128)S(1)}, f32[1,4096]{1,0:T(1,128)S(1)}, f32[96,128]{1,0:T(8,128)S(1)}) custom-call(f32[8,128]{1,0:T(8,128)S(1)} %bitcast.6, bf16[96,4096]{1,0:T(8,128)(2,1)S(1)} %copy-done.3, bf16[4096,128]{1,0:T(8,128)(2,1)S(1)} %get-tuple-element.16.turned, bf16[96,4096]{1,0:T(8,128)(2,1)S(1)} %copy-done.2, ...), custom_call_target="tpu_custom_call" | custom-call | flops 8000000000 | bytes 4000000 | tf_op jit(solution)/shard_map/inner/pallas_call | solution.py:306
  32.9 0.0 copy-start.4
  33.0 0.3 collective-permute-done.1.final
  33.3 1.6 %collective-permute-done.early = bf16[3,136,128]{2,1,0:T(8,128)(2,1)S(1)} collective-permute-done((bf16[3,136,128]{2,1,0:T(8,128)(2,1)S(1)}, bf16[3,136,128]{2,1,0:T(8,128)(2,1)S(1)}, u32[]{:S(2)}, u32[]{:S(2)}) %collective-permute-start) | collective-permute-done | bytes 104480 | tf_op jit(solution)/shard_map/ppermute | solution.py:304
  34.8 0.3 scan.1
  35.1 13.0 %all_to_all.19 = bf16[16,128,128]{2,1,0:T(8,128)(2,1)S(1)} all-to-all(bf16[16,128,128]{2,1,0:T(8,128)(2,1)S(1)} %get-tuple-element.25), channel_id=1, replica_groups={{0,1,2,3,8,9,10,11,16,17,18,19,24,25,26,27},{4,5,6,7,12,13,14,15,20,21,..., dimensions={0} | all-to-all | bytes 1048576 | tf_op jit(solution)/shard_map/all_to_all | solution.py:332
  48.1 0.0 copy-done.4
  48.1 1.7 %norm.1 = bf16[96,4096]{1,0:T(8,128)(2,1)} custom-call(f32[96,128]{1,0:T(8,128)S(1)} %get-tuple-element.19.idcol, f32[1,128]{1,0:T(1,128)S(1)} %get-tuple-element.24.before, f32[1,4096]{1,0:T(1,128)S(1)} %get-tuple-element.23.after.rates, bf16[96,4096]{1,0:T(8,128)(2,1)S(1)} %copy-done.3, bf16[2048,128]{1,0:T(8,128)(2,1)S(1)} %bitcast.3, ...), custom_call_target="tpu_custom_call" | custom-call | tf_op jit(solution)/shard_map/norm/pallas_call | solution.py:335
  (2 shorter events, 0.0 us)
Async XLA Ops:
  1.3 11.8 %all-to-all-start = ((f32[8,1,128]{2,1,0:T(1,128)}), f32[8,1,128]{2,1,0:T(1,128)S(1)}, u32[]{:S(2)}, u32[]{:S(2)}) async-start(f32[8,1,128]{2,1,0:T(1,128)} %broadcast_in_dim.4), calls=%async_computation | async-start | bytes 8192 | tf_op jit(solution)/shard_map/all_to_all | solution.py:265
  9.2 1.1 %copy-start = (bf16[96,4096]{1,0:T(8,128)(2,1)S(1)}, bf16[96,4096]{1,0:T(8,128)(2,1)}, u32[]{:S(2)}) copy-start(bf16[96,4096]{1,0:T(8,128)(2,1)} %k_ref.1) | copy-start | bytes 2359300
  10.3 1.1 %copy-start.1 = (bf16[96,4096]{1,0:T(8,128)(2,1)S(1)}, bf16[96,4096]{1,0:T(8,128)(2,1)}, u32[]{:S(2)}) copy-start(bf16[96,4096]{1,0:T(8,128)(2,1)} %v_ref.3) | copy-start | bytes 2359300
  13.2 18.5 %copy-start.2 = (bf16[96,4096]{1,0:T(8,128)(2,1)S(1)}, bf16[96,4096]{1,0:T(8,128)(2,1)}, u32[]{:S(2)}) copy-start(bf16[96,4096]{1,0:T(8,128)(2,1)} %v_ref.3) | copy-start | bytes 2359300
  13.2 18.5 %copy-start.3 = (bf16[96,4096]{1,0:T(8,128)(2,1)S(1)}, bf16[96,4096]{1,0:T(8,128)(2,1)}, u32[]{:S(2)}) copy-start(bf16[96,4096]{1,0:T(8,128)(2,1)} %q_ref.3) | copy-start | bytes 2359300
  26.8 8.1 %collective-permute-start = (bf16[3,136,128]{2,1,0:T(8,128)(2,1)S(1)}, bf16[3,136,128]{2,1,0:T(8,128)(2,1)S(1)}, u32[]{:S(2)}, u32[]{:S(2)}) collective-permute-start(bf16[3,136,128]{2,1,0:T(8,128)(2,1)S(1)} %get-tuple-element.18.after), channel_id=1, source_target_pairs={{0,4},{1,5},{2,6},{3,7},{4,0},{5,1},{6,2},{7,3},{8,12},{9,13},{10,... | collective-permute-start | bytes 313352 | tf_op jit(solution)/shard_map/ppermute | solution.py:304
  28.3 5.0 %collective-permute-start.1 = (bf16[1,136,128]{2,1,0:T(8,128)(2,1)S(1)}, bf16[1,136,128]{2,1,0:T(8,128)(2,1)S(1)}, u32[]{:S(2)}, u32[]{:S(2)}) collective-permute-start(bf16[1,136,128]{2,1,0:T(8,128)(2,1)S(1)} %get-tuple-element.22), channel_id=1, source_target_pairs={{0,4},{1,5},{2,6},{3,7},{8,12},{9,13},{10,14},{11,15},{16,20},{17,... | collective-permute-start | bytes 104456 | tf_op jit(solution)/shard_map/ppermute | solution.py:305
  32.9 15.2 %copy-start.4 = (f32[4096]{0:T(1024)S(1)}, f32[4096]{0:T(1024)}, u32[]{:S(2)}) copy-start(f32[4096]{0:T(1024)} %param.11) | copy-start | bytes 49156

commit v27 on v26

--- a/solution.py
+++ b/solution.py
@@ -177,7 +177,7 @@
         def step(j, carry):
             state, last = carry
             at = c * chunks + j
-            out_ref[at] = state.astype(out_ref.dtype)
+            out_ref[newest - at] = state.astype(out_ref.dtype)
             fresh, own = split(in_ref[newest - at], rows)
             return fresh + jnp.where(own == last, one[...], 0.0) * state, own
 
@@ -192,17 +192,26 @@
     over_own(over_other(carry, final[0], later), slices - 1)
 
 
-def norm_kernel(idcol, before, rates, q_ref, s_ref, inner_ref, gain, out_ref, raw, done, sems):
+def norm_kernel(group, idcol, before, rates, q_ref, s_ref, inner_ref, gain, out_ref, raw, done, sems):
     tokens, width = q_ref.shape
     lane = lax.broadcasted_iota(jnp.int32, (HD, LANES), 1)
     place = lax.broadcasted_iota(jnp.int32, (tokens, LANES), 0)
     age = jnp.where(idcol[...] == before[...], (place + 1).astype(jnp.float32), NEVER)
     zero = jnp.zeros((HD, LANES), s_ref.dtype)
+    rows = s_ref.shape[0] // group
+    size = min(rows, HD)
     total = jnp.zeros((tokens, LANES), jnp.float32)
     for j in range(0, width // LANES, 2):
         square = []
         for one in (0, 1):
-            state = s_ref[(j + one) * HD : (j + one + 1) * HD, :]
+            state = []
+            for at in range((j + one) * HD, (j + one + 1) * HD, size):
+                owner, start = divmod(at, rows)
+                start += (group - 1 - owner) * rows
+                state.append(s_ref[start : start + size, :])
+            if len(state) > 1:
+                state = [jnp.concatenate([s.astype(jnp.float32) for s in state], 0).astype(zero.dtype)]
+            state = state[0]
             for half in (jnp.where(lane < HD, state, zero), jnp.where(lane < HD, zero, state)):
                 square.append(jnp.concatenate([zero, half] if one else [half, zero], 1))
         columns = slice(j * LANES, (j + 2) * LANES)
@@ -330,10 +339,12 @@
         name="scan",
     )(stored, one, half, pieces, early, final, rates)
     states = lax.all_to_all(
-        moved, axes, split_axis=0, concat_axis=0, axis_index_groups=groups, tiled=True
+        moved,
+        axes, split_axis=0, concat_axis=0, tiled=True,
+        axis_index_groups=[members_of[::-1] for members_of in groups],
     )
     return pl.pallas_call(
-        norm_kernel,
+        functools.partial(norm_kernel, group),
         in_specs=[vmem] * 7,
         out_specs=pl.BlockSpec(memory_space=pl.ANY),
         out_shape=shape((tokens, width), jnp.bfloat16),

time: 50.1 us -> 49.3 us (0.984)
  blocking collectives: 25.4 us -> 24.6 us
    all_to_all x1, blocking collectives: 13 us -> 12.1 us  [local(): lax.all_to_all(moved, axes, split_axis=0, concat_axis=0, tiled=True, axis...]
where the time goes in v27:
time: 49.3 us; the launch traced here: 48.9 us
  blocking collectives  24.6 us (50%)
  starting transfers between devices  12.7 us (26%)
  Pallas kernels  4.65 us (9%)
  waiting for transfers between devices  3.29 us (7%)
  local copies, waits for them, and re-layouts  2.88 us (6%)
  other arithmetic  0.75 us (2%)
    all_to_all x1, blocking collectives, local(): lax.all_to_all(ends, axes, split_axis=0, concat_axis=0, tiled=True, axis_...  12.5 us
    all_to_all x1, blocking collectives, local(): lax.all_to_all(moved, axes, split_axis=0, concat_axis=0, tiled=True, axis...  12.1 us
    all_to_all x1, starting transfers between devices, local(): lax.all_to_all(jnp.broadcast_to(own[None, :], tile.shape), 'uly', split_a...  7.81 us
    ppermute x1, starting transfers between devices, local(): lax.ppermute(final_end, axes, [(low, high) for low, high in swap if low <...  3.36 us
    unnamed x10, local copies, waits for them, and re-layouts  2.28 us
    pallas_call x1, Pallas kernels, local(): pl.pallas_call(functools.partial(norm_kernel, group), in_specs=[vmem] * 7...  1.67 us
    ppermute x1, waiting for transfers between devices, local(): early = lax.ppermute(early_ends, axes, swap)  1.57 us
    ppermute x1, starting transfers between devices, local(): early = lax.ppermute(early_ends, axes, swap)  1.52 us
  transfers between devices with their start and end apart: 3, of which 3 were waited for; matrix products, arithmetic and copies ran while one was open for 0% of the time, Pallas kernels for 3%

profile of v27, /device:TPU:0, one launch (start us, length us, event | category | flops | bytes accessed | tf_op | source)
XLA Modules:
  0.0 48.9 jit_solution(4630751928199460130)
XLA Ops:
  0.0 0.7 %convert_add_fusion = f32[128]{0:T(128)S(1)} fusion(s32[96]{0:T(128)} %param.9, f32[8]{0:T(128)} %param.10), kind=kLoop, calls=%fused_computation | loop fusion | flops 256 | bytes 928 | tf_op jit(solution)/shard_map/add | solution.py:270
  0.7 0.6 %broadcast_in_dim.4 = f32[8,1,128]{2,1,0:T(1,128)} broadcast(f32[128]{0:T(128)S(1)} %convert_add_fusion), dimensions={2} | broadcast | bytes 4608 | tf_op jit(solution)/shard_map/broadcast_in_dim | solution.py:275
  1.3 7.8 %all-to-all-start = ((f32[8,1,128]{2,1,0:T(1,128)}), f32[8,1,128]{2,1,0:T(1,128)S(1)}, u32[]{:S(2)}, u32[]{:S(2)}) async-start(f32[8,1,128]{2,1,0:T(1,128)} %broadcast_in_dim.4), calls=%async_computation | async-start | bytes 8192 | tf_op jit(solution)/shard_map/all_to_all | solution.py:274
  9.2 0.0 copy-start
  9.2 1.1 %copy-done = bf16[96,4096]{1,0:T(8,128)(2,1)S(1)} copy-done((bf16[96,4096]{1,0:T(8,128)(2,1)S(1)}, bf16[96,4096]{1,0:T(8,128)(2,1)}, u32[]{:S(2)}) %copy-start) | copy-done | bytes 786456
  10.3 0.0 copy-start.1
  10.3 1.1 %copy-done.1 = bf16[96,4096]{1,0:T(8,128)(2,1)S(1)} copy-done((bf16[96,4096]{1,0:T(8,128)(2,1)S(1)}, bf16[96,4096]{1,0:T(8,128)(2,1)}, u32[]{:S(2)}) %copy-start.1) | copy-done | bytes 786456
  11.4 0.4 turn.1
  11.8 1.4 %all-to-all-done = f32[8,1,128]{2,1,0:T(1,128)S(1)} async-done(((f32[8,1,128]{2,1,0:T(1,128)}), f32[8,1,128]{2,1,0:T(1,128)S(1)}, u32[]{:S(2)}, u32[]{:S(2)}) %all-to-all-start) | async-done | bytes 4128 | tf_op jit(solution)/shard_map/all_to_all | solution.py:274
  13.2 0.9 %ends.1 = bf16[16,136,128]{2,1,0:T(8,128)(2,1)S(1)} custom-call(f32[8,128]{1,0:T(8,128)S(1)} %bitcast.4, bf16[4096,128]{1,0:T(8,128)(2,1)S(1)} %get-tuple-element.16.turned, bf16[128,4096]{1,0:T(8,128)(2,1)S(1)} %get-tuple-element.17.v_ref), custom_call_target="tpu_custom_call" | custom-call | tf_op jit(solution)/shard_map/ends/pallas_call | solution.py:287
  14.1 12.5 %all_to_all.18.in_ref = bf16[16,136,128]{2,1,0:T(8,128)(2,1)S(1)} all-to-all(bf16[16,136,128]{2,1,0:T(8,128)(2,1)S(1)} %ends.1), channel_id=1, replica_groups={{27,26,25,24,19,18,17,16,11,10,9,8,3,2,1,0},{31,30,29,28,23,22,21,20,15..., dimensions={0} | all-to-all | bytes 1114112 | tf_op jit(solution)/shard_map/all_to_all | solution.py:295
  26.6 0.2 half.1
  26.8 1.5 %collective-permute-start = (bf16[3,136,128]{2,1,0:T(8,128)(2,1)S(1)}, bf16[3,136,128]{2,1,0:T(8,128)(2,1)S(1)}, u32[]{:S(2)}, u32[]{:S(2)}) collective-permute-start(bf16[3,136,128]{2,1,0:T(8,128)(2,1)S(1)} %get-tuple-element.18.after), channel_id=1, source_target_pairs={{0,4},{1,5},{2,6},{3,7},{4,0},{5,1},{6,2},{7,3},{8,12},{9,13},{10,... | collective-permute-start | bytes 313352 | tf_op jit(solution)/shard_map/ppermute | solution.py:313
  28.3 3.4 %collective-permute-start.1 = (bf16[1,136,128]{2,1,0:T(8,128)(2,1)S(1)}, bf16[1,136,128]{2,1,0:T(8,128)(2,1)S(1)}, u32[]{:S(2)}, u32[]{:S(2)}) collective-permute-start(bf16[1,136,128]{2,1,0:T(8,128)(2,1)S(1)} %get-tuple-element.22), channel_id=1, source_target_pairs={{0,4},{1,5},{2,6},{3,7},{8,12},{9,13},{10,14},{11,15},{16,20},{17,... | collective-permute-start | bytes 104456 | tf_op jit(solution)/shard_map/ppermute | solution.py:314
  31.7 0.0 copy-done.2
  31.7 0.0 copy-done.3
  31.7 1.2 %inner.1 = (f32[96,4096]{1,0:T(8,128)S(1)}, f32[1,4096]{1,0:T(1,128)S(1)}, f32[96,128]{1,0:T(8,128)S(1)}) custom-call(f32[8,128]{1,0:T(8,128)S(1)} %bitcast.6, bf16[96,4096]{1,0:T(8,128)(2,1)S(1)} %copy-done.3, bf16[4096,128]{1,0:T(8,128)(2,1)S(1)} %get-tuple-element.16.turned, bf16[96,4096]{1,0:T(8,128)(2,1)S(1)} %copy-done.2, ...), custom_call_target="tpu_custom_call" | custom-call | flops 8000000000 | bytes 4000000 | tf_op jit(solution)/shard_map/inner/pallas_call | solution.py:315
  32.9 0.0 copy-start.4
  33.0 0.3 collective-permute-done.1.final
  33.3 1.6 %collective-permute-done.early = bf16[3,136,128]{2,1,0:T(8,128)(2,1)S(1)} collective-permute-done((bf16[3,136,128]{2,1,0:T(8,128)(2,1)S(1)}, bf16[3,136,128]{2,1,0:T(8,128)(2,1)S(1)}, u32[]{:S(2)}, u32[]{:S(2)}) %collective-permute-start) | collective-permute-done | bytes 104480 | tf_op jit(solution)/shard_map/ppermute | solution.py:313
  34.8 0.3 scan.1
  35.1 12.1 %all_to_all.19 = bf16[16,128,128]{2,1,0:T(8,128)(2,1)S(1)} all-to-all(bf16[16,128,128]{2,1,0:T(8,128)(2,1)S(1)} %get-tuple-element.25), channel_id=1, replica_groups={{27,26,25,24,19,18,17,16,11,10,9,8,3,2,1,0},{31,30,29,28,23,22,21,20,15..., dimensions={0} | all-to-all | bytes 1048576 | tf_op jit(solution)/shard_map/all_to_all | solution.py:341
  47.2 0.0 copy-done.4
  47.2 1.7 %norm.1 = bf16[96,4096]{1,0:T(8,128)(2,1)} custom-call(f32[96,128]{1,0:T(8,128)S(1)} %get-tuple-element.19.idcol, f32[1,128]{1,0:T(1,128)S(1)} %get-tuple-element.24.before, f32[1,4096]{1,0:T(1,128)S(1)} %get-tuple-element.23.after.rates, bf16[96,4096]{1,0:T(8,128)(2,1)S(1)} %copy-done.3, bf16[2048,128]{1,0:T(8,128)(2,1)S(1)} %bitcast.3, ...), custom_call_target="tpu_custom_call" | custom-call | tf_op jit(solution)/shard_map/norm/pallas_call | solution.py:346
  (2 shorter events, 0.0 us)
Async XLA Ops:
  1.3 11.8 %all-to-all-start = ((f32[8,1,128]{2,1,0:T(1,128)}), f32[8,1,128]{2,1,0:T(1,128)S(1)}, u32[]{:S(2)}, u32[]{:S(2)}) async-start(f32[8,1,128]{2,1,0:T(1,128)} %broadcast_in_dim.4), calls=%async_computation | async-start | bytes 8192 | tf_op jit(solution)/shard_map/all_to_all | solution.py:274
  9.2 1.1 %copy-start = (bf16[96,4096]{1,0:T(8,128)(2,1)S(1)}, bf16[96,4096]{1,0:T(8,128)(2,1)}, u32[]{:S(2)}) copy-start(bf16[96,4096]{1,0:T(8,128)(2,1)} %k_ref.1) | copy-start | bytes 2359300
  10.3 1.1 %copy-start.1 = (bf16[96,4096]{1,0:T(8,128)(2,1)S(1)}, bf16[96,4096]{1,0:T(8,128)(2,1)}, u32[]{:S(2)}) copy-start(bf16[96,4096]{1,0:T(8,128)(2,1)} %v_ref.3) | copy-start | bytes 2359300
  13.2 18.5 %copy-start.2 = (bf16[96,4096]{1,0:T(8,128)(2,1)S(1)}, bf16[96,4096]{1,0:T(8,128)(2,1)}, u32[]{:S(2)}) copy-start(bf16[96,4096]{1,0:T(8,128)(2,1)} %v_ref.3) | copy-start | bytes 2359300
  13.2 18.5 %copy-start.3 = (bf16[96,4096]{1,0:T(8,128)(2,1)S(1)}, bf16[96,4096]{1,0:T(8,128)(2,1)}, u32[]{:S(2)}) copy-start(bf16[96,4096]{1,0:T(8,128)(2,1)} %q_ref.3) | copy-start | bytes 2359300
  26.8 8.1 %collective-permute-start = (bf16[3,136,128]{2,1,0:T(8,128)(2,1)S(1)}, bf16[3,136,128]{2,1,0:T(8,128)(2,1)S(1)}, u32[]{:S(2)}, u32[]{:S(2)}) collective-permute-start(bf16[3,136,128]{2,1,0:T(8,128)(2,1)S(1)} %get-tuple-element.18.after), channel_id=1, source_target_pairs={{0,4},{1,5},{2,6},{3,7},{4,0},{5,1},{6,2},{7,3},{8,12},{9,13},{10,... | collective-permute-start | bytes 313352 | tf_op jit(solution)/shard_map/ppermute | solution.py:313
  28.3 5.0 %collective-permute-start.1 = (bf16[1,136,128]{2,1,0:T(8,128)(2,1)S(1)}, bf16[1,136,128]{2,1,0:T(8,128)(2,1)S(1)}, u32[]{:S(2)}, u32[]{:S(2)}) collective-permute-start(bf16[1,136,128]{2,1,0:T(8,128)(2,1)S(1)} %get-tuple-element.22), channel_id=1, source_target_pairs={{0,4},{1,5},{2,6},{3,7},{8,12},{9,13},{10,14},{11,15},{16,20},{17,... | collective-permute-start | bytes 104456 | tf_op jit(solution)/shard_map/ppermute | solution.py:314
  32.9 14.3 %copy-start.4 = (f32[4096]{0:T(1024)S(1)}, f32[4096]{0:T(1024)}, u32[]{:S(2)}) copy-start(f32[4096]{0:T(1024)} %param.11) | copy-start | bytes 49156

commit v28 on v27

--- a/solution.py
+++ b/solution.py
@@ -83,7 +83,7 @@
             size = min(rows, HD)
             for at in range(0, HD, size):
                 owner, start = divmod((j + one) * HD + at, rows)
-                out_ref[group - 1 - owner, start : start + size, :] = state[at : at + size].astype(
+                out_ref[(owner + group // 2) % group, start : start + size, :] = state[at : at + size].astype(
                     jnp.bfloat16
                 )
 
@@ -121,12 +121,16 @@
     return count if count <= 8 else 1
 
 
+def half_way(at, count):
+    return lax.rem(at + count // 2, count)
+
+
 def split(piece, rows):
     return piece[:rows].astype(jnp.float32), piece[rows : rows + 1].astype(jnp.float32)
 
 
 def half_kernel(here, tokens, chunks, stored, in_ref, early_ref, final_ref, one, half):
-    slices, newest = early_ref.shape[0] + 1, in_ref.shape[0] - 1
+    slices, count = early_ref.shape[0] + 1, in_ref.shape[0]
     rows = one.shape[0]
     owner = lax.axis_index("ctx") * chunks + lax.rem(lax.axis_index("uly"), chunks)
     share = min(rows, HD)
@@ -140,13 +144,13 @@
     def slice_end(c, ref, at):
         def step(j, carry):
             state, last = carry
-            fresh, own = split(in_ref[newest - c * chunks - j], rows)
+            fresh, own = split(in_ref[half_way(c * chunks + j, count)], rows)
             return fresh + jnp.where(own == last, one[...], 0.0) * state, own
 
-        begin = split(in_ref[newest - c * chunks], rows)
+        begin = split(in_ref[half_way(c * chunks, count)], rows)
         state, _ = lax.fori_loop(1, chunks, step, begin, unroll=few(chunks - 1))
         ref[at, :rows, :] = state.astype(ref.dtype)
-        ref[at, rows:, :] = in_ref[newest - c * chunks - chunks + 1][rows:]
+        ref[at, rows:, :] = in_ref[half_way(c * chunks + chunks - 1, count)][rows:]
 
     def early(c, _):
         slice_end(c, early_ref, c)
@@ -157,7 +161,7 @@
 
 
 def scan_kernel(chunks, stored, one, half, in_ref, early, final, after, out_ref, before):
-    slices, newest = early.shape[0] + 1, in_ref.shape[0] - 1
+    slices, count = early.shape[0] + 1, in_ref.shape[0]
     rows = one.shape[0]
     ctx, uly = lax.axis_index("ctx"), lax.axis_index("uly")
     later = uly >= chunks
@@ -177,8 +181,8 @@
         def step(j, carry):
             state, last = carry
             at = c * chunks + j
-            out_ref[newest - at] = state.astype(out_ref.dtype)
-            fresh, own = split(in_ref[newest - at], rows)
+            out_ref[count - 1 - at] = state.astype(out_ref.dtype)
+            fresh, own = split(in_ref[half_way(at, count)], rows)
             return fresh + jnp.where(own == last, one[...], 0.0) * state, own
 
         return lax.fori_loop(0, chunks, step, carry, unroll=few(chunks))
@@ -295,7 +299,7 @@
     pieces = lax.all_to_all(
         ends,
         axes, split_axis=0, concat_axis=0, tiled=True,
-        axis_index_groups=[members_of[::-1] for members_of in groups],
+        axis_index_groups=[members_of[group // 2 :] + members_of[: group // 2] for members_of in groups],
     )
     early_ends, final_end, one, half = pl.pallas_call(
         functools.partial(half_kernel, here, tokens, chunks),

time: 49.3 us -> 50.3 us (1.020)
  blocking collectives: 24.6 us -> 25.7 us
    all_to_all x1, blocking collectives: 12.5 us -> 13.5 us  [local(): lax.all_to_all(ends, axes, split_axis=0, concat_axis=0, tiled=True, axis_...]
where the time goes in v28:
time: 50.3 us; the launch traced here: 50 us
  blocking collectives  25.7 us (51%)
  starting transfers between devices  12.7 us (25%)
  Pallas kernels  4.66 us (9%)
  waiting for transfers between devices  3.28 us (7%)
  local copies, waits for them, and re-layouts  2.88 us (6%)
  other arithmetic  0.75 us (1%)
    all_to_all x1, blocking collectives, local(): lax.all_to_all(ends, axes, split_axis=0, concat_axis=0, tiled=True, axis_...  13.5 us
    all_to_all x1, blocking collectives, local(): lax.all_to_all(moved, axes, split_axis=0, concat_axis=0, tiled=True, axis...  12.1 us
    all_to_all x1, starting transfers between devices, local(): lax.all_to_all(jnp.broadcast_to(own[None, :], tile.shape), 'uly', split_a...  7.81 us
    ppermute x1, starting transfers between devices, local(): lax.ppermute(final_end, axes, [(low, high) for low, high in swap if low <...  3.33 us
    unnamed x10, local copies, waits for them, and re-layouts  2.28 us
    pallas_call x1, Pallas kernels, local(): pl.pallas_call(functools.partial(norm_kernel, group), in_specs=[vmem] * 7...  1.67 us
    ppermute x1, waiting for transfers between devices, local(): early = lax.ppermute(early_ends, axes, swap)  1.56 us
    ppermute x1, starting transfers between devices, local(): early = lax.ppermute(early_ends, axes, swap)  1.56 us
  transfers between devices with their start and end apart: 3, of which 3 were waited for; matrix products, arithmetic and copies ran while one was open for 0% of the time, Pallas kernels for 3%

profile of v28, /device:TPU:0, one launch (start us, length us, event | category | flops | bytes accessed | tf_op | source)
XLA Modules:
  0.0 50.0 jit_solution(4432809997322429806)
XLA Ops:
  0.0 0.7 %convert_add_fusion = f32[128]{0:T(128)S(1)} fusion(s32[96]{0:T(128)} %param.9, f32[8]{0:T(128)} %param.10), kind=kLoop, calls=%fused_computation | loop fusion | flops 256 | bytes 928 | tf_op jit(solution)/shard_map/add | solution.py:274
  0.7 0.6 %broadcast_in_dim.4 = f32[8,1,128]{2,1,0:T(1,128)} broadcast(f32[128]{0:T(128)S(1)} %convert_add_fusion), dimensions={2} | broadcast | bytes 4608 | tf_op jit(solution)/shard_map/broadcast_in_dim | solution.py:279
  1.3 7.8 %all-to-all-start = ((f32[8,1,128]{2,1,0:T(1,128)}), f32[8,1,128]{2,1,0:T(1,128)S(1)}, u32[]{:S(2)}, u32[]{:S(2)}) async-start(f32[8,1,128]{2,1,0:T(1,128)} %broadcast_in_dim.4), calls=%async_computation | async-start | bytes 8192 | tf_op jit(solution)/shard_map/all_to_all | solution.py:278
  9.2 0.0 copy-start
  9.2 1.1 %copy-done = bf16[96,4096]{1,0:T(8,128)(2,1)S(1)} copy-done((bf16[96,4096]{1,0:T(8,128)(2,1)S(1)}, bf16[96,4096]{1,0:T(8,128)(2,1)}, u32[]{:S(2)}) %copy-start) | copy-done | bytes 786456
  10.3 0.0 copy-start.1
  10.3 1.1 %copy-done.1 = bf16[96,4096]{1,0:T(8,128)(2,1)S(1)} copy-done((bf16[96,4096]{1,0:T(8,128)(2,1)S(1)}, bf16[96,4096]{1,0:T(8,128)(2,1)}, u32[]{:S(2)}) %copy-start.1) | copy-done | bytes 786456
  11.4 0.4 turn.1
  11.8 1.4 %all-to-all-done = f32[8,1,128]{2,1,0:T(1,128)S(1)} async-done(((f32[8,1,128]{2,1,0:T(1,128)}), f32[8,1,128]{2,1,0:T(1,128)S(1)}, u32[]{:S(2)}, u32[]{:S(2)}) %all-to-all-start) | async-done | bytes 4128 | tf_op jit(solution)/shard_map/all_to_all | solution.py:278
  13.2 0.9 %ends.1 = bf16[16,136,128]{2,1,0:T(8,128)(2,1)S(1)} custom-call(f32[8,128]{1,0:T(8,128)S(1)} %bitcast.4, bf16[4096,128]{1,0:T(8,128)(2,1)S(1)} %get-tuple-element.16.turned, bf16[128,4096]{1,0:T(8,128)(2,1)S(1)} %get-tuple-element.17.v_ref), custom_call_target="tpu_custom_call" | custom-call | tf_op jit(solution)/shard_map/ends/pallas_call | solution.py:291
  14.1 13.5 %all_to_all.18.in_ref = bf16[16,136,128]{2,1,0:T(8,128)(2,1)S(1)} all-to-all(bf16[16,136,128]{2,1,0:T(8,128)(2,1)S(1)} %ends.1), channel_id=1, replica_groups={{16,17,18,19,24,25,26,27,0,1,2,3,8,9,10,11},{20,21,22,23,28,29,30,31,4,..., dimensions={0} | all-to-all | bytes 1114112 | tf_op jit(solution)/shard_map/all_to_all | solution.py:299
  27.6 0.2 half.1
  27.9 1.6 %collective-permute-start = (bf16[3,136,128]{2,1,0:T(8,128)(2,1)S(1)}, bf16[3,136,128]{2,1,0:T(8,128)(2,1)S(1)}, u32[]{:S(2)}, u32[]{:S(2)}) collective-permute-start(bf16[3,136,128]{2,1,0:T(8,128)(2,1)S(1)} %get-tuple-element.18.after), channel_id=1, source_target_pairs={{0,4},{1,5},{2,6},{3,7},{4,0},{5,1},{6,2},{7,3},{8,12},{9,13},{10,... | collective-permute-start | bytes 313352 | tf_op jit(solution)/shard_map/ppermute | solution.py:317
  29.4 3.3 %collective-permute-start.1 = (bf16[1,136,128]{2,1,0:T(8,128)(2,1)S(1)}, bf16[1,136,128]{2,1,0:T(8,128)(2,1)S(1)}, u32[]{:S(2)}, u32[]{:S(2)}) collective-permute-start(bf16[1,136,128]{2,1,0:T(8,128)(2,1)S(1)} %get-tuple-element.22), channel_id=1, source_target_pairs={{0,4},{1,5},{2,6},{3,7},{8,12},{9,13},{10,14},{11,15},{16,20},{17,... | collective-permute-start | bytes 104456 | tf_op jit(solution)/shard_map/ppermute | solution.py:318
  32.7 0.0 copy-done.2
  32.8 0.0 copy-done.3
  32.8 1.2 %inner.1 = (f32[96,4096]{1,0:T(8,128)S(1)}, f32[1,4096]{1,0:T(1,128)S(1)}, f32[96,128]{1,0:T(8,128)S(1)}) custom-call(f32[8,128]{1,0:T(8,128)S(1)} %bitcast.6, bf16[96,4096]{1,0:T(8,128)(2,1)S(1)} %copy-done.3, bf16[4096,128]{1,0:T(8,128)(2,1)S(1)} %get-tuple-element.16.turned, bf16[96,4096]{1,0:T(8,128)(2,1)S(1)} %copy-done.2, ...), custom_call_target="tpu_custom_call" | custom-call | flops 8000000000 | bytes 4000000 | tf_op jit(solution)/shard_map/inner/pallas_call | solution.py:319
  34.0 0.0 copy-start.4
  34.0 0.3 collective-permute-done.1.final
  34.3 1.6 %collective-permute-done.early = bf16[3,136,128]{2,1,0:T(8,128)(2,1)S(1)} collective-permute-done((bf16[3,136,128]{2,1,0:T(8,128)(2,1)S(1)}, bf16[3,136,128]{2,1,0:T(8,128)(2,1)S(1)}, u32[]{:S(2)}, u32[]{:S(2)}) %collective-permute-start) | collective-permute-done | bytes 104480 | tf_op jit(solution)/shard_map/ppermute | solution.py:317
  35.9 0.3 scan.1
  36.2 12.1 %all_to_all.19 = bf16[16,128,128]{2,1,0:T(8,128)(2,1)S(1)} all-to-all(bf16[16,128,128]{2,1,0:T(8,128)(2,1)S(1)} %get-tuple-element.25), channel_id=1, replica_groups={{27,26,25,24,19,18,17,16,11,10,9,8,3,2,1,0},{31,30,29,28,23,22,21,20,15..., dimensions={0} | all-to-all | bytes 1048576 | tf_op jit(solution)/shard_map/all_to_all | solution.py:345
  48.3 0.0 copy-done.4
  48.3 1.7 %norm.1 = bf16[96,4096]{1,0:T(8,128)(2,1)} custom-call(f32[96,128]{1,0:T(8,128)S(1)} %get-tuple-element.19.idcol, f32[1,128]{1,0:T(1,128)S(1)} %get-tuple-element.24.before, f32[1,4096]{1,0:T(1,128)S(1)} %get-tuple-element.23.after.rates, bf16[96,4096]{1,0:T(8,128)(2,1)S(1)} %copy-done.3, bf16[2048,128]{1,0:T(8,128)(2,1)S(1)} %bitcast.3, ...), custom_call_target="tpu_custom_call" | custom-call | tf_op jit(solution)/shard_map/norm/pallas_call | solution.py:350
  (2 shorter events, 0.0 us)
Async XLA Ops:
  1.3 11.8 %all-to-all-start = ((f32[8,1,128]{2,1,0:T(1,128)}), f32[8,1,128]{2,1,0:T(1,128)S(1)}, u32[]{:S(2)}, u32[]{:S(2)}) async-start(f32[8,1,128]{2,1,0:T(1,128)} %broadcast_in_dim.4), calls=%async_computation | async-start | bytes 8192 | tf_op jit(solution)/shard_map/all_to_all | solution.py:278
  9.2 1.1 %copy-start = (bf16[96,4096]{1,0:T(8,128)(2,1)S(1)}, bf16[96,4096]{1,0:T(8,128)(2,1)}, u32[]{:S(2)}) copy-start(bf16[96,4096]{1,0:T(8,128)(2,1)} %k_ref.1) | copy-start | bytes 2359300
  10.3 1.1 %copy-start.1 = (bf16[96,4096]{1,0:T(8,128)(2,1)S(1)}, bf16[96,4096]{1,0:T(8,128)(2,1)}, u32[]{:S(2)}) copy-start(bf16[96,4096]{1,0:T(8,128)(2,1)} %v_ref.3) | copy-start | bytes 2359300
  13.2 19.6 %copy-start.2 = (bf16[96,4096]{1,0:T(8,128)(2,1)S(1)}, bf16[96,4096]{1,0:T(8,128)(2,1)}, u32[]{:S(2)}) copy-start(bf16[96,4096]{1,0:T(8,128)(2,1)} %v_ref.3) | copy-start | bytes 2359300
  13.2 19.6 %copy-start.3 = (bf16[96,4096]{1,0:T(8,128)(2,1)S(1)}, bf16[96,4096]{1,0:T(8,128)(2,1)}, u32[]{:S(2)}) copy-start(bf16[96,4096]{1,0:T(8,128)(2,1)} %q_ref.3) | copy-start | bytes 2359300
  27.9 8.1 %collective-permute-start = (bf16[3,136,128]{2,1,0:T(8,128)(2,1)S(1)}, bf16[3,136,128]{2,1,0:T(8,128)(2,1)S(1)}, u32[]{:S(2)}, u32[]{:S(2)}) collective-permute-start(bf16[3,136,128]{2,1,0:T(8,128)(2,1)S(1)} %get-tuple-element.18.after), channel_id=1, source_target_pairs={{0,4},{1,5},{2,6},{3,7},{4,0},{5,1},{6,2},{7,3},{8,12},{9,13},{10,... | collective-permute-start | bytes 313352 | tf_op jit(solution)/shard_map/ppermute | solution.py:317
  29.4 4.9 %collective-permute-start.1 = (bf16[1,136,128]{2,1,0:T(8,128)(2,1)S(1)}, bf16[1,136,128]{2,1,0:T(8,128)(2,1)S(1)}, u32[]{:S(2)}, u32[]{:S(2)}) collective-permute-start(bf16[1,136,128]{2,1,0:T(8,128)(2,1)S(1)} %get-tuple-element.22), channel_id=1, source_target_pairs={{0,4},{1,5},{2,6},{3,7},{8,12},{9,13},{10,14},{11,15},{16,20},{17,... | collective-permute-start | bytes 104456 | tf_op jit(solution)/shard_map/ppermute | solution.py:318
  34.0 14.3 %copy-start.4 = (f32[4096]{0:T(1024)S(1)}, f32[4096]{0:T(1024)}, u32[]{:S(2)}) copy-start(f32[4096]{0:T(1024)} %param.11) | copy-start | bytes 49156

commit v29 on v27

--- a/solution.py
+++ b/solution.py
@@ -22,7 +22,7 @@
     lane = lax.broadcasted_iota(jnp.int32, (1, LANES), 1)
     rates = []
     for head in (2 * pair, 2 * pair + 1):
-        at = lax.rem(lax.div(head, here) + members // 2, members)
+        at = lax.rem(lax.div(head, here) + members - members // 4, members)
         row = stored[pl.ds(at, 1), :]
         rates.append(
             jnp.sum(jnp.where(lane == lax.rem(head, here), row, 0.0), axis=1, keepdims=True)
@@ -32,7 +32,7 @@
 
 def own_ids(stored, tokens):
     members = stored.shape[0]
-    at = lax.rem(lax.axis_index("uly") + members // 2, members)
+    at = lax.rem(lax.axis_index("uly") + members - members // 4, members)
     row = stored[pl.ds(at, 1), :]
     fill = jnp.full((1, LANES - tokens), -1.0, jnp.float32)
     return jnp.concatenate([row[:, LANES - tokens :], fill], 1)
@@ -64,7 +64,7 @@
     for j in range(0, width // LANES, 2):
         weighted = []
         for head in range(2 * j, 2 * j + 4):
-            weight = jnp.exp(-rate_of(stored, (head + members // 2 * here) % (members * here), here) * age)
+            weight = jnp.exp(-rate_of(stored, (head - members // 4 * here) % (members * here), here) * age)
             keys = turned[head * HD : (head + 1) * HD, :].astype(jnp.float32)
             keys = keys.reshape(HD // 8, 8, LANES) * weight[None]
             weighted.append(keys.reshape(HD, LANES))
@@ -107,7 +107,7 @@
             stacked, turned[columns, :], preferred_element_type=jnp.float32
         )
         rates = [
-            rate_of(stored, (2 * j + one + members // 2 * here) % (members * here), here)
+            rate_of(stored, (2 * j + one - members // 4 * here) % (members * here), here)
             for one in (0, 1)
         ]
         weight = jnp.concatenate([jnp.exp(-rate * age) for rate in rates], 0)
@@ -162,7 +162,7 @@
     ctx, uly = lax.axis_index("ctx"), lax.axis_index("uly")
     later = uly >= chunks
     members = stored.shape[0]
-    at = lax.rem(uly + members - 1 + members // 2, members)
+    at = lax.rem(uly + members - 1 + members - members // 4, members)
     _, slice_before = split(early[jnp.maximum(ctx - 1, 0)], rows)
     first = jnp.where(ctx > 0, slice_before, -1.0)
     before[...] = jnp.where(uly > 0, stored[pl.ds(at, 1), LANES - 1 :], first)
@@ -270,7 +270,7 @@
     own = jnp.pad(decay_rate, (0, LANES - here)) + jnp.pad(
         doc_ids, (LANES - tokens, 0)
     ).astype(jnp.float32)
-    turned_round = [[(u + members // 2) % members for u in range(members)]]
+    turned_round = [[(u + members // 4) % members for u in range(members)]]
     stored = lax.all_to_all(
         jnp.broadcast_to(own[None, :], tile.shape),
         "uly", split_axis=0, concat_axis=0, axis_index_groups=turned_round, tiled=True,

time: 49.3 us -> 50.2 us (1.018)
  waiting for transfers between devices: 3.29 us -> 4.19 us
    ppermute x1, starting transfers between devices: 1.52 us -> 0.62 us  [local(): early = lax.ppermute(early_ends, axes, swap)]
    ppermute x1, starting transfers between devices: 3.36 us -> 4.26 us  [local(): lax.ppermute(final_end, axes, [(low, high) for low, high in swap if low <...]
    all_to_all x1, waiting for transfers between devices: 1.4 us -> 2.29 us  [local(): lax.all_to_all(jnp.broadcast_to(own[None, :], tile.shape), 'uly', split_a...]
where the time goes in v29:
time: 50.2 us; the launch traced here: 49.8 us
  blocking collectives  24.6 us (49%)
  starting transfers between devices  12.7 us (25%)
  Pallas kernels  4.65 us (9%)
  waiting for transfers between devices  4.19 us (8%)
  local copies, waits for them, and re-layouts  2.88 us (6%)
  other arithmetic  0.75 us (1%)
    all_to_all x1, blocking collectives, local(): lax.all_to_all(ends, axes, split_axis=0, concat_axis=0, tiled=True, axis_...  12.5 us
    all_to_all x1, blocking collectives, local(): lax.all_to_all(moved, axes, split_axis=0, concat_axis=0, tiled=True, axis...  12.1 us
    all_to_all x1, starting transfers between devices, local(): lax.all_to_all(jnp.broadcast_to(own[None, :], tile.shape), 'uly', split_a...  7.81 us
    ppermute x1, starting transfers between devices, local(): lax.ppermute(final_end, axes, [(low, high) for low, high in swap if low <...  4.26 us
    all_to_all x1, waiting for transfers between devices, local(): lax.all_to_all(jnp.broadcast_to(own[None, :], tile.shape), 'uly', split_a...  2.29 us
    unnamed x10, local copies, waits for them, and re-layouts  2.28 us
    pallas_call x1, Pallas kernels, local(): pl.pallas_call(functools.partial(norm_kernel, group), in_specs=[vmem] * 7...  1.67 us
    ppermute x1, waiting for transfers between devices, local(): early = lax.ppermute(early_ends, axes, swap)  1.57 us
  transfers between devices with their start and end apart: 3, of which 3 were waited for; matrix products, arithmetic and copies ran while one was open for 0% of the time, Pallas kernels for 3%

profile of v29, /device:TPU:0, one launch (start us, length us, event | category | flops | bytes accessed | tf_op | source)
XLA Modules:
  0.0 49.8 jit_solution(7635129856625657346)
XLA Ops:
  0.0 0.7 %convert_add_fusion = f32[128]{0:T(128)S(1)} fusion(s32[96]{0:T(128)} %param.9, f32[8]{0:T(128)} %param.10), kind=kLoop, calls=%fused_computation | loop fusion | flops 256 | bytes 928 | tf_op jit(solution)/shard_map/add | solution.py:270
  0.7 0.6 %broadcast_in_dim.4 = f32[8,1,128]{2,1,0:T(1,128)} broadcast(f32[128]{0:T(128)S(1)} %convert_add_fusion), dimensions={2} | broadcast | bytes 4608 | tf_op jit(solution)/shard_map/broadcast_in_dim | solution.py:275
  1.3 7.8 %all-to-all-start = ((f32[8,1,128]{2,1,0:T(1,128)}), f32[8,1,128]{2,1,0:T(1,128)S(1)}, u32[]{:S(2)}, u32[]{:S(2)}) async-start(f32[8,1,128]{2,1,0:T(1,128)} %broadcast_in_dim.4), calls=%async_computation | async-start | bytes 8192 | tf_op jit(solution)/shard_map/all_to_all | solution.py:274
  9.2 0.0 copy-start
  9.2 1.1 %copy-done = bf16[96,4096]{1,0:T(8,128)(2,1)S(1)} copy-done((bf16[96,4096]{1,0:T(8,128)(2,1)S(1)}, bf16[96,4096]{1,0:T(8,128)(2,1)}, u32[]{:S(2)}) %copy-start) | copy-done | bytes 786456
  10.3 0.0 copy-start.1
  10.3 1.1 %copy-done.1 = bf16[96,4096]{1,0:T(8,128)(2,1)S(1)} copy-done((bf16[96,4096]{1,0:T(8,128)(2,1)S(1)}, bf16[96,4096]{1,0:T(8,128)(2,1)}, u32[]{:S(2)}) %copy-start.1) | copy-done | bytes 786456
  11.4 0.4 turn.1
  11.8 2.3 %all-to-all-done = f32[8,1,128]{2,1,0:T(1,128)S(1)} async-done(((f32[8,1,128]{2,1,0:T(1,128)}), f32[8,1,128]{2,1,0:T(1,128)S(1)}, u32[]{:S(2)}, u32[]{:S(2)}) %all-to-all-start) | async-done | bytes 4128 | tf_op jit(solution)/shard_map/all_to_all | solution.py:274
  14.1 0.9 %ends.1 = bf16[16,136,128]{2,1,0:T(8,128)(2,1)S(1)} custom-call(f32[8,128]{1,0:T(8,128)S(1)} %bitcast.4, bf16[4096,128]{1,0:T(8,128)(2,1)S(1)} %get-tuple-element.16.turned, bf16[128,4096]{1,0:T(8,128)(2,1)S(1)} %get-tuple-element.17.v_ref), custom_call_target="tpu_custom_call" | custom-call | tf_op jit(solution)/shard_map/ends/pallas_call | solution.py:287
  15.0 12.5 %all_to_all.18.in_ref = bf16[16,136,128]{2,1,0:T(8,128)(2,1)S(1)} all-to-all(bf16[16,136,128]{2,1,0:T(8,128)(2,1)S(1)} %ends.1), channel_id=1, replica_groups={{27,26,25,24,19,18,17,16,11,10,9,8,3,2,1,0},{31,30,29,28,23,22,21,20,15..., dimensions={0} | all-to-all | bytes 1114112 | tf_op jit(solution)/shard_map/all_to_all | solution.py:295
  27.5 0.2 half.1
  27.7 0.6 %collective-permute-start = (bf16[3,136,128]{2,1,0:T(8,128)(2,1)S(1)}, bf16[3,136,128]{2,1,0:T(8,128)(2,1)S(1)}, u32[]{:S(2)}, u32[]{:S(2)}) collective-permute-start(bf16[3,136,128]{2,1,0:T(8,128)(2,1)S(1)} %get-tuple-element.18.after), channel_id=1, source_target_pairs={{0,4},{1,5},{2,6},{3,7},{4,0},{5,1},{6,2},{7,3},{8,12},{9,13},{10,... | collective-permute-start | bytes 313352 | tf_op jit(solution)/shard_map/ppermute | solution.py:313
  28.3 4.3 %collective-permute-start.1 = (bf16[1,136,128]{2,1,0:T(8,128)(2,1)S(1)}, bf16[1,136,128]{2,1,0:T(8,128)(2,1)S(1)}, u32[]{:S(2)}, u32[]{:S(2)}) collective-permute-start(bf16[1,136,128]{2,1,0:T(8,128)(2,1)S(1)} %get-tuple-element.22), channel_id=1, source_target_pairs={{0,4},{1,5},{2,6},{3,7},{8,12},{9,13},{10,14},{11,15},{16,20},{17,... | collective-permute-start | bytes 104456 | tf_op jit(solution)/shard_map/ppermute | solution.py:314
  32.6 0.0 copy-done.2
  32.6 0.0 copy-done.3
  32.6 1.2 %inner.1 = (f32[96,4096]{1,0:T(8,128)S(1)}, f32[1,4096]{1,0:T(1,128)S(1)}, f32[96,128]{1,0:T(8,128)S(1)}) custom-call(f32[8,128]{1,0:T(8,128)S(1)} %bitcast.6, bf16[96,4096]{1,0:T(8,128)(2,1)S(1)} %copy-done.3, bf16[4096,128]{1,0:T(8,128)(2,1)S(1)} %get-tuple-element.16.turned, bf16[96,4096]{1,0:T(8,128)(2,1)S(1)} %copy-done.2, ...), custom_call_target="tpu_custom_call" | custom-call | flops 8000000000 | bytes 4000000 | tf_op jit(solution)/shard_map/inner/pallas_call | solution.py:315
  33.8 0.0 copy-start.4
  33.9 0.3 collective-permute-done.1.final
  34.2 1.6 %collective-permute-done.early = bf16[3,136,128]{2,1,0:T(8,128)(2,1)S(1)} collective-permute-done((bf16[3,136,128]{2,1,0:T(8,128)(2,1)S(1)}, bf16[3,136,128]{2,1,0:T(8,128)(2,1)S(1)}, u32[]{:S(2)}, u32[]{:S(2)}) %collective-permute-start) | collective-permute-done | bytes 104480 | tf_op jit(solution)/shard_map/ppermute | solution.py:313
  35.8 0.3 scan.1
  36.0 12.1 %all_to_all.19 = bf16[16,128,128]{2,1,0:T(8,128)(2,1)S(1)} all-to-all(bf16[16,128,128]{2,1,0:T(8,128)(2,1)S(1)} %get-tuple-element.25), channel_id=1, replica_groups={{27,26,25,24,19,18,17,16,11,10,9,8,3,2,1,0},{31,30,29,28,23,22,21,20,15..., dimensions={0} | all-to-all | bytes 1048576 | tf_op jit(solution)/shard_map/all_to_all | solution.py:341
  48.1 0.0 copy-done.4
  48.1 1.7 %norm.1 = bf16[96,4096]{1,0:T(8,128)(2,1)} custom-call(f32[96,128]{1,0:T(8,128)S(1)} %get-tuple-element.19.idcol, f32[1,128]{1,0:T(1,128)S(1)} %get-tuple-element.24.before, f32[1,4096]{1,0:T(1,128)S(1)} %get-tuple-element.23.after.rates, bf16[96,4096]{1,0:T(8,128)(2,1)S(1)} %copy-done.3, bf16[2048,128]{1,0:T(8,128)(2,1)S(1)} %bitcast.3, ...), custom_call_target="tpu_custom_call" | custom-call | tf_op jit(solution)/shard_map/norm/pallas_call | solution.py:346
  (2 shorter events, 0.0 us)
Async XLA Ops:
  1.3 12.7 %all-to-all-start = ((f32[8,1,128]{2,1,0:T(1,128)}), f32[8,1,128]{2,1,0:T(1,128)S(1)}, u32[]{:S(2)}, u32[]{:S(2)}) async-start(f32[8,1,128]{2,1,0:T(1,128)} %broadcast_in_dim.4), calls=%async_computation | async-start | bytes 8192 | tf_op jit(solution)/shard_map/all_to_all | solution.py:274
  9.2 1.1 %copy-start = (bf16[96,4096]{1,0:T(8,128)(2,1)S(1)}, bf16[96,4096]{1,0:T(8,128)(2,1)}, u32[]{:S(2)}) copy-start(bf16[96,4096]{1,0:T(8,128)(2,1)} %k_ref.1) | copy-start | bytes 2359300
  10.3 1.1 %copy-start.1 = (bf16[96,4096]{1,0:T(8,128)(2,1)S(1)}, bf16[96,4096]{1,0:T(8,128)(2,1)}, u32[]{:S(2)}) copy-start(bf16[96,4096]{1,0:T(8,128)(2,1)} %v_ref.3) | copy-start | bytes 2359300
  14.1 18.5 %copy-start.2 = (bf16[96,4096]{1,0:T(8,128)(2,1)S(1)}, bf16[96,4096]{1,0:T(8,128)(2,1)}, u32[]{:S(2)}) copy-start(bf16[96,4096]{1,0:T(8,128)(2,1)} %v_ref.3) | copy-start | bytes 2359300
  14.1 18.5 %copy-start.3 = (bf16[96,4096]{1,0:T(8,128)(2,1)S(1)}, bf16[96,4096]{1,0:T(8,128)(2,1)}, u32[]{:S(2)}) copy-start(bf16[96,4096]{1,0:T(8,128)(2,1)} %q_ref.3) | copy-start | bytes 2359300
  27.7 8.1 %collective-permute-start = (bf16[3,136,128]{2,1,0:T(8,128)(2,1)S(1)}, bf16[3,136,128]{2,1,0:T(8,128)(2,1)S(1)}, u32[]{:S(2)}, u32[]{:S(2)}) collective-permute-start(bf16[3,136,128]{2,1,0:T(8,128)(2,1)S(1)} %get-tuple-element.18.after), channel_id=1, source_target_pairs={{0,4},{1,5},{2,6},{3,7},{4,0},{5,1},{6,2},{7,3},{8,12},{9,13},{10,... | collective-permute-start | bytes 313352 | tf_op jit(solution)/shard_map/ppermute | solution.py:313
  28.3 5.9 %collective-permute-start.1 = (bf16[1,136,128]{2,1,0:T(8,128)(2,1)S(1)}, bf16[1,136,128]{2,1,0:T(8,128)(2,1)S(1)}, u32[]{:S(2)}, u32[]{:S(2)}) collective-permute-start(bf16[1,136,128]{2,1,0:T(8,128)(2,1)S(1)} %get-tuple-element.22), channel_id=1, source_target_pairs={{0,4},{1,5},{2,6},{3,7},{8,12},{9,13},{10,14},{11,15},{16,20},{17,... | collective-permute-start | bytes 104456 | tf_op jit(solution)/shard_map/ppermute | solution.py:314
  33.8 14.3 %copy-start.4 = (f32[4096]{0:T(1024)S(1)}, f32[4096]{0:T(1024)}, u32[]{:S(2)}) copy-start(f32[4096]{0:T(1024)} %param.11) | copy-start | bytes 49156

commit v30 on v29

--- a/solution.py
+++ b/solution.py
@@ -22,7 +22,7 @@
     lane = lax.broadcasted_iota(jnp.int32, (1, LANES), 1)
     rates = []
     for head in (2 * pair, 2 * pair + 1):
-        at = lax.rem(lax.div(head, here) + members - members // 4, members)
+        at = lax.rem(lax.div(head, here) + members // 2 - 1, members)
         row = stored[pl.ds(at, 1), :]
         rates.append(
             jnp.sum(jnp.where(lane == lax.rem(head, here), row, 0.0), axis=1, keepdims=True)
@@ -32,7 +32,7 @@
 
 def own_ids(stored, tokens):
     members = stored.shape[0]
-    at = lax.rem(lax.axis_index("uly") + members - members // 4, members)
+    at = lax.rem(lax.axis_index("uly") + members // 2 - 1, members)
     row = stored[pl.ds(at, 1), :]
     fill = jnp.full((1, LANES - tokens), -1.0, jnp.float32)
     return jnp.concatenate([row[:, LANES - tokens :], fill], 1)
@@ -64,7 +64,7 @@
     for j in range(0, width // LANES, 2):
         weighted = []
         for head in range(2 * j, 2 * j + 4):
-            weight = jnp.exp(-rate_of(stored, (head - members // 4 * here) % (members * here), here) * age)
+            weight = jnp.exp(-rate_of(stored, (head + (members // 2 - 1) * here) % (members * here), here) * age)
             keys = turned[head * HD : (head + 1) * HD, :].astype(jnp.float32)
             keys = keys.reshape(HD // 8, 8, LANES) * weight[None]
             weighted.append(keys.reshape(HD, LANES))
@@ -107,7 +107,7 @@
             stacked, turned[columns, :], preferred_element_type=jnp.float32
         )
         rates = [
-            rate_of(stored, (2 * j + one - members // 4 * here) % (members * here), here)
+            rate_of(stored, (2 * j + one + (members // 2 - 1) * here) % (members * here), here)
             for one in (0, 1)
         ]
         weight = jnp.concatenate([jnp.exp(-rate * age) for rate in rates], 0)
@@ -162,7 +162,7 @@
     ctx, uly = lax.axis_index("ctx"), lax.axis_index("uly")
     later = uly >= chunks
     members = stored.shape[0]
-    at = lax.rem(uly + members - 1 + members - members // 4, members)
+    at = lax.rem(uly + members - 1 + members // 2 - 1, members)
     _, slice_before = split(early[jnp.maximum(ctx - 1, 0)], rows)
     first = jnp.where(ctx > 0, slice_before, -1.0)
     before[...] = jnp.where(uly > 0, stored[pl.ds(at, 1), LANES - 1 :], first)
@@ -270,7 +270,7 @@
     own = jnp.pad(decay_rate, (0, LANES - here)) + jnp.pad(
         doc_ids, (LANES - tokens, 0)
     ).astype(jnp.float32)
-    turned_round = [[(u + members // 4) % members for u in range(members)]]
+    turned_round = [[(u + members // 2 + 1) % members for u in range(members)]]
     stored = lax.all_to_all(
         jnp.broadcast_to(own[None, :], tile.shape),
         "uly", split_axis=0, concat_axis=0, axis_index_groups=turned_round, tiled=True,

time: 50.2 us -> 48.7 us (0.970)
  waiting for transfers between devices: 4.19 us -> 2.39 us
    all_to_all x1, waiting for transfers between devices: 2.29 us -> 0.49 us  [local(): lax.all_to_all(jnp.broadcast_to(own[None, :], tile.shape), 'uly', split_a...]
    ppermute x1, starting transfers between devices: 0.62 us -> 1.54 us  [local(): early = lax.ppermute(early_ends, axes, swap)]
    ppermute x1, starting transfers between devices: 4.26 us -> 3.35 us  [local(): lax.ppermute(final_end, axes, [(low, high) for low, high in swap if low <...]
where the time goes in v30:
time: 48.7 us; the launch traced here: 48.4 us
  blocking collectives  24.6 us (51%)
  starting transfers between devices  13.1 us (27%)
  Pallas kernels  4.65 us (10%)
  local copies, waits for them, and re-layouts  2.88 us (6%)
  waiting for transfers between devices  2.39 us (5%)
  other arithmetic  0.75 us (2%)
    all_to_all x1, blocking collectives, local(): lax.all_to_all(ends, axes, split_axis=0, concat_axis=0, tiled=True, axis_...  12.5 us
    all_to_all x1, blocking collectives, local(): lax.all_to_all(moved, axes, split_axis=0, concat_axis=0, tiled=True, axis...  12.1 us
    all_to_all x1, starting transfers between devices, local(): lax.all_to_all(jnp.broadcast_to(own[None, :], tile.shape), 'uly', split_a...  8.19 us
    ppermute x1, starting transfers between devices, local(): lax.ppermute(final_end, axes, [(low, high) for low, high in swap if low <...  3.35 us
    unnamed x10, local copies, waits for them, and re-layouts  2.28 us
    pallas_call x1, Pallas kernels, local(): pl.pallas_call(functools.partial(norm_kernel, group), in_specs=[vmem] * 7...  1.67 us
    ppermute x1, waiting for transfers between devices, local(): early = lax.ppermute(early_ends, axes, swap)  1.57 us
    ppermute x1, starting transfers between devices, local(): early = lax.ppermute(early_ends, axes, swap)  1.54 us
  transfers between devices with their start and end apart: 3, of which 3 were waited for; matrix products, arithmetic and copies ran while one was open for 0% of the time, Pallas kernels for 3%

profile of v30, /device:TPU:0, one launch (start us, length us, event | category | flops | bytes accessed | tf_op | source)
XLA Modules:
  0.0 48.4 jit_solution(2669363740904336165)
XLA Ops:
  0.0 0.7 %convert_add_fusion = f32[128]{0:T(128)S(1)} fusion(s32[96]{0:T(128)} %param.9, f32[8]{0:T(128)} %param.10), kind=kLoop, calls=%fused_computation | loop fusion | flops 256 | bytes 928 | tf_op jit(solution)/shard_map/add | solution.py:270
  0.7 0.6 %broadcast_in_dim.4 = f32[8,1,128]{2,1,0:T(1,128)} broadcast(f32[128]{0:T(128)S(1)} %convert_add_fusion), dimensions={2} | broadcast | bytes 4608 | tf_op jit(solution)/shard_map/broadcast_in_dim | solution.py:275
  1.3 8.2 %all-to-all-start = ((f32[8,1,128]{2,1,0:T(1,128)}), f32[8,1,128]{2,1,0:T(1,128)S(1)}, u32[]{:S(2)}, u32[]{:S(2)}) async-start(f32[8,1,128]{2,1,0:T(1,128)} %broadcast_in_dim.4), calls=%async_computation | async-start | bytes 8192 | tf_op jit(solution)/shard_map/all_to_all | solution.py:274
  9.5 0.0 copy-start
  9.5 1.1 %copy-done = bf16[96,4096]{1,0:T(8,128)(2,1)S(1)} copy-done((bf16[96,4096]{1,0:T(8,128)(2,1)S(1)}, bf16[96,4096]{1,0:T(8,128)(2,1)}, u32[]{:S(2)}) %copy-start) | copy-done | bytes 786456
  10.7 0.0 copy-start.1
  10.7 1.1 %copy-done.1 = bf16[96,4096]{1,0:T(8,128)(2,1)S(1)} copy-done((bf16[96,4096]{1,0:T(8,128)(2,1)S(1)}, bf16[96,4096]{1,0:T(8,128)(2,1)}, u32[]{:S(2)}) %copy-start.1) | copy-done | bytes 786456
  11.8 0.4 turn.1
  12.2 0.5 %all-to-all-done = f32[8,1,128]{2,1,0:T(1,128)S(1)} async-done(((f32[8,1,128]{2,1,0:T(1,128)}), f32[8,1,128]{2,1,0:T(1,128)S(1)}, u32[]{:S(2)}, u32[]{:S(2)}) %all-to-all-start) | async-done | bytes 4128 | tf_op jit(solution)/shard_map/all_to_all | solution.py:274
  12.7 0.9 %ends.1 = bf16[16,136,128]{2,1,0:T(8,128)(2,1)S(1)} custom-call(f32[8,128]{1,0:T(8,128)S(1)} %bitcast.4, bf16[4096,128]{1,0:T(8,128)(2,1)S(1)} %get-tuple-element.16.turned, bf16[128,4096]{1,0:T(8,128)(2,1)S(1)} %get-tuple-element.17.v_ref), custom_call_target="tpu_custom_call" | custom-call | tf_op jit(solution)/shard_map/ends/pallas_call | solution.py:287
  13.6 12.5 %all_to_all.18.in_ref = bf16[16,136,128]{2,1,0:T(8,128)(2,1)S(1)} all-to-all(bf16[16,136,128]{2,1,0:T(8,128)(2,1)S(1)} %ends.1), channel_id=1, replica_groups={{27,26,25,24,19,18,17,16,11,10,9,8,3,2,1,0},{31,30,29,28,23,22,21,20,15..., dimensions={0} | all-to-all | bytes 1114112 | tf_op jit(solution)/shard_map/all_to_all | solution.py:295
  26.0 0.2 half.1
  26.3 1.5 %collective-permute-start = (bf16[3,136,128]{2,1,0:T(8,128)(2,1)S(1)}, bf16[3,136,128]{2,1,0:T(8,128)(2,1)S(1)}, u32[]{:S(2)}, u32[]{:S(2)}) collective-permute-start(bf16[3,136,128]{2,1,0:T(8,128)(2,1)S(1)} %get-tuple-element.18.after), channel_id=1, source_target_pairs={{0,4},{1,5},{2,6},{3,7},{4,0},{5,1},{6,2},{7,3},{8,12},{9,13},{10,... | collective-permute-start | bytes 313352 | tf_op jit(solution)/shard_map/ppermute | solution.py:313
  27.8 3.3 %collective-permute-start.1 = (bf16[1,136,128]{2,1,0:T(8,128)(2,1)S(1)}, bf16[1,136,128]{2,1,0:T(8,128)(2,1)S(1)}, u32[]{:S(2)}, u32[]{:S(2)}) collective-permute-start(bf16[1,136,128]{2,1,0:T(8,128)(2,1)S(1)} %get-tuple-element.22), channel_id=1, source_target_pairs={{0,4},{1,5},{2,6},{3,7},{8,12},{9,13},{10,14},{11,15},{16,20},{17,... | collective-permute-start | bytes 104456 | tf_op jit(solution)/shard_map/ppermute | solution.py:314
  31.1 0.0 copy-done.2
  31.2 0.0 copy-done.3
  31.2 1.2 %inner.1 = (f32[96,4096]{1,0:T(8,128)S(1)}, f32[1,4096]{1,0:T(1,128)S(1)}, f32[96,128]{1,0:T(8,128)S(1)}) custom-call(f32[8,128]{1,0:T(8,128)S(1)} %bitcast.6, bf16[96,4096]{1,0:T(8,128)(2,1)S(1)} %copy-done.3, bf16[4096,128]{1,0:T(8,128)(2,1)S(1)} %get-tuple-element.16.turned, bf16[96,4096]{1,0:T(8,128)(2,1)S(1)} %copy-done.2, ...), custom_call_target="tpu_custom_call" | custom-call | flops 8000000000 | bytes 4000000 | tf_op jit(solution)/shard_map/inner/pallas_call | solution.py:315
  32.4 0.0 copy-start.4
  32.4 0.3 collective-permute-done.1.final
  32.7 1.6 %collective-permute-done.early = bf16[3,136,128]{2,1,0:T(8,128)(2,1)S(1)} collective-permute-done((bf16[3,136,128]{2,1,0:T(8,128)(2,1)S(1)}, bf16[3,136,128]{2,1,0:T(8,128)(2,1)S(1)}, u32[]{:S(2)}, u32[]{:S(2)}) %collective-permute-start) | collective-permute-done | bytes 104480 | tf_op jit(solution)/shard_map/ppermute | solution.py:313
  34.3 0.3 scan.1
  34.6 12.1 %all_to_all.19 = bf16[16,128,128]{2,1,0:T(8,128)(2,1)S(1)} all-to-all(bf16[16,128,128]{2,1,0:T(8,128)(2,1)S(1)} %get-tuple-element.25), channel_id=1, replica_groups={{27,26,25,24,19,18,17,16,11,10,9,8,3,2,1,0},{31,30,29,28,23,22,21,20,15..., dimensions={0} | all-to-all | bytes 1048576 | tf_op jit(solution)/shard_map/all_to_all | solution.py:341
  46.7 0.0 copy-done.4
  46.7 1.7 %norm.1 = bf16[96,4096]{1,0:T(8,128)(2,1)} custom-call(f32[96,128]{1,0:T(8,128)S(1)} %get-tuple-element.19.idcol, f32[1,128]{1,0:T(1,128)S(1)} %get-tuple-element.24.before, f32[1,4096]{1,0:T(1,128)S(1)} %get-tuple-element.23.after.rates, bf16[96,4096]{1,0:T(8,128)(2,1)S(1)} %copy-done.3, bf16[2048,128]{1,0:T(8,128)(2,1)S(1)} %bitcast.3, ...), custom_call_target="tpu_custom_call" | custom-call | tf_op jit(solution)/shard_map/norm/pallas_call | solution.py:346
  (2 shorter events, 0.0 us)
Async XLA Ops:
  1.3 11.3 %all-to-all-start = ((f32[8,1,128]{2,1,0:T(1,128)}), f32[8,1,128]{2,1,0:T(1,128)S(1)}, u32[]{:S(2)}, u32[]{:S(2)}) async-start(f32[8,1,128]{2,1,0:T(1,128)} %broadcast_in_dim.4), calls=%async_computation | async-start | bytes 8192 | tf_op jit(solution)/shard_map/all_to_all | solution.py:274
  9.5 1.1 %copy-start = (bf16[96,4096]{1,0:T(8,128)(2,1)S(1)}, bf16[96,4096]{1,0:T(8,128)(2,1)}, u32[]{:S(2)}) copy-start(bf16[96,4096]{1,0:T(8,128)(2,1)} %k_ref.1) | copy-start | bytes 2359300
  10.7 1.1 %copy-start.1 = (bf16[96,4096]{1,0:T(8,128)(2,1)S(1)}, bf16[96,4096]{1,0:T(8,128)(2,1)}, u32[]{:S(2)}) copy-start(bf16[96,4096]{1,0:T(8,128)(2,1)} %v_ref.3) | copy-start | bytes 2359300
  12.7 18.5 %copy-start.2 = (bf16[96,4096]{1,0:T(8,128)(2,1)S(1)}, bf16[96,4096]{1,0:T(8,128)(2,1)}, u32[]{:S(2)}) copy-start(bf16[96,4096]{1,0:T(8,128)(2,1)} %v_ref.3) | copy-start | bytes 2359300
  12.7 18.5 %copy-start.3 = (bf16[96,4096]{1,0:T(8,128)(2,1)S(1)}, bf16[96,4096]{1,0:T(8,128)(2,1)}, u32[]{:S(2)}) copy-start(bf16[96,4096]{1,0:T(8,128)(2,1)} %q_ref.3) | copy-start | bytes 2359300
  26.3 8.1 %collective-permute-start = (bf16[3,136,128]{2,1,0:T(8,128)(2,1)S(1)}, bf16[3,136,128]{2,1,0:T(8,128)(2,1)S(1)}, u32[]{:S(2)}, u32[]{:S(2)}) collective-permute-start(bf16[3,136,128]{2,1,0:T(8,128)(2,1)S(1)} %get-tuple-element.18.after), channel_id=1, source_target_pairs={{0,4},{1,5},{2,6},{3,7},{4,0},{5,1},{6,2},{7,3},{8,12},{9,13},{10,... | collective-permute-start | bytes 313352 | tf_op jit(solution)/shard_map/ppermute | solution.py:313
  27.8 5.0 %collective-permute-start.1 = (bf16[1,136,128]{2,1,0:T(8,128)(2,1)S(1)}, bf16[1,136,128]{2,1,0:T(8,128)(2,1)S(1)}, u32[]{:S(2)}, u32[]{:S(2)}) collective-permute-start(bf16[1,136,128]{2,1,0:T(8,128)(2,1)S(1)} %get-tuple-element.22), channel_id=1, source_target_pairs={{0,4},{1,5},{2,6},{3,7},{8,12},{9,13},{10,14},{11,15},{16,20},{17,... | collective-permute-start | bytes 104456 | tf_op jit(solution)/shard_map/ppermute | solution.py:314
  32.4 14.3 %copy-start.4 = (f32[4096]{0:T(1024)S(1)}, f32[4096]{0:T(1024)}, u32[]{:S(2)}) copy-start(f32[4096]{0:T(1024)} %param.11) | copy-start | bytes 49156

commit v31 on v30

--- a/solution.py
+++ b/solution.py
@@ -22,7 +22,7 @@
     lane = lax.broadcasted_iota(jnp.int32, (1, LANES), 1)
     rates = []
     for head in (2 * pair, 2 * pair + 1):
-        at = lax.rem(lax.div(head, here) + members // 2 - 1, members)
+        at = lax.rem(lax.div(head, here) + members // 2 - 2, members)
         row = stored[pl.ds(at, 1), :]
         rates.append(
             jnp.sum(jnp.where(lane == lax.rem(head, here), row, 0.0), axis=1, keepdims=True)
@@ -32,7 +32,7 @@
 
 def own_ids(stored, tokens):
     members = stored.shape[0]
-    at = lax.rem(lax.axis_index("uly") + members // 2 - 1, members)
+    at = lax.rem(lax.axis_index("uly") + members // 2 - 2, members)
     row = stored[pl.ds(at, 1), :]
     fill = jnp.full((1, LANES - tokens), -1.0, jnp.float32)
     return jnp.concatenate([row[:, LANES - tokens :], fill], 1)
@@ -64,7 +64,7 @@
     for j in range(0, width // LANES, 2):
         weighted = []
         for head in range(2 * j, 2 * j + 4):
-            weight = jnp.exp(-rate_of(stored, (head + (members // 2 - 1) * here) % (members * here), here) * age)
+            weight = jnp.exp(-rate_of(stored, (head + (members // 2 - 2) * here) % (members * here), here) * age)
             keys = turned[head * HD : (head + 1) * HD, :].astype(jnp.float32)
             keys = keys.reshape(HD // 8, 8, LANES) * weight[None]
             weighted.append(keys.reshape(HD, LANES))
@@ -107,7 +107,7 @@
             stacked, turned[columns, :], preferred_element_type=jnp.float32
         )
         rates = [
-            rate_of(stored, (2 * j + one + (members // 2 - 1) * here) % (members * here), here)
+            rate_of(stored, (2 * j + one + (members // 2 - 2) * here) % (members * here), here)
             for one in (0, 1)
         ]
         weight = jnp.concatenate([jnp.exp(-rate * age) for rate in rates], 0)
@@ -162,7 +162,7 @@
     ctx, uly = lax.axis_index("ctx"), lax.axis_index("uly")
     later = uly >= chunks
     members = stored.shape[0]
-    at = lax.rem(uly + members - 1 + members // 2 - 1, members)
+    at = lax.rem(uly + members - 1 + members // 2 - 2, members)
     _, slice_before = split(early[jnp.maximum(ctx - 1, 0)], rows)
     first = jnp.where(ctx > 0, slice_before, -1.0)
     before[...] = jnp.where(uly > 0, stored[pl.ds(at, 1), LANES - 1 :], first)
@@ -270,7 +270,7 @@
     own = jnp.pad(decay_rate, (0, LANES - here)) + jnp.pad(
         doc_ids, (LANES - tokens, 0)
     ).astype(jnp.float32)
-    turned_round = [[(u + members // 2 + 1) % members for u in range(members)]]
+    turned_round = [[(u + members // 2 + 2) % members for u in range(members)]]
     stored = lax.all_to_all(
         jnp.broadcast_to(own[None, :], tile.shape),
         "uly", split_axis=0, concat_axis=0, axis_index_groups=turned_round, tiled=True,

time: 48.7 us -> 49.3 us (1.012)
    ppermute x1, starting transfers between devices: 1.54 us -> 2.42 us  [local(): early = lax.ppermute(early_ends, axes, swap)]
    ppermute x1, starting transfers between devices: 3.35 us -> 2.47 us  [local(): lax.ppermute(final_end, axes, [(low, high) for low, high in swap if low <...]
where the time goes in v31:
time: 49.3 us; the launch traced here: 48.9 us
  blocking collectives  25 us (51%)
  starting transfers between devices  13.2 us (27%)
  Pallas kernels  4.65 us (9%)
  local copies, waits for them, and re-layouts  2.88 us (6%)
  waiting for transfers between devices  2.4 us (5%)
  other arithmetic  0.75 us (2%)
    all_to_all x1, blocking collectives, local(): lax.all_to_all(moved, axes, split_axis=0, concat_axis=0, tiled=True, axis...  12.5 us
    all_to_all x1, blocking collectives, local(): lax.all_to_all(ends, axes, split_axis=0, concat_axis=0, tiled=True, axis_...  12.5 us
    all_to_all x1, starting transfers between devices, local(): lax.all_to_all(jnp.broadcast_to(own[None, :], tile.shape), 'uly', split_a...  8.27 us
    ppermute x1, starting transfers between devices, local(): lax.ppermute(final_end, axes, [(low, high) for low, high in swap if low <...  2.47 us
    ppermute x1, starting transfers between devices, local(): early = lax.ppermute(early_ends, axes, swap)  2.42 us
    unnamed x10, local copies, waits for them, and re-layouts  2.28 us
    pallas_call x1, Pallas kernels, local(): pl.pallas_call(functools.partial(norm_kernel, group), in_specs=[vmem] * 7...  1.67 us
    ppermute x1, waiting for transfers between devices, local(): early = lax.ppermute(early_ends, axes, swap)  1.57 us
  transfers between devices with their start and end apart: 3, of which 3 were waited for; matrix products, arithmetic and copies ran while one was open for 0% of the time, Pallas kernels for 3%

profile of v31, /device:TPU:0, one launch (start us, length us, event | category | flops | bytes accessed | tf_op | source)
XLA Modules:
  0.0 48.9 jit_solution(4233126020229520833)
XLA Ops:
  0.0 0.7 %convert_add_fusion = f32[128]{0:T(128)S(1)} fusion(s32[96]{0:T(128)} %param.9, f32[8]{0:T(128)} %param.10), kind=kLoop, calls=%fused_computation | loop fusion | flops 256 | bytes 928 | tf_op jit(solution)/shard_map/add | solution.py:270
  0.7 0.6 %broadcast_in_dim.4 = f32[8,1,128]{2,1,0:T(1,128)} broadcast(f32[128]{0:T(128)S(1)} %convert_add_fusion), dimensions={2} | broadcast | bytes 4608 | tf_op jit(solution)/shard_map/broadcast_in_dim | solution.py:275
  1.3 8.3 %all-to-all-start = ((f32[8,1,128]{2,1,0:T(1,128)}), f32[8,1,128]{2,1,0:T(1,128)S(1)}, u32[]{:S(2)}, u32[]{:S(2)}) async-start(f32[8,1,128]{2,1,0:T(1,128)} %broadcast_in_dim.4), calls=%async_computation | async-start | bytes 8192 | tf_op jit(solution)/shard_map/all_to_all | solution.py:274
  9.6 0.0 copy-start
  9.6 1.1 %copy-done = bf16[96,4096]{1,0:T(8,128)(2,1)S(1)} copy-done((bf16[96,4096]{1,0:T(8,128)(2,1)S(1)}, bf16[96,4096]{1,0:T(8,128)(2,1)}, u32[]{:S(2)}) %copy-start) | copy-done | bytes 786456
  10.7 0.0 copy-start.1
  10.7 1.1 %copy-done.1 = bf16[96,4096]{1,0:T(8,128)(2,1)S(1)} copy-done((bf16[96,4096]{1,0:T(8,128)(2,1)S(1)}, bf16[96,4096]{1,0:T(8,128)(2,1)}, u32[]{:S(2)}) %copy-start.1) | copy-done | bytes 786456
  11.9 0.4 turn.1
  12.2 0.5 %all-to-all-done = f32[8,1,128]{2,1,0:T(1,128)S(1)} async-done(((f32[8,1,128]{2,1,0:T(1,128)}), f32[8,1,128]{2,1,0:T(1,128)S(1)}, u32[]{:S(2)}, u32[]{:S(2)}) %all-to-all-start) | async-done | bytes 4128 | tf_op jit(solution)/shard_map/all_to_all | solution.py:274
  12.8 0.9 %ends.1 = bf16[16,136,128]{2,1,0:T(8,128)(2,1)S(1)} custom-call(f32[8,128]{1,0:T(8,128)S(1)} %bitcast.4, bf16[4096,128]{1,0:T(8,128)(2,1)S(1)} %get-tuple-element.16.turned, bf16[128,4096]{1,0:T(8,128)(2,1)S(1)} %get-tuple-element.17.v_ref), custom_call_target="tpu_custom_call" | custom-call | tf_op jit(solution)/shard_map/ends/pallas_call | solution.py:287
  13.7 12.5 %all_to_all.18.in_ref = bf16[16,136,128]{2,1,0:T(8,128)(2,1)S(1)} all-to-all(bf16[16,136,128]{2,1,0:T(8,128)(2,1)S(1)} %ends.1), channel_id=1, replica_groups={{27,26,25,24,19,18,17,16,11,10,9,8,3,2,1,0},{31,30,29,28,23,22,21,20,15..., dimensions={0} | all-to-all | bytes 1114112 | tf_op jit(solution)/shard_map/all_to_all | solution.py:295
  26.1 0.2 half.1
  26.4 2.4 %collective-permute-start = (bf16[3,136,128]{2,1,0:T(8,128)(2,1)S(1)}, bf16[3,136,128]{2,1,0:T(8,128)(2,1)S(1)}, u32[]{:S(2)}, u32[]{:S(2)}) collective-permute-start(bf16[3,136,128]{2,1,0:T(8,128)(2,1)S(1)} %get-tuple-element.18.after), channel_id=1, source_target_pairs={{0,4},{1,5},{2,6},{3,7},{4,0},{5,1},{6,2},{7,3},{8,12},{9,13},{10,... | collective-permute-start | bytes 313352 | tf_op jit(solution)/shard_map/ppermute | solution.py:313
  28.8 2.5 %collective-permute-start.1 = (bf16[1,136,128]{2,1,0:T(8,128)(2,1)S(1)}, bf16[1,136,128]{2,1,0:T(8,128)(2,1)S(1)}, u32[]{:S(2)}, u32[]{:S(2)}) collective-permute-start(bf16[1,136,128]{2,1,0:T(8,128)(2,1)S(1)} %get-tuple-element.22), channel_id=1, source_target_pairs={{0,4},{1,5},{2,6},{3,7},{8,12},{9,13},{10,14},{11,15},{16,20},{17,... | collective-permute-start | bytes 104456 | tf_op jit(solution)/shard_map/ppermute | solution.py:314
  31.2 0.0 copy-done.2
  31.3 0.0 copy-done.3
  31.3 1.2 %inner.1 = (f32[96,4096]{1,0:T(8,128)S(1)}, f32[1,4096]{1,0:T(1,128)S(1)}, f32[96,128]{1,0:T(8,128)S(1)}) custom-call(f32[8,128]{1,0:T(8,128)S(1)} %bitcast.6, bf16[96,4096]{1,0:T(8,128)(2,1)S(1)} %copy-done.3, bf16[4096,128]{1,0:T(8,128)(2,1)S(1)} %get-tuple-element.16.turned, bf16[96,4096]{1,0:T(8,128)(2,1)S(1)} %copy-done.2, ...), custom_call_target="tpu_custom_call" | custom-call | flops 8000000000 | bytes 4000000 | tf_op jit(solution)/shard_map/inner/pallas_call | solution.py:315
  32.5 0.0 copy-start.4
  32.5 0.3 collective-permute-done.1.final
  32.8 1.6 %collective-permute-done.early = bf16[3,136,128]{2,1,0:T(8,128)(2,1)S(1)} collective-permute-done((bf16[3,136,128]{2,1,0:T(8,128)(2,1)S(1)}, bf16[3,136,128]{2,1,0:T(8,128)(2,1)S(1)}, u32[]{:S(2)}, u32[]{:S(2)}) %collective-permute-start) | collective-permute-done | bytes 104480 | tf_op jit(solution)/shard_map/ppermute | solution.py:313
  34.4 0.3 scan.1
  34.7 12.5 %all_to_all.19 = bf16[16,128,128]{2,1,0:T(8,128)(2,1)S(1)} all-to-all(bf16[16,128,128]{2,1,0:T(8,128)(2,1)S(1)} %get-tuple-element.25), channel_id=1, replica_groups={{27,26,25,24,19,18,17,16,11,10,9,8,3,2,1,0},{31,30,29,28,23,22,21,20,15..., dimensions={0} | all-to-all | bytes 1048576 | tf_op jit(solution)/shard_map/all_to_all | solution.py:341
  47.2 0.0 copy-done.4
  47.2 1.7 %norm.1 = bf16[96,4096]{1,0:T(8,128)(2,1)} custom-call(f32[96,128]{1,0:T(8,128)S(1)} %get-tuple-element.19.idcol, f32[1,128]{1,0:T(1,128)S(1)} %get-tuple-element.24.before, f32[1,4096]{1,0:T(1,128)S(1)} %get-tuple-element.23.after.rates, bf16[96,4096]{1,0:T(8,128)(2,1)S(1)} %copy-done.3, bf16[2048,128]{1,0:T(8,128)(2,1)S(1)} %bitcast.3, ...), custom_call_target="tpu_custom_call" | custom-call | tf_op jit(solution)/shard_map/norm/pallas_call | solution.py:346
  (2 shorter events, 0.0 us)
Async XLA Ops:
  1.3 11.4 %all-to-all-start = ((f32[8,1,128]{2,1,0:T(1,128)}), f32[8,1,128]{2,1,0:T(1,128)S(1)}, u32[]{:S(2)}, u32[]{:S(2)}) async-start(f32[8,1,128]{2,1,0:T(1,128)} %broadcast_in_dim.4), calls=%async_computation | async-start | bytes 8192 | tf_op jit(solution)/shard_map/all_to_all | solution.py:274
  9.6 1.1 %copy-start = (bf16[96,4096]{1,0:T(8,128)(2,1)S(1)}, bf16[96,4096]{1,0:T(8,128)(2,1)}, u32[]{:S(2)}) copy-start(bf16[96,4096]{1,0:T(8,128)(2,1)} %k_ref.1) | copy-start | bytes 2359300
  10.7 1.1 %copy-start.1 = (bf16[96,4096]{1,0:T(8,128)(2,1)S(1)}, bf16[96,4096]{1,0:T(8,128)(2,1)}, u32[]{:S(2)}) copy-start(bf16[96,4096]{1,0:T(8,128)(2,1)} %v_ref.3) | copy-start | bytes 2359300
  12.8 18.5 %copy-start.2 = (bf16[96,4096]{1,0:T(8,128)(2,1)S(1)}, bf16[96,4096]{1,0:T(8,128)(2,1)}, u32[]{:S(2)}) copy-start(bf16[96,4096]{1,0:T(8,128)(2,1)} %v_ref.3) | copy-start | bytes 2359300
  12.8 18.5 %copy-start.3 = (bf16[96,4096]{1,0:T(8,128)(2,1)S(1)}, bf16[96,4096]{1,0:T(8,128)(2,1)}, u32[]{:S(2)}) copy-start(bf16[96,4096]{1,0:T(8,128)(2,1)} %q_ref.3) | copy-start | bytes 2359300
  26.4 8.1 %collective-permute-start = (bf16[3,136,128]{2,1,0:T(8,128)(2,1)S(1)}, bf16[3,136,128]{2,1,0:T(8,128)(2,1)S(1)}, u32[]{:S(2)}, u32[]{:S(2)}) collective-permute-start(bf16[3,136,128]{2,1,0:T(8,128)(2,1)S(1)} %get-tuple-element.18.after), channel_id=1, source_target_pairs={{0,4},{1,5},{2,6},{3,7},{4,0},{5,1},{6,2},{7,3},{8,12},{9,13},{10,... | collective-permute-start | bytes 313352 | tf_op jit(solution)/shard_map/ppermute | solution.py:313
  28.8 4.1 %collective-permute-start.1 = (bf16[1,136,128]{2,1,0:T(8,128)(2,1)S(1)}, bf16[1,136,128]{2,1,0:T(8,128)(2,1)S(1)}, u32[]{:S(2)}, u32[]{:S(2)}) collective-permute-start(bf16[1,136,128]{2,1,0:T(8,128)(2,1)S(1)} %get-tuple-element.22), channel_id=1, source_target_pairs={{0,4},{1,5},{2,6},{3,7},{8,12},{9,13},{10,14},{11,15},{16,20},{17,... | collective-permute-start | bytes 104456 | tf_op jit(solution)/shard_map/ppermute | solution.py:314
  32.5 14.7 %copy-start.4 = (f32[4096]{0:T(1024)S(1)}, f32[4096]{0:T(1024)}, u32[]{:S(2)}) copy-start(f32[4096]{0:T(1024)} %param.11) | copy-start | bytes 49156

commit v32 on v30

--- a/solution.py
+++ b/solution.py
@@ -49,7 +49,7 @@
         turned[columns, :] = jnp.transpose(block).astype(turned.dtype)
 
 
-def ends_kernel(here, tokens, stored, turned, v_ref, out_ref):
+def ends_kernel(here, tokens, chunks, stored, turned, v_ref, out_ref):
     width = v_ref.shape[1]
     members = stored.shape[0]
     group, rows = out_ref.shape[0], out_ref.shape[1] - MARK
@@ -83,7 +83,7 @@
             size = min(rows, HD)
             for at in range(0, HD, size):
                 owner, start = divmod((j + one) * HD + at, rows)
-                out_ref[group - 1 - owner, start : start + size, :] = state[at : at + size].astype(
+                out_ref[(2 * group - 1 - owner - chunks) % group, start : start + size, :] = state[at : at + size].astype(
                     jnp.bfloat16
                 )
 
@@ -140,13 +140,13 @@
     def slice_end(c, ref, at):
         def step(j, carry):
             state, last = carry
-            fresh, own = split(in_ref[newest - c * chunks - j], rows)
+            fresh, own = split(in_ref[lax.rem(2 * newest + 1 - chunks - (c * chunks + j), newest + 1)], rows)
             return fresh + jnp.where(own == last, one[...], 0.0) * state, own
 
-        begin = split(in_ref[newest - c * chunks], rows)
+        begin = split(in_ref[lax.rem(2 * newest + 1 - chunks - (c * chunks), newest + 1)], rows)
         state, _ = lax.fori_loop(1, chunks, step, begin, unroll=few(chunks - 1))
         ref[at, :rows, :] = state.astype(ref.dtype)
-        ref[at, rows:, :] = in_ref[newest - c * chunks - chunks + 1][rows:]
+        ref[at, rows:, :] = in_ref[lax.rem(2 * newest + 1 - chunks - (c * chunks + chunks - 1), newest + 1)][rows:]
 
     def early(c, _):
         slice_end(c, early_ref, c)
@@ -178,7 +178,7 @@
             state, last = carry
             at = c * chunks + j
             out_ref[newest - at] = state.astype(out_ref.dtype)
-            fresh, own = split(in_ref[newest - at], rows)
+            fresh, own = split(in_ref[lax.rem(2 * newest + 1 - chunks - (at), newest + 1)], rows)
             return fresh + jnp.where(own == last, one[...], 0.0) * state, own
 
         return lax.fori_loop(0, chunks, step, carry, unroll=few(chunks))
@@ -285,7 +285,7 @@
         name="turn",
     )(keys, values)
     ends = pl.pallas_call(
-        functools.partial(ends_kernel, here, tokens),
+        functools.partial(ends_kernel, here, tokens, chunks),
         in_specs=[vmem] * 3,
         out_specs=vmem,
         out_shape=shape((group, rows + MARK, LANES), jnp.bfloat16),
@@ -295,7 +295,7 @@
     pieces = lax.all_to_all(
         ends,
         axes, split_axis=0, concat_axis=0, tiled=True,
-        axis_index_groups=[members_of[::-1] for members_of in groups],
+        axis_index_groups=[members_of[::-1][chunks:] + members_of[::-1][:chunks] for members_of in groups],
     )
     early_ends, final_end, one, half = pl.pallas_call(
         functools.partial(half_kernel, here, tokens, chunks),

time: 48.7 us -> 49.4 us (1.014)
  blocking collectives: 24.6 us -> 25.2 us
    ppermute x1, starting transfers between devices: 3.35 us -> 2.55 us  [local(): lax.ppermute(final_end, axes, [(low, high) for low, high in swap if low <...]
    ppermute x1, starting transfers between devices: 1.54 us -> 2.33 us  [local(): early = lax.ppermute(early_ends, axes, swap)]
where the time goes in v32:
time: 49.4 us; the launch traced here: 49 us
  blocking collectives  25.2 us (51%)
  starting transfers between devices  13.1 us (27%)
  Pallas kernels  4.66 us (9%)
  local copies, waits for them, and re-layouts  2.88 us (6%)
  waiting for transfers between devices  2.4 us (5%)
  other arithmetic  0.75 us (2%)
    all_to_all x1, blocking collectives, local(): lax.all_to_all(ends, axes, split_axis=0, concat_axis=0, tiled=True, axis_...  12.8 us
    all_to_all x1, blocking collectives, local(): lax.all_to_all(moved, axes, split_axis=0, concat_axis=0, tiled=True, axis...  12.5 us
    all_to_all x1, starting transfers between devices, local(): lax.all_to_all(jnp.broadcast_to(own[None, :], tile.shape), 'uly', split_a...  8.19 us
    ppermute x1, starting transfers between devices, local(): lax.ppermute(final_end, axes, [(low, high) for low, high in swap if low <...  2.55 us
    ppermute x1, starting transfers between devices, local(): early = lax.ppermute(early_ends, axes, swap)  2.33 us
    unnamed x10, local copies, waits for them, and re-layouts  2.28 us
    pallas_call x1, Pallas kernels, local(): pl.pallas_call(functools.partial(norm_kernel, group), in_specs=[vmem] * 7...  1.67 us
    ppermute x1, waiting for transfers between devices, local(): early = lax.ppermute(early_ends, axes, swap)  1.58 us
  transfers between devices with their start and end apart: 3, of which 3 were waited for; matrix products, arithmetic and copies ran while one was open for 0% of the time, Pallas kernels for 3%

profile of v32, /device:TPU:0, one launch (start us, length us, event | category | flops | bytes accessed | tf_op | source)
XLA Modules:
  0.0 49.0 jit_solution(9693122711993208589)
XLA Ops:
  0.0 0.7 %convert_add_fusion = f32[128]{0:T(128)S(1)} fusion(s32[96]{0:T(128)} %param.9, f32[8]{0:T(128)} %param.10), kind=kLoop, calls=%fused_computation | loop fusion | flops 256 | bytes 928 | tf_op jit(solution)/shard_map/add | solution.py:270
  0.7 0.6 %broadcast_in_dim.4 = f32[8,1,128]{2,1,0:T(1,128)} broadcast(f32[128]{0:T(128)S(1)} %convert_add_fusion), dimensions={2} | broadcast | bytes 4608 | tf_op jit(solution)/shard_map/broadcast_in_dim | solution.py:275
  1.3 8.2 %all-to-all-start = ((f32[8,1,128]{2,1,0:T(1,128)}), f32[8,1,128]{2,1,0:T(1,128)S(1)}, u32[]{:S(2)}, u32[]{:S(2)}) async-start(f32[8,1,128]{2,1,0:T(1,128)} %broadcast_in_dim.4), calls=%async_computation | async-start | bytes 8192 | tf_op jit(solution)/shard_map/all_to_all | solution.py:274
  9.5 0.0 copy-start
  9.5 1.1 %copy-done = bf16[96,4096]{1,0:T(8,128)(2,1)S(1)} copy-done((bf16[96,4096]{1,0:T(8,128)(2,1)S(1)}, bf16[96,4096]{1,0:T(8,128)(2,1)}, u32[]{:S(2)}) %copy-start) | copy-done | bytes 786456
  10.7 0.0 copy-start.1
  10.7 1.1 %copy-done.1 = bf16[96,4096]{1,0:T(8,128)(2,1)S(1)} copy-done((bf16[96,4096]{1,0:T(8,128)(2,1)S(1)}, bf16[96,4096]{1,0:T(8,128)(2,1)}, u32[]{:S(2)}) %copy-start.1) | copy-done | bytes 786456
  11.8 0.4 turn.1
  12.2 0.5 all-to-all-done
  12.7 0.9 %ends.1 = bf16[16,136,128]{2,1,0:T(8,128)(2,1)S(1)} custom-call(f32[8,128]{1,0:T(8,128)S(1)} %bitcast.4, bf16[4096,128]{1,0:T(8,128)(2,1)S(1)} %get-tuple-element.16.turned, bf16[128,4096]{1,0:T(8,128)(2,1)S(1)} %get-tuple-element.17.v_ref), custom_call_target="tpu_custom_call" | custom-call | tf_op jit(solution)/shard_map/ends/pallas_call | solution.py:287
  13.6 12.8 %all_to_all.18.in_ref = bf16[16,136,128]{2,1,0:T(8,128)(2,1)S(1)} all-to-all(bf16[16,136,128]{2,1,0:T(8,128)(2,1)S(1)} %ends.1), channel_id=1, replica_groups={{19,18,17,16,11,10,9,8,3,2,1,0,27,26,25,24},{23,22,21,20,15,14,13,12,7,..., dimensions={0} | all-to-all | bytes 1114112 | tf_op jit(solution)/shard_map/all_to_all | solution.py:295
  26.3 0.2 half.1
  26.5 2.3 %collective-permute-start = (bf16[3,136,128]{2,1,0:T(8,128)(2,1)S(1)}, bf16[3,136,128]{2,1,0:T(8,128)(2,1)S(1)}, u32[]{:S(2)}, u32[]{:S(2)}) collective-permute-start(bf16[3,136,128]{2,1,0:T(8,128)(2,1)S(1)} %get-tuple-element.18.after), channel_id=1, source_target_pairs={{0,4},{1,5},{2,6},{3,7},{4,0},{5,1},{6,2},{7,3},{8,12},{9,13},{10,... | collective-permute-start | bytes 313352 | tf_op jit(solution)/shard_map/ppermute | solution.py:313
  28.9 2.6 %collective-permute-start.1 = (bf16[1,136,128]{2,1,0:T(8,128)(2,1)S(1)}, bf16[1,136,128]{2,1,0:T(8,128)(2,1)S(1)}, u32[]{:S(2)}, u32[]{:S(2)}) collective-permute-start(bf16[1,136,128]{2,1,0:T(8,128)(2,1)S(1)} %get-tuple-element.22), channel_id=1, source_target_pairs={{0,4},{1,5},{2,6},{3,7},{8,12},{9,13},{10,14},{11,15},{16,20},{17,... | collective-permute-start | bytes 104456 | tf_op jit(solution)/shard_map/ppermute | solution.py:314
  31.4 0.0 copy-done.2
  31.4 0.0 copy-done.3
  31.4 1.2 %inner.1 = (f32[96,4096]{1,0:T(8,128)S(1)}, f32[1,4096]{1,0:T(1,128)S(1)}, f32[96,128]{1,0:T(8,128)S(1)}) custom-call(f32[8,128]{1,0:T(8,128)S(1)} %bitcast.6, bf16[96,4096]{1,0:T(8,128)(2,1)S(1)} %copy-done.3, bf16[4096,128]{1,0:T(8,128)(2,1)S(1)} %get-tuple-element.16.turned, bf16[96,4096]{1,0:T(8,128)(2,1)S(1)} %copy-done.2, ...), custom_call_target="tpu_custom_call" | custom-call | flops 8000000000 | bytes 4000000 | tf_op jit(solution)/shard_map/inner/pallas_call | solution.py:315
  32.7 0.0 copy-start.4
  32.7 0.3 collective-permute-done.1.final
  33.0 1.6 %collective-permute-done.early = bf16[3,136,128]{2,1,0:T(8,128)(2,1)S(1)} collective-permute-done((bf16[3,136,128]{2,1,0:T(8,128)(2,1)S(1)}, bf16[3,136,128]{2,1,0:T(8,128)(2,1)S(1)}, u32[]{:S(2)}, u32[]{:S(2)}) %collective-permute-start) | collective-permute-done | bytes 104480 | tf_op jit(solution)/shard_map/ppermute | solution.py:313
  34.6 0.3 scan.1
  34.9 12.5 %all_to_all.19 = bf16[16,128,128]{2,1,0:T(8,128)(2,1)S(1)} all-to-all(bf16[16,128,128]{2,1,0:T(8,128)(2,1)S(1)} %get-tuple-element.25), channel_id=1, replica_groups={{27,26,25,24,19,18,17,16,11,10,9,8,3,2,1,0},{31,30,29,28,23,22,21,20,15..., dimensions={0} | all-to-all | bytes 1048576 | tf_op jit(solution)/shard_map/all_to_all | solution.py:341
  47.4 0.0 copy-done.4
  47.4 1.7 %norm.1 = bf16[96,4096]{1,0:T(8,128)(2,1)} custom-call(f32[96,128]{1,0:T(8,128)S(1)} %get-tuple-element.19.idcol, f32[1,128]{1,0:T(1,128)S(1)} %get-tuple-element.24.before, f32[1,4096]{1,0:T(1,128)S(1)} %get-tuple-element.23.after.rates, bf16[96,4096]{1,0:T(8,128)(2,1)S(1)} %copy-done.3, bf16[2048,128]{1,0:T(8,128)(2,1)S(1)} %bitcast.3, ...), custom_call_target="tpu_custom_call" | custom-call | tf_op jit(solution)/shard_map/norm/pallas_call | solution.py:346
  (2 shorter events, 0.0 us)
Async XLA Ops:
  1.3 11.3 %all-to-all-start = ((f32[8,1,128]{2,1,0:T(1,128)}), f32[8,1,128]{2,1,0:T(1,128)S(1)}, u32[]{:S(2)}, u32[]{:S(2)}) async-start(f32[8,1,128]{2,1,0:T(1,128)} %broadcast_in_dim.4), calls=%async_computation | async-start | bytes 8192 | tf_op jit(solution)/shard_map/all_to_all | solution.py:274
  9.5 1.1 %copy-start = (bf16[96,4096]{1,0:T(8,128)(2,1)S(1)}, bf16[96,4096]{1,0:T(8,128)(2,1)}, u32[]{:S(2)}) copy-start(bf16[96,4096]{1,0:T(8,128)(2,1)} %k_ref.1) | copy-start | bytes 2359300
  10.7 1.1 %copy-start.1 = (bf16[96,4096]{1,0:T(8,128)(2,1)S(1)}, bf16[96,4096]{1,0:T(8,128)(2,1)}, u32[]{:S(2)}) copy-start(bf16[96,4096]{1,0:T(8,128)(2,1)} %v_ref.3) | copy-start | bytes 2359300
  12.7 18.8 %copy-start.2 = (bf16[96,4096]{1,0:T(8,128)(2,1)S(1)}, bf16[96,4096]{1,0:T(8,128)(2,1)}, u32[]{:S(2)}) copy-start(bf16[96,4096]{1,0:T(8,128)(2,1)} %v_ref.3) | copy-start | bytes 2359300
  12.7 18.8 %copy-start.3 = (bf16[96,4096]{1,0:T(8,128)(2,1)S(1)}, bf16[96,4096]{1,0:T(8,128)(2,1)}, u32[]{:S(2)}) copy-start(bf16[96,4096]{1,0:T(8,128)(2,1)} %q_ref.3) | copy-start | bytes 2359300
  26.5 8.1 %collective-permute-start = (bf16[3,136,128]{2,1,0:T(8,128)(2,1)S(1)}, bf16[3,136,128]{2,1,0:T(8,128)(2,1)S(1)}, u32[]{:S(2)}, u32[]{:S(2)}) collective-permute-start(bf16[3,136,128]{2,1,0:T(8,128)(2,1)S(1)} %get-tuple-element.18.after), channel_id=1, source_target_pairs={{0,4},{1,5},{2,6},{3,7},{4,0},{5,1},{6,2},{7,3},{8,12},{9,13},{10,... | collective-permute-start | bytes 313352 | tf_op jit(solution)/shard_map/ppermute | solution.py:313
  28.9 4.2 %collective-permute-start.1 = (bf16[1,136,128]{2,1,0:T(8,128)(2,1)S(1)}, bf16[1,136,128]{2,1,0:T(8,128)(2,1)S(1)}, u32[]{:S(2)}, u32[]{:S(2)}) collective-permute-start(bf16[1,136,128]{2,1,0:T(8,128)(2,1)S(1)} %get-tuple-element.22), channel_id=1, source_target_pairs={{0,4},{1,5},{2,6},{3,7},{8,12},{9,13},{10,14},{11,15},{16,20},{17,... | collective-permute-start | bytes 104456 | tf_op jit(solution)/shard_map/ppermute | solution.py:314
  32.7 14.7 %copy-start.4 = (f32[4096]{0:T(1024)S(1)}, f32[4096]{0:T(1024)}, u32[]{:S(2)}) copy-start(f32[4096]{0:T(1024)} %param.11) | copy-start | bytes 49156

commit v33 on v30

--- a/solution.py
+++ b/solution.py
@@ -177,7 +177,7 @@
         def step(j, carry):
             state, last = carry
             at = c * chunks + j
-            out_ref[newest - at] = state.astype(out_ref.dtype)
+            out_ref[lax.rem(2 * newest + 1 - chunks - at, newest + 1)] = state.astype(out_ref.dtype)
             fresh, own = split(in_ref[newest - at], rows)
             return fresh + jnp.where(own == last, one[...], 0.0) * state, own
 
@@ -192,7 +192,7 @@
     over_own(over_other(carry, final[0], later), slices - 1)
 
 
-def norm_kernel(group, idcol, before, rates, q_ref, s_ref, inner_ref, gain, out_ref, raw, done, sems):
+def norm_kernel(group, chunks, idcol, before, rates, q_ref, s_ref, inner_ref, gain, out_ref, raw, done, sems):
     tokens, width = q_ref.shape
     lane = lax.broadcasted_iota(jnp.int32, (HD, LANES), 1)
     place = lax.broadcasted_iota(jnp.int32, (tokens, LANES), 0)
@@ -207,7 +207,7 @@
             state = []
             for at in range((j + one) * HD, (j + one + 1) * HD, size):
                 owner, start = divmod(at, rows)
-                start += (group - 1 - owner) * rows
+                start += (2 * group - 1 - owner - chunks) % group * rows
                 state.append(s_ref[start : start + size, :])
             if len(state) > 1:
                 state = [jnp.concatenate([s.astype(jnp.float32) for s in state], 0).astype(zero.dtype)]
@@ -341,10 +341,10 @@
     states = lax.all_to_all(
         moved,
         axes, split_axis=0, concat_axis=0, tiled=True,
-        axis_index_groups=[members_of[::-1] for members_of in groups],
+        axis_index_groups=[members_of[::-1][chunks:] + members_of[::-1][:chunks] for members_of in groups],
     )
     return pl.pallas_call(
-        functools.partial(norm_kernel, group),
+        functools.partial(norm_kernel, group, chunks),
         in_specs=[vmem] * 7,
         out_specs=pl.BlockSpec(memory_space=pl.ANY),
         out_shape=shape((tokens, width), jnp.bfloat16),

time: 48.7 us -> 49 us (level)
  no operation moved by 1% of the time
where the time goes in v33:
time: 49 us; the launch traced here: 48.7 us
  blocking collectives  24.9 us (51%)
  starting transfers between devices  13.1 us (27%)
  Pallas kernels  4.65 us (9%)
  local copies, waits for them, and re-layouts  2.88 us (6%)
  waiting for transfers between devices  2.39 us (5%)
  other arithmetic  0.75 us (2%)
    all_to_all x1, blocking collectives, local(): lax.all_to_all(ends, axes, split_axis=0, concat_axis=0, tiled=True, axis_...  12.5 us
    all_to_all x1, blocking collectives, local(): lax.all_to_all(moved, axes, split_axis=0, concat_axis=0, tiled=True, axis...  12.4 us
    all_to_all x1, starting transfers between devices, local(): lax.all_to_all(jnp.broadcast_to(own[None, :], tile.shape), 'uly', split_a...  8.19 us
    ppermute x1, starting transfers between devices, local(): lax.ppermute(final_end, axes, [(low, high) for low, high in swap if low <...  3.35 us
    unnamed x10, local copies, waits for them, and re-layouts  2.28 us
    pallas_call x1, Pallas kernels, local(): pl.pallas_call(functools.partial(norm_kernel, group, chunks), in_specs=[v...  1.67 us
    ppermute x1, waiting for transfers between devices, local(): early = lax.ppermute(early_ends, axes, swap)  1.57 us
    ppermute x1, starting transfers between devices, local(): early = lax.ppermute(early_ends, axes, swap)  1.54 us
  transfers between devices with their start and end apart: 3, of which 3 were waited for; matrix products, arithmetic and copies ran while one was open for 0% of the time, Pallas kernels for 3%

profile of v33, /device:TPU:0, one launch (start us, length us, event | category | flops | bytes accessed | tf_op | source)
XLA Modules:
  0.0 48.7 jit_solution(16071288875319639620)
XLA Ops:
  0.0 0.7 %convert_add_fusion = f32[128]{0:T(128)S(1)} fusion(s32[96]{0:T(128)} %param.9, f32[8]{0:T(128)} %param.10), kind=kLoop, calls=%fused_computation | loop fusion | flops 256 | bytes 928 | tf_op jit(solution)/shard_map/add | solution.py:270
  0.7 0.6 %broadcast_in_dim.4 = f32[8,1,128]{2,1,0:T(1,128)} broadcast(f32[128]{0:T(128)S(1)} %convert_add_fusion), dimensions={2} | broadcast | bytes 4608 | tf_op jit(solution)/shard_map/broadcast_in_dim | solution.py:275
  1.3 8.2 %all-to-all-start = ((f32[8,1,128]{2,1,0:T(1,128)}), f32[8,1,128]{2,1,0:T(1,128)S(1)}, u32[]{:S(2)}, u32[]{:S(2)}) async-start(f32[8,1,128]{2,1,0:T(1,128)} %broadcast_in_dim.4), calls=%async_computation | async-start | bytes 8192 | tf_op jit(solution)/shard_map/all_to_all | solution.py:274
  9.5 0.0 copy-start
  9.5 1.1 %copy-done = bf16[96,4096]{1,0:T(8,128)(2,1)S(1)} copy-done((bf16[96,4096]{1,0:T(8,128)(2,1)S(1)}, bf16[96,4096]{1,0:T(8,128)(2,1)}, u32[]{:S(2)}) %copy-start) | copy-done | bytes 786456
  10.7 0.0 copy-start.1
  10.7 1.1 %copy-done.1 = bf16[96,4096]{1,0:T(8,128)(2,1)S(1)} copy-done((bf16[96,4096]{1,0:T(8,128)(2,1)S(1)}, bf16[96,4096]{1,0:T(8,128)(2,1)}, u32[]{:S(2)}) %copy-start.1) | copy-done | bytes 786456
  11.8 0.4 turn.1
  12.2 0.5 %all-to-all-done = f32[8,1,128]{2,1,0:T(1,128)S(1)} async-done(((f32[8,1,128]{2,1,0:T(1,128)}), f32[8,1,128]{2,1,0:T(1,128)S(1)}, u32[]{:S(2)}, u32[]{:S(2)}) %all-to-all-start) | async-done | bytes 4128 | tf_op jit(solution)/shard_map/all_to_all | solution.py:274
  12.7 0.9 %ends.1 = bf16[16,136,128]{2,1,0:T(8,128)(2,1)S(1)} custom-call(f32[8,128]{1,0:T(8,128)S(1)} %bitcast.4, bf16[4096,128]{1,0:T(8,128)(2,1)S(1)} %get-tuple-element.16.turned, bf16[128,4096]{1,0:T(8,128)(2,1)S(1)} %get-tuple-element.17.v_ref), custom_call_target="tpu_custom_call" | custom-call | tf_op jit(solution)/shard_map/ends/pallas_call | solution.py:287
  13.6 12.5 %all_to_all.18.in_ref = bf16[16,136,128]{2,1,0:T(8,128)(2,1)S(1)} all-to-all(bf16[16,136,128]{2,1,0:T(8,128)(2,1)S(1)} %ends.1), channel_id=1, replica_groups={{27,26,25,24,19,18,17,16,11,10,9,8,3,2,1,0},{31,30,29,28,23,22,21,20,15..., dimensions={0} | all-to-all | bytes 1114112 | tf_op jit(solution)/shard_map/all_to_all | solution.py:295
  26.0 0.2 half.1
  26.3 1.5 %collective-permute-start = (bf16[3,136,128]{2,1,0:T(8,128)(2,1)S(1)}, bf16[3,136,128]{2,1,0:T(8,128)(2,1)S(1)}, u32[]{:S(2)}, u32[]{:S(2)}) collective-permute-start(bf16[3,136,128]{2,1,0:T(8,128)(2,1)S(1)} %get-tuple-element.18.after), channel_id=1, source_target_pairs={{0,4},{1,5},{2,6},{3,7},{4,0},{5,1},{6,2},{7,3},{8,12},{9,13},{10,... | collective-permute-start | bytes 313352 | tf_op jit(solution)/shard_map/ppermute | solution.py:313
  27.8 3.3 %collective-permute-start.1 = (bf16[1,136,128]{2,1,0:T(8,128)(2,1)S(1)}, bf16[1,136,128]{2,1,0:T(8,128)(2,1)S(1)}, u32[]{:S(2)}, u32[]{:S(2)}) collective-permute-start(bf16[1,136,128]{2,1,0:T(8,128)(2,1)S(1)} %get-tuple-element.22), channel_id=1, source_target_pairs={{0,4},{1,5},{2,6},{3,7},{8,12},{9,13},{10,14},{11,15},{16,20},{17,... | collective-permute-start | bytes 104456 | tf_op jit(solution)/shard_map/ppermute | solution.py:314
  31.1 0.0 copy-done.2
  31.2 0.0 copy-done.3
  31.2 1.2 %inner.1 = (f32[96,4096]{1,0:T(8,128)S(1)}, f32[1,4096]{1,0:T(1,128)S(1)}, f32[96,128]{1,0:T(8,128)S(1)}) custom-call(f32[8,128]{1,0:T(8,128)S(1)} %bitcast.6, bf16[96,4096]{1,0:T(8,128)(2,1)S(1)} %copy-done.3, bf16[4096,128]{1,0:T(8,128)(2,1)S(1)} %get-tuple-element.16.turned, bf16[96,4096]{1,0:T(8,128)(2,1)S(1)} %copy-done.2, ...), custom_call_target="tpu_custom_call" | custom-call | flops 8000000000 | bytes 4000000 | tf_op jit(solution)/shard_map/inner/pallas_call | solution.py:315
  32.4 0.0 copy-start.4
  32.4 0.3 collective-permute-done.1.final
  32.7 1.6 %collective-permute-done.early = bf16[3,136,128]{2,1,0:T(8,128)(2,1)S(1)} collective-permute-done((bf16[3,136,128]{2,1,0:T(8,128)(2,1)S(1)}, bf16[3,136,128]{2,1,0:T(8,128)(2,1)S(1)}, u32[]{:S(2)}, u32[]{:S(2)}) %collective-permute-start) | collective-permute-done | bytes 104480 | tf_op jit(solution)/shard_map/ppermute | solution.py:313
  34.3 0.3 scan.1
  34.6 12.4 %all_to_all.19 = bf16[16,128,128]{2,1,0:T(8,128)(2,1)S(1)} all-to-all(bf16[16,128,128]{2,1,0:T(8,128)(2,1)S(1)} %get-tuple-element.25), channel_id=1, replica_groups={{19,18,17,16,11,10,9,8,3,2,1,0,27,26,25,24},{23,22,21,20,15,14,13,12,7,..., dimensions={0} | all-to-all | bytes 1048576 | tf_op jit(solution)/shard_map/all_to_all | solution.py:341
  47.0 0.0 copy-done.4
  47.0 1.7 %norm.1 = bf16[96,4096]{1,0:T(8,128)(2,1)} custom-call(f32[96,128]{1,0:T(8,128)S(1)} %get-tuple-element.19.idcol, f32[1,128]{1,0:T(1,128)S(1)} %get-tuple-element.24.before, f32[1,4096]{1,0:T(1,128)S(1)} %get-tuple-element.23.after.rates, bf16[96,4096]{1,0:T(8,128)(2,1)S(1)} %copy-done.3, bf16[2048,128]{1,0:T(8,128)(2,1)S(1)} %bitcast.3, ...), custom_call_target="tpu_custom_call" | custom-call | tf_op jit(solution)/shard_map/norm/pallas_call | solution.py:346
  (2 shorter events, 0.0 us)
Async XLA Ops:
  1.3 11.3 %all-to-all-start = ((f32[8,1,128]{2,1,0:T(1,128)}), f32[8,1,128]{2,1,0:T(1,128)S(1)}, u32[]{:S(2)}, u32[]{:S(2)}) async-start(f32[8,1,128]{2,1,0:T(1,128)} %broadcast_in_dim.4), calls=%async_computation | async-start | bytes 8192 | tf_op jit(solution)/shard_map/all_to_all | solution.py:274
  9.5 1.1 %copy-start = (bf16[96,4096]{1,0:T(8,128)(2,1)S(1)}, bf16[96,4096]{1,0:T(8,128)(2,1)}, u32[]{:S(2)}) copy-start(bf16[96,4096]{1,0:T(8,128)(2,1)} %k_ref.1) | copy-start | bytes 2359300
  10.7 1.1 %copy-start.1 = (bf16[96,4096]{1,0:T(8,128)(2,1)S(1)}, bf16[96,4096]{1,0:T(8,128)(2,1)}, u32[]{:S(2)}) copy-start(bf16[96,4096]{1,0:T(8,128)(2,1)} %v_ref.3) | copy-start | bytes 2359300
  12.7 18.5 %copy-start.2 = (bf16[96,4096]{1,0:T(8,128)(2,1)S(1)}, bf16[96,4096]{1,0:T(8,128)(2,1)}, u32[]{:S(2)}) copy-start(bf16[96,4096]{1,0:T(8,128)(2,1)} %v_ref.3) | copy-start | bytes 2359300
  12.7 18.5 %copy-start.3 = (bf16[96,4096]{1,0:T(8,128)(2,1)S(1)}, bf16[96,4096]{1,0:T(8,128)(2,1)}, u32[]{:S(2)}) copy-start(bf16[96,4096]{1,0:T(8,128)(2,1)} %q_ref.3) | copy-start | bytes 2359300
  26.3 8.1 %collective-permute-start = (bf16[3,136,128]{2,1,0:T(8,128)(2,1)S(1)}, bf16[3,136,128]{2,1,0:T(8,128)(2,1)S(1)}, u32[]{:S(2)}, u32[]{:S(2)}) collective-permute-start(bf16[3,136,128]{2,1,0:T(8,128)(2,1)S(1)} %get-tuple-element.18.after), channel_id=1, source_target_pairs={{0,4},{1,5},{2,6},{3,7},{4,0},{5,1},{6,2},{7,3},{8,12},{9,13},{10,... | collective-permute-start | bytes 313352 | tf_op jit(solution)/shard_map/ppermute | solution.py:313
  27.8 5.0 %collective-permute-start.1 = (bf16[1,136,128]{2,1,0:T(8,128)(2,1)S(1)}, bf16[1,136,128]{2,1,0:T(8,128)(2,1)S(1)}, u32[]{:S(2)}, u32[]{:S(2)}) collective-permute-start(bf16[1,136,128]{2,1,0:T(8,128)(2,1)S(1)} %get-tuple-element.22), channel_id=1, source_target_pairs={{0,4},{1,5},{2,6},{3,7},{8,12},{9,13},{10,14},{11,15},{16,20},{17,... | collective-permute-start | bytes 104456 | tf_op jit(solution)/shard_map/ppermute | solution.py:314
  32.4 14.6 %copy-start.4 = (f32[4096]{0:T(1024)S(1)}, f32[4096]{0:T(1024)}, u32[]{:S(2)}) copy-start(f32[4096]{0:T(1024)} %param.11) | copy-start | bytes 49156
